TPU v7x, 32 devices: a whole 2x2x4 slice. The times are simulated.
32 devices in a mesh: dp: 8 (over y, x, core), tensor: 4 (over z).
Axes of the slice: x: 2, y: 2, z: 4, core: 2. Of those that a mesh axis runs over, the one named last changes fastest.
Arguments:
- tokens: bfloat16 [16384, 1536], P(('dp', 'tensor')), may hold values from -6 to 6
- cotangent: bfloat16 [16384, 1536], P(('dp', 'tensor')), may hold values from -6 to 6
- seq_lengths: int32 [8, 4], P('dp'), may hold values from 1 to 1537, as said below
- attn_gain: bfloat16 [1536], P('dp'), may hold values from 0.25 to 1.75
- q_weight: bfloat16 [1536, 1536], P('dp', 'tensor'), may hold values from -0.15625 to 0.15625
- key_projection: bfloat16 [1536, 768], P('dp', 'tensor'), may hold values from -0.15625 to 0.15625
- value_projection: bfloat16 [1536, 768], P('dp', 'tensor'), may hold values from -0.15625 to 0.15625
- out_weight: bfloat16 [1536, 1536], P('dp', 'tensor'), may hold values from -0.875 to 0.875
- mlp_gain: bfloat16 [1536], P('dp'), may hold values from 0.25 to 1.75
- gate_weight: bfloat16 [1536, 4096], P('dp', 'tensor'), may hold values from -0.15625 to 0.15625
- up_weight: bfloat16 [1536, 4096], P('dp', 'tensor'), may hold values from -0.15625 to 0.15625
- down_weight: bfloat16 [1536, 4096], P('dp', 'tensor'), may hold values from -0.09375 to 0.09375
Outputs:
- output: bfloat16 [16384, 1536], P(('dp', 'tensor'))
- input_grad: float32 [16384, 1536], P(('dp', 'tensor'))
- attn_gain_grad: float32 [1536], P('dp')
- q_weight_grad: float32 [1536, 1536], P('dp', 'tensor')
- k_weight_grad: float32 [1536, 768], P('dp', 'tensor')
- v_weight_grad: float32 [1536, 768], P('dp', 'tensor')
- out_weight_grad: float32 [1536, 1536], P('dp', 'tensor')
- mlp_gain_grad: float32 [1536], P('dp')
- gate_weight_grad: float32 [1536, 4096], P('dp', 'tensor')
- up_weight_grad: float32 [1536, 4096], P('dp', 'tensor')
- down_weight_grad: float32 [1536, 4096], P('dp', 'tensor')
Inputs may be any that keep to these rules, and one draw needn't show every extreme that they name: Each row of seq_lengths sums to 2048. In each row one document, at a position drawn from the seed, has exactly 1537 tokens; the other documents of the row together hold 511 tokens.
All inputs are finite; a program needn't handle non-finite values.
Results may differ from a plain program's by a relative error of at most 0.02.
Values may be sent and summed in bfloat16 or wider, within the bound.
No kernel may reach another device: no remote copies, remote signals or barrier semaphores. Data moves between devices by JAX's collectives and lax.ppermute only.
A program may use at most 192 MiB of HBM per device.

v0:
```python
import functools
import math

import jax
import jax.numpy as jnp
import numpy as np
from jax import lax
from jax.experimental import pallas as pl
from jax.experimental.pallas import tpu as pltpu
from jax.sharding import Mesh
from jax.sharding import PartitionSpec as P

HD = 96
HALF = HD // 2
PAD = 128
STEPS = 2
SUB = 256
TILE = 512

EPSILON = 1e-05
ROTARY_BASE = 100000.0
MASKED = -1e30
LOG2E = math.log2(math.e)

AXES = ("yx", "core", "zh", "zl")
FLIP = [(0, 1), (1, 0)]


def norm_rows(values, gain):
    row_scale = lax.rsqrt(jnp.mean(values * values, axis=-1, keepdims=True) + EPSILON)
    return (row_scale, (values * row_scale * gain).astype(jnp.bfloat16))


def norm_back(values, row_scale, gain, upstream):
    weighted = upstream * gain
    inner_sum = jnp.mean(weighted * values, axis=-1, keepdims=True)
    grad_in = row_scale * weighted - values * (row_scale * row_scale * row_scale) * inner_sum
    gain_part = jnp.sum(upstream * (values * row_scale), axis=0)
    return (grad_in, gain_part)


def document_layout(lengths, group_rows):
    flat_lengths = lengths.reshape(-1)
    doc_ends = jnp.cumsum(flat_lengths)
    rows = jnp.arange(group_rows, dtype=jnp.int32)
    passed = (rows[:, None] >= doc_ends[None, :]).astype(jnp.int32)
    return (rows, jnp.sum(passed * flat_lengths[None, :], axis=1))


def rotary_tables(positions):
    exponents = jnp.arange(HALF, dtype=jnp.float32) * (2.0 / HD)
    inverse = ROTARY_BASE ** (-exponents)
    angles = positions.astype(jnp.float32)[:, None] * inverse[None, :]
    cosine, sine = jnp.cos(angles), jnp.sin(angles)
    gap = jnp.zeros((positions.shape[0], PAD // 2 - HALF), jnp.float32)
    return (
        jnp.concatenate([cosine, gap, cosine, gap], axis=1),
        jnp.concatenate([-sine, gap, sine, gap], axis=1),
    )


def rows_product(left, right):
    return lax.dot_general(
        left, right, (((0,), (0,)), ((), ())), preferred_element_type=jnp.float32
    )


def times_transpose(left, right):
    return lax.dot_general(
        left, right, (((1,), (1,)), ((), ())), preferred_element_type=jnp.float32
    )


def dot32(left, right):
    return jnp.dot(left, right, preferred_element_type=jnp.float32)


def stage(*values):
    return lax.optimization_barrier(values)


def spread(columns, heads):
    matrix = np.zeros((columns, len(heads) * PAD), np.float32)
    for at, first in enumerate(heads):
        for half in range(2):
            for i in range(HALF):
                matrix[first + half * HALF + i, at * PAD + half * (PAD // 2) + i] = 1.0
    return matrix


def turn(x, cosine, sine):
    return x * cosine + pltpu.roll(x, PAD // 2, 1) * sine


def rows_at(t, size):
    return pl.ds(pl.multiple_of(t * size, size), size)


def forward_kernel(pieces, ratio, *refs):
    place, low, full, cosine, sine, start, spread_in, gather_out = refs[:8]
    heads = spread_in.shape[0]
    refs = refs[8:]
    qkv, context, refs = refs[0], refs[1 : 1 + pieces], refs[1 + pieces :]
    log_sum, refs = refs[:heads], refs[heads:]
    q_s, k_s, v_s, s_s, top_s, acc = refs
    tiles = q_s.shape[0]
    all_subs = qkv.shape[0] // SUB
    piece_subs = all_subs // pieces
    scale = LOG2E * HD ** (-0.5)
    ones_lane = lax.broadcasted_iota(jnp.int32, (SUB, PAD), 1) == PAD - 1

    def prepare(r, carry):
        t = place[r]
        at = rows_at(t, SUB)
        cos_t, sin_t = cosine[at, :], sine[at, :]
        tile, half = t // (TILE // SUB), t % (TILE // SUB)
        for g in range(heads):
            wide = dot32(qkv[rows_at(r, SUB), :], spread_in[g])
            for h in range(ratio):
                query = turn(wide[:, h * PAD : (h + 1) * PAD], cos_t, sin_t) * scale
                first = pl.multiple_of(h * TILE + half * SUB, SUB)
                q_s[tile, g, pl.ds(first, SUB), :] = query.astype(jnp.bfloat16)
            key = turn(wide[:, ratio * PAD : (ratio + 1) * PAD], cos_t, sin_t)
            k_s[g, at, :] = key.astype(jnp.bfloat16)
            value = jnp.where(ones_lane, 1.0, wide[:, (ratio + 1) * PAD :])
            v_s[g, at, :] = value.astype(jnp.bfloat16)
        return carry

    lax.fori_loop(0, all_subs, prepare, 0)

    def query_tile(i, carry):
        starts = jnp.concatenate([start[rows_at(i, TILE), :]] * ratio, axis=0)
        top_s[...] = jnp.full_like(top_s, MASKED)

        def scores(j, masked, diagonal):
            for g in range(heads):
                s = times_transpose(q_s[i, g], k_s[g, rows_at(j, TILE), :])
                if masked:
                    key_at = lax.broadcasted_iota(jnp.int32, s.shape, 1)
                    allowed = key_at + j * TILE >= starts
                    if diagonal:
                        query_at = lax.rem(lax.broadcasted_iota(jnp.int32, s.shape, 0), TILE)
                        allowed = allowed & (key_at <= query_at)
                    s = jnp.where(allowed, s, MASKED)
                s_s[g, j] = s
                peak = s[:, :PAD]
                for c in range(1, TILE // PAD):
                    peak = jnp.maximum(peak, s[:, c * PAD : (c + 1) * PAD])
                top_s[g] = jnp.maximum(top_s[g], peak)

        def loop(first, last, masked):
            def run(j, c):
                scores(j, masked, False)
                return c

            lax.fori_loop(first, last, run, 0)

        loop(low[i], full[i], True)
        loop(full[i], i, False)
        scores(i, True, True)
        tops = [jnp.max(top_s[g], axis=1, keepdims=True) for g in range(heads)]
        acc[...] = jnp.zeros_like(acc)

        def weigh(j, c):
            for g in range(heads):
                p = jnp.exp2(s_s[g, j] - tops[g]).astype(jnp.bfloat16)
                acc[g] += dot32(p, v_s[g, rows_at(j, TILE), :])
            return c

        lax.fori_loop(low[i], i + 1, weigh, 0)
        packed = None
        for g in range(heads):
            total = acc[g][:, PAD - 1 :]
            out = acc[g] * (1.0 / total)
            sums = jnp.broadcast_to(tops[g] + jnp.log(total) * LOG2E, (ratio * TILE, PAD))
            log_sum[g][i] = sums.T[:1, :]
            wide = jnp.concatenate(
                [out[h * TILE : (h + 1) * TILE, :] for h in range(ratio)], axis=1
            ).astype(jnp.bfloat16)
            part = dot32(wide, gather_out[g])
            packed = part if packed is None else packed + part
        subs = tiles * (TILE // SUB)
        for half in range(TILE // SUB):
            r = place[subs + i * (TILE // SUB) + half]
            part = packed[half * SUB : (half + 1) * SUB, :].astype(jnp.bfloat16)
            for k in range(pieces):

                @pl.when(r // piece_subs == k)
                def store(k=k, part=part, r=r):
                    context[k][rows_at(r % piece_subs, SUB), :] = part

        return carry

    lax.fori_loop(0, tiles, query_tile, 0)


def backward_kernel(pieces, ratio, more, *refs):
    place, low, full, cosine, sine, start, refs = *refs[:6], refs[6:]
    heads = refs[0].shape[0]
    spread_in, spread_out, gather_in, refs = *refs[:3], refs[3:]
    log_sum, refs = refs[:heads], refs[heads:]
    d_context, context, qkv, refs = refs[:pieces], refs[pieces : 2 * pieces], refs[2 * pieces], refs[2 * pieces + 1 :]
    earlier, refs = (refs[0], refs[1:]) if more else (None, refs)
    d_qkv, refs = refs[0], refs[1:]
    q_s, k_s, kt_s, v_s, do_s, delta_s, log_s, dq_acc, dk_acc, dv_acc, dq_s = refs
    tiles = q_s.shape[0]
    all_subs = qkv.shape[0] // SUB
    piece_subs = all_subs // pieces
    scale = HD ** (-0.5)
    per_tile = TILE // SUB

    for k in range(pieces):

        def prepare(r, carry, k=k):
            t = place[k * piece_subs + r]
            rel = rows_at(r, SUB)
            at = rows_at(t, SUB)
            cos_t, sin_t = cosine[at, :], sine[at, :]
            for g in range(heads):
                wide = dot32(qkv[rows_at(k * piece_subs + r, SUB), :], spread_in[g])
                d_out = dot32(d_context[k][rel, :], spread_out[g])
                out = dot32(context[k][rel, :], spread_out[g])
                for h in range(ratio):
                    cols = slice(h * PAD, (h + 1) * PAD)
                    rows = slice(h * SUB, (h + 1) * SUB)
                    query = turn(wide[:, cols], cos_t, sin_t) * (scale * LOG2E)
                    q_s[t, g, rows, :] = query.astype(jnp.bfloat16)
                    do_s[t, g, rows, :] = d_out[:, cols].astype(jnp.bfloat16)
                    delta = jnp.sum((d_out[:, cols] * out[:, cols]).T, axis=0, keepdims=True)
                    delta_s[t * heads + g, :, rows] = delta
                    first = pl.multiple_of(h * TILE + t % per_tile * SUB, SUB)
                    log_s[t * heads + g, :, rows] = log_sum[g][t // per_tile, :, pl.ds(first, SUB)]
                key = turn(wide[:, ratio * PAD : (ratio + 1) * PAD], cos_t, sin_t)
                k_s[g, t] = key.astype(jnp.bfloat16)
                kt_s[g, t] = key.T.astype(jnp.bfloat16)
                v_s[g, t] = wide[:, (ratio + 1) * PAD :].astype(jnp.bfloat16)
                dk_acc[g, t] = jnp.zeros((SUB, PAD), jnp.float32)
                dv_acc[g, t] = jnp.zeros((SUB, PAD), jnp.float32)
            return carry

        lax.fori_loop(0, piece_subs, prepare, 0)

    def query_tile(i, carry):
        dq_acc[...] = jnp.zeros_like(dq_acc)

        def step(j, masked, diagonal):
            for g in range(heads):
                queries, d_out = q_s[i, g], do_s[i, g]
                s = times_transpose(k_s[g, j], queries)
                if masked:
                    key_at = lax.broadcasted_iota(jnp.int32, s.shape, 0)
                    allowed = key_at + j * SUB >= start[i]
                    if diagonal:
                        query_at = lax.rem(lax.broadcasted_iota(jnp.int32, s.shape, 1), SUB)
                        allowed = allowed & (key_at <= query_at)
                    s = jnp.where(allowed, s, MASKED)
                p = jnp.exp2(s - log_s[i * heads + g])
                d_p = times_transpose(v_s[g, j], d_out)
                d_s = (p * (d_p - delta_s[i * heads + g])).astype(jnp.bfloat16)
                dv_acc[g, j] += dot32(p.astype(jnp.bfloat16), d_out)
                dk_acc[g, j] += dot32(d_s, queries)
                dq_acc[g] += dot32(kt_s[g, j], d_s)

        def loop(first, last, masked):
            def run(j, c):
                step(j, masked, False)
                return c

            lax.fori_loop(first, last, run, 0)

        loop(low[i], full[i], True)
        loop(full[i], i, False)
        step(i, True, True)
        at = rows_at(i, SUB)
        cos_t, sin_t = cosine[at, :], sine[at, :]
        for g in range(heads):
            grad = dq_acc[g].T * scale
            for h in range(ratio):
                piece = turn(grad[h * SUB : (h + 1) * SUB, :], cos_t, -sin_t)
                dq_s[g, i, :, h * PAD : (h + 1) * PAD] = piece.astype(jnp.bfloat16)
        return carry

    lax.fori_loop(0, tiles, query_tile, 0)

    def finish(r, carry):
        t = place[r]
        at = rows_at(t, SUB)
        rel = rows_at(r, SUB)
        packed = None
        for g in range(heads):
            key = turn(dk_acc[g, t] * (1.0 / LOG2E), cosine[at, :], -sine[at, :])
            wide = jnp.concatenate(
                [dq_s[g, t], key.astype(jnp.bfloat16), dv_acc[g, t].astype(jnp.bfloat16)], axis=1
            )
            part = dot32(wide, gather_in[g])
            packed = part if packed is None else packed + part
        packed = packed.astype(jnp.bfloat16)
        d_qkv[rel, :] = packed + earlier[rel, :] if more else packed
        return carry

    lax.fori_loop(0, all_subs, finish, 0)


SMEM = pl.BlockSpec(memory_space=pltpu.SMEM)
VMEM = pl.BlockSpec(memory_space=pltpu.VMEM)
ANY = pl.BlockSpec(memory_space=pl.ANY)


def small_cost(transcendentals=0):
    return pl.CostEstimate(flops=1 << 20, bytes_accessed=1 << 16, transcendentals=transcendentals)


def head_matrices(head, q_heads, kv_heads):
    ratio = q_heads // kv_heads
    queries = [(head * ratio + r) * HD for r in range(ratio)]
    key, value = (q_heads + head) * HD, (q_heads + kv_heads + head) * HD
    inner = spread((q_heads + 2 * kv_heads) * HD, [*queries, key, value])
    outer = spread(q_heads * HD, queries)
    return jnp.asarray(inner, jnp.bfloat16), jnp.asarray(outer, jnp.bfloat16)


def stacked_matrices(q_heads, kv_heads):
    pairs = [head_matrices(head, q_heads, kv_heads) for head in range(kv_heads)]
    return jnp.stack([inner for inner, _ in pairs]), jnp.stack([outer for _, outer in pairs])


def attend(qkv, pieces, layout, q_heads, kv_heads):
    place, low, full, cosine, sine, start_column = layout
    ratio, rows = q_heads // kv_heads, qkv.shape[0]
    tiles, lanes = rows // TILE, ratio * TILE
    bf16, f32 = jnp.bfloat16, jnp.float32
    inner, outer = stacked_matrices(q_heads, kv_heads)
    outs = pl.pallas_call(
        functools.partial(forward_kernel, pieces, ratio),
        out_shape=[
            *[jax.ShapeDtypeStruct((rows // pieces, q_heads * HD), bf16)] * pieces,
            *[jax.ShapeDtypeStruct((tiles, 1, lanes), f32)] * kv_heads,
        ],
        in_specs=[SMEM] * 3 + [VMEM] * 6,
        out_specs=[VMEM] * (pieces + kv_heads),
        scratch_shapes=[
            pltpu.VMEM((tiles, kv_heads, lanes, PAD), bf16),
            pltpu.VMEM((kv_heads, rows, PAD), bf16),
            pltpu.VMEM((kv_heads, rows, PAD), bf16),
            pltpu.VMEM((kv_heads, tiles, lanes, TILE), f32),
            pltpu.VMEM((kv_heads, lanes, PAD), f32),
            pltpu.VMEM((kv_heads, lanes, PAD), f32),
        ],
        compiler_params=pltpu.CompilerParams(vmem_limit_bytes=60 * 2**20),
        cost_estimate=small_cost(),
        name="attention_forward",
    )(place, low, full, cosine, sine, start_column, inner, jnp.swapaxes(outer, 1, 2), qkv)
    return outs[:pieces], outs[pieces:]


def attend_back(heads, qkv, d_context, context, sums, earlier, layout, q_heads, kv_heads):
    place, low, full, cosine, sine, start_row = layout
    pieces, ratio, rows = len(context), q_heads // kv_heads, qkv.shape[0]
    tiles, lanes, count = rows // SUB, ratio * SUB, len(heads)
    bf16, f32 = jnp.bfloat16, jnp.float32
    inner, outer = stacked_matrices(q_heads, kv_heads)
    inner, outer = inner[heads[0] : heads[0] + count], outer[heads[0] : heads[0] + count]
    return pl.pallas_call(
        functools.partial(backward_kernel, pieces, ratio, bool(earlier)),
        out_shape=jax.ShapeDtypeStruct(qkv.shape, bf16),
        in_specs=[SMEM] * 3 + [VMEM] * (7 + count + 2 * pieces + len(earlier)),
        out_specs=VMEM,
        scratch_shapes=[
            pltpu.VMEM((tiles, count, lanes, PAD), bf16),
            pltpu.VMEM((count, tiles, SUB, PAD), bf16),
            pltpu.VMEM((count, tiles, PAD, SUB), bf16),
            pltpu.VMEM((count, tiles, SUB, PAD), bf16),
            pltpu.VMEM((tiles, count, lanes, PAD), bf16),
            pltpu.VMEM((tiles * count, 1, lanes), f32),
            pltpu.VMEM((tiles * count, 1, lanes), f32),
            pltpu.VMEM((count, PAD, lanes), f32),
            pltpu.VMEM((count, tiles, SUB, PAD), f32),
            pltpu.VMEM((count, tiles, SUB, PAD), f32),
            pltpu.VMEM((count, tiles, SUB, ratio * PAD), bf16),
        ],
        compiler_params=pltpu.CompilerParams(vmem_limit_bytes=60 * 2**20),
        cost_estimate=small_cost(),
        name=f"attention_backward_{heads[0]}",
    )(
        place, low, full, cosine, sine, start_row, inner, outer, jnp.swapaxes(inner, 1, 2),
        *[sums[h] for h in heads], *d_context, *context, qkv, *earlier,
    )


def fetch(me, where, sources, target, sems):
    copies = []
    for n, (source, (j, deep, first, column, taken)) in enumerate(zip(sources, where, strict=True)):
        cols = min(source.shape[1] - taken, target.shape[1] - column)
        at = pl.ds(pl.multiple_of((me[0] ^ j) * deep + first, 16), source.shape[0])
        if cols != source.shape[1]:
            source = source.at[:, taken : taken + cols]
        copies.append(pltpu.make_async_copy(source, target.at[at, column : column + cols], sems.at[n]))
    return copies


def take_rows(parts, target):
    rows = target.shape[0]
    at = 0
    for part in parts:

        @pl.when(pl.program_id(0) == at // rows)
        def take(part=part, at=at):
            target[at % rows : at % rows + part.shape[0], :] = part[...]

        at += part.shape[0]


def at_first_step(copies, what):
    @pl.when(pl.program_id(0) == 0)
    def run():
        for copy in copies:
            what(copy)


def project_kernel(count, where, more, me, *refs):
    parts, gain, refs = refs[:count], refs[count], refs[count + 1 :]
    sources, refs = refs[: len(where[0])], refs[len(where[0]) :]
    norm_all, qkv_all, weight, sems, rows_s = refs[2 if more else 0 :]
    copies = fetch(me, where[0], sources, weight, sems)
    at_first_step(copies, lambda copy: copy.start())
    take_rows(parts, rows_s)
    x = rows_s[...].astype(jnp.float32)
    scale = lax.rsqrt(jnp.mean(x * x, axis=-1, keepdims=True) + EPSILON)
    norm_all[...] = (x * scale * gain[...]).astype(jnp.bfloat16)
    at_first_step(copies, lambda copy: copy.wait())
    qkv_all[...] = dot32(norm_all[...], weight[...]).astype(jnp.bfloat16)


def gate_kernel(count, where, more, me, *refs):
    parts, refs = refs[:count], refs[count:]
    sources, refs = refs[: len(where[0])], refs[len(where[0]) :]
    norm_all, gate_up_all, hidden_all, weight, sems = refs[3 if more else 0 :]
    hidden_cols = hidden_all.shape[1]
    copies = fetch(me, where[0], sources, weight, sems)
    at_first_step(copies, lambda copy: copy.start())
    take_rows(parts, norm_all)
    at_first_step(copies, lambda copy: copy.wait())
    x = norm_all[...]
    width = min(512, hidden_cols)
    for at in range(0, hidden_cols, width):
        gate_at = slice(at, at + width)
        up_at = slice(hidden_cols + at, hidden_cols + at + width)
        gate = dot32(x, weight[:, gate_at])
        up = dot32(x, weight[:, up_at])
        gate_up_all[:, gate_at] = gate
        gate_up_all[:, up_at] = up
        hidden_all[:, gate_at] = (gate * (1.0 / (1.0 + jnp.exp(-gate))) * up).astype(jnp.bfloat16)


def gate_back_kernel(count, where, more, me, *refs):
    parts, gate_up_all, hidden_other, refs = refs[:count], *refs[count : count + 2], refs[count + 2 :]
    gate_up, refs = refs[: len(where[0])], refs[len(where[0]) :]
    down, refs = refs[: len(where[1])], refs[len(where[1]) :]
    refs = refs[2 if more else 0 :]
    grad_all, d_gate_up_all, d_norm_own, d_norm_sib, out_own, out_sib = refs[:6]
    w_gate_up, gate_up_sems, w_down, down_sems = refs[6:]
    hidden_cols = w_down.shape[1]
    down_copies = fetch(me, where[1], down, w_down, down_sems)
    copies = fetch(me, where[0], gate_up, w_gate_up, gate_up_sems)
    at_first_step(down_copies + copies, lambda copy: copy.start())
    take_rows(parts, grad_all)
    at_first_step(down_copies, lambda copy: copy.wait())
    dy = grad_all[...]
    width = min(512, hidden_cols)
    for at in range(0, hidden_cols, width):
        gate_at = slice(at, at + width)
        up_at = slice(hidden_cols + at, hidden_cols + at + width)
        d_hidden = dot32(dy, w_down[:, gate_at])
        gate, up = gate_up_all[:, gate_at], gate_up_all[:, up_at]
        sigmoid = 1.0 / (1.0 + jnp.exp(-gate))
        d_gate = d_hidden * up * sigmoid * (1.0 + gate * (1.0 - sigmoid))
        d_gate_up_all[:, gate_at] = d_gate.astype(jnp.bfloat16)
        d_gate_up_all[:, up_at] = (d_hidden * (gate * sigmoid)).astype(jnp.bfloat16)
    out = times_transpose(hidden_other[...], w_down[...]).astype(jnp.bfloat16)
    at_first_step(copies, lambda copy: copy.wait())
    d_norm = times_transpose(d_gate_up_all[...], w_gate_up[...]).astype(jnp.bfloat16)

    @pl.when(pl.program_id(0) == 0)
    def to_own():
        d_norm_own[...] = d_norm
        out_own[...] = out

    @pl.when(pl.program_id(0) != 0)
    def to_sibling():
        d_norm_sib[...] = d_norm
        out_sib[...] = out


def piece_call(kernel, name, k, pieces, me, parts, whole, tiled, fetched, earlier, outs):
    tile, width = sum(x.shape[0] for x in parts) // STEPS, parts[0].shape[1]
    count = len(parts)

    def rows_of(piece):
        return lambda i: (piece * STEPS + i, 0)

    sources = [x for arrays, _, _ in fetched for x in arrays]
    first_earlier = 1 + count + len(whole) + len(tiled) + len(sources)
    scratch = []
    for arrays, _, cols in fetched:
        scratch += [pltpu.VMEM((width, cols), jnp.bfloat16), pltpu.SemaphoreType.DMA((len(arrays),))]
    if kernel is project_kernel:
        scratch.append(pltpu.VMEM((tile, width), jnp.bfloat16))
    return pl.pallas_call(
        functools.partial(kernel, count, tuple(where for _, where, _ in fetched), bool(earlier)),
        grid=(STEPS,),
        out_shape=[
            jax.ShapeDtypeStruct((pieces * STEPS * tile if span == "all" else tile, columns), kind)
            for columns, kind, span in outs
        ],
        in_specs=[
            SMEM,
            *(pl.BlockSpec(x.shape, lambda i: (0, 0)) for x in parts),
            *(pl.BlockSpec(x.shape, lambda i: (0, 0)) for x in whole),
            *(pl.BlockSpec((tile, x.shape[1]), rows_of(piece)) for x, piece in tiled),
            *[ANY] * (len(sources) + len(earlier)),
        ],
        out_specs=[
            pl.BlockSpec((tile, columns), rows_of(k) if span == "all" else lambda i: (0, 0))
            for columns, kind, span in outs
        ],
        scratch_shapes=scratch,
        input_output_aliases={first_earlier + n: n for n in range(len(earlier))},
        compiler_params=pltpu.CompilerParams(vmem_limit_bytes=60 * 2**20),
        cost_estimate=small_cost(),
        name=f"{name}_{k}",
    )(me, *parts, *whole, *(x for x, _ in tiled), *sources, *earlier)


def assemble_kernel(where, me, *refs):
    sources, whole, sems = refs[: len(where)], refs[len(where)], refs[len(where) + 1]
    copies = fetch(me, where, sources, whole, sems)
    for copy in copies:
        copy.start()
    for copy in copies:
        copy.wait()


def assemble(name, me, arrays, where, rows, cols):
    return pl.pallas_call(
        functools.partial(assemble_kernel, where),
        out_shape=jax.ShapeDtypeStruct((rows, cols), arrays[0].dtype),
        in_specs=[SMEM, *[ANY] * len(arrays)],
        out_specs=VMEM,
        scratch_shapes=[pltpu.SemaphoreType.DMA((len(arrays),))],
        compiler_params=pltpu.CompilerParams(vmem_limit_bytes=60 * 2**20),
        cost_estimate=small_cost(),
        name=name,
    )(me, *arrays)


def flip(x, axis):
    return lax.ppermute(x, axis, FLIP)


CROSS = [(1, 2), (2, 1)]
OUT = [(0, 1), (3, 2), (2, 0), (1, 3)]
BACK = [(1, 0), (2, 3), (0, 2), (3, 1)]


def crossed(x, perm):
    return lax.ppermute(x, ("core", "zh"), perm)


def straight():
    return lax.axis_index("core") == lax.axis_index("zh")


def swap(x):
    return jnp.where(straight(), x, crossed(x, CROSS))


def send_z(w):
    return crossed(w, OUT), crossed(w, CROSS)


def pair_of(w, out, cross):
    zh = lax.axis_index("zh")
    x = jnp.where(straight(), w, cross)
    return jnp.concatenate([jnp.where(zh == 0, x, out), jnp.where(zh == 0, out, x)], axis=0)


def give_z(part):
    zh = lax.axis_index("zh")
    half = part.shape[0] // 2
    upper, lower = part[:half], part[half:]
    return jnp.where(zh == 0, upper, lower), jnp.where(zh == 0, lower, upper)


def sum_z(keep, back, cross):
    return back.astype(jnp.float32) + jnp.where(straight(), keep, cross).astype(jnp.float32)


def shift(x, e, k):
    n = lax.axis_size("zl")
    return lax.ppermute(
        x, ("core", "zl"), [(c * n + l, (c ^ e) * n + (l + k) % n) for c in range(2) for l in range(n)]
    )


def from_near(x, k):
    n = lax.axis_size("zl")
    return lax.ppermute(x, "zl", [((j + k) % n, j) for j in range(n)])


def to_near(x, k):
    n = lax.axis_size("zl")
    return lax.ppermute(x, "zl", [(j, (j + k) % n) for j in range(n)])


def across(x, j):
    n = lax.axis_size("yx")
    return lax.ppermute(x, "yx", [(a, a ^ j) for a in range(n)])


def neighbours(x):
    count = lax.axis_size("yx")
    return [across(x, j) for j in range(1, count if count != 4 else 3)]


def diagonal(taken):
    if lax.axis_size("yx") != 4:
        return []
    half = taken[0].shape[0] // 2
    return [across(taken[1][:half], 1), across(taken[0][half:], 2)]


def blocks_of(own, taken, halves, column=0, source_column=0):
    deep = own.shape[0]
    arrays = [own, *taken, *halves]
    where = [(j, deep, 0, column, source_column) for j in range(1 + len(taken))]
    where += [(3, deep, n * deep // 2, column, source_column) for n in range(len(halves))]
    return arrays, tuple(where)


def whole_weight(w):
    return [w], ((0, 0, 0, 0, 0),)


def block_of(grad, j, columns):
    size = grad.shape[0] // lax.axis_size("yx")
    first = (lax.axis_index("yx") ^ j) * size
    return lax.dynamic_slice(grad, (first, columns[0]), (size, columns[1] - columns[0]))


def send_yx(grad, columns):
    count = lax.axis_size("yx")
    if count != 4:
        return [across(block_of(grad, j, columns), j) for j in range(1, count)]
    far = block_of(grad, 3, columns)
    half = far.shape[0] // 2
    return [across(far[:half], 1), across(far[half:], 2)]


def join_yx(grad, columns, taken):
    if lax.axis_size("yx") != 4:
        return taken, block_of(grad, 0, columns)
    half = taken[0].shape[0]
    one, two = block_of(grad, 1, columns), block_of(grad, 2, columns)
    one = jnp.concatenate([one[:half], one[half:] + taken[1]], axis=0)
    two = jnp.concatenate([two[:half] + taken[0], two[half:]], axis=0)
    return [across(one, 1), across(two, 2)], block_of(grad, 0, columns)


def total_yx(taken, own):
    total = own.astype(jnp.float32)
    for part in taken:
        total = total + part.astype(jnp.float32)
    return total.astype(jnp.bfloat16)


def body(
    tokens,
    cotangent,
    seq_lengths,
    attn_gain,
    q_weight,
    key_projection,
    value_projection,
    out_weight,
    mlp_gain,
    gate_weight,
    up_weight,
    down_weight,
):
    bf16, f32 = jnp.bfloat16, jnp.float32
    core, zl, yx = lax.axis_index("core"), lax.axis_index("zl"), lax.axis_index("yx")
    near = lax.axis_size("zl")
    others = range(1, near)
    rows = tokens.shape[0]
    group_rows = 2 * near * rows
    query_cols, key_cols = q_weight.shape[1], key_projection.shape[1]
    qkv_cols = query_cols + 2 * key_cols
    q_heads, kv_heads = query_cols // HD, key_cols // HD
    hidden_cols = gate_weight.shape[1]
    me = yx.astype(jnp.int32).reshape(1)

    qkv_shard = jnp.concatenate([q_weight, key_projection, value_projection], axis=1)
    gate_up_shard = jnp.concatenate([gate_weight, up_weight], axis=1)
    part_rows = rows // 2
    upper = swap(tokens[:part_rows])
    shard = jnp.concatenate([qkv_shard, out_weight], axis=1)
    shard_moved = send_z(shard)
    lengths = swap(seq_lengths)
    gains = lax.all_gather(jnp.stack([attn_gain, mlp_gain]), ("yx", "core"), axis=1, tiled=True).astype(f32)
    upper, lengths, second_part, gains, *shard_moved = stage(upper, lengths, tokens[part_rows:], gains, *shard_moved)
    gain_one, gain_two = gains[0], gains[1]

    upper_far = [from_near(upper, k) for k in others]
    lower = swap(second_part)
    pair, out_pair = (
        pair_of(*(x[:, cols] for x in (shard, *shard_moved))) for cols in (slice(0, qkv_cols), slice(qkv_cols, None))
    )
    taken = neighbours(pair)
    upper_sib = flip(upper, "core")

    subs = jnp.arange(group_rows // SUB, dtype=jnp.int32)
    per_device = rows // SUB
    source, within = subs // per_device, subs % per_device
    there_core, there_zl = (source % 2) ^ core, (source // 2 + zl) % near
    to_order = (there_core * near + there_zl) * per_device + within
    from_order = (((source % near - zl) % near) * 2 + ((source // near) ^ core)) * per_device + within
    place = jnp.concatenate([to_order, from_order])
    row_at, doc_start = document_layout(lengths, group_rows)
    cosine, sine = rotary_tables(row_at - doc_start)

    def bounds(size):
        tile_start = doc_start.reshape(-1, size)
        tile = jnp.arange(group_rows // size, dtype=jnp.int32)
        low = tile_start[:, 0] // size
        return low, jnp.minimum((tile_start[:, -1] + size - 1) // size, tile)

    start_row = jnp.tile(doc_start.reshape(-1, 1, SUB), (1, 1, q_heads // kv_heads))
    layout = (place, *bounds(TILE), cosine, sine, doc_start[:, None])
    layout_back = (place, *bounds(SUB), cosine, sine, start_row)
    lower, upper_sib, out_pair, *moved = stage(lower, upper_sib, out_pair, *upper_far, *taken, *layout, *layout_back)
    upper_far, moved = moved[: near - 1], moved[near - 1 :]
    taken, moved = moved[: len(taken)], moved[len(taken) :]
    layout, layout_back = moved[: len(layout)], moved[len(layout) :]

    lower_far = [from_near(lower, k) for k in others]
    lower_sib = flip(lower, "core")
    out_far = [from_near(out_pair, k) for k in others]
    blocks = blocks_of(pair, taken, diagonal(taken))
    projecting = [(*blocks, qkv_cols)]
    gain_row = gain_one[None]
    outs = [(tokens.shape[1], bf16, "all"), (qkv_cols, bf16, "all")]
    parts = [upper, lower, upper_sib, lower_sib]
    normed = piece_call(project_kernel, "project", 0, near, me, parts, [gain_row], [], projecting, [], outs)
    gate_up_shard, *moved = stage(gate_up_shard, *lower_far, *out_far, *normed)
    lower_far, out_far, normed = moved[: near - 1], moved[near - 1 : 2 * near - 2], moved[2 * near - 2 :]

    out_own = jnp.concatenate([out_pair, *out_far], axis=1)
    out_taken = neighbours(out_own)
    for k in others:
        parts = [upper_far[k - 1], lower_far[k - 1], flip(upper_far[k - 1], "core"), flip(lower_far[k - 1], "core")]
        normed = piece_call(project_kernel, "project", k, near, me, parts, [gain_row], [], projecting, normed, outs)
    norm_one, qkv = normed
    gate_up_shard, qkv, out_own, *out_taken = stage(gate_up_shard, qkv, out_own, *out_taken)

    gate_up_moved = send_z(gate_up_shard)
    out_halves = diagonal(out_taken)
    context, sums = attend(qkv, 2 * near, layout, q_heads, kv_heads)
    down_shard, cotangent, *moved = stage(down_weight, cotangent, *context, *gate_up_moved, *out_halves)
    context, gate_up_moved, out_halves = moved[: 2 * near], moved[2 * near : 2 * near + 2], moved[2 * near + 2 :]

    quarters = {(0, 0): context[0]}
    for k in range(near):
        for e in range(2):
            if (e, k) != (0, 0):
                quarters[e, (near - k) % near] = shift(context[2 * k + e], e, k)
    pairs = [
        pair_of(*(x[:, n * hidden_cols : (n + 1) * hidden_cols] for x in (gate_up_shard, *gate_up_moved)))
        for n in range(2)
    ]
    gate_taken = neighbours(pairs[0])
    order = [(e, k) for e in range(2) for k in range(near)]
    up_pair, down_shard, cotangent, *moved = stage(
        pairs[1], down_shard, cotangent, *(quarters[at] for at in order), *gate_taken, *out_halves
    )
    quarters, moved = moved[: 2 * near], moved[2 * near :]
    gate_taken, out_halves = moved[: len(gate_taken)], moved[len(gate_taken) :]

    up_taken = neighbours(up_pair)
    cot_upper = crossed(cotangent[:part_rows], CROSS)
    w_out_near = assemble(
        "assemble_out", me, *blocks_of(out_own, out_taken, out_halves), tokens.shape[1], near * query_cols
    )
    w_out_sib = flip(w_out_near, "core")
    residual = jnp.concatenate([upper, lower], axis=0).astype(f32)
    scale_one = lax.rsqrt(jnp.mean(residual * residual, axis=-1, keepdims=True) + EPSILON)
    w_out_sib, w_out_near, scale_one, cotangent, cot_upper, down_shard, *up_taken = stage(
        w_out_sib, w_out_near, scale_one, cotangent, cot_upper, down_shard, *up_taken
    )

    gate_halves = diagonal(gate_taken)
    down_moved = send_z(down_shard)
    own_context = jnp.concatenate(quarters[:near], axis=1)
    sib_context = jnp.concatenate(quarters[near:], axis=1)
    mid = residual + times_transpose(own_context, w_out_near) + times_transpose(sib_context, w_out_sib)
    scale_two, norm_two = norm_rows(mid, gain_two)
    norm_two, cotangent, cot_upper, *moved = stage(norm_two, cotangent, cot_upper, *gate_halves, *down_moved)
    gate_halves, down_moved = moved[:-2], moved[-2:]

    upper_far = [from_near(norm_two[:part_rows], k) for k in others]
    up_halves = diagonal(up_taken)
    norm_sib = flip(norm_two, "core")
    cot_lower = crossed(cotangent[part_rows:], CROSS)
    w_down = lax.all_gather(pair_of(down_shard, *down_moved), "yx", axis=0, tiled=True)
    w_project = assemble("assemble_project", me, *blocks, tokens.shape[1], qkv_cols)
    norm_two, cotangent, cot_upper, cot_lower, norm_sib, w_project, *moved = stage(
        norm_two, cotangent, cot_upper, cot_lower, norm_sib, w_project, *upper_far, *up_halves
    )
    upper_far, up_halves = moved[: near - 1], moved[near - 1 :]

    lower_far = [from_near(norm_two[part_rows:], k) for k in others]
    upper_far_sib = [flip(x, "core") for x in upper_far]
    cot_upper = jnp.where(straight(), cotangent[:part_rows], cot_upper)
    cot_lower = jnp.where(straight(), cotangent[part_rows:], cot_lower)
    cot_upper_sib = flip(cot_upper, "core")
    gate_blocks = blocks_of(pairs[0], gate_taken, gate_halves)
    up_blocks = blocks_of(up_pair, up_taken, up_halves, hidden_cols)
    gate_up = ([*gate_blocks[0], *up_blocks[0]], gate_blocks[1] + up_blocks[1], 2 * hidden_cols)
    outs = [(norm_two.shape[1], bf16, "all"), (2 * hidden_cols, f32, "all"), (hidden_cols, bf16, "all")]
    earlier = piece_call(gate_kernel, "gate", 0, near, me, [norm_two, norm_sib], [], [], [gate_up], [], outs)
    cot_lower, cot_upper, cot_upper_sib, *moved = stage(
        cot_lower, cot_upper, cot_upper_sib, *lower_far, *upper_far_sib, *earlier
    )
    lower_far, upper_far_sib, earlier = moved[: near - 1], moved[near - 1 : 2 * near - 2], moved[2 * near - 2 :]

    cot_upper_far = [from_near(cot_upper, k) for k in others]
    cot_lower_sib = flip(cot_lower, "core")
    for k in others:
        parts = [upper_far[k - 1], lower_far[k - 1], upper_far_sib[k - 1], flip(lower_far[k - 1], "core")]
        earlier = piece_call(gate_kernel, "gate", k, near, me, parts, [], [], [gate_up], earlier, outs)
    cot_lower, cot_lower_sib, w_down, *moved = stage(cot_lower, cot_lower_sib, w_down, *cot_upper_far, *earlier)
    cot_upper_far, earlier = moved[: near - 1], moved[near - 1 :]
    norm_two_all, gate_up_all, hidden_all = earlier

    cot_lower_far = [from_near(cot_lower, k) for k in others]
    cot_upper_far_sib = [flip(x, "core") for x in cot_upper_far]
    down = (*whole_weight(w_down), hidden_cols)
    width = norm_two.shape[1]
    outs = [(width, bf16, "all"), (2 * hidden_cols, bf16, "all")]
    outs += [(width, bf16, "own"), (width, bf16, "sibling")] * 2

    def way_back(k, parts, earlier):
        tiled = [(gate_up_all, k), (hidden_all, (k + 1) % near)]
        return piece_call(gate_back_kernel, "gate_back", k, near, me, parts, [], tiled, [gate_up, down], earlier, outs)

    def joined(own, sib):
        return own.astype(f32) + flip(sib, "core").astype(f32)

    grad_all, d_gate_up_all, *near_back = way_back(0, [cot_upper, cot_lower, cot_upper_sib, cot_lower_sib], [])
    grad_all, d_gate_up_all, *moved = stage(
        grad_all, d_gate_up_all, *near_back, *cot_lower_far, *cot_upper_far_sib
    )
    near_back, cot_lower_far, cot_upper_far_sib = moved[:4], moved[4 : near + 3], moved[near + 3 :]

    out_sum = joined(*near_back[2:]).astype(bf16)
    cot_lower_far_sib = [flip(x, "core") for x in cot_lower_far]
    out_sum, *cot_lower_far_sib = stage(out_sum, *cot_lower_far_sib)
    out_upper = to_near(out_sum[:part_rows], 1 % near)
    back = []
    for k in others:
        parts = [cot_upper_far[k - 1], cot_lower_far[k - 1], cot_upper_far_sib[k - 1], cot_lower_far_sib[k - 1]]
        grad_all, d_gate_up_all, *more = way_back(k, parts, [grad_all, d_gate_up_all])
        back.append(more)
    grad_all, d_gate_up_all, out_upper, *far_back = stage(
        grad_all, d_gate_up_all, out_upper, *(x for more in back for x in more)
    )
    d_norm_sent = [joined(*far_back[4 * n : 4 * n + 2]).astype(bf16) for n in range(near - 1)]
    out_far_back = [far_back[4 * n + 2 : 4 * n + 4] for n in range(near - 1)]
    grad_all, d_gate_up_all, near_own, near_sib, *d_norm_sent = stage(
        grad_all, d_gate_up_all, *near_back[:2], *d_norm_sent
    )

    moved_upper = [to_near(d_norm_sent[k - 1][:part_rows], k) for k in others]
    grad_gate_up = rows_product(norm_two_all, d_gate_up_all).astype(bf16)
    grad_gate_up, grad_all, near_own, near_sib, *moved = stage(
        grad_gate_up, grad_all, near_own, near_sib, *moved_upper, *d_norm_sent
    )
    moved_upper, d_norm_sent = moved[: near - 1], moved[near - 1 :]

    moved_lower = [to_near(d_norm_sent[k - 1][part_rows:], k) for k in others]
    gate_up_part = lax.psum_scatter(grad_gate_up, "yx", scatter_dimension=0, tiled=True)
    d_norm_two = joined(near_own, near_sib)
    grad_down = rows_product(grad_all, hidden_all).astype(bf16)
    grad_down, d_norm_two, out_sum, *moved_lower = stage(grad_down, d_norm_two, out_sum, *moved_lower)

    out_lower = to_near(out_sum[part_rows:], 1 % near)
    down_part = lax.psum_scatter(grad_down, "yx", scatter_dimension=0, tiled=True)
    for one, two in zip(moved_upper, moved_lower, strict=True):
        d_norm_two = d_norm_two + jnp.concatenate([one, two], axis=0).astype(f32)
    own_cotangent = jnp.concatenate([cot_upper, cot_lower], axis=0).astype(f32)
    mid_back, _ = norm_back(mid, scale_two, gain_two, d_norm_two)
    d_mid = own_cotangent + mid_back
    d_attn = d_mid.astype(bf16)
    both = [dot32(d_attn, w).astype(bf16) for w in (w_out_near, w_out_sib)]
    d_quarters = [both[e][:, k * query_cols : (k + 1) * query_cols] for e, k in order]
    d_attn, out_lower, *d_quarters = stage(d_attn, out_lower, *d_quarters)

    d_context = [None] * (2 * near)
    for (e, k), x in zip(order, d_quarters, strict=True):
        d_context[(near - k) % near * 2 + e] = x if (e, k) == (0, 0) else shift(x, e, k)
    grad_out_sib = flip(rows_product(d_attn, sib_context).astype(bf16), "core")
    grad_out = (rows_product(d_attn, own_context) + grad_out_sib.astype(f32)).astype(bf16)
    output_own = mid + joined(*out_far_back[-1]) + jnp.concatenate([out_upper, out_lower], axis=0).astype(f32)
    for n in range(near - 2):
        output_own = output_own + to_near(joined(*out_far_back[n]).astype(bf16), n + 2).astype(f32)
    output_own = output_own.astype(bf16)
    grad_out, output_own, gate_up_part, *d_context = stage(grad_out, output_own, gate_up_part, *d_context)

    output_crossed = crossed(output_own, CROSS)
    gate_up_keep, gate_up_give = give_z(gate_up_part)
    gate_up_back = crossed(gate_up_give, BACK)
    out_part = lax.psum_scatter(grad_out, "yx", scatter_dimension=0, tiled=True)
    d_qkv = attend_back(list(range(kv_heads)), qkv, d_context, context, sums, [], layout_back, q_heads, kv_heads)
    d_qkv, output_crossed, gate_up_back, gate_up_keep, down_part = stage(
        d_qkv, output_crossed, gate_up_back, gate_up_keep, down_part
    )

    def back_part(k):
        own, sib = (d_qkv[(2 * k + e) * rows : (2 * k + e + 1) * rows] for e in range(2))
        taken = flip(times_transpose(sib, w_project).astype(bf16), "core")
        return times_transpose(own, w_project) + taken.astype(f32)

    gate_up_cross = crossed(gate_up_keep, CROSS)
    d_sent = [back_part(k).astype(bf16) for k in others]
    d_qkv, gate_up_cross, down_part, *d_sent = stage(d_qkv, gate_up_cross, down_part, *d_sent)

    d_upper = [to_near(d_sent[k - 1][:part_rows], k) for k in others]
    down_keep, down_give = give_z(down_part)
    down_home = [crossed(down_give, BACK), crossed(down_keep, CROSS)]
    grad_project = rows_product(norm_one, d_qkv).astype(bf16)
    project_sent = send_yx(grad_project, (0, qkv_cols))
    total = back_part(0)
    total, grad_project, *moved = stage(total, grad_project, *d_upper, *d_sent, *project_sent, *down_home)
    d_upper, d_sent, project_sent, down_home = (
        moved[: near - 1], moved[near - 1 : 2 * near - 2], moved[2 * near - 2 : -2], moved[-2:],
    )

    d_lower = [to_near(d_sent[k - 1][part_rows:], k) for k in others]
    project_rest, project_own = join_yx(grad_project, (0, qkv_cols), project_sent)

    def input_part(at, moved):
        part = total[at]
        for x in moved:
            part = part + x.astype(f32)
        back, _ = norm_back(residual[at], scale_one[at], gain_one, part)
        return (d_mid[at] + back).astype(bf16)

    input_upper = input_part(slice(0, part_rows), d_upper)
    upper_crossed = crossed(input_upper, CROSS)
    total, input_upper, upper_crossed, out_part, *moved = stage(
        total, input_upper, upper_crossed, out_part, *d_lower, *project_rest
    )
    d_lower, project_rest = moved[: near - 1], moved[near - 1 :]

    project_keep, project_give = give_z(total_yx(project_rest, project_own))
    project_home = [crossed(project_give, BACK), crossed(project_keep, CROSS)]
    input_lower = input_part(slice(part_rows, rows), d_lower)
    lower_crossed = crossed(input_lower, CROSS)
    out_moved = [to_near(out_part[:, k * query_cols : (k + 1) * query_cols], k) for k in others]
    out_quarter = out_part[:, :query_cols].astype(f32)
    for part in out_moved:
        out_quarter = out_quarter + part.astype(f32)
    out_keep, out_give = give_z(out_quarter.astype(bf16))
    out_home = [crossed(out_give, BACK), crossed(out_keep, CROSS)]
    grad_project = sum_z(project_keep, *project_home)
    grad_out = sum_z(out_keep, *out_home)
    grad_down = sum_z(down_keep, *down_home)
    grad_gate_up = sum_z(gate_up_keep, gate_up_back, gate_up_cross)
    output = jnp.where(straight(), output_own, output_crossed)
    input_grad = jnp.concatenate(
        [
            jnp.where(straight(), input_upper, upper_crossed),
            jnp.where(straight(), input_lower, lower_crossed),
        ],
        axis=0,
    ).astype(f32)
    gain_grads = lax.psum(
        jnp.stack(
            [
                jnp.sum(qkv_shard.astype(f32) * grad_project, axis=1),
                jnp.sum(gate_up_shard.astype(f32) * grad_gate_up, axis=1),
            ]
        ),
        ("zh", "zl"),
    ) / jnp.stack([attn_gain, mlp_gain]).astype(f32)
    return (
        output,
        input_grad,
        gain_grads[0],
        grad_project[:, :query_cols],
        grad_project[:, query_cols : query_cols + key_cols],
        grad_project[:, query_cols + key_cols :],
        grad_out,
        gain_grads[1],
        grad_gate_up[:, :hidden_cols],
        grad_gate_up[:, hidden_cols:],
        grad_down,
    )


def solution(mesh):
    dp, tensor = mesh.shape["dp"], mesh.shape["tensor"]
    fine = Mesh(mesh.devices.reshape(dp // 2, 2, 2, tensor // 2), AXES)
    by_rows, by_dp, by_both = P(AXES, None), P(("yx", "core")), P(("yx", "core"), ("zh", "zl"))
    return jax.shard_map(
        body,
        mesh=fine,
        in_specs=(
            by_rows, by_rows, P(("yx", "core"), None), by_dp, by_both, by_both, by_both, by_both,
            by_dp, by_both, by_both, by_both,
        ),
        out_specs=(
            by_rows, by_rows, by_dp, by_both, by_both, by_both, by_both, by_dp, by_both, by_both, by_both,
        ),
        check_vma=False,
    )
```

profile of v0, /device:TPU:16, one launch (start us, length us, event | category | flops | bytes accessed | tf_op | source)
XLA Modules:
  0.0 695.7 jit_solution(1451796086156878596)
XLA Ops:
  19.6 9.3 %all-gather = bf16[8,192,2]{1,2,0:T(2,128)(2,1)S(1)} all-gather(bf16[1,192,2]{1,2,0:T(2,128)(2,1)S(1)} %fusion.18), channel_id=1, replica_groups=mesh['yx'=4,'core'=2,'zh'=2,'zl'=2] {'yx','core'}, dimensions={0}, use_global_device_ids=true | all-gather | bytes 6912 | tf_op jit(solution)/shard_map/all_gather | solution.py:709
  29.6 16.0 %collective-permute-done.1 = s32[1,4]{1,0:T(1,128)S(1)} collective-permute-done((s32[1,4]{1,0:T(1,128)S(1)}, s32[1,4]{1,0:T(1,128)S(1)}, u32[]{:S(2)}, u32[]{:S(2)}) %collective-permute-start.1) | collective-permute-done | bytes 48 | tf_op jit(solution)/shard_map/ppermute | solution.py:566
  47.0 5.8 collective-permute-start.6
  61.4 5.7 fusion.10
  87.4 6.6 collective-permute-done.12.refs_8_.refs_3_
  95.7 7.9 %project_0.1 = (bf16[2048,1536]{1,0:T(8,128)(2,1)}, bf16[2048,768]{1,0:T(8,128)(2,1)}) custom-call(s32[1]{0:T(128)} %bitcast.7.me, bf16[256,1536]{1,0:T(8,128)(2,1)} %copy-done.4, bf16[256,1536]{1,0:T(8,128)(2,1)} %copy-done.1, bf16[256,1536]{1,0:T(8,128)(2,1)} %collective-permute-done.5.refs_2_, bf16[256,1536]{1,0:T(8,128)(2,1)} %collective-permute-done.11.refs_3_, ...), custom_call_target="tpu_custom_call" | custom-call | flops 1048576 | bytes 65536 | tf_op jit(solution)/shard_map/project_0/pallas_call | solution.py:508
  112.6 7.9 %project_1.1 = (bf16[2048,1536]{1,0:T(8,128)(2,1)}, bf16[2048,768]{1,0:T(8,128)(2,1)}) custom-call(s32[1]{0:T(128)} %bitcast.7.me, bf16[256,1536]{1,0:T(8,128)(2,1)} %collective-permute-done.6.refs_0_, bf16[256,1536]{1,0:T(8,128)(2,1)} %collective-permute-done.9.refs_1_, ...), custom_call_target="tpu_custom_call", output_to_operand_aliasing={{0}: (11, {}), {1}: (12, {})} | custom-call | flops 1048576 | bytes 65536 | tf_op jit(solution)/shard_map/project_1/pallas_call | solution.py:508
  120.5 5.8 collective-permute-done.16.refs_1_
  134.7 29.1 %attention_forward.1 = (bf16[512,384]{1,0:T(8,128)(2,1)}, bf16[512,384]{1,0:T(8,128)(2,1)}, bf16[512,384]{1,0:T(8,128)(2,1)}, bf16[512,384]{1,0:T(8,128)(2,1)}, ...) custom-call(s32[16]{0:T(128)} %pad_add_fusion.refs_0_, s32[4]{0:T(128)} %get-tuple-element.224.refs_1_, ...), custom_call_target="tpu_custom_call" | custom-call | flops 1048576 | bytes 65536 | tf_op jit(solution)/shard_map/attention_forward/pallas_call | solution.py:333
  168.9 8.9 %collective-permute-done.22 = bf16[512,384]{1,0:T(8,128)(2,1)S(1)} collective-permute-done((bf16[512,384]{1,0:T(8,128)(2,1)S(1)}, bf16[512,384]{1,0:T(8,128)(2,1)S(1)}, u32[]{:S(2)}, u32[]{:S(2)}) %collective-permute-start.22) | collective-permute-done | bytes 393248 | tf_op jit(solution)/shard_map/ppermute | solution.py:600
  197.5 15.9 %collective-permute-done.28 = bf16[256,1536]{1,0:T(8,128)(2,1)S(1)} collective-permute-done((bf16[256,1536]{1,0:T(8,128)(2,1)S(1)}, bf16[256,1536]{1,0:T(8,128)(2,1)S(1)}, u32[]{:S(2)}, u32[]{:S(2)}) %collective-permute-start.28) | collective-permute-done | bytes 786464 | tf_op jit(solution)/shard_map/ppermute | solution.py:566
  227.5 6.1 collective-permute-done.34
  239.1 5.1 collective-permute-start.35
  252.7 12.3 %collective-permute-done.38.refs_10_.refs_12_.refs_14_ = bf16[192,1024]{1,0:T(8,128)(2,1)S(1)} collective-permute-done((bf16[192,1024]{1,0:T(8,128)(2,1)}, bf16[192,1024]{1,0:T(8,128)(2,1)S(1)}, u32[]{:S(2)}, u32[]{:S(2)}) %collective-permute-start.38) | collective-permute-done | bytes 393248 | tf_op jit(solution)/shard_map/ppermute | solution.py:617
  265.4 8.0 %collective-permute-done.37.refs_0_ = bf16[256,1536]{1,0:T(8,128)(2,1)} collective-permute-done((bf16[256,1536]{1,0:T(8,128)(2,1)}, bf16[256,1536]{1,0:T(8,128)(2,1)}, u32[]{:S(2)}, u32[]{:S(2)}) %collective-permute-start.37) | collective-permute-done | bytes 786464 | tf_op jit(solution)/shard_map/ppermute | solution.py:607
  279.5 14.7 %gate_0.1 = (bf16[2048,1536]{1,0:T(8,128)(2,1)}, f32[2048,2048]{1,0:T(8,128)}, bf16[2048,1024]{1,0:T(8,128)(2,1)}) custom-call(s32[1]{0:T(128)} %bitcast.7.me, bf16[512,1536]{1,0:T(8,128)(2,1)} %multiply_convert_fusion.refs_0_, bf16[512,1536]{1,0:T(8,128)(2,1)} %collective-permute-done.36.refs_1_, bf16[384,1024]{1,0:T(8,128)(2,1)} %copy-done.7, ...), custom_call_target="tpu_custom_call" | custom-call | flops 1048576 | bytes 65536 | tf_op jit(solution)/shard_map/gate_0/pallas_call | solution.py:508
  300.4 14.2 %gate_1.1 = (bf16[2048,1536]{1,0:T(8,128)(2,1)}, f32[2048,2048]{1,0:T(8,128)}, bf16[2048,1024]{1,0:T(8,128)(2,1)}) custom-call(s32[1]{0:T(128)} %bitcast.7.me, bf16[256,1536]{1,0:T(8,128)(2,1)} %collective-permute-done.37.refs_0_, bf16[256,1536]{1,0:T(8,128)(2,1)} %collective-permute-done.41.refs_1_, ...), custom_call_target="tpu_custom_call", output_to_operand_aliasing={{0}: (15, {}), {1}: (16, {}), {2}: (17, {})} | custom-call | flops 1048576 | bytes 65536 | tf_op jit(solution)/shard_map/gate_1/pallas_call | solution.py:508
  319.8 27.4 %gate_back_0.1 = (bf16[2048,1536]{1,0:T(8,128)(2,1)}, bf16[2048,2048]{1,0:T(8,128)(2,1)}, bf16[512,1536]{1,0:T(8,128)(2,1)}, bf16[512,1536]{1,0:T(8,128)(2,1)}, ...) custom-call(s32[1]{0:T(128)} %bitcast.7.me, bf16[256,1536]{1,0:T(8,128)(2,1)} %get-tuple-element.281.refs_0_, ...), custom_call_target="tpu_custom_call" | custom-call | flops 1048576 | bytes 65536 | tf_op jit(solution)/shard_map/gate_back_0/pallas_call | solution.py:508
  355.5 27.2 %gate_back_1.1 = (bf16[2048,1536]{1,0:T(8,128)(2,1)}, bf16[2048,2048]{1,0:T(8,128)(2,1)}, bf16[512,1536]{1,0:T(8,128)(2,1)}, bf16[512,1536]{1,0:T(8,128)(2,1)}, ...) custom-call(s32[1]{0:T(128)} %bitcast.7.me, ...), custom_call_target="tpu_custom_call", output_to_operand_aliasing={{0}: (18, {}), {1}: (19, {})} | custom-call | flops 1048576 | bytes 65536 | tf_op jit(solution)/shard_map/gate_back_1/pallas_call | solution.py:508
  392.0 19.3 %convolution_convert_fusion = bf16[1536,2048]{1,0:T(8,128)(2,1)} fusion(bf16[2048,1536]{1,0:T(8,128)(2,1)} %get-tuple-element.294, bf16[2048,2048]{1,0:T(8,128)(2,1)} %get-tuple-element.327), kind=kOutput, calls=%fused_computation | convolution fusion | flops 12888047616 | bytes 20971520 | tf_op jit(solution)/shard_map/dot_general | solution.py:63
  414.1 12.3 %convolution_convert_fusion.1 = bf16[1536,1024]{1,0:T(8,128)(2,1)} fusion(bf16[2048,1536]{1,0:T(8,128)(2,1)} %get-tuple-element.332, bf16[2048,1024]{1,0:T(8,128)(2,1)} %get-tuple-element.299.refs_5_), kind=kOutput, calls=%fused_computation.2 | convolution fusion | flops 6444023808 | bytes 13631488 | tf_op jit(solution)/shard_map/dot_general | solution.py:63
  447.4 6.8 collective-permute-done.55
  469.3 6.5 collective-permute-done.60.refs_14_
  484.5 45.5 %attention_backward_0.1 = bf16[2048,768]{1,0:T(8,128)(2,1)} custom-call(s32[16]{0:T(128)} %pad_add_fusion.refs_0_, s32[8]{0:T(128)} %get-tuple-element.352.refs_1_, s32[8]{0:T(128)} %get-tuple-element.353.refs_2_, f32[2048,128]{1,0:T(8,128)} %get-tuple-element.354.refs_3_, f32[2048,128]{1,0:T(8,128)} %get-tuple-element.355.refs_4_, ...), custom_call_target="tpu_custom_call" | custom-call | flops 1048576 | bytes 65536 | tf_op jit(solution)/shard_map/attention_backward_0/pallas_call | solution.py:363
  533.6 5.0 convolution_convert_fusion.5
  540.5 5.7 collective-permute-start.63
  553.0 11.4 %collective-permute-done.63 = bf16[192,2048]{1,0:T(8,128)(2,1)S(1)} collective-permute-done((bf16[192,2048]{1,0:T(8,128)(2,1)}, bf16[192,2048]{1,0:T(8,128)(2,1)S(1)}, u32[]{:S(2)}, u32[]{:S(2)}) %collective-permute-start.63) | collective-permute-done | bytes 786464 | tf_op jit(solution)/shard_map/ppermute | solution.py:566
  567.5 5.6 convolution_convert_fusion.2
  585.6 9.7 %collective-permute-done.70 = bf16[192,1024]{1,0:T(8,128)(2,1)S(1)} collective-permute-done((bf16[192,1024]{1,0:T(8,128)(2,1)S(1)}, bf16[192,1024]{1,0:T(8,128)(2,1)S(1)}, u32[]{:S(2)}, u32[]{:S(2)}) %collective-permute-start.70) | collective-permute-done | bytes 393248 | tf_op jit(solution)/shard_map/ppermute | solution.py:566
  619.5 6.3 collective-permute-done.72
  642.4 20.1 %collective-permute-done.77 = bf16[192,768]{1,0:T(8,128)(2,1)S(1)} collective-permute-done((bf16[192,768]{1,0:T(8,128)(2,1)S(1)}, bf16[192,768]{1,0:T(8,128)(2,1)S(1)}, u32[]{:S(2)}, u32[]{:S(2)}) %collective-permute-start.77) | collective-permute-done | bytes 294944 | tf_op jit(solution)/shard_map/ppermute | solution.py:566
  665.9 9.1 %psum.7 = f32[2,192]{1,0:T(2,128)S(1)} all-reduce(f32[2,192]{1,0:T(2,128)S(1)} %pad_maximum_fusion.14), channel_id=1, replica_groups=mesh['yx'=4,'core'=2,'zh'=2,'zl'=2] {'zh','zl'}, use_global_device_ids=true, to_apply=%region_12.13 | all-reduce | flops 384 | bytes 3072 | tf_op jit(solution)/shard_map/psum | solution.py:986
  (466 shorter events, 283.0 us)
Async XLA Ops:
  7.2 310.8 %all-gather.3.cloned.1.call-start = ((), (), s32[]{:S(2)}) async-start(), calls=%async_computation.3 | async-start | bytes 3932160 | tf_op jit(solution)/shard_map/all_gather | solution.py:813
  9.3 37.6 %collective-permute-start.2 = (bf16[192,1152]{1,0:T(8,128)(2,1)}, bf16[192,1152]{1,0:T(8,128)(2,1)}, u32[]{:S(2)}, u32[]{:S(2)}) collective-permute-start(bf16[192,1152]{1,0:T(8,128)(2,1)} %concatenate.64), channel_id=1, source_target_pairs={{0,2},{6,4},{4,0},{2,6},{1,3},{7,5},{5,1},{3,7},{8,10},{14,12},{12... | collective-permute-start | bytes 1327112 | tf_op jit(solution)/shard_map/ppermute | solution.py:566
  9.3 37.6 %collective-permute-start.3 = (bf16[192,1152]{1,0:T(8,128)(2,1)}, bf16[192,1152]{1,0:T(8,128)(2,1)}, u32[]{:S(2)}, u32[]{:S(2)}) collective-permute-start(bf16[192,1152]{1,0:T(8,128)(2,1)} %concatenate.64), channel_id=1, source_target_pairs={{2,4},{4,2},{3,5},{5,3},{10,12},{12,10},{11,13},{13,11},{18,20},{2... | collective-permute-start | bytes 1327112 | tf_op jit(solution)/shard_map/ppermute | solution.py:566
  12.4 33.2 %collective-permute-start = (bf16[256,1536]{1,0:T(8,128)(2,1)S(1)}, bf16[256,1536]{1,0:T(8,128)(2,1)}, u32[]{:S(2)}, u32[]{:S(2)}) collective-permute-start(bf16[256,1536]{1,0:T(8,128)(2,1)S(1)} %slice.231), channel_id=1, source_target_pairs={{2,4},{4,2},{3,5},{5,3},{10,12},{12,10},{11,13},{13,11},{18,20},{2... | collective-permute-start | bytes 2359304 | tf_op jit(solution)/shard_map/ppermute | solution.py:566
  17.0 28.6 %collective-permute-start.1 = (s32[1,4]{1,0:T(1,128)S(1)}, s32[1,4]{1,0:T(1,128)S(1)}, u32[]{:S(2)}, u32[]{:S(2)}) collective-permute-start(s32[1,4]{1,0:T(1,128)S(1)} %copy-done.86), channel_id=1, source_target_pairs={{2,4},{4,2},{3,5},{5,3},{10,12},{12,10},{11,13},{13,11},{18,20},{2... | collective-permute-start | bytes 56 | tf_op jit(solution)/shard_map/ppermute | solution.py:566
  47.0 33.5 %collective-permute-start.5 = (bf16[256,1536]{1,0:T(8,128)(2,1)S(1)}, bf16[256,1536]{1,0:T(8,128)(2,1)}, u32[]{:S(2)}, u32[]{:S(2)}) collective-permute-start(bf16[256,1536]{1,0:T(8,128)(2,1)S(1)} %get-tuple-element.202.refs_0_), channel_id=1, source_target_pairs={{0,4},{4,0},{1,5},{5,1},{2,6},{6,2},{3,7},{7,3},{8,12},{12,8},{9,1... | collective-permute-start | bytes 2359304 | tf_op jit(solution)/shard_map/ppermute | solution.py:557
  47.0 33.4 %collective-permute-start.6 = (bf16[256,1536]{1,0:T(8,128)(2,1)S(1)}, bf16[256,1536]{1,0:T(8,128)(2,1)}, u32[]{:S(2)}, u32[]{:S(2)}) collective-permute-start(bf16[256,1536]{1,0:T(8,128)(2,1)S(1)} %get-tuple-element.202.refs_0_), channel_id=1, source_target_pairs={{1,0},{0,1},{3,2},{2,3},{5,4},{4,5},{7,6},{6,7},{9,8},{8,9},{11,10... | collective-permute-start | bytes 2359304 | tf_op jit(solution)/shard_map/ppermute | solution.py:607
  80.6 27.9 %collective-permute-start.9 = (bf16[256,1536]{1,0:T(8,128)(2,1)S(1)}, bf16[256,1536]{1,0:T(8,128)(2,1)}, u32[]{:S(2)}, u32[]{:S(2)}) collective-permute-start(bf16[256,1536]{1,0:T(8,128)(2,1)S(1)} %broadcast_select_fusion.5.refs_1_), channel_id=1, source_target_pairs={{1,0},{0,1},{3,2},{2,3},{5,4},{4,5},{7,6},{6,7},{9,8},{8,9},{11,10... | collective-permute-start | bytes 2359304 | tf_op jit(solution)/shard_map/ppermute | solution.py:607
  126.6 37.3 %collective-permute-start.18 = (bf16[192,2048]{1,0:T(8,128)(2,1)S(1)}, bf16[192,2048]{1,0:T(8,128)(2,1)S(1)}, u32[]{:S(2)}, u32[]{:S(2)}) collective-permute-start(bf16[192,2048]{1,0:T(8,128)(2,1)S(1)} %pad_maximum_fusion.5), channel_id=1, source_target_pairs={{0,2},{6,4},{4,0},{2,6},{1,3},{7,5},{5,1},{3,7},{8,10},{14,12},{12... | collective-permute-start | bytes 2359304 | tf_op jit(solution)/shard_map/ppermute | solution.py:566
  126.6 37.3 %collective-permute-start.19 = (bf16[192,2048]{1,0:T(8,128)(2,1)S(1)}, bf16[192,2048]{1,0:T(8,128)(2,1)S(1)}, u32[]{:S(2)}, u32[]{:S(2)}) collective-permute-start(bf16[192,2048]{1,0:T(8,128)(2,1)S(1)} %pad_maximum_fusion.5), channel_id=1, source_target_pairs={{2,4},{4,2},{3,5},{5,3},{10,12},{12,10},{11,13},{13,11},{18,20},{2... | collective-permute-start | bytes 2359304 | tf_op jit(solution)/shard_map/ppermute | solution.py:566
  130.7 33.2 %collective-permute-start.20 = (bf16[192,768]{1,0:T(8,128)(2,1)}, bf16[192,768]{1,0:T(8,128)(2,1)S(1)}, u32[]{:S(2)}, u32[]{:S(2)}) collective-permute-start(bf16[192,768]{1,0:T(8,128)(2,1)} %slice.245), channel_id=1, source_target_pairs={{0,8},{8,0},{16,24},{24,16},{1,9},{9,1},{17,25},{25,17},{2,10},{10... | collective-permute-start | bytes 884744 | tf_op jit(solution)/shard_map/ppermute | solution.py:617
  133.1 30.8 %collective-permute-start.21 = (bf16[192,768]{1,0:T(8,128)(2,1)}, bf16[192,768]{1,0:T(8,128)(2,1)}, u32[]{:S(2)}, u32[]{:S(2)}) collective-permute-start(bf16[192,768]{1,0:T(8,128)(2,1)} %slice.246), channel_id=1, source_target_pairs={{0,16},{8,24},{16,0},{24,8},{1,17},{9,25},{17,1},{25,9},{2,18},{10... | collective-permute-start | bytes 884744 | tf_op jit(solution)/shard_map/ppermute | solution.py:617
  186.4 28.5 %collective-permute-start.27 = (bf16[1536,768]{1,0:T(8,128)(2,1)}, bf16[1536,768]{1,0:T(8,128)(2,1)S(1)}, u32[]{:S(2)}, u32[]{:S(2)}) collective-permute-start(bf16[1536,768]{1,0:T(8,128)(2,1)} %assemble_out.1), channel_id=1, source_target_pairs={{0,4},{4,0},{1,5},{5,1},{2,6},{6,2},{3,7},{7,3},{8,12},{12,8},{9,1... | collective-permute-start | bytes 7077896 | tf_op jit(solution)/shard_map/ppermute | solution.py:557
  187.4 27.5 %collective-permute-start.29 = (bf16[384,1024]{1,0:T(8,128)(2,1)S(1)}, bf16[384,1024]{1,0:T(8,128)(2,1)S(1)}, u32[]{:S(2)}, u32[]{:S(2)}) collective-permute-start(bf16[384,1024]{1,0:T(8,128)(2,1)S(1)} %pad_maximum_fusion.6.refs_7_.refs_9_.refs_11_), channel_id=1, source_target_pairs={{0,8},{8,0},{16,24},{24,16},{1,9},{9,1},{17,25},{25,17},{2,10},{10... | collective-permute-start | bytes 2359304 | tf_op jit(solution)/shard_map/ppermute | solution.py:617
  188.8 26.0 %collective-permute-start.30 = (bf16[384,1024]{1,0:T(8,128)(2,1)S(1)}, bf16[384,1024]{1,0:T(8,128)(2,1)S(1)}, u32[]{:S(2)}, u32[]{:S(2)}) collective-permute-start(bf16[384,1024]{1,0:T(8,128)(2,1)S(1)} %pad_maximum_fusion.6.refs_7_.refs_9_.refs_11_), channel_id=1, source_target_pairs={{0,16},{8,24},{16,0},{24,8},{1,17},{9,25},{17,1},{25,9},{2,18},{10... | collective-permute-start | bytes 2359304 | tf_op jit(solution)/shard_map/ppermute | solution.py:617
  196.5 29.5 %collective-permute-start.31 = (bf16[192,1024]{1,0:T(8,128)(2,1)S(1)}, bf16[192,1024]{1,0:T(8,128)(2,1)S(1)}, u32[]{:S(2)}, u32[]{:S(2)}) collective-permute-start(bf16[192,1024]{1,0:T(8,128)(2,1)S(1)} %slice.254), channel_id=1, source_target_pairs={{0,8},{8,0},{16,24},{24,16},{1,9},{9,1},{17,25},{25,17},{2,10},{10... | collective-permute-start | bytes 1179656 | tf_op jit(solution)/shard_map/ppermute | solution.py:617
  234.7 245.2 %reduce-scatter.4.cloned.1.call-start = ((), (), s32[]{:S(2)}) async-start(), calls=%async_computation.4 | async-start | bytes 7864320 | tf_op jit(solution)/shard_map/reduce_scatter | solution.py:890
  234.7 38.6 %collective-permute-start.36 = (bf16[512,1536]{1,0:T(8,128)(2,1)}, bf16[512,1536]{1,0:T(8,128)(2,1)}, u32[]{:S(2)}, u32[]{:S(2)}) collective-permute-start(bf16[512,1536]{1,0:T(8,128)(2,1)} %multiply_convert_fusion.refs_0_), channel_id=1, source_target_pairs={{0,4},{4,0},{1,5},{5,1},{2,6},{6,2},{3,7},{7,3},{8,12},{12,8},{9,1... | collective-permute-start | bytes 4718600 | tf_op jit(solution)/shard_map/ppermute | solution.py:557
  239.1 26.2 %collective-permute-start.35 = (bf16[256,1536]{1,0:T(8,128)(2,1)}, bf16[256,1536]{1,0:T(8,128)(2,1)}, u32[]{:S(2)}, u32[]{:S(2)}) collective-permute-start(bf16[256,1536]{1,0:T(8,128)(2,1)} %slice.256), channel_id=1, source_target_pairs={{2,4},{4,2},{3,5},{5,3},{10,12},{12,10},{11,13},{13,11},{18,20},{2... | collective-permute-start | bytes 2359304 | tf_op jit(solution)/shard_map/ppermute | solution.py:566
  244.3 29.1 %collective-permute-start.37 = (bf16[256,1536]{1,0:T(8,128)(2,1)}, bf16[256,1536]{1,0:T(8,128)(2,1)}, u32[]{:S(2)}, u32[]{:S(2)}) collective-permute-start(bf16[256,1536]{1,0:T(8,128)(2,1)} %slice.257), channel_id=1, source_target_pairs={{1,0},{0,1},{3,2},{2,3},{5,4},{4,5},{7,6},{6,7},{9,8},{8,9},{11,10... | collective-permute-start | bytes 2359304 | tf_op jit(solution)/shard_map/ppermute | solution.py:607
  318.1 29.2 %collective-permute-start.46 = (bf16[256,1536]{1,0:T(8,128)(2,1)}, bf16[256,1536]{1,0:T(8,128)(2,1)}, u32[]{:S(2)}, u32[]{:S(2)}) collective-permute-start(bf16[256,1536]{1,0:T(8,128)(2,1)} %get-tuple-element.293.refs_1_), channel_id=1, source_target_pairs={{1,0},{0,1},{3,2},{2,3},{5,4},{4,5},{7,6},{6,7},{9,8},{8,9},{11,10... | collective-permute-start | bytes 2359304 | tf_op jit(solution)/shard_map/ppermute | solution.py:607
  319.8 27.4 %collective-permute-start.47 = (bf16[256,1536]{1,0:T(8,128)(2,1)}, bf16[256,1536]{1,0:T(8,128)(2,1)}, u32[]{:S(2)}, u32[]{:S(2)}) collective-permute-start(bf16[256,1536]{1,0:T(8,128)(2,1)} %collective-permute-done.44.refs_0_), channel_id=1, source_target_pairs={{0,4},{4,0},{1,5},{5,1},{2,6},{6,2},{3,7},{7,3},{8,12},{12,8},{9,1... | collective-permute-start | bytes 2359304 | tf_op jit(solution)/shard_map/ppermute | solution.py:557
  355.2 27.5 %collective-permute-start.50 = (bf16[256,1536]{1,0:T(8,128)(2,1)}, bf16[256,1536]{1,0:T(8,128)(2,1)}, u32[]{:S(2)}, u32[]{:S(2)}) collective-permute-start(bf16[256,1536]{1,0:T(8,128)(2,1)} %slice.263), channel_id=1, source_target_pairs={{0,1},{1,0},{2,3},{3,2},{4,5},{5,4},{6,7},{7,6},{8,9},{9,8},{10,11... | collective-permute-start | bytes 2359304 | tf_op jit(solution)/shard_map/ppermute | solution.py:612
  411.3 118.7 %reduce-scatter.6.cloned.1.call-start = ((), (), s32[]{:S(2)}) async-start(), calls=%async_computation.5 | async-start | bytes 3932160 | tf_op jit(solution)/shard_map/reduce_scatter | solution.py:896
  437.5 173.1 %reduce-scatter.8.cloned.1.call-start = ((), (), s32[]{:S(2)}) async-start(), calls=%async_computation.6 | async-start | bytes 2949120 | tf_op jit(solution)/shard_map/reduce_scatter | solution.py:921
  479.9 53.6 %collective-permute-start.61 = (bf16[512,1536]{1,0:T(8,128)(2,1)S(1)}, bf16[512,1536]{1,0:T(8,128)(2,1)S(1)}, u32[]{:S(2)}, u32[]{:S(2)}) collective-permute-start(bf16[512,1536]{1,0:T(8,128)(2,1)S(1)} %copy-done.29), channel_id=1, source_target_pairs={{2,4},{4,2},{3,5},{5,3},{10,12},{12,10},{11,13},{13,11},{18,20},{2... | collective-permute-start | bytes 4718600 | tf_op jit(solution)/shard_map/ppermute | solution.py:566
  484.5 49.1 %collective-permute-start.62 = (bf16[192,2048]{1,0:T(8,128)(2,1)}, bf16[192,2048]{1,0:T(8,128)(2,1)}, u32[]{:S(2)}, u32[]{:S(2)}) collective-permute-start(bf16[192,2048]{1,0:T(8,128)(2,1)} %get-tuple-element.418), channel_id=1, source_target_pairs={{2,0},{4,6},{0,4},{6,2},{3,1},{5,7},{1,5},{7,3},{10,8},{12,14},{8,... | collective-permute-start | bytes 2359304 | tf_op jit(solution)/shard_map/ppermute | solution.py:566
  565.9 29.4 %collective-permute-start.66 = (bf16[256,1536]{1,0:T(8,128)(2,1)S(1)}, bf16[256,1536]{1,0:T(8,128)(2,1)S(1)}, u32[]{:S(2)}, u32[]{:S(2)}) collective-permute-start(bf16[256,1536]{1,0:T(8,128)(2,1)S(1)} %slice.277), channel_id=1, source_target_pairs={{0,1},{1,0},{2,3},{3,2},{4,5},{5,4},{6,7},{7,6},{8,9},{9,8},{10,11... | collective-permute-start | bytes 2359304 | tf_op jit(solution)/shard_map/ppermute | solution.py:612
  630.8 56.1 %collective-permute-start.75 = (bf16[256,1536]{1,0:T(8,128)(2,1)}, bf16[256,1536]{1,0:T(8,128)(2,1)S(1)}, u32[]{:S(2)}, u32[]{:S(2)}) collective-permute-start(bf16[256,1536]{1,0:T(8,128)(2,1)} %fusion.2), channel_id=1, source_target_pairs={{2,4},{4,2},{3,5},{5,3},{10,12},{12,10},{11,13},{13,11},{18,20},{2... | collective-permute-start | bytes 2359304 | tf_op jit(solution)/shard_map/ppermute | solution.py:566
  637.1 25.4 %collective-permute-start.77 = (bf16[192,768]{1,0:T(8,128)(2,1)S(1)}, bf16[192,768]{1,0:T(8,128)(2,1)S(1)}, u32[]{:S(2)}, u32[]{:S(2)}) collective-permute-start(bf16[192,768]{1,0:T(8,128)(2,1)S(1)} %get-tuple-element.440), channel_id=1, source_target_pairs={{2,4},{4,2},{3,5},{5,3},{10,12},{12,10},{11,13},{13,11},{18,20},{2... | collective-permute-start | bytes 884744 | tf_op jit(solution)/shard_map/ppermute | solution.py:566
  639.2 26.4 %collective-permute-start.76 = (bf16[192,768]{1,0:T(8,128)(2,1)S(1)}, bf16[192,768]{1,0:T(8,128)(2,1)S(1)}, u32[]{:S(2)}, u32[]{:S(2)}) collective-permute-start(bf16[192,768]{1,0:T(8,128)(2,1)S(1)} %get-tuple-element.439), channel_id=1, source_target_pairs={{2,0},{4,6},{0,4},{6,2},{3,1},{5,7},{1,5},{7,3},{10,8},{12,14},{8,... | collective-permute-start | bytes 884744 | tf_op jit(solution)/shard_map/ppermute | solution.py:566
  639.4 35.7 %collective-permute-start.78 = (bf16[384,384]{1,0:T(8,128)(2,1)S(1)}, bf16[384,384]{1,0:T(8,128)(2,1)S(1)}, u32[]{:S(2)}, u32[]{:S(2)}) collective-permute-start(bf16[384,384]{1,0:T(8,128)(2,1)S(1)} %slice.302), channel_id=1, source_target_pairs={{0,1},{1,0},{2,3},{3,2},{4,5},{5,4},{6,7},{7,6},{8,9},{9,8},{10,11... | collective-permute-start | bytes 884744 | tf_op jit(solution)/shard_map/ppermute | solution.py:612
  (147 other events, 1934.8 us)
Sparse Core Ops, SparseCore 0:
  234.8 54.8 all-gather.2
  411.4 68.4 reduce-scatter.3
  482.9 43.9 reduce-scatter.5
  540.6 43.0 reduce-scatter.7
where the time goes:
time: 708 us; the launch traced here: 696 us
  waiting for transfers between devices  210 us (30%)
  Pallas kernels  180 us (25%)
  starting transfers between devices  106 us (15%)
  other arithmetic  67.9 us (10%)
  matrix products  59.2 us (8%)
  local copies, waits for them, and re-layouts  38.4 us (5%)
  blocking collectives  18.5 us (3%)
  between operations  15.5 us (2%)
    pallas_call x6, Pallas kernels, piece_call(): pl.pallas_call(functools.partial(kernel, count, tuple((where for _, where...  99.3 us
    ppermute x22, waiting for transfers between devices, crossed(): return lax.ppermute(x, ('core', 'zh'), perm)  97.9 us
    ppermute x22, starting transfers between devices, crossed(): return lax.ppermute(x, ('core', 'zh'), perm)  55.7 us
    pallas_call x1, Pallas kernels, attend_back(): pl.pallas_call(functools.partial(backward_kernel, pieces, ratio, bool(ear...  45.5 us
    dot_general x5, matrix products, rows_product(): lax.dot_general(left, right, (((0,), (0,)), ((), ())), preferred_element_...  41.5 us
    ppermute x20, waiting for transfers between devices, across(): return lax.ppermute(x, 'yx', [(a, a ^ j) for a in range(n)])  38.2 us
    pallas_call x1, Pallas kernels, attend(): pl.pallas_call(functools.partial(forward_kernel, pieces, ratio), out_shap...  29.1 us
    ppermute x7, waiting for transfers between devices, from_near(): return lax.ppermute(x, 'zl', [((j + k) % n, j) for j in range(n)])  19.9 us
  transfers between devices with their start and end apart: 85, of which 36 were waited for; matrix products, arithmetic and copies ran while one was open for 20% of the time, Pallas kernels for 25%

commit v1 on v0

--- a/solution.py
+++ b/solution.py
@@ -13,7 +13,7 @@
 HD = 96
 HALF = HD // 2
 PAD = 128
-STEPS = 2
+STEPS = 4
 SUB = 256
 TILE = 512
 
@@ -400,14 +400,16 @@
 
 def take_rows(parts, target):
     rows = target.shape[0]
-    at = 0
-    for part in parts:
-
-        @pl.when(pl.program_id(0) == at // rows)
-        def take(part=part, at=at):
-            target[at % rows : at % rows + part.shape[0], :] = part[...]
-
-        at += part.shape[0]
+    for step in range(STEPS):
+
+        @pl.when(pl.program_id(0) == step)
+        def take(step=step):
+            at = 0
+            for part in parts:
+                first, last = max(at, step * rows), min(at + part.shape[0], (step + 1) * rows)
+                if first < last:
+                    target[first - step * rows : last - step * rows, :] = part[first - at : last - at, :]
+                at += part.shape[0]
 
 
 def at_first_step(copies, what):
@@ -431,104 +433,133 @@
     qkv_all[...] = dot32(norm_all[...], weight[...]).astype(jnp.bfloat16)
 
 
-def gate_kernel(count, where, more, me, *refs):
-    parts, refs = refs[:count], refs[count:]
-    sources, refs = refs[: len(where[0])], refs[len(where[0]) :]
-    norm_all, gate_up_all, hidden_all, weight, sems = refs[3 if more else 0 :]
-    hidden_cols = hidden_all.shape[1]
-    copies = fetch(me, where[0], sources, weight, sems)
+def mlp_kernel(counts, where, first, last, me, *refs):
+    refs = list(refs)
+
+    def take(count):
+        some, refs[:count] = refs[:count], []
+        return some
+
+    if first:
+        norm_parts, grad_parts = take(counts[0]), take(counts[1])
+    else:
+        norm_all, grad_all, d_norm_before, out_before = take(4)
+    gate_up, down = take(len(where[0])), take(len(where[1]))
+    if first:
+        norm_all, grad_all = take(2)
+    hidden_all, d_gate_up_all = take(2)
+    d_norm_refs, out_refs = take(2 if last else 1), take(2 if last else 1)
+    w_gate_up, gate_up_sems, w_down, down_sems = refs
+    copies = fetch(me, where[0], gate_up, w_gate_up, gate_up_sems) + fetch(me, where[1], down, w_down, down_sems)
     at_first_step(copies, lambda copy: copy.start())
-    take_rows(parts, norm_all)
+    if first:
+        take_rows(norm_parts, norm_all)
+        take_rows(grad_parts, grad_all)
     at_first_step(copies, lambda copy: copy.wait())
-    x = norm_all[...]
+    x, dy = norm_all[...], grad_all[...]
+    hidden_cols = w_down.shape[1]
     width = min(512, hidden_cols)
     for at in range(0, hidden_cols, width):
         gate_at = slice(at, at + width)
         up_at = slice(hidden_cols + at, hidden_cols + at + width)
-        gate = dot32(x, weight[:, gate_at])
-        up = dot32(x, weight[:, up_at])
-        gate_up_all[:, gate_at] = gate
-        gate_up_all[:, up_at] = up
-        hidden_all[:, gate_at] = (gate * (1.0 / (1.0 + jnp.exp(-gate))) * up).astype(jnp.bfloat16)
-
-
-def gate_back_kernel(count, where, more, me, *refs):
-    parts, gate_up_all, hidden_other, refs = refs[:count], *refs[count : count + 2], refs[count + 2 :]
-    gate_up, refs = refs[: len(where[0])], refs[len(where[0]) :]
-    down, refs = refs[: len(where[1])], refs[len(where[1]) :]
-    refs = refs[2 if more else 0 :]
-    grad_all, d_gate_up_all, d_norm_own, d_norm_sib, out_own, out_sib = refs[:6]
-    w_gate_up, gate_up_sems, w_down, down_sems = refs[6:]
-    hidden_cols = w_down.shape[1]
-    down_copies = fetch(me, where[1], down, w_down, down_sems)
-    copies = fetch(me, where[0], gate_up, w_gate_up, gate_up_sems)
-    at_first_step(down_copies + copies, lambda copy: copy.start())
-    take_rows(parts, grad_all)
-    at_first_step(down_copies, lambda copy: copy.wait())
-    dy = grad_all[...]
-    width = min(512, hidden_cols)
-    for at in range(0, hidden_cols, width):
-        gate_at = slice(at, at + width)
-        up_at = slice(hidden_cols + at, hidden_cols + at + width)
+        gate = dot32(x, w_gate_up[:, gate_at])
+        up = dot32(x, w_gate_up[:, up_at])
         d_hidden = dot32(dy, w_down[:, gate_at])
-        gate, up = gate_up_all[:, gate_at], gate_up_all[:, up_at]
         sigmoid = 1.0 / (1.0 + jnp.exp(-gate))
+        silu = gate * sigmoid
+        hidden_all[:, gate_at] = (silu * up).astype(jnp.bfloat16)
         d_gate = d_hidden * up * sigmoid * (1.0 + gate * (1.0 - sigmoid))
         d_gate_up_all[:, gate_at] = d_gate.astype(jnp.bfloat16)
-        d_gate_up_all[:, up_at] = (d_hidden * (gate * sigmoid)).astype(jnp.bfloat16)
-    out = times_transpose(hidden_other[...], w_down[...]).astype(jnp.bfloat16)
-    at_first_step(copies, lambda copy: copy.wait())
-    d_norm = times_transpose(d_gate_up_all[...], w_gate_up[...]).astype(jnp.bfloat16)
-
-    @pl.when(pl.program_id(0) == 0)
-    def to_own():
-        d_norm_own[...] = d_norm
-        out_own[...] = out
-
-    @pl.when(pl.program_id(0) != 0)
-    def to_sibling():
-        d_norm_sib[...] = d_norm
-        out_sib[...] = out
-
-
-def piece_call(kernel, name, k, pieces, me, parts, whole, tiled, fetched, earlier, outs):
+        d_gate_up_all[:, up_at] = (d_hidden * silu).astype(jnp.bfloat16)
+    d_norm = times_transpose(d_gate_up_all[...], w_gate_up[...])
+    out = times_transpose(hidden_all[...], w_down[...])
+    if not first:
+        d_norm = d_norm + d_norm_before[...].astype(jnp.float32)
+        out = out + out_before[...].astype(jnp.float32)
+    for n in range(len(out_refs)):
+
+        @pl.when(pl.program_id(0) * len(out_refs) // STEPS == n)
+        def store(n=n):
+            d_norm_refs[n][...] = d_norm.astype(jnp.bfloat16)
+            out_refs[n][...] = out.astype(jnp.bfloat16)
+
+
+def mlp_call(k, count, me, norm, grad, before, gate_up, down):
+    first, last = k == 0, k == count - 1
+    rows, width = sum(x.shape[0] for x in norm), norm[0].shape[1]
+    tile = rows // STEPS
+    hidden_cols = down[2]
+
+    def here(i):
+        return (i, 0)
+
+    def half(n):
+        return lambda i: (jnp.clip(i - n * STEPS // 2, 0, STEPS // 2 - 1), 0)
+
+    def tiles(cols):
+        return pl.BlockSpec((tile, cols), here)
+
+    sources = [*gate_up[0], *down[0]]
+    if first:
+        taken, specs = [*norm, *grad], [pl.BlockSpec(x.shape, lambda i: (0, 0)) for x in (*norm, *grad)]
+    else:
+        taken = [*norm, *grad, *before]
+        specs = [tiles(width)] * 4
+    shapes, out_specs = [], []
+    for cols in ([width, width] if first else []) + [hidden_cols, 2 * hidden_cols]:
+        shapes.append(jax.ShapeDtypeStruct((rows, cols), jnp.bfloat16))
+        out_specs.append(tiles(cols))
+    for _ in range(2):
+        for n in range(2 if last else 1):
+            shapes.append(jax.ShapeDtypeStruct((rows // 2 if last else rows, width), jnp.bfloat16))
+            out_specs.append(pl.BlockSpec((tile, width), half(n) if last else here))
+    return pl.pallas_call(
+        functools.partial(mlp_kernel, (len(norm), len(grad)), (gate_up[1], down[1]), first, last),
+        grid=(STEPS,),
+        out_shape=shapes,
+        in_specs=[SMEM, *specs, *[ANY] * len(sources)],
+        out_specs=out_specs,
+        scratch_shapes=[
+            pltpu.VMEM((width, 2 * hidden_cols), jnp.bfloat16),
+            pltpu.SemaphoreType.DMA((len(gate_up[0]),)),
+            pltpu.VMEM((width, hidden_cols), jnp.bfloat16),
+            pltpu.SemaphoreType.DMA((len(down[0]),)),
+        ],
+        compiler_params=pltpu.CompilerParams(vmem_limit_bytes=60 * 2**20),
+        cost_estimate=small_cost(),
+        name=f"mlp_{k}",
+    )(me, *taken, *sources)
+
+
+def project_piece(k, pieces, me, parts, gain, weight, earlier):
     tile, width = sum(x.shape[0] for x in parts) // STEPS, parts[0].shape[1]
     count = len(parts)
-
-    def rows_of(piece):
-        return lambda i: (piece * STEPS + i, 0)
-
-    sources = [x for arrays, _, _ in fetched for x in arrays]
-    first_earlier = 1 + count + len(whole) + len(tiled) + len(sources)
-    scratch = []
-    for arrays, _, cols in fetched:
-        scratch += [pltpu.VMEM((width, cols), jnp.bfloat16), pltpu.SemaphoreType.DMA((len(arrays),))]
-    if kernel is project_kernel:
-        scratch.append(pltpu.VMEM((tile, width), jnp.bfloat16))
+    arrays, where, cols = weight
+    first_earlier = 2 + count + len(arrays)
+
+    def here(i):
+        return (k * STEPS + i, 0)
+
     return pl.pallas_call(
-        functools.partial(kernel, count, tuple(where for _, where, _ in fetched), bool(earlier)),
+        functools.partial(project_kernel, count, (where,), bool(earlier)),
         grid=(STEPS,),
-        out_shape=[
-            jax.ShapeDtypeStruct((pieces * STEPS * tile if span == "all" else tile, columns), kind)
-            for columns, kind, span in outs
-        ],
+        out_shape=[jax.ShapeDtypeStruct((pieces * STEPS * tile, n), jnp.bfloat16) for n in (width, cols)],
         in_specs=[
             SMEM,
-            *(pl.BlockSpec(x.shape, lambda i: (0, 0)) for x in parts),
-            *(pl.BlockSpec(x.shape, lambda i: (0, 0)) for x in whole),
-            *(pl.BlockSpec((tile, x.shape[1]), rows_of(piece)) for x, piece in tiled),
-            *[ANY] * (len(sources) + len(earlier)),
+            *(pl.BlockSpec(x.shape, lambda i: (0, 0)) for x in (*parts, gain)),
+            *[ANY] * (len(arrays) + len(earlier)),
         ],
-        out_specs=[
-            pl.BlockSpec((tile, columns), rows_of(k) if span == "all" else lambda i: (0, 0))
-            for columns, kind, span in outs
+        out_specs=[pl.BlockSpec((tile, n), here) for n in (width, cols)],
+        scratch_shapes=[
+            pltpu.VMEM((width, cols), jnp.bfloat16),
+            pltpu.SemaphoreType.DMA((len(arrays),)),
+            pltpu.VMEM((tile, width), jnp.bfloat16),
         ],
-        scratch_shapes=scratch,
         input_output_aliases={first_earlier + n: n for n in range(len(earlier))},
         compiler_params=pltpu.CompilerParams(vmem_limit_bytes=60 * 2**20),
         cost_estimate=small_cost(),
-        name=f"{name}_{k}",
-    )(me, *parts, *whole, *(x for x, _ in tiled), *sources, *earlier)
+        name=f"project_{k}",
+    )(me, *parts, gain, *arrays, *earlier)
 
 
 def assemble_kernel(where, me, *refs):
@@ -744,208 +775,178 @@
 
     lower_far = [from_near(lower, k) for k in others]
     lower_sib = flip(lower, "core")
+    gate_up_out = crossed(gate_up_shard, OUT)
+    blocks = blocks_of(pair, taken, diagonal(taken))
+    projecting = (*blocks, qkv_cols)
+    gain_row = gain_one[None]
+    normed = project_piece(0, near, me, [upper, lower, upper_sib, lower_sib], gain_row, projecting, [])
+    gate_up_shard, gate_up_out, *moved = stage(gate_up_shard, gate_up_out, *lower_far, *normed)
+    lower_far, normed = moved[: near - 1], moved[near - 1 :]
+
+    gate_up_cross = crossed(gate_up_shard, CROSS)
     out_far = [from_near(out_pair, k) for k in others]
-    blocks = blocks_of(pair, taken, diagonal(taken))
-    projecting = [(*blocks, qkv_cols)]
-    gain_row = gain_one[None]
-    outs = [(tokens.shape[1], bf16, "all"), (qkv_cols, bf16, "all")]
-    parts = [upper, lower, upper_sib, lower_sib]
-    normed = piece_call(project_kernel, "project", 0, near, me, parts, [gain_row], [], projecting, [], outs)
-    gate_up_shard, *moved = stage(gate_up_shard, *lower_far, *out_far, *normed)
-    lower_far, out_far, normed = moved[: near - 1], moved[near - 1 : 2 * near - 2], moved[2 * near - 2 :]
-
-    out_own = jnp.concatenate([out_pair, *out_far], axis=1)
-    out_taken = neighbours(out_own)
     for k in others:
         parts = [upper_far[k - 1], lower_far[k - 1], flip(upper_far[k - 1], "core"), flip(lower_far[k - 1], "core")]
-        normed = piece_call(project_kernel, "project", k, near, me, parts, [gain_row], [], projecting, normed, outs)
+        normed = project_piece(k, near, me, parts, gain_row, projecting, normed)
     norm_one, qkv = normed
-    gate_up_shard, qkv, out_own, *out_taken = stage(gate_up_shard, qkv, out_own, *out_taken)
-
-    gate_up_moved = send_z(gate_up_shard)
-    out_halves = diagonal(out_taken)
+    gate_up_cross, qkv, down_shard, *out_far = stage(gate_up_cross, qkv, down_weight, *out_far)
+
+    gate_up_pair = pair_of(gate_up_shard, gate_up_out, gate_up_cross)
+    gate_up_taken = neighbours(gate_up_pair)
+    gate_up_far = [from_near(gate_up_pair, k) for k in others]
+    down_moved = send_z(down_shard)
+    w_out_near = lax.all_gather(jnp.concatenate([out_pair, *out_far], axis=1), "yx", axis=0, tiled=True)
     context, sums = attend(qkv, 2 * near, layout, q_heads, kv_heads)
-    down_shard, cotangent, *moved = stage(down_weight, cotangent, *context, *gate_up_moved, *out_halves)
-    context, gate_up_moved, out_halves = moved[: 2 * near], moved[2 * near : 2 * near + 2], moved[2 * near + 2 :]
+    cotangent, *moved = stage(cotangent, *context, *down_moved, *gate_up_far, *gate_up_taken)
+    context, down_moved, moved = moved[: 2 * near], moved[2 * near : 2 * near + 2], moved[2 * near + 2 :]
+    gate_up_far, gate_up_taken = moved[: near - 1], moved[near - 1 :]
 
     quarters = {(0, 0): context[0]}
     for k in range(near):
         for e in range(2):
             if (e, k) != (0, 0):
                 quarters[e, (near - k) % near] = shift(context[2 * k + e], e, k)
-    pairs = [
-        pair_of(*(x[:, n * hidden_cols : (n + 1) * hidden_cols] for x in (gate_up_shard, *gate_up_moved)))
-        for n in range(2)
-    ]
-    gate_taken = neighbours(pairs[0])
     order = [(e, k) for e in range(2) for k in range(near)]
-    up_pair, down_shard, cotangent, *moved = stage(
-        pairs[1], down_shard, cotangent, *(quarters[at] for at in order), *gate_taken, *out_halves
-    )
-    quarters, moved = moved[: 2 * near], moved[2 * near :]
-    gate_taken, out_halves = moved[: len(gate_taken)], moved[len(gate_taken) :]
-
-    up_taken = neighbours(up_pair)
+    gate_up_halves = diagonal(gate_up_taken)
+    down_pair = pair_of(down_weight, *down_moved)
+    down_pair, cotangent, w_out_near, *moved = stage(
+        down_pair, cotangent, w_out_near, *(quarters[at] for at in order), *gate_up_halves
+    )
+    quarters, gate_up_halves = moved[: 2 * near], moved[2 * near :]
+
+    w_out_sib = flip(w_out_near, "core")
+    down_taken = neighbours(down_pair)
+    down_far = [from_near(down_pair, k) for k in others]
     cot_upper = crossed(cotangent[:part_rows], CROSS)
-    w_out_near = assemble(
-        "assemble_out", me, *blocks_of(out_own, out_taken, out_halves), tokens.shape[1], near * query_cols
-    )
-    w_out_sib = flip(w_out_near, "core")
     residual = jnp.concatenate([upper, lower], axis=0).astype(f32)
     scale_one = lax.rsqrt(jnp.mean(residual * residual, axis=-1, keepdims=True) + EPSILON)
-    w_out_sib, w_out_near, scale_one, cotangent, cot_upper, down_shard, *up_taken = stage(
-        w_out_sib, w_out_near, scale_one, cotangent, cot_upper, down_shard, *up_taken
-    )
-
-    gate_halves = diagonal(gate_taken)
-    down_moved = send_z(down_shard)
+    w_out_sib, w_out_near, scale_one, cotangent, cot_upper, *moved = stage(
+        w_out_sib, w_out_near, scale_one, cotangent, cot_upper, *down_far, *down_taken
+    )
+    down_far, down_taken = moved[: near - 1], moved[near - 1 :]
+
+    gate_cols, up_cols = (slice(n * hidden_cols, (n + 1) * hidden_cols) for n in range(2))
+    down_halves = diagonal(down_taken)
+    cot_lower = crossed(cotangent[part_rows:], CROSS)
+    gate_far_taken = [x for far in gate_up_far for x in neighbours(far[:, gate_cols])]
     own_context = jnp.concatenate(quarters[:near], axis=1)
     sib_context = jnp.concatenate(quarters[near:], axis=1)
     mid = residual + times_transpose(own_context, w_out_near) + times_transpose(sib_context, w_out_sib)
     scale_two, norm_two = norm_rows(mid, gain_two)
-    norm_two, cotangent, cot_upper, *moved = stage(norm_two, cotangent, cot_upper, *gate_halves, *down_moved)
-    gate_halves, down_moved = moved[:-2], moved[-2:]
-
-    upper_far = [from_near(norm_two[:part_rows], k) for k in others]
-    up_halves = diagonal(up_taken)
-    norm_sib = flip(norm_two, "core")
-    cot_lower = crossed(cotangent[part_rows:], CROSS)
-    w_down = lax.all_gather(pair_of(down_shard, *down_moved), "yx", axis=0, tiled=True)
-    w_project = assemble("assemble_project", me, *blocks, tokens.shape[1], qkv_cols)
-    norm_two, cotangent, cot_upper, cot_lower, norm_sib, w_project, *moved = stage(
-        norm_two, cotangent, cot_upper, cot_lower, norm_sib, w_project, *upper_far, *up_halves
-    )
-    upper_far, up_halves = moved[: near - 1], moved[near - 1 :]
-
-    lower_far = [from_near(norm_two[part_rows:], k) for k in others]
-    upper_far_sib = [flip(x, "core") for x in upper_far]
-    cot_upper = jnp.where(straight(), cotangent[:part_rows], cot_upper)
-    cot_lower = jnp.where(straight(), cotangent[part_rows:], cot_lower)
-    cot_upper_sib = flip(cot_upper, "core")
-    gate_blocks = blocks_of(pairs[0], gate_taken, gate_halves)
-    up_blocks = blocks_of(up_pair, up_taken, up_halves, hidden_cols)
-    gate_up = ([*gate_blocks[0], *up_blocks[0]], gate_blocks[1] + up_blocks[1], 2 * hidden_cols)
-    outs = [(norm_two.shape[1], bf16, "all"), (2 * hidden_cols, f32, "all"), (hidden_cols, bf16, "all")]
-    earlier = piece_call(gate_kernel, "gate", 0, near, me, [norm_two, norm_sib], [], [], [gate_up], [], outs)
-    cot_lower, cot_upper, cot_upper_sib, *moved = stage(
-        cot_lower, cot_upper, cot_upper_sib, *lower_far, *upper_far_sib, *earlier
-    )
-    lower_far, upper_far_sib, earlier = moved[: near - 1], moved[near - 1 : 2 * near - 2], moved[2 * near - 2 :]
-
-    cot_upper_far = [from_near(cot_upper, k) for k in others]
-    cot_lower_sib = flip(cot_lower, "core")
+    cot = jnp.where(
+        straight(), cotangent, jnp.concatenate([cot_upper, cot_lower], axis=0)
+    )
+    norm_two, cot, *moved = stage(norm_two, cot, *down_halves, *gate_far_taken)
+    down_halves, gate_far_taken = moved[: len(down_halves)], moved[len(down_halves) :]
+    norm_sib, cot_sib = flip(norm_two, "core"), flip(cot, "core")
+    norm_sib, cot_sib, *gate_far_taken = stage(norm_sib, cot_sib, *gate_far_taken)
+
+    def split(items):
+        step = len(items) // max(near - 1, 1)
+        return [items[n * step : (n + 1) * step] for n in range(near - 1)]
+
+    gate_far_halves = [x for t in split(gate_far_taken) for x in diagonal(t)]
+    up_far_taken = [x for far in gate_up_far for x in neighbours(far[:, up_cols])]
+    gate_up = (*blocks_of(gate_up_pair, gate_up_taken, gate_up_halves), 2 * hidden_cols)
+    down = (*blocks_of(down_pair, down_taken, down_halves), hidden_cols)
+    norm_all, grad_all, hidden, d_gate_up, *sums_so_far = mlp_call(
+        0, near, me, [norm_two, norm_sib], [cot, cot_sib], [], gate_up, down
+    )
+    norm_all, grad_all, hidden, d_gate_up, *moved = stage(
+        norm_all, grad_all, hidden, d_gate_up, *sums_so_far, *gate_far_halves, *up_far_taken
+    )
+    sums_so_far, moved = moved[: len(sums_so_far)], moved[len(sums_so_far) :]
+    gate_far_halves, up_far_taken = moved[: len(gate_far_halves)], moved[len(gate_far_halves) :]
+
+    up_far_halves = [x for t in split(up_far_taken) for x in diagonal(t)]
+    down_far_taken = [x for far in down_far for x in neighbours(far)]
+    grads_gate_up = [rows_product(norm_all, d_gate_up).astype(bf16)]
+    grad_all, hidden, grads_gate_up[0], *moved = stage(
+        grad_all, hidden, grads_gate_up[0], *up_far_halves, *down_far_taken
+    )
+    up_far_halves, down_far_taken = moved[: len(up_far_halves)], moved[len(up_far_halves) :]
+
+    gate_up_parts = [lax.psum_scatter(grads_gate_up[0], "yx", scatter_dimension=0, tiled=True)]
+    down_far_halves = [x for t in split(down_far_taken) for x in diagonal(t)]
+    grads_down = [rows_product(grad_all, hidden).astype(bf16)]
+    norm_all, grad_all, grads_down[0], *down_far_halves = stage(norm_all, grad_all, grads_down[0], *down_far_halves)
+
     for k in others:
-        parts = [upper_far[k - 1], lower_far[k - 1], upper_far_sib[k - 1], flip(lower_far[k - 1], "core")]
-        earlier = piece_call(gate_kernel, "gate", k, near, me, parts, [], [], [gate_up], earlier, outs)
-    cot_lower, cot_lower_sib, w_down, *moved = stage(cot_lower, cot_lower_sib, w_down, *cot_upper_far, *earlier)
-    cot_upper_far, earlier = moved[: near - 1], moved[near - 1 :]
-    norm_two_all, gate_up_all, hidden_all = earlier
-
-    cot_lower_far = [from_near(cot_lower, k) for k in others]
-    cot_upper_far_sib = [flip(x, "core") for x in cot_upper_far]
-    down = (*whole_weight(w_down), hidden_cols)
-    width = norm_two.shape[1]
-    outs = [(width, bf16, "all"), (2 * hidden_cols, bf16, "all")]
-    outs += [(width, bf16, "own"), (width, bf16, "sibling")] * 2
-
-    def way_back(k, parts, earlier):
-        tiled = [(gate_up_all, k), (hidden_all, (k + 1) % near)]
-        return piece_call(gate_back_kernel, "gate_back", k, near, me, parts, [], tiled, [gate_up, down], earlier, outs)
-
-    def joined(own, sib):
-        return own.astype(f32) + flip(sib, "core").astype(f32)
-
-    grad_all, d_gate_up_all, *near_back = way_back(0, [cot_upper, cot_lower, cot_upper_sib, cot_lower_sib], [])
-    grad_all, d_gate_up_all, *moved = stage(
-        grad_all, d_gate_up_all, *near_back, *cot_lower_far, *cot_upper_far_sib
-    )
-    near_back, cot_lower_far, cot_upper_far_sib = moved[:4], moved[4 : near + 3], moved[near + 3 :]
-
-    out_sum = joined(*near_back[2:]).astype(bf16)
-    cot_lower_far_sib = [flip(x, "core") for x in cot_lower_far]
-    out_sum, *cot_lower_far_sib = stage(out_sum, *cot_lower_far_sib)
-    out_upper = to_near(out_sum[:part_rows], 1 % near)
-    back = []
-    for k in others:
-        parts = [cot_upper_far[k - 1], cot_lower_far[k - 1], cot_upper_far_sib[k - 1], cot_lower_far_sib[k - 1]]
-        grad_all, d_gate_up_all, *more = way_back(k, parts, [grad_all, d_gate_up_all])
-        back.append(more)
-    grad_all, d_gate_up_all, out_upper, *far_back = stage(
-        grad_all, d_gate_up_all, out_upper, *(x for more in back for x in more)
-    )
-    d_norm_sent = [joined(*far_back[4 * n : 4 * n + 2]).astype(bf16) for n in range(near - 1)]
-    out_far_back = [far_back[4 * n + 2 : 4 * n + 4] for n in range(near - 1)]
-    grad_all, d_gate_up_all, near_own, near_sib, *d_norm_sent = stage(
-        grad_all, d_gate_up_all, *near_back[:2], *d_norm_sent
-    )
-
-    moved_upper = [to_near(d_norm_sent[k - 1][:part_rows], k) for k in others]
-    grad_gate_up = rows_product(norm_two_all, d_gate_up_all).astype(bf16)
-    grad_gate_up, grad_all, near_own, near_sib, *moved = stage(
-        grad_gate_up, grad_all, near_own, near_sib, *moved_upper, *d_norm_sent
-    )
-    moved_upper, d_norm_sent = moved[: near - 1], moved[near - 1 :]
-
-    moved_lower = [to_near(d_norm_sent[k - 1][part_rows:], k) for k in others]
-    gate_up_part = lax.psum_scatter(grad_gate_up, "yx", scatter_dimension=0, tiled=True)
-    d_norm_two = joined(near_own, near_sib)
-    grad_down = rows_product(grad_all, hidden_all).astype(bf16)
-    grad_down, d_norm_two, out_sum, *moved_lower = stage(grad_down, d_norm_two, out_sum, *moved_lower)
-
-    out_lower = to_near(out_sum[part_rows:], 1 % near)
-    down_part = lax.psum_scatter(grad_down, "yx", scatter_dimension=0, tiled=True)
-    for one, two in zip(moved_upper, moved_lower, strict=True):
-        d_norm_two = d_norm_two + jnp.concatenate([one, two], axis=0).astype(f32)
-    own_cotangent = jnp.concatenate([cot_upper, cot_lower], axis=0).astype(f32)
+        n = k - 1
+        gate_blocks = blocks_of(gate_up_far[n][:, gate_cols], split(gate_far_taken)[n], split(gate_far_halves)[n])
+        up_blocks = blocks_of(gate_up_far[n][:, up_cols], split(up_far_taken)[n], split(up_far_halves)[n], hidden_cols)
+        gate_up = ([*gate_blocks[0], *up_blocks[0]], gate_blocks[1] + up_blocks[1], 2 * hidden_cols)
+        down = (*blocks_of(down_far[n], split(down_far_taken)[n], split(down_far_halves)[n]), hidden_cols)
+        hidden, d_gate_up, *sums_so_far = mlp_call(k, near, me, [norm_all], [grad_all], sums_so_far, gate_up, down)
+        if k < near - 1:
+            grads_gate_up.append(rows_product(norm_all, d_gate_up).astype(bf16))
+            grads_down.append(rows_product(grad_all, hidden).astype(bf16))
+    d_norm_own, d_norm_sib, out_own, out_sib = sums_so_far
+    d_norm_own, d_norm_sib, out_own, out_sib, hidden, d_gate_up = stage(
+        d_norm_own, d_norm_sib, out_own, out_sib, hidden, d_gate_up
+    )
+
+    d_norm_two = d_norm_own.astype(f32) + flip(d_norm_sib, "core").astype(f32)
+    grads_gate_up.append(rows_product(norm_all, d_gate_up).astype(bf16))
+    d_norm_two, out_sib, grads_gate_up[-1] = stage(d_norm_two, out_sib, grads_gate_up[-1])
+    gate_up_parts += [lax.psum_scatter(x, "yx", scatter_dimension=0, tiled=True) for x in grads_gate_up[1:]]
     mid_back, _ = norm_back(mid, scale_two, gain_two, d_norm_two)
-    d_mid = own_cotangent + mid_back
+    d_mid = cot.astype(f32) + mid_back
     d_attn = d_mid.astype(bf16)
     both = [dot32(d_attn, w).astype(bf16) for w in (w_out_near, w_out_sib)]
     d_quarters = [both[e][:, k * query_cols : (k + 1) * query_cols] for e, k in order]
-    d_attn, out_lower, *d_quarters = stage(d_attn, out_lower, *d_quarters)
+    d_attn, out_sib, hidden, *d_quarters = stage(d_attn, out_sib, hidden, *d_quarters)
 
     d_context = [None] * (2 * near)
     for (e, k), x in zip(order, d_quarters, strict=True):
         d_context[(near - k) % near * 2 + e] = x if (e, k) == (0, 0) else shift(x, e, k)
+    grads_down.append(rows_product(grad_all, hidden).astype(bf16))
     grad_out_sib = flip(rows_product(d_attn, sib_context).astype(bf16), "core")
     grad_out = (rows_product(d_attn, own_context) + grad_out_sib.astype(f32)).astype(bf16)
-    output_own = mid + joined(*out_far_back[-1]) + jnp.concatenate([out_upper, out_lower], axis=0).astype(f32)
-    for n in range(near - 2):
-        output_own = output_own + to_near(joined(*out_far_back[n]).astype(bf16), n + 2).astype(f32)
-    output_own = output_own.astype(bf16)
-    grad_out, output_own, gate_up_part, *d_context = stage(grad_out, output_own, gate_up_part, *d_context)
+    output_own = (mid + out_own.astype(f32) + flip(out_sib, "core").astype(f32)).astype(bf16)
+    grad_out, output_own, *moved = stage(grad_out, output_own, *d_context, *gate_up_parts, *grads_down)
+    d_context, moved = moved[: 2 * near], moved[2 * near :]
+    gate_up_parts, grads_down = moved[:near], moved[near:]
 
     output_crossed = crossed(output_own, CROSS)
-    gate_up_keep, gate_up_give = give_z(gate_up_part)
-    gate_up_back = crossed(gate_up_give, BACK)
+    gate_up_near = [to_near(gate_up_parts[k], k) for k in others]
+    w_project = assemble("assemble_project", me, *blocks, tokens.shape[1], qkv_cols)
+    down_parts = [lax.psum_scatter(x, "yx", scatter_dimension=0, tiled=True) for x in grads_down]
     out_part = lax.psum_scatter(grad_out, "yx", scatter_dimension=0, tiled=True)
     d_qkv = attend_back(list(range(kv_heads)), qkv, d_context, context, sums, [], layout_back, q_heads, kv_heads)
-    d_qkv, output_crossed, gate_up_back, gate_up_keep, down_part = stage(
-        d_qkv, output_crossed, gate_up_back, gate_up_keep, down_part
-    )
+    d_qkv, output_crossed, w_project, *moved = stage(d_qkv, output_crossed, w_project, *gate_up_near)
+    gate_up_near = moved
+
+    def summed(parts):
+        total = parts[0].astype(f32)
+        for part in parts[1:]:
+            total = total + part.astype(f32)
+        return total.astype(bf16)
 
     def back_part(k):
         own, sib = (d_qkv[(2 * k + e) * rows : (2 * k + e + 1) * rows] for e in range(2))
         taken = flip(times_transpose(sib, w_project).astype(bf16), "core")
         return times_transpose(own, w_project) + taken.astype(f32)
 
+    gate_up_keep, gate_up_give = give_z(summed([gate_up_parts[0], *gate_up_near]))
+    gate_up_back = crossed(gate_up_give, BACK)
+    d_sent = [back_part(k).astype(bf16) for k in others]
+    d_qkv, gate_up_back, gate_up_keep, *d_sent = stage(d_qkv, gate_up_back, gate_up_keep, *d_sent)
+
+    d_upper = [to_near(d_sent[k - 1][:part_rows], k) for k in others]
     gate_up_cross = crossed(gate_up_keep, CROSS)
-    d_sent = [back_part(k).astype(bf16) for k in others]
-    d_qkv, gate_up_cross, down_part, *d_sent = stage(d_qkv, gate_up_cross, down_part, *d_sent)
-
-    d_upper = [to_near(d_sent[k - 1][:part_rows], k) for k in others]
-    down_keep, down_give = give_z(down_part)
-    down_home = [crossed(down_give, BACK), crossed(down_keep, CROSS)]
     grad_project = rows_product(norm_one, d_qkv).astype(bf16)
     project_sent = send_yx(grad_project, (0, qkv_cols))
     total = back_part(0)
-    total, grad_project, *moved = stage(total, grad_project, *d_upper, *d_sent, *project_sent, *down_home)
-    d_upper, d_sent, project_sent, down_home = (
-        moved[: near - 1], moved[near - 1 : 2 * near - 2], moved[2 * near - 2 : -2], moved[-2:],
-    )
+    total, grad_project, gate_up_cross, *moved = stage(
+        total, grad_project, gate_up_cross, *d_upper, *d_sent, *project_sent, *down_parts
+    )
+    d_upper, d_sent, moved = moved[: near - 1], moved[near - 1 : 2 * near - 2], moved[2 * near - 2 :]
+    project_sent, down_parts = moved[:-near], moved[-near:]
 
     d_lower = [to_near(d_sent[k - 1][part_rows:], k) for k in others]
     project_rest, project_own = join_yx(grad_project, (0, qkv_cols), project_sent)
+    down_near = [to_near(down_parts[k], k) for k in others]
 
     def input_part(at, moved):
         part = total[at]
@@ -957,14 +958,16 @@
     input_upper = input_part(slice(0, part_rows), d_upper)
     upper_crossed = crossed(input_upper, CROSS)
     total, input_upper, upper_crossed, out_part, *moved = stage(
-        total, input_upper, upper_crossed, out_part, *d_lower, *project_rest
-    )
-    d_lower, project_rest = moved[: near - 1], moved[near - 1 :]
+        total, input_upper, upper_crossed, out_part, *d_lower, *project_rest, *down_near
+    )
+    d_lower, project_rest, down_near = moved[: near - 1], moved[near - 1 : -(near - 1)], moved[-(near - 1) :]
 
     project_keep, project_give = give_z(total_yx(project_rest, project_own))
     project_home = [crossed(project_give, BACK), crossed(project_keep, CROSS)]
     input_lower = input_part(slice(part_rows, rows), d_lower)
     lower_crossed = crossed(input_lower, CROSS)
+    down_keep, down_give = give_z(summed([down_parts[0], *down_near]))
+    down_home = [crossed(down_give, BACK), crossed(down_keep, CROSS)]
     out_moved = [to_near(out_part[:, k * query_cols : (k + 1) * query_cols], k) for k in others]
     out_quarter = out_part[:, :query_cols].astype(f32)
     for part in out_moved:

time: 708 us -> 733 us (1.035)
  waiting for transfers between devices: 210 us -> 240 us
  Pallas kernels: 180 us -> 157 us
  blocking collectives: 18.5 us -> 29.8 us
  matrix products: 59.2 us -> 69.3 us
    reduce_scatter x2 -> x4, waiting for transfers between devices: 4.09 us -> 45.1 us  [the longest x3 45.1 us: body(): lax.psum_scatter(x, 'yx', scatter_dimension=0, tiled=True)]
    pallas_call x6 -> x4, Pallas kernels: 99.3 us -> 79.3 us  [the longest x2 62.1 us: mlp_call(): pl.pallas_call(functools.partial(mlp_kernel, (len(norm), len(grad)), (gat...]
    ppermute x7 -> x5, waiting for transfers between devices: 18 us -> 30.2 us  [to_near(): return lax.ppermute(x, 'zl', [(j, (j + k) % n) for j in range(n)])]
    psum x1, blocking collectives: 9.13 us -> 20.9 us  [body(): lax.psum(jnp.stack([jnp.sum(qkv_shard.astype(f32) * grad_project, axis=1)...]
    ppermute x19 -> x12, waiting for transfers between devices: 12.1 us -> 2.41 us  [flip(): return lax.ppermute(x, axis, FLIP)]
    ppermute x7 -> x5, waiting for transfers between devices: 19.9 us -> 10.7 us  [from_near(): return lax.ppermute(x, 'zl', [((j + k) % n, j) for j in range(n)])]
    ppermute x20 -> x28, starting transfers between devices: 18.8 us -> 27.9 us  [across(): return lax.ppermute(x, 'yx', [(a, a ^ j) for a in range(n)])]
    dot_general x5 -> x7, matrix products: 41.5 us -> 49.8 us  [rows_product(): lax.dot_general(left, right, (((0,), (0,)), ((), ())), preferred_element_...]
  transfers between devices with their start and end apart: 85 -> 84, of which waited for: 36 -> 37; matrix products, arithmetic and copies ran while one was open for 20% -> 21% of each run, Pallas kernels for 25% -> 22%
where the time goes in v1:
time: 733 us; the launch traced here: 725 us
  waiting for transfers between devices  240 us (33%)
  Pallas kernels  157 us (21%)
  starting transfers between devices  109 us (15%)
  other arithmetic  70.4 us (10%)
  matrix products  69.3 us (9%)
  local copies, waits for them, and re-layouts  34.1 us (5%)
  blocking collectives  29.8 us (4%)
  between operations  16.1 us (2%)
    ppermute x22, waiting for transfers between devices, crossed(): return lax.ppermute(x, ('core', 'zh'), perm)  90.7 us
    pallas_call x2, Pallas kernels, mlp_call(): pl.pallas_call(functools.partial(mlp_kernel, (len(norm), len(grad)), (gat...  62.1 us
    ppermute x22, starting transfers between devices, crossed(): return lax.ppermute(x, ('core', 'zh'), perm)  54.8 us
    dot_general x7, matrix products, rows_product(): lax.dot_general(left, right, (((0,), (0,)), ((), ())), preferred_element_...  49.8 us
    pallas_call x1, Pallas kernels, attend_back(): pl.pallas_call(functools.partial(backward_kernel, pieces, ratio, bool(ear...  45.6 us
    reduce_scatter x3, waiting for transfers between devices, body(): lax.psum_scatter(x, 'yx', scatter_dimension=0, tiled=True)  45.1 us
    ppermute x28, waiting for transfers between devices, across(): return lax.ppermute(x, 'yx', [(a, a ^ j) for a in range(n)])  42.6 us
    ppermute x5, waiting for transfers between devices, to_near(): return lax.ppermute(x, 'zl', [(j, (j + k) % n) for j in range(n)])  30.2 us
  transfers between devices with their start and end apart: 84, of which 37 were waited for; matrix products, arithmetic and copies ran while one was open for 21% of the time, Pallas kernels for 22%

profile of v1, /device:TPU:16, one launch (start us, length us, event | category | flops | bytes accessed | tf_op | source)
XLA Modules:
  0.0 725.0 jit_solution(5129004319766601369)
XLA Ops:
  18.9 8.9 %all-gather = bf16[8,192,2]{1,2,0:T(2,128)(2,1)S(1)} all-gather(bf16[1,192,2]{1,2,0:T(2,128)(2,1)S(1)} %fusion.18), channel_id=1, replica_groups=mesh['yx'=4,'core'=2,'zh'=2,'zl'=2] {'yx','core'}, dimensions={0}, use_global_device_ids=true | all-gather | bytes 6912 | tf_op jit(solution)/shard_map/all_gather | solution.py:740
  31.4 6.4 collective-permute-done.1
  37.9 9.5 %collective-permute-done = bf16[256,1536]{1,0:T(8,128)(2,1)} collective-permute-done((bf16[256,1536]{1,0:T(8,128)(2,1)S(1)}, bf16[256,1536]{1,0:T(8,128)(2,1)}, u32[]{:S(2)}, u32[]{:S(2)}) %collective-permute-start) | collective-permute-done | bytes 786464 | tf_op jit(solution)/shard_map/ppermute | solution.py:597
  62.8 5.7 fusion.10
  90.0 6.0 collective-permute-done.12.refs_8_.refs_3_
  97.9 8.6 %project_0.1 = (bf16[2048,1536]{1,0:T(8,128)(2,1)}, bf16[2048,768]{1,0:T(8,128)(2,1)}) custom-call(s32[1]{0:T(128)} %bitcast.7.me, bf16[256,1536]{1,0:T(8,128)(2,1)} %copy-done.5, bf16[256,1536]{1,0:T(8,128)(2,1)} %copy-done.1, bf16[256,1536]{1,0:T(8,128)(2,1)} %collective-permute-done.5.refs_2_, bf16[256,1536]{1,0:T(8,128)(2,1)} %copy-done.61, ...), custom_call_target="tpu_custom_call" | custom-call | flops 1048576 | bytes 65536 | tf_op jit(solution)/shard_map/project_0/pallas_call | solution.py:543
  106.5 5.2 collective-permute-done.10.refs_1_
  117.9 8.5 %project_1.1 = (bf16[2048,1536]{1,0:T(8,128)(2,1)}, bf16[2048,768]{1,0:T(8,128)(2,1)}) custom-call(s32[1]{0:T(128)} %bitcast.7.me, bf16[256,1536]{1,0:T(8,128)(2,1)} %collective-permute-done.6.refs_0_, bf16[256,1536]{1,0:T(8,128)(2,1)} %collective-permute-done.10.refs_1_, ...), custom_call_target="tpu_custom_call", output_to_operand_aliasing={{0}: (11, {}), {1}: (12, {})} | custom-call | flops 1048576 | bytes 65536 | tf_op jit(solution)/shard_map/project_1/pallas_call | solution.py:543
  126.5 5.5 collective-permute-done.17
  144.3 29.2 %attention_forward.1 = (bf16[512,384]{1,0:T(8,128)(2,1)}, bf16[512,384]{1,0:T(8,128)(2,1)}, bf16[512,384]{1,0:T(8,128)(2,1)}, bf16[512,384]{1,0:T(8,128)(2,1)}, ...) custom-call(s32[16]{0:T(128)} %pad_add_fusion.refs_0_, s32[4]{0:T(128)} %get-tuple-element.183.refs_1_, ...), custom_call_target="tpu_custom_call" | custom-call | flops 1048576 | bytes 65536 | tf_op jit(solution)/shard_map/attention_forward/pallas_call | solution.py:333
  185.9 7.8 %collective-permute-done.23 = bf16[512,384]{1,0:T(8,128)(2,1)S(1)} collective-permute-done((bf16[512,384]{1,0:T(8,128)(2,1)S(1)}, bf16[512,384]{1,0:T(8,128)(2,1)S(1)}, u32[]{:S(2)}, u32[]{:S(2)}) %collective-permute-start.23) | collective-permute-done | bytes 393248 | tf_op jit(solution)/shard_map/ppermute | solution.py:631
  193.7 5.3 collective-permute-done.25
  204.1 6.0 collective-permute-start.29
  213.4 21.4 %collective-permute-done.29 = bf16[256,1536]{1,0:T(8,128)(2,1)S(1)} collective-permute-done((bf16[256,1536]{1,0:T(8,128)(2,1)S(1)}, bf16[256,1536]{1,0:T(8,128)(2,1)S(1)}, u32[]{:S(2)}, u32[]{:S(2)}) %collective-permute-start.29) | collective-permute-done | bytes 786464 | tf_op jit(solution)/shard_map/ppermute | solution.py:597
  245.6 10.4 %collective-permute-done.33 = bf16[256,1536]{1,0:T(8,128)(2,1)S(1)} collective-permute-done((bf16[256,1536]{1,0:T(8,128)(2,1)S(1)}, bf16[256,1536]{1,0:T(8,128)(2,1)S(1)}, u32[]{:S(2)}, u32[]{:S(2)}) %collective-permute-start.33) | collective-permute-done | bytes 786464 | tf_op jit(solution)/shard_map/ppermute | solution.py:597
  266.2 31.4 %mlp_0.1 = (bf16[1024,1536]{1,0:T(8,128)(2,1)}, bf16[1024,1536]{1,0:T(8,128)(2,1)}, bf16[1024,1024]{1,0:T(8,128)(2,1)}, bf16[1024,2048]{1,0:T(8,128)(2,1)}, bf16...) custom-call(s32[1]{0:T(128)} %bitcast.7.me, bf16[512,1536]{1,0:T(8,128)(2,1)} %copy-done.20, ...), custom_call_target="tpu_custom_call" | custom-call | flops 1048576 | bytes 65536 | tf_op jit(solution)/shard_map/mlp_0/pallas_call | solution.py:516
  303.6 11.3 %convolution_convert_fusion.1 = bf16[1536,2048]{1,0:T(8,128)(2,1)} fusion(bf16[1024,1536]{1,0:T(8,128)(2,1)} %get-tuple-element.262.refs_0_, bf16[1024,2048]{1,0:T(8,128)(2,1)} %get-tuple-element.254), kind=kOutput, calls=%fused_computation.1 | convolution fusion | flops 6445596672 | bytes 13631488 | tf_op jit(solution)/shard_map/dot_general | solution.py:63
  318.5 6.7 collective-permute-done.44.refs_12_
  330.1 8.4 %convolution_convert_fusion.3 = bf16[1536,1024]{1,0:T(8,128)(2,1)} fusion(bf16[1024,1536]{1,0:T(8,128)(2,1)} %get-tuple-element.263.refs_1_, bf16[1024,1024]{1,0:T(8,128)(2,1)} %get-tuple-element.259), kind=kOutput, calls=%fused_computation.4 | convolution fusion | flops 3222798336 | bytes 8388608 | tf_op jit(solution)/shard_map/dot_general | solution.py:63
  338.5 6.7 collective-permute-done.49.refs_18_
  347.5 30.7 %mlp_1.1 = (bf16[1024,1024]{1,0:T(8,128)(2,1)}, bf16[1024,2048]{1,0:T(8,128)(2,1)}, bf16[512,1536]{1,0:T(8,128)(2,1)}, bf16[512,1536]{1,0:T(8,128)(2,1)}, bf16[5...) custom-call(s32[1]{0:T(128)} %bitcast.7.me, bf16[1024,1536]{1,0:T(8,128)(2,1)} %get-tuple-element.262.refs_0_, ...), custom_call_target="tpu_custom_call" | custom-call | flops 1048576 | bytes 65536 | tf_op jit(solution)/shard_map/mlp_1/pallas_call | solution.py:516
  378.4 12.4 %convolution_convert_fusion = bf16[1536,2048]{1,0:T(8,128)(2,1)} fusion(bf16[1024,1536]{1,0:T(8,128)(2,1)} %get-tuple-element.262.refs_0_, bf16[1024,2048]{1,0:T(8,128)(2,1)} %get-tuple-element.281), kind=kOutput, calls=%fused_computation | convolution fusion | flops 6445596672 | bytes 13631488 | tf_op jit(solution)/shard_map/dot_general | solution.py:63
  428.5 45.1 %reduce-scatter.8.cloned.1.call-done = bf16[384,2048]{1,0:T(8,128)(2,1)} async-done(((bf16[1536,2048]{1,0:T(8,128)(2,1)}), bf16[384,2048]{1,0:T(8,128)(2,1)}) %reduce-scatter.8.cloned.1.call-update) | async-done | bytes 1572880 | tf_op jit(solution)/shard_map/reduce_scatter | solution.py:892
  480.9 45.6 %attention_backward_0.1 = bf16[2048,768]{1,0:T(8,128)(2,1)} custom-call(s32[16]{0:T(128)} %pad_add_fusion.refs_0_, s32[8]{0:T(128)} %get-tuple-element.298.refs_1_, s32[8]{0:T(128)} %get-tuple-element.299.refs_2_, f32[2048,128]{1,0:T(8,128)} %get-tuple-element.300.refs_3_, f32[2048,128]{1,0:T(8,128)} %get-tuple-element.301.refs_4_, ...), custom_call_target="tpu_custom_call" | custom-call | flops 1048576 | bytes 65536 | tf_op jit(solution)/shard_map/attention_backward_0/pallas_call | solution.py:363
  542.5 13.6 %collective-permute-done.58 = bf16[192,2048]{1,0:T(8,128)(2,1)} collective-permute-done((bf16[192,2048]{1,0:T(8,128)(2,1)}, bf16[192,2048]{1,0:T(8,128)(2,1)}, u32[]{:S(2)}, u32[]{:S(2)}) %collective-permute-start.58) | collective-permute-done | bytes 786464 | tf_op jit(solution)/shard_map/ppermute | solution.py:597
  564.8 5.5 convolution_convert_fusion.4
  578.7 8.3 %collective-permute-done.62 = bf16[256,1536]{1,0:T(8,128)(2,1)} collective-permute-done((bf16[256,1536]{1,0:T(8,128)(2,1)S(1)}, bf16[256,1536]{1,0:T(8,128)(2,1)}, u32[]{:S(2)}, u32[]{:S(2)}) %collective-permute-start.62) | collective-permute-done | bytes 786464 | tf_op jit(solution)/shard_map/ppermute | solution.py:643
  610.1 8.9 %collective-permute-done.67 = bf16[384,768]{1,0:T(8,128)(2,1)} collective-permute-done((bf16[384,768]{1,0:T(8,128)(2,1)}, bf16[384,768]{1,0:T(8,128)(2,1)}, u32[]{:S(2)}, u32[]{:S(2)}) %collective-permute-start.67) | collective-permute-done | bytes 589856 | tf_op jit(solution)/shard_map/ppermute | solution.py:648
  620.3 13.4 %collective-permute-done.66 = bf16[256,1536]{1,0:T(8,128)(2,1)} collective-permute-done((bf16[256,1536]{1,0:T(8,128)(2,1)}, bf16[256,1536]{1,0:T(8,128)(2,1)}, u32[]{:S(2)}, u32[]{:S(2)}) %collective-permute-start.66) | collective-permute-done | bytes 786464 | tf_op jit(solution)/shard_map/ppermute | solution.py:643
  633.7 8.4 %collective-permute-done.69 = bf16[384,1024]{1,0:T(8,128)(2,1)} collective-permute-done((bf16[384,1024]{1,0:T(8,128)(2,1)}, bf16[384,1024]{1,0:T(8,128)(2,1)}, u32[]{:S(2)}, u32[]{:S(2)}) %collective-permute-start.69) | collective-permute-done | bytes 786464 | tf_op jit(solution)/shard_map/ppermute | solution.py:643
  664.8 16.5 %collective-permute-done.71 = bf16[192,768]{1,0:T(8,128)(2,1)S(1)} collective-permute-done((bf16[192,768]{1,0:T(8,128)(2,1)S(1)}, bf16[192,768]{1,0:T(8,128)(2,1)S(1)}, u32[]{:S(2)}, u32[]{:S(2)}) %collective-permute-start.71) | collective-permute-done | bytes 294944 | tf_op jit(solution)/shard_map/ppermute | solution.py:597
  689.6 20.9 %psum.7 = f32[2,192]{1,0:T(2,128)S(1)} all-reduce(f32[2,192]{1,0:T(2,128)S(1)} %pad_maximum_fusion.12), channel_id=1, replica_groups=mesh['yx'=4,'core'=2,'zh'=2,'zl'=2] {'zh','zl'}, use_global_device_ids=true, to_apply=%region_14.15 | all-reduce | flops 384 | bytes 3072 | tf_op jit(solution)/shard_map/psum | solution.py:989
  (483 shorter events, 270.6 us)
Async XLA Ops:
  7.2 192.7 %all-gather.3.cloned.1.call-start = ((), (), s32[]{:S(2)}) async-start(), calls=%async_computation.5 | async-start | bytes 2949120 | tf_op jit(solution)/shard_map/all_gather | solution.py:798
  8.6 41.0 %collective-permute-start.3 = (bf16[192,1152]{1,0:T(8,128)(2,1)S(1)}, bf16[192,1152]{1,0:T(8,128)(2,1)}, u32[]{:S(2)}, u32[]{:S(2)}) collective-permute-start(bf16[192,1152]{1,0:T(8,128)(2,1)S(1)} %concatenate.55), channel_id=1, source_target_pairs={{2,4},{4,2},{3,5},{5,3},{10,12},{12,10},{11,13},{13,11},{18,20},{2... | collective-permute-start | bytes 1327112 | tf_op jit(solution)/shard_map/ppermute | solution.py:597
  10.5 39.0 %collective-permute-start.2 = (bf16[192,1152]{1,0:T(8,128)(2,1)S(1)}, bf16[192,1152]{1,0:T(8,128)(2,1)}, u32[]{:S(2)}, u32[]{:S(2)}) collective-permute-start(bf16[192,1152]{1,0:T(8,128)(2,1)S(1)} %concatenate.55), channel_id=1, source_target_pairs={{0,2},{6,4},{4,0},{2,6},{1,3},{7,5},{5,1},{3,7},{8,10},{14,12},{12... | collective-permute-start | bytes 1327112 | tf_op jit(solution)/shard_map/ppermute | solution.py:597
  135.7 292.7 %reduce-scatter.6.cloned.1.call-start = ((), (), s32[]{:S(2)}) async-start(), calls=%async_computation.6 | async-start | bytes 7864320 | tf_op jit(solution)/shard_map/reduce_scatter | solution.py:869
  137.2 40.1 %collective-permute-start.22 = (bf16[384,2048]{1,0:T(8,128)(2,1)S(1)}, bf16[384,2048]{1,0:T(8,128)(2,1)S(1)}, u32[]{:S(2)}, u32[]{:S(2)}) collective-permute-start(bf16[384,2048]{1,0:T(8,128)(2,1)S(1)} %pad_maximum_fusion.refs_4_), channel_id=1, source_target_pairs={{0,16},{8,24},{16,0},{24,8},{1,17},{9,25},{17,1},{25,9},{2,18},{10... | collective-permute-start | bytes 4718600 | tf_op jit(solution)/shard_map/ppermute | solution.py:648
  137.8 40.3 %collective-permute-start.21 = (bf16[384,2048]{1,0:T(8,128)(2,1)S(1)}, bf16[384,2048]{1,0:T(8,128)(2,1)}, u32[]{:S(2)}, u32[]{:S(2)}) collective-permute-start(bf16[384,2048]{1,0:T(8,128)(2,1)S(1)} %pad_maximum_fusion.refs_4_), channel_id=1, source_target_pairs={{0,8},{8,0},{16,24},{24,16},{1,9},{9,1},{17,25},{25,17},{2,10},{10... | collective-permute-start | bytes 4718600 | tf_op jit(solution)/shard_map/ppermute | solution.py:648
  138.3 39.8 %collective-permute-start.20 = (bf16[384,2048]{1,0:T(8,128)(2,1)S(1)}, bf16[384,2048]{1,0:T(8,128)(2,1)}, u32[]{:S(2)}, u32[]{:S(2)}) collective-permute-start(bf16[384,2048]{1,0:T(8,128)(2,1)S(1)} %pad_maximum_fusion.refs_4_), channel_id=1, source_target_pairs={{1,0},{0,1},{3,2},{2,3},{5,4},{4,5},{7,6},{6,7},{9,8},{8,9},{11,10... | collective-permute-start | bytes 4718600 | tf_op jit(solution)/shard_map/ppermute | solution.py:638
  140.6 33.8 %collective-permute-start.19 = (bf16[192,1024]{1,0:T(8,128)(2,1)S(1)}, bf16[192,1024]{1,0:T(8,128)(2,1)}, u32[]{:S(2)}, u32[]{:S(2)}) collective-permute-start(bf16[192,1024]{1,0:T(8,128)(2,1)S(1)} %copy-done.67), channel_id=1, source_target_pairs={{2,4},{4,2},{3,5},{5,3},{10,12},{12,10},{11,13},{13,11},{18,20},{2... | collective-permute-start | bytes 1179656 | tf_op jit(solution)/shard_map/ppermute | solution.py:597
  142.7 31.7 %collective-permute-start.18 = (bf16[192,1024]{1,0:T(8,128)(2,1)S(1)}, bf16[192,1024]{1,0:T(8,128)(2,1)}, u32[]{:S(2)}, u32[]{:S(2)}) collective-permute-start(bf16[192,1024]{1,0:T(8,128)(2,1)S(1)} %copy-done.67), channel_id=1, source_target_pairs={{0,2},{6,4},{4,0},{2,6},{1,3},{7,5},{5,1},{3,7},{8,10},{14,12},{12... | collective-permute-start | bytes 1179656 | tf_op jit(solution)/shard_map/ppermute | solution.py:597
  199.9 36.9 %collective-permute-start.28 = (bf16[1536,768]{1,0:T(8,128)(2,1)}, bf16[1536,768]{1,0:T(8,128)(2,1)S(1)}, u32[]{:S(2)}, u32[]{:S(2)}) collective-permute-start(bf16[1536,768]{1,0:T(8,128)(2,1)} %all-gather.3.cloned.1.call-done), channel_id=1, source_target_pairs={{0,4},{4,0},{1,5},{5,1},{2,6},{6,2},{3,7},{7,3},{8,12},{12,8},{9,1... | collective-permute-start | bytes 7077896 | tf_op jit(solution)/shard_map/ppermute | solution.py:588
  201.5 35.0 %collective-permute-start.32 = (bf16[384,1024]{1,0:T(8,128)(2,1)}, bf16[384,1024]{1,0:T(8,128)(2,1)S(1)}, u32[]{:S(2)}, u32[]{:S(2)}) collective-permute-start(bf16[384,1024]{1,0:T(8,128)(2,1)} %pad_maximum_fusion.5.refs_9_), channel_id=1, source_target_pairs={{0,16},{8,24},{16,0},{24,8},{1,17},{9,25},{17,1},{25,9},{2,18},{10... | collective-permute-start | bytes 2359304 | tf_op jit(solution)/shard_map/ppermute | solution.py:648
  202.5 34.3 %collective-permute-start.31 = (bf16[384,1024]{1,0:T(8,128)(2,1)}, bf16[384,1024]{1,0:T(8,128)(2,1)S(1)}, u32[]{:S(2)}, u32[]{:S(2)}) collective-permute-start(bf16[384,1024]{1,0:T(8,128)(2,1)} %pad_maximum_fusion.5.refs_9_), channel_id=1, source_target_pairs={{0,8},{8,0},{16,24},{24,16},{1,9},{9,1},{17,25},{25,17},{2,10},{10... | collective-permute-start | bytes 2359304 | tf_op jit(solution)/shard_map/ppermute | solution.py:648
  203.0 33.8 %collective-permute-start.30 = (bf16[384,1024]{1,0:T(8,128)(2,1)}, bf16[384,1024]{1,0:T(8,128)(2,1)}, u32[]{:S(2)}, u32[]{:S(2)}) collective-permute-start(bf16[384,1024]{1,0:T(8,128)(2,1)} %pad_maximum_fusion.5.refs_9_), channel_id=1, source_target_pairs={{1,0},{0,1},{3,2},{2,3},{5,4},{4,5},{7,6},{6,7},{9,8},{8,9},{11,10... | collective-permute-start | bytes 2359304 | tf_op jit(solution)/shard_map/ppermute | solution.py:638
  257.7 40.0 %collective-permute-start.43 = (bf16[384,1024]{1,0:T(8,128)(2,1)}, bf16[384,1024]{1,0:T(8,128)(2,1)}, u32[]{:S(2)}, u32[]{:S(2)}) collective-permute-start(bf16[384,1024]{1,0:T(8,128)(2,1)} %get-tuple-element.365.refs_9_), channel_id=1, source_target_pairs={{0,16},{8,24},{16,0},{24,8},{1,17},{9,25},{17,1},{25,9},{2,18},{10... | collective-permute-start | bytes 2359304 | tf_op jit(solution)/shard_map/ppermute | solution.py:648
  258.5 39.5 %collective-permute-start.42 = (bf16[384,1024]{1,0:T(8,128)(2,1)}, bf16[384,1024]{1,0:T(8,128)(2,1)}, u32[]{:S(2)}, u32[]{:S(2)}) collective-permute-start(bf16[384,1024]{1,0:T(8,128)(2,1)} %get-tuple-element.365.refs_9_), channel_id=1, source_target_pairs={{0,8},{8,0},{16,24},{24,16},{1,9},{9,1},{17,25},{25,17},{2,10},{10... | collective-permute-start | bytes 2359304 | tf_op jit(solution)/shard_map/ppermute | solution.py:648
  262.4 35.6 %collective-permute-start.41 = (bf16[192,1024]{1,0:T(8,128)(2,1)S(1)}, bf16[192,1024]{1,0:T(8,128)(2,1)}, u32[]{:S(2)}, u32[]{:S(2)}) collective-permute-start(bf16[192,1024]{1,0:T(8,128)(2,1)S(1)} %slice.231), channel_id=1, source_target_pairs={{0,16},{8,24},{16,0},{24,8},{1,17},{9,25},{17,1},{25,9},{2,18},{10... | collective-permute-start | bytes 1179656 | tf_op jit(solution)/shard_map/ppermute | solution.py:648
  263.4 34.6 %collective-permute-start.40 = (bf16[192,1024]{1,0:T(8,128)(2,1)S(1)}, bf16[192,1024]{1,0:T(8,128)(2,1)}, u32[]{:S(2)}, u32[]{:S(2)}) collective-permute-start(bf16[192,1024]{1,0:T(8,128)(2,1)S(1)} %slice.230), channel_id=1, source_target_pairs={{0,8},{8,0},{16,24},{24,16},{1,9},{9,1},{17,25},{25,17},{2,10},{10... | collective-permute-start | bytes 1179656 | tf_op jit(solution)/shard_map/ppermute | solution.py:648
  265.2 49.7 %collective-permute-start.47 = (bf16[384,1024]{1,0:T(8,128)(2,1)}, bf16[384,1024]{1,0:T(8,128)(2,1)}, u32[]{:S(2)}, u32[]{:S(2)}) collective-permute-start(bf16[384,1024]{1,0:T(8,128)(2,1)} %collective-permute-done.30.refs_14_), channel_id=1, source_target_pairs={{0,16},{8,24},{16,0},{24,8},{1,17},{9,25},{17,1},{25,9},{2,18},{10... | collective-permute-start | bytes 2359304 | tf_op jit(solution)/shard_map/ppermute | solution.py:648
  325.2 148.3 %reduce-scatter.8.cloned.1.call-start = ((), (), s32[]{:S(2)}) async-start(), calls=%async_computation.7 | async-start | bytes 7864320 | tf_op jit(solution)/shard_map/reduce_scatter | solution.py:892
  394.9 194.3 %reduce-scatter.10.cloned.1.call-start = ((), (), s32[]{:S(2)}) async-start(), calls=%async_computation.8 | async-start | bytes 3932160 | tf_op jit(solution)/shard_map/reduce_scatter | solution.py:914
  473.6 115.7 %reduce-scatter.12.cloned.1.call-start = ((), (), s32[]{:S(2)}) async-start(), calls=%async_computation.9 | async-start | bytes 3932160 | tf_op jit(solution)/shard_map/reduce_scatter | solution.py:914
  474.2 136.0 %reduce-scatter.14.cloned.1.call-start = ((), (), s32[]{:S(2)}) async-start(), calls=%async_computation.10 | async-start | bytes 2949120 | tf_op jit(solution)/shard_map/reduce_scatter | solution.py:915
  474.2 52.4 %collective-permute-start.57 = (bf16[384,2048]{1,0:T(8,128)(2,1)}, bf16[384,2048]{1,0:T(8,128)(2,1)}, u32[]{:S(2)}, u32[]{:S(2)}) collective-permute-start(bf16[384,2048]{1,0:T(8,128)(2,1)} %reduce-scatter.8.cloned.1.call-done), channel_id=1, source_target_pairs={{0,1},{1,0},{2,3},{3,2},{4,5},{5,4},{6,7},{7,6},{8,9},{9,8},{10,11... | collective-permute-start | bytes 4718600 | tf_op jit(solution)/shard_map/ppermute | solution.py:643
  475.7 51.7 %collective-permute-start.56 = (bf16[512,1536]{1,0:T(8,128)(2,1)S(1)}, bf16[512,1536]{1,0:T(8,128)(2,1)S(1)}, u32[]{:S(2)}, u32[]{:S(2)}) collective-permute-start(bf16[512,1536]{1,0:T(8,128)(2,1)S(1)} %copy-done.21), channel_id=1, source_target_pairs={{2,4},{4,2},{3,5},{5,3},{10,12},{12,10},{11,13},{13,11},{18,20},{2... | collective-permute-start | bytes 4718600 | tf_op jit(solution)/shard_map/ppermute | solution.py:597
  600.0 33.7 %collective-permute-start.66 = (bf16[256,1536]{1,0:T(8,128)(2,1)}, bf16[256,1536]{1,0:T(8,128)(2,1)}, u32[]{:S(2)}, u32[]{:S(2)}) collective-permute-start(bf16[256,1536]{1,0:T(8,128)(2,1)} %slice.254), channel_id=1, source_target_pairs={{0,1},{1,0},{2,3},{3,2},{4,5},{5,4},{6,7},{7,6},{8,9},{9,8},{10,11... | collective-permute-start | bytes 2359304 | tf_op jit(solution)/shard_map/ppermute | solution.py:643
  600.3 41.8 %collective-permute-start.69 = (bf16[384,1024]{1,0:T(8,128)(2,1)}, bf16[384,1024]{1,0:T(8,128)(2,1)}, u32[]{:S(2)}, u32[]{:S(2)}) collective-permute-start(bf16[384,1024]{1,0:T(8,128)(2,1)} %reduce-scatter.12.cloned.1.call-done), channel_id=1, source_target_pairs={{0,1},{1,0},{2,3},{3,2},{4,5},{5,4},{6,7},{7,6},{8,9},{9,8},{10,11... | collective-permute-start | bytes 2359304 | tf_op jit(solution)/shard_map/ppermute | solution.py:643
  649.8 31.6 %collective-permute-start.71 = (bf16[192,768]{1,0:T(8,128)(2,1)S(1)}, bf16[192,768]{1,0:T(8,128)(2,1)S(1)}, u32[]{:S(2)}, u32[]{:S(2)}) collective-permute-start(bf16[192,768]{1,0:T(8,128)(2,1)S(1)} %get-tuple-element.385), channel_id=1, source_target_pairs={{2,0},{4,6},{0,4},{6,2},{3,1},{5,7},{1,5},{7,3},{10,8},{12,14},{8,... | collective-permute-start | bytes 884744 | tf_op jit(solution)/shard_map/ppermute | solution.py:597
  652.3 32.4 %collective-permute-start.72 = (bf16[192,768]{1,0:T(8,128)(2,1)S(1)}, bf16[192,768]{1,0:T(8,128)(2,1)S(1)}, u32[]{:S(2)}, u32[]{:S(2)}) collective-permute-start(bf16[192,768]{1,0:T(8,128)(2,1)S(1)} %get-tuple-element.386), channel_id=1, source_target_pairs={{2,4},{4,2},{3,5},{5,3},{10,12},{12,10},{11,13},{13,11},{18,20},{2... | collective-permute-start | bytes 884744 | tf_op jit(solution)/shard_map/ppermute | solution.py:597
  654.2 58.4 %collective-permute-start.76 = (bf16[192,1024]{1,0:T(8,128)(2,1)}, bf16[192,1024]{1,0:T(8,128)(2,1)}, u32[]{:S(2)}, u32[]{:S(2)}) collective-permute-start(bf16[192,1024]{1,0:T(8,128)(2,1)} %get-tuple-element.378), channel_id=1, source_target_pairs={{2,0},{4,6},{0,4},{6,2},{3,1},{5,7},{1,5},{7,3},{10,8},{12,14},{8,... | collective-permute-start | bytes 1179656 | tf_op jit(solution)/shard_map/ppermute | solution.py:597
  654.3 58.3 %collective-permute-start.77 = (bf16[192,1024]{1,0:T(8,128)(2,1)S(1)}, bf16[192,1024]{1,0:T(8,128)(2,1)}, u32[]{:S(2)}, u32[]{:S(2)}) collective-permute-start(bf16[192,1024]{1,0:T(8,128)(2,1)S(1)} %get-tuple-element.377), channel_id=1, source_target_pairs={{2,4},{4,2},{3,5},{5,3},{10,12},{12,10},{11,13},{13,11},{18,20},{2... | collective-permute-start | bytes 1179656 | tf_op jit(solution)/shard_map/ppermute | solution.py:597
  662.8 52.8 %collective-permute-start.70 = (bf16[256,1536]{1,0:T(8,128)(2,1)}, bf16[256,1536]{1,0:T(8,128)(2,1)S(1)}, u32[]{:S(2)}, u32[]{:S(2)}) collective-permute-start(bf16[256,1536]{1,0:T(8,128)(2,1)} %fusion.2), channel_id=1, source_target_pairs={{2,4},{4,2},{3,5},{5,3},{10,12},{12,10},{11,13},{13,11},{18,20},{2... | collective-permute-start | bytes 2359304 | tf_op jit(solution)/shard_map/ppermute | solution.py:597
  681.4 33.4 %collective-permute-start.74 = (bf16[192,384]{1,0:T(8,128)(2,1)S(1)}, bf16[192,384]{1,0:T(8,128)(2,1)S(1)}, u32[]{:S(2)}, u32[]{:S(2)}) collective-permute-start(bf16[192,384]{1,0:T(8,128)(2,1)S(1)} %get-tuple-element.388), channel_id=1, source_target_pairs={{2,0},{4,6},{0,4},{6,2},{3,1},{5,7},{1,5},{7,3},{10,8},{12,14},{8,... | collective-permute-start | bytes 442376 | tf_op jit(solution)/shard_map/ppermute | solution.py:597
  (156 other events, 2049.9 us)
Sparse Core Ops, SparseCore 0:
  135.9 47.9 all-gather.2
  325.3 74.9 reduce-scatter.5
  403.3 70.2 reduce-scatter.7
  476.4 43.9 reduce-scatter.9
  523.2 43.9 reduce-scatter.11
  570.1 40.0 reduce-scatter.13

commit v2 on v0

--- a/solution.py
+++ b/solution.py
@@ -13,7 +13,7 @@
 HD = 96
 HALF = HD // 2
 PAD = 128
-STEPS = 2
+STEPS = 4
 SUB = 256
 TILE = 512
 
@@ -400,14 +400,16 @@
 
 def take_rows(parts, target):
     rows = target.shape[0]
-    at = 0
-    for part in parts:
-
-        @pl.when(pl.program_id(0) == at // rows)
-        def take(part=part, at=at):
-            target[at % rows : at % rows + part.shape[0], :] = part[...]
-
-        at += part.shape[0]
+    for step in range(STEPS):
+
+        @pl.when(pl.program_id(0) == step)
+        def take(step=step):
+            at = 0
+            for part in parts:
+                first, last = max(at, step * rows), min(at + part.shape[0], (step + 1) * rows)
+                if first < last:
+                    target[first - step * rows : last - step * rows, :] = part[first - at : last - at, :]
+                at += part.shape[0]
 
 
 def at_first_step(copies, what):
@@ -431,12 +433,26 @@
     qkv_all[...] = dot32(norm_all[...], weight[...]).astype(jnp.bfloat16)
 
 
+def by_half(refs, value):
+    for n, ref in enumerate(refs):
+
+        @pl.when(pl.program_id(0) * 2 // STEPS == n)
+        def store(ref=ref):
+            ref[...] = value
+
+
 def gate_kernel(count, where, more, me, *refs):
     parts, refs = refs[:count], refs[count:]
-    sources, refs = refs[: len(where[0])], refs[len(where[0]) :]
-    norm_all, gate_up_all, hidden_all, weight, sems = refs[3 if more else 0 :]
+    with_out = len(where) > 1
+    sources, refs = refs[: sum(map(len, where))], refs[sum(map(len, where)) :]
+    norm_all, gate_up_all, hidden_all, *refs = refs[3 if more else 0 :]
+    out_refs, refs = (refs[:2], refs[2:]) if with_out else ((), refs)
+    weight, sems, *refs = refs
     hidden_cols = hidden_all.shape[1]
-    copies = fetch(me, where[0], sources, weight, sems)
+    copies = fetch(me, where[0], sources[: len(where[0])], weight, sems)
+    if with_out:
+        w_down, down_sems = refs
+        copies += fetch(me, where[1], sources[len(where[0]) :], w_down, down_sems)
     at_first_step(copies, lambda copy: copy.start())
     take_rows(parts, norm_all)
     at_first_step(copies, lambda copy: copy.wait())
@@ -450,15 +466,18 @@
         gate_up_all[:, gate_at] = gate
         gate_up_all[:, up_at] = up
         hidden_all[:, gate_at] = (gate * (1.0 / (1.0 + jnp.exp(-gate))) * up).astype(jnp.bfloat16)
+    if with_out:
+        by_half(out_refs, times_transpose(hidden_all[...], w_down[...]).astype(jnp.bfloat16))
 
 
 def gate_back_kernel(count, where, more, me, *refs):
-    parts, gate_up_all, hidden_other, refs = refs[:count], *refs[count : count + 2], refs[count + 2 :]
+    parts, gate_up_all, hidden_here, refs = refs[:count], *refs[count : count + 2], refs[count + 2 :]
     gate_up, refs = refs[: len(where[0])], refs[len(where[0]) :]
     down, refs = refs[: len(where[1])], refs[len(where[1]) :]
-    refs = refs[2 if more else 0 :]
-    grad_all, d_gate_up_all, d_norm_own, d_norm_sib, out_own, out_sib = refs[:6]
-    w_gate_up, gate_up_sems, w_down, down_sems = refs[6:]
+    grad_all, d_gate_up_all, *refs = refs[2 if more else 0 :]
+    d_norm_refs, refs = refs[:2], refs[2:]
+    out_refs, refs = ((), refs) if more else (refs[:2], refs[2:])
+    w_gate_up, gate_up_sems, w_down, down_sems = refs
     hidden_cols = w_down.shape[1]
     down_copies = fetch(me, where[1], down, w_down, down_sems)
     copies = fetch(me, where[0], gate_up, w_gate_up, gate_up_sems)
@@ -476,19 +495,10 @@
         d_gate = d_hidden * up * sigmoid * (1.0 + gate * (1.0 - sigmoid))
         d_gate_up_all[:, gate_at] = d_gate.astype(jnp.bfloat16)
         d_gate_up_all[:, up_at] = (d_hidden * (gate * sigmoid)).astype(jnp.bfloat16)
-    out = times_transpose(hidden_other[...], w_down[...]).astype(jnp.bfloat16)
+    if not more:
+        by_half(out_refs, times_transpose(hidden_here[...], w_down[...]).astype(jnp.bfloat16))
     at_first_step(copies, lambda copy: copy.wait())
-    d_norm = times_transpose(d_gate_up_all[...], w_gate_up[...]).astype(jnp.bfloat16)
-
-    @pl.when(pl.program_id(0) == 0)
-    def to_own():
-        d_norm_own[...] = d_norm
-        out_own[...] = out
-
-    @pl.when(pl.program_id(0) != 0)
-    def to_sibling():
-        d_norm_sib[...] = d_norm
-        out_sib[...] = out
+    by_half(d_norm_refs, times_transpose(d_gate_up_all[...], w_gate_up[...]).astype(jnp.bfloat16))
 
 
 def piece_call(kernel, name, k, pieces, me, parts, whole, tiled, fetched, earlier, outs):
@@ -497,6 +507,10 @@
 
     def rows_of(piece):
         return lambda i: (piece * STEPS + i, 0)
+
+    def half_of(span):
+        first = 0 if span == "own" else STEPS // 2
+        return lambda i: (jnp.clip(i - first, 0, STEPS // 2 - 1), 0)
 
     sources = [x for arrays, _, _ in fetched for x in arrays]
     first_earlier = 1 + count + len(whole) + len(tiled) + len(sources)
@@ -509,7 +523,7 @@
         functools.partial(kernel, count, tuple(where for _, where, _ in fetched), bool(earlier)),
         grid=(STEPS,),
         out_shape=[
-            jax.ShapeDtypeStruct((pieces * STEPS * tile if span == "all" else tile, columns), kind)
+            jax.ShapeDtypeStruct(((pieces * STEPS if span == "all" else STEPS // 2) * tile, columns), kind)
             for columns, kind, span in outs
         ],
         in_specs=[
@@ -520,7 +534,7 @@
             *[ANY] * (len(sources) + len(earlier)),
         ],
         out_specs=[
-            pl.BlockSpec((tile, columns), rows_of(k) if span == "all" else lambda i: (0, 0))
+            pl.BlockSpec((tile, columns), rows_of(k) if span == "all" else half_of(span))
             for columns, kind, span in outs
         ],
         scratch_shapes=scratch,
@@ -787,94 +801,104 @@
 
     up_taken = neighbours(up_pair)
     cot_upper = crossed(cotangent[:part_rows], CROSS)
+    down_out = crossed(down_shard, OUT)
     w_out_near = assemble(
         "assemble_out", me, *blocks_of(out_own, out_taken, out_halves), tokens.shape[1], near * query_cols
     )
     w_out_sib = flip(w_out_near, "core")
     residual = jnp.concatenate([upper, lower], axis=0).astype(f32)
     scale_one = lax.rsqrt(jnp.mean(residual * residual, axis=-1, keepdims=True) + EPSILON)
-    w_out_sib, w_out_near, scale_one, cotangent, cot_upper, down_shard, *up_taken = stage(
-        w_out_sib, w_out_near, scale_one, cotangent, cot_upper, down_shard, *up_taken
-    )
-
-    gate_halves = diagonal(gate_taken)
-    down_moved = send_z(down_shard)
+    w_out_sib, w_out_near, scale_one, cotangent, cot_upper, down_shard, down_out, *up_taken = stage(
+        w_out_sib, w_out_near, scale_one, cotangent, cot_upper, down_shard, down_out, *up_taken
+    )
+
+    gate_halves, up_halves = diagonal(gate_taken), diagonal(up_taken)
+    down_cross = crossed(down_shard, CROSS)
     own_context = jnp.concatenate(quarters[:near], axis=1)
     sib_context = jnp.concatenate(quarters[near:], axis=1)
     mid = residual + times_transpose(own_context, w_out_near) + times_transpose(sib_context, w_out_sib)
     scale_two, norm_two = norm_rows(mid, gain_two)
-    norm_two, cotangent, cot_upper, *moved = stage(norm_two, cotangent, cot_upper, *gate_halves, *down_moved)
-    gate_halves, down_moved = moved[:-2], moved[-2:]
+    norm_two, cotangent, cot_upper, down_cross, *moved = stage(
+        norm_two, cotangent, cot_upper, down_cross, *gate_halves, *up_halves
+    )
+    gate_halves, up_halves = moved[: len(gate_halves)], moved[len(gate_halves) :]
+    norm_sib = flip(norm_two, "core")
+    down_pair = pair_of(down_shard, down_out, down_cross)
+    norm_two, norm_sib, down_pair = stage(norm_two, norm_sib, down_pair)
 
     upper_far = [from_near(norm_two[:part_rows], k) for k in others]
-    up_halves = diagonal(up_taken)
-    norm_sib = flip(norm_two, "core")
+    down_taken = neighbours(down_pair)
     cot_lower = crossed(cotangent[part_rows:], CROSS)
-    w_down = lax.all_gather(pair_of(down_shard, *down_moved), "yx", axis=0, tiled=True)
-    w_project = assemble("assemble_project", me, *blocks, tokens.shape[1], qkv_cols)
-    norm_two, cotangent, cot_upper, cot_lower, norm_sib, w_project, *moved = stage(
-        norm_two, cotangent, cot_upper, cot_lower, norm_sib, w_project, *upper_far, *up_halves
-    )
-    upper_far, up_halves = moved[: near - 1], moved[near - 1 :]
-
-    lower_far = [from_near(norm_two[part_rows:], k) for k in others]
-    upper_far_sib = [flip(x, "core") for x in upper_far]
-    cot_upper = jnp.where(straight(), cotangent[:part_rows], cot_upper)
-    cot_lower = jnp.where(straight(), cotangent[part_rows:], cot_lower)
-    cot_upper_sib = flip(cot_upper, "core")
     gate_blocks = blocks_of(pairs[0], gate_taken, gate_halves)
     up_blocks = blocks_of(up_pair, up_taken, up_halves, hidden_cols)
     gate_up = ([*gate_blocks[0], *up_blocks[0]], gate_blocks[1] + up_blocks[1], 2 * hidden_cols)
     outs = [(norm_two.shape[1], bf16, "all"), (2 * hidden_cols, f32, "all"), (hidden_cols, bf16, "all")]
     earlier = piece_call(gate_kernel, "gate", 0, near, me, [norm_two, norm_sib], [], [], [gate_up], [], outs)
-    cot_lower, cot_upper, cot_upper_sib, *moved = stage(
-        cot_lower, cot_upper, cot_upper_sib, *lower_far, *upper_far_sib, *earlier
-    )
-    lower_far, upper_far_sib, earlier = moved[: near - 1], moved[near - 1 : 2 * near - 2], moved[2 * near - 2 :]
-
-    cot_upper_far = [from_near(cot_upper, k) for k in others]
-    cot_lower_sib = flip(cot_lower, "core")
-    for k in others:
-        parts = [upper_far[k - 1], lower_far[k - 1], upper_far_sib[k - 1], flip(lower_far[k - 1], "core")]
-        earlier = piece_call(gate_kernel, "gate", k, near, me, parts, [], [], [gate_up], earlier, outs)
-    cot_lower, cot_lower_sib, w_down, *moved = stage(cot_lower, cot_lower_sib, w_down, *cot_upper_far, *earlier)
-    cot_upper_far, earlier = moved[: near - 1], moved[near - 1 :]
-    norm_two_all, gate_up_all, hidden_all = earlier
-
-    cot_lower_far = [from_near(cot_lower, k) for k in others]
-    cot_upper_far_sib = [flip(x, "core") for x in cot_upper_far]
-    down = (*whole_weight(w_down), hidden_cols)
+    norm_two, cot_lower, *moved = stage(norm_two, cot_lower, *upper_far, *down_taken, *earlier)
+    upper_far, moved = moved[: near - 1], moved[near - 1 :]
+    down_taken, earlier = moved[: len(down_taken)], moved[len(down_taken) :]
+
+    lower_far = [from_near(norm_two[part_rows:], k) for k in others]
+    upper_far_sib = [flip(x, "core") for x in upper_far]
+    down_halves = diagonal(down_taken)
+    cot = jnp.where(straight(), cotangent, jnp.concatenate([cot_upper, cot_lower], axis=0))
+    cot_sib = flip(cot, "core")
+    w_project = assemble("assemble_project", me, *blocks, tokens.shape[1], qkv_cols)
+    cot, cot_sib, w_project, *moved = stage(cot, cot_sib, w_project, *lower_far, *upper_far_sib, *down_halves)
+    lower_far, upper_far_sib, down_halves = moved[: near - 1], moved[near - 1 : 2 * near - 2], moved[2 * near - 2 :]
+    lower_far_sib = [flip(x, "core") for x in lower_far]
+
+    cot_upper_far = [from_near(cot[:part_rows], k) for k in others]
+    down = (*blocks_of(down_pair, down_taken, down_halves), hidden_cols)
     width = norm_two.shape[1]
-    outs = [(width, bf16, "all"), (2 * hidden_cols, bf16, "all")]
-    outs += [(width, bf16, "own"), (width, bf16, "sibling")] * 2
+    gate_outs, outs = outs, [(width, bf16, "all"), (2 * hidden_cols, bf16, "all")]
+    halves = [(width, bf16, "own"), (width, bf16, "sibling")]
 
     def way_back(k, parts, earlier):
-        tiled = [(gate_up_all, k), (hidden_all, (k + 1) % near)]
-        return piece_call(gate_back_kernel, "gate_back", k, near, me, parts, [], tiled, [gate_up, down], earlier, outs)
+        tiled, results = [(gate_up_all, k), (hidden_all, k)], outs + halves * (1 if earlier else 2)
+        return piece_call(gate_back_kernel, "gate_back", k, near, me, parts, [], tiled, [gate_up, down], earlier, results)
 
     def joined(own, sib):
         return own.astype(f32) + flip(sib, "core").astype(f32)
 
-    grad_all, d_gate_up_all, *near_back = way_back(0, [cot_upper, cot_lower, cot_upper_sib, cot_lower_sib], [])
+    norm_two_all, gate_up_all, hidden_all = earlier
+    grad_all, d_gate_up_all, *near_back = way_back(0, [cot, cot_sib], [])
+    cot, *moved = stage(
+        cot, norm_two_all, gate_up_all, hidden_all, grad_all, d_gate_up_all, *near_back, *cot_upper_far, *lower_far_sib
+    )
+    earlier, moved = moved[:3], moved[3:]
+    grad_all, d_gate_up_all, *moved = moved
+    near_back, cot_upper_far, lower_far_sib = moved[:4], moved[4 : near + 3], moved[near + 3 :]
+
+    cot_lower_far = [from_near(cot[part_rows:], k) for k in others]
+    cot_upper_far_sib = [flip(x, "core") for x in cot_upper_far]
+    out_far = []
+    for k in others:
+        parts = [upper_far[k - 1], lower_far[k - 1], upper_far_sib[k - 1], lower_far_sib[k - 1]]
+        *earlier, out_own, out_sib = piece_call(
+            gate_kernel, "gate", k, near, me, parts, [], [], [gate_up, down], earlier, gate_outs + halves
+        )
+        out_far += [out_own, out_sib]
     grad_all, d_gate_up_all, *moved = stage(
-        grad_all, d_gate_up_all, *near_back, *cot_lower_far, *cot_upper_far_sib
-    )
-    near_back, cot_lower_far, cot_upper_far_sib = moved[:4], moved[4 : near + 3], moved[near + 3 :]
-
-    out_sum = joined(*near_back[2:]).astype(bf16)
+        grad_all, d_gate_up_all, *near_back, *cot_lower_far, *cot_upper_far_sib, *earlier, *out_far
+    )
+    near_back, cot_lower_far, moved = moved[:4], moved[4 : near + 3], moved[near + 3 :]
+    cot_upper_far_sib, earlier, out_far = moved[: near - 1], moved[near - 1 : near + 2], moved[near + 2 :]
+    norm_two_all, gate_up_all, hidden_all = earlier
     cot_lower_far_sib = [flip(x, "core") for x in cot_lower_far]
-    out_sum, *cot_lower_far_sib = stage(out_sum, *cot_lower_far_sib)
-    out_upper = to_near(out_sum[:part_rows], 1 % near)
+    out_sums = [joined(*out_far[2 * n : 2 * n + 2]).astype(bf16) for n in range(near - 1)]
+    moved = stage(*cot_lower_far_sib, *out_sums)
+    cot_lower_far_sib, out_sums = moved[: near - 1], moved[near - 1 :]
+
+    out_upper = [to_near(out_sums[k - 1][:part_rows], k) for k in others]
     back = []
     for k in others:
         parts = [cot_upper_far[k - 1], cot_lower_far[k - 1], cot_upper_far_sib[k - 1], cot_lower_far_sib[k - 1]]
         grad_all, d_gate_up_all, *more = way_back(k, parts, [grad_all, d_gate_up_all])
         back.append(more)
-    grad_all, d_gate_up_all, out_upper, *far_back = stage(
-        grad_all, d_gate_up_all, out_upper, *(x for more in back for x in more)
-    )
-    d_norm_sent = [joined(*far_back[4 * n : 4 * n + 2]).astype(bf16) for n in range(near - 1)]
-    out_far_back = [far_back[4 * n + 2 : 4 * n + 4] for n in range(near - 1)]
+    grad_all, d_gate_up_all, *moved = stage(grad_all, d_gate_up_all, *(x for more in back for x in more), *out_upper)
+    far_back, out_upper = moved[: 2 * near - 2], moved[2 * near - 2 :]
+    d_norm_sent = [joined(*far_back[2 * n : 2 * n + 2]).astype(bf16) for n in range(near - 1)]
     grad_all, d_gate_up_all, near_own, near_sib, *d_norm_sent = stage(
         grad_all, d_gate_up_all, *near_back[:2], *d_norm_sent
     )
@@ -890,28 +914,29 @@
     gate_up_part = lax.psum_scatter(grad_gate_up, "yx", scatter_dimension=0, tiled=True)
     d_norm_two = joined(near_own, near_sib)
     grad_down = rows_product(grad_all, hidden_all).astype(bf16)
-    grad_down, d_norm_two, out_sum, *moved_lower = stage(grad_down, d_norm_two, out_sum, *moved_lower)
-
-    out_lower = to_near(out_sum[part_rows:], 1 % near)
+    grad_down, d_norm_two, *moved = stage(grad_down, d_norm_two, *out_sums, *moved_lower)
+    out_sums, moved_lower = moved[: near - 1], moved[near - 1 :]
+
+    out_lower = [to_near(out_sums[k - 1][part_rows:], k) for k in others]
     down_part = lax.psum_scatter(grad_down, "yx", scatter_dimension=0, tiled=True)
     for one, two in zip(moved_upper, moved_lower, strict=True):
         d_norm_two = d_norm_two + jnp.concatenate([one, two], axis=0).astype(f32)
-    own_cotangent = jnp.concatenate([cot_upper, cot_lower], axis=0).astype(f32)
     mid_back, _ = norm_back(mid, scale_two, gain_two, d_norm_two)
-    d_mid = own_cotangent + mid_back
+    d_mid = cot.astype(f32) + mid_back
     d_attn = d_mid.astype(bf16)
     both = [dot32(d_attn, w).astype(bf16) for w in (w_out_near, w_out_sib)]
     d_quarters = [both[e][:, k * query_cols : (k + 1) * query_cols] for e, k in order]
-    d_attn, out_lower, *d_quarters = stage(d_attn, out_lower, *d_quarters)
+    d_attn, *moved = stage(d_attn, *d_quarters, *out_lower)
+    d_quarters, out_lower = moved[: 2 * near], moved[2 * near :]
 
     d_context = [None] * (2 * near)
     for (e, k), x in zip(order, d_quarters, strict=True):
         d_context[(near - k) % near * 2 + e] = x if (e, k) == (0, 0) else shift(x, e, k)
     grad_out_sib = flip(rows_product(d_attn, sib_context).astype(bf16), "core")
     grad_out = (rows_product(d_attn, own_context) + grad_out_sib.astype(f32)).astype(bf16)
-    output_own = mid + joined(*out_far_back[-1]) + jnp.concatenate([out_upper, out_lower], axis=0).astype(f32)
-    for n in range(near - 2):
-        output_own = output_own + to_near(joined(*out_far_back[n]).astype(bf16), n + 2).astype(f32)
+    output_own = mid + joined(*near_back[2:])
+    for one, two in zip(out_upper, out_lower, strict=True):
+        output_own = output_own + jnp.concatenate([one, two], axis=0).astype(f32)
     output_own = output_own.astype(bf16)
     grad_out, output_own, gate_up_part, *d_context = stage(grad_out, output_own, gate_up_part, *d_context)
 

time: 708 us -> 703 us (level)
  waiting for transfers between devices: 210 us -> 201 us
    ppermute x20 -> x24, waiting for transfers between devices: 38.2 us -> 28.7 us  [across(): return lax.ppermute(x, 'yx', [(a, a ^ j) for a in range(n)])]
    ppermute x20 -> x24, starting transfers between devices: 18.8 us -> 24.5 us  [across(): return lax.ppermute(x, 'yx', [(a, a ^ j) for a in range(n)])]
  transfers between devices with their start and end apart: 85 -> 87, of which waited for: 36 -> 34; matrix products, arithmetic and copies ran while one was open for 20% -> 20% of each run, Pallas kernels for 25% -> 25%
where the time goes in v2:
time: 703 us; the launch traced here: 695 us
  waiting for transfers between devices  201 us (29%)
  Pallas kernels  178 us (25%)
  starting transfers between devices  105 us (15%)
  other arithmetic  67.1 us (10%)
  matrix products  58.4 us (8%)
  local copies, waits for them, and re-layouts  44.6 us (6%)
  blocking collectives  25 us (4%)
  between operations  15.8 us (2%)
    ppermute x22, waiting for transfers between devices, crossed(): return lax.ppermute(x, ('core', 'zh'), perm)  102 us
    pallas_call x6, Pallas kernels, piece_call(): pl.pallas_call(functools.partial(kernel, count, tuple((where for _, where...  97 us
    ppermute x22, starting transfers between devices, crossed(): return lax.ppermute(x, ('core', 'zh'), perm)  53.3 us
    pallas_call x1, Pallas kernels, attend_back(): pl.pallas_call(functools.partial(backward_kernel, pieces, ratio, bool(ear...  45.2 us
    dot_general x5, matrix products, rows_product(): lax.dot_general(left, right, (((0,), (0,)), ((), ())), preferred_element_...  40.7 us
    pallas_call x1, Pallas kernels, attend(): pl.pallas_call(functools.partial(forward_kernel, pieces, ratio), out_shap...  29.2 us
    ppermute x24, waiting for transfers between devices, across(): return lax.ppermute(x, 'yx', [(a, a ^ j) for a in range(n)])  28.7 us
    ppermute x24, starting transfers between devices, across(): return lax.ppermute(x, 'yx', [(a, a ^ j) for a in range(n)])  24.5 us
  transfers between devices with their start and end apart: 87, of which 34 were waited for; matrix products, arithmetic and copies ran while one was open for 20% of the time, Pallas kernels for 25%

profile of v2, /device:TPU:16, one launch (start us, length us, event | category | flops | bytes accessed | tf_op | source)
XLA Modules:
  0.0 695.0 jit_solution(4204509654550909694)
XLA Ops:
  19.7 9.3 %all-gather = bf16[8,192,2]{1,2,0:T(2,128)(2,1)S(1)} all-gather(bf16[1,192,2]{1,2,0:T(2,128)(2,1)S(1)} %fusion.18), channel_id=1, replica_groups=mesh['yx'=4,'core'=2,'zh'=2,'zl'=2] {'yx','core'}, dimensions={0}, use_global_device_ids=true | all-gather | bytes 6912 | tf_op jit(solution)/shard_map/all_gather | solution.py:723
  29.7 15.9 %collective-permute-done.1 = s32[1,4]{1,0:T(1,128)S(1)} collective-permute-done((s32[1,4]{1,0:T(1,128)S(1)}, s32[1,4]{1,0:T(1,128)S(1)}, u32[]{:S(2)}, u32[]{:S(2)}) %collective-permute-start.1) | collective-permute-done | bytes 48 | tf_op jit(solution)/shard_map/ppermute | solution.py:580
  54.0 5.8 collective-permute-start.6
  61.9 5.7 fusion.10
  75.2 9.6 %collective-permute-done.4 = bf16[256,1536]{1,0:T(8,128)(2,1)} collective-permute-done((bf16[256,1536]{1,0:T(8,128)(2,1)S(1)}, bf16[256,1536]{1,0:T(8,128)(2,1)}, u32[]{:S(2)}, u32[]{:S(2)}) %collective-permute-start.4) | collective-permute-done | bytes 786464 | tf_op jit(solution)/shard_map/ppermute | solution.py:580
  91.5 6.8 collective-permute-done.12.refs_8_.refs_3_
  100.0 8.5 %project_0.1 = (bf16[2048,1536]{1,0:T(8,128)(2,1)}, bf16[2048,768]{1,0:T(8,128)(2,1)}) custom-call(s32[1]{0:T(128)} %bitcast.7.me, bf16[256,1536]{1,0:T(8,128)(2,1)} %copy-done.4, bf16[256,1536]{1,0:T(8,128)(2,1)} %copy-done.1, bf16[256,1536]{1,0:T(8,128)(2,1)} %collective-permute-done.5.refs_2_, bf16[256,1536]{1,0:T(8,128)(2,1)} %collective-permute-done.11.refs_3_, ...), custom_call_target="tpu_custom_call" | custom-call | flops 1048576 | bytes 65536 | tf_op jit(solution)/shard_map/project_0/pallas_call | solution.py:522
  116.9 8.5 %project_1.1 = (bf16[2048,1536]{1,0:T(8,128)(2,1)}, bf16[2048,768]{1,0:T(8,128)(2,1)}) custom-call(s32[1]{0:T(128)} %bitcast.7.me, bf16[256,1536]{1,0:T(8,128)(2,1)} %collective-permute-done.6.refs_0_, bf16[256,1536]{1,0:T(8,128)(2,1)} %collective-permute-done.9.refs_1_, ...), custom_call_target="tpu_custom_call", output_to_operand_aliasing={{0}: (11, {}), {1}: (12, {})} | custom-call | flops 1048576 | bytes 65536 | tf_op jit(solution)/shard_map/project_1/pallas_call | solution.py:522
  139.9 29.2 %attention_forward.1 = (bf16[512,384]{1,0:T(8,128)(2,1)}, bf16[512,384]{1,0:T(8,128)(2,1)}, bf16[512,384]{1,0:T(8,128)(2,1)}, bf16[512,384]{1,0:T(8,128)(2,1)}, ...) custom-call(s32[16]{0:T(128)} %pad_add_fusion.refs_0_, s32[4]{0:T(128)} %get-tuple-element.235.refs_1_, ...), custom_call_target="tpu_custom_call" | custom-call | flops 1048576 | bytes 65536 | tf_op jit(solution)/shard_map/attention_forward/pallas_call | solution.py:333
  174.1 9.1 %collective-permute-done.22 = bf16[512,384]{1,0:T(8,128)(2,1)S(1)} collective-permute-done((bf16[512,384]{1,0:T(8,128)(2,1)S(1)}, bf16[512,384]{1,0:T(8,128)(2,1)S(1)}, u32[]{:S(2)}, u32[]{:S(2)}) %collective-permute-start.22) | collective-permute-done | bytes 393248 | tf_op jit(solution)/shard_map/ppermute | solution.py:614
  201.4 12.5 %collective-permute-done.29 = bf16[192,1024]{1,0:T(8,128)(2,1)S(1)} collective-permute-done((bf16[192,1024]{1,0:T(8,128)(2,1)S(1)}, bf16[192,1024]{1,0:T(8,128)(2,1)S(1)}, u32[]{:S(2)}, u32[]{:S(2)}) %collective-permute-start.29) | collective-permute-done | bytes 393248 | tf_op jit(solution)/shard_map/ppermute | solution.py:580
  214.9 11.3 %collective-permute-done.28 = bf16[256,1536]{1,0:T(8,128)(2,1)S(1)} collective-permute-done((bf16[256,1536]{1,0:T(8,128)(2,1)S(1)}, bf16[256,1536]{1,0:T(8,128)(2,1)S(1)}, u32[]{:S(2)}, u32[]{:S(2)}) %collective-permute-start.28) | collective-permute-done | bytes 786464 | tf_op jit(solution)/shard_map/ppermute | solution.py:580
  242.8 5.4 collective-permute-done.32
  259.0 14.0 %gate_0.1 = (bf16[2048,1536]{1,0:T(8,128)(2,1)}, f32[2048,2048]{1,0:T(8,128)}, bf16[2048,1024]{1,0:T(8,128)(2,1)}) custom-call(s32[1]{0:T(128)} %bitcast.7.me, bf16[512,1536]{1,0:T(8,128)(2,1)} %copy-done.13, bf16[512,1536]{1,0:T(8,128)(2,1)} %copy-done.50, bf16[384,1024]{1,0:T(8,128)(2,1)} %copy-done.7, bf16[384,1024]{1,0:T(8,128)(2,1)} %copy-done.9, ...), custom_call_target="tpu_custom_call" | custom-call | flops 1048576 | bytes 65536 | tf_op jit(solution)/shard_map/gate_0/pallas_call | solution.py:522
  273.0 9.3 %collective-permute-done.39.refs_0_ = bf16[256,1536]{1,0:T(8,128)(2,1)} collective-permute-done((bf16[256,1536]{1,0:T(8,128)(2,1)}, bf16[256,1536]{1,0:T(8,128)(2,1)}, u32[]{:S(2)}, u32[]{:S(2)}) %collective-permute-start.39) | collective-permute-done | bytes 786464 | tf_op jit(solution)/shard_map/ppermute | solution.py:621
  311.1 25.2 %gate_back_0.1 = (bf16[2048,1536]{1,0:T(8,128)(2,1)}, bf16[2048,2048]{1,0:T(8,128)(2,1)}, bf16[512,1536]{1,0:T(8,128)(2,1)}, bf16[512,1536]{1,0:T(8,128)(2,1)}, ...) custom-call(s32[1]{0:T(128)} %bitcast.7.me, bf16[512,1536]{1,0:T(8,128)(2,1)} %maximum_select_fusion.refs_0_, ...), custom_call_target="tpu_custom_call" | custom-call | flops 1048576 | bytes 65536 | tf_op jit(solution)/shard_map/gate_back_0/pallas_call | solution.py:522
  338.9 19.3 %gate_1.1 = (bf16[2048,1536]{1,0:T(8,128)(2,1)}, f32[2048,2048]{1,0:T(8,128)}, bf16[2048,1024]{1,0:T(8,128)(2,1)}, bf16[512,1536]{1,0:T(8,128)(2,1)}, bf16[512,1536]{1,0:T(8,128)(2,1)}) custom-call(s32[1]{0:T(128)} %bitcast.7.me, bf16[256,1536]{1,0:T(8,128)(2,1)} %collective-permute-done.39.refs_0_, ...), custom_call_target="tpu_custom_call", output_to_operand_aliasing={{0}: (20, {}), {1}: (21, {}), {2}: (22, {})} | custom-call | flops 1048576 | bytes 65536 | tf_op jit(solution)/shard_map/gate_1/pallas_call | solution.py:522
  367.8 21.5 %gate_back_1.1 = (bf16[2048,1536]{1,0:T(8,128)(2,1)}, bf16[2048,2048]{1,0:T(8,128)(2,1)}, bf16[512,1536]{1,0:T(8,128)(2,1)}, bf16[512,1536]{1,0:T(8,128)(2,1)}) custom-call(s32[1]{0:T(128)} %bitcast.7.me, bf16[256,1536]{1,0:T(8,128)(2,1)} %collective-permute-done.47.refs_0_, ...), custom_call_target="tpu_custom_call", output_to_operand_aliasing={{0}: (22, {}), {1}: (23, {})} | custom-call | flops 1048576 | bytes 65536 | tf_op jit(solution)/shard_map/gate_back_1/pallas_call | solution.py:522
  397.5 19.2 %convolution_convert_fusion = bf16[1536,2048]{1,0:T(8,128)(2,1)} fusion(bf16[2048,1536]{1,0:T(8,128)(2,1)} %get-tuple-element.328, bf16[2048,2048]{1,0:T(8,128)(2,1)} %get-tuple-element.349), kind=kOutput, calls=%fused_computation | convolution fusion | flops 12888047616 | bytes 20971520 | tf_op jit(solution)/shard_map/dot_general | solution.py:63
  420.3 11.4 %convolution_convert_fusion.1 = bf16[1536,1024]{1,0:T(8,128)(2,1)} fusion(bf16[2048,1536]{1,0:T(8,128)(2,1)} %get-tuple-element.354, bf16[2048,1024]{1,0:T(8,128)(2,1)} %get-tuple-element.335.refs_5_), kind=kOutput, calls=%fused_computation.2 | convolution fusion | flops 6444023808 | bytes 13631488 | tf_op jit(solution)/shard_map/dot_general | solution.py:63
  444.2 5.8 fusion.19
  474.7 6.7 collective-permute-done.63.refs_14_
  481.4 5.9 reduce-scatter.4.cloned.1.call-done
  491.9 45.2 %attention_backward_0.1 = bf16[2048,768]{1,0:T(8,128)(2,1)} custom-call(s32[16]{0:T(128)} %pad_add_fusion.refs_0_, s32[8]{0:T(128)} %get-tuple-element.374.refs_1_, s32[8]{0:T(128)} %get-tuple-element.375.refs_2_, f32[2048,128]{1,0:T(8,128)} %get-tuple-element.376.refs_3_, f32[2048,128]{1,0:T(8,128)} %get-tuple-element.377.refs_4_, ...), custom_call_target="tpu_custom_call" | custom-call | flops 1048576 | bytes 65536 | tf_op jit(solution)/shard_map/attention_backward_0/pallas_call | solution.py:363
  547.9 5.7 collective-permute-start.66
  560.4 11.4 %collective-permute-done.66 = bf16[192,2048]{1,0:T(8,128)(2,1)S(1)} collective-permute-done((bf16[192,2048]{1,0:T(8,128)(2,1)}, bf16[192,2048]{1,0:T(8,128)(2,1)S(1)}, u32[]{:S(2)}, u32[]{:S(2)}) %collective-permute-start.66) | collective-permute-done | bytes 786464 | tf_op jit(solution)/shard_map/ppermute | solution.py:580
  575.0 5.7 convolution_convert_fusion.2
  593.1 9.7 %collective-permute-done.73 = bf16[192,1024]{1,0:T(8,128)(2,1)S(1)} collective-permute-done((bf16[192,1024]{1,0:T(8,128)(2,1)S(1)}, bf16[192,1024]{1,0:T(8,128)(2,1)S(1)}, u32[]{:S(2)}, u32[]{:S(2)}) %collective-permute-start.73) | collective-permute-done | bytes 393248 | tf_op jit(solution)/shard_map/ppermute | solution.py:580
  618.3 12.6 %collective-permute-done.74 = bf16[256,1536]{1,0:T(8,128)(2,1)} collective-permute-done((bf16[256,1536]{1,0:T(8,128)(2,1)}, bf16[256,1536]{1,0:T(8,128)(2,1)}, u32[]{:S(2)}, u32[]{:S(2)}) %collective-permute-start.74) | collective-permute-done | bytes 786464 | tf_op jit(solution)/shard_map/ppermute | solution.py:580
  630.9 6.2 collective-permute-done.75
  657.0 10.0 %collective-permute-done.80 = bf16[192,768]{1,0:T(8,128)(2,1)S(1)} collective-permute-done((bf16[192,768]{1,0:T(8,128)(2,1)S(1)}, bf16[192,768]{1,0:T(8,128)(2,1)S(1)}, u32[]{:S(2)}, u32[]{:S(2)}) %collective-permute-start.80) | collective-permute-done | bytes 294944 | tf_op jit(solution)/shard_map/ppermute | solution.py:580
  667.3 15.7 %psum.7 = f32[2,192]{1,0:T(2,128)S(1)} all-reduce(f32[2,192]{1,0:T(2,128)S(1)} %pad_maximum_fusion.14), channel_id=1, replica_groups=mesh['yx'=4,'core'=2,'zh'=2,'zl'=2] {'zh','zl'}, use_global_device_ids=true, to_apply=%region_12.13 | all-reduce | flops 384 | bytes 3072 | tf_op jit(solution)/shard_map/psum | solution.py:1011
  (483 shorter events, 281.0 us)
Async XLA Ops:
  7.2 480.1 %reduce-scatter.4.cloned.1.call-start = ((), (), s32[]{:S(2)}) async-start(), calls=%async_computation.3 | async-start | bytes 7864320 | tf_op jit(solution)/shard_map/reduce_scatter | solution.py:914
  9.3 37.7 %collective-permute-start.2 = (bf16[192,1152]{1,0:T(8,128)(2,1)}, bf16[192,1152]{1,0:T(8,128)(2,1)}, u32[]{:S(2)}, u32[]{:S(2)}) collective-permute-start(bf16[192,1152]{1,0:T(8,128)(2,1)} %concatenate.64), channel_id=1, source_target_pairs={{0,2},{6,4},{4,0},{2,6},{1,3},{7,5},{5,1},{3,7},{8,10},{14,12},{12... | collective-permute-start | bytes 1327112 | tf_op jit(solution)/shard_map/ppermute | solution.py:580
  9.3 37.7 %collective-permute-start.3 = (bf16[192,1152]{1,0:T(8,128)(2,1)}, bf16[192,1152]{1,0:T(8,128)(2,1)}, u32[]{:S(2)}, u32[]{:S(2)}) collective-permute-start(bf16[192,1152]{1,0:T(8,128)(2,1)} %concatenate.64), channel_id=1, source_target_pairs={{2,4},{4,2},{3,5},{5,3},{10,12},{12,10},{11,13},{13,11},{18,20},{2... | collective-permute-start | bytes 1327112 | tf_op jit(solution)/shard_map/ppermute | solution.py:580
  12.5 33.2 %collective-permute-start = (bf16[256,1536]{1,0:T(8,128)(2,1)S(1)}, bf16[256,1536]{1,0:T(8,128)(2,1)}, u32[]{:S(2)}, u32[]{:S(2)}) collective-permute-start(bf16[256,1536]{1,0:T(8,128)(2,1)S(1)} %slice.237), channel_id=1, source_target_pairs={{2,4},{4,2},{3,5},{5,3},{10,12},{12,10},{11,13},{13,11},{18,20},{2... | collective-permute-start | bytes 2359304 | tf_op jit(solution)/shard_map/ppermute | solution.py:580
  17.2 28.5 %collective-permute-start.1 = (s32[1,4]{1,0:T(1,128)S(1)}, s32[1,4]{1,0:T(1,128)S(1)}, u32[]{:S(2)}, u32[]{:S(2)}) collective-permute-start(s32[1,4]{1,0:T(1,128)S(1)} %copy-done.91), channel_id=1, source_target_pairs={{2,4},{4,2},{3,5},{5,3},{10,12},{12,10},{11,13},{13,11},{18,20},{2... | collective-permute-start | bytes 56 | tf_op jit(solution)/shard_map/ppermute | solution.py:580
  48.8 37.2 %collective-permute-start.7 = (bf16[384,768]{1,0:T(8,128)(2,1)S(1)}, bf16[384,768]{1,0:T(8,128)(2,1)S(1)}, u32[]{:S(2)}, u32[]{:S(2)}) collective-permute-start(bf16[384,768]{1,0:T(8,128)(2,1)S(1)} %pad_maximum_fusion.9.refs_5_.refs_0_), channel_id=1, source_target_pairs={{0,8},{8,0},{16,24},{24,16},{1,9},{9,1},{17,25},{25,17},{2,10},{10... | collective-permute-start | bytes 1769480 | tf_op jit(solution)/shard_map/ppermute | solution.py:631
  50.4 35.6 %collective-permute-start.8 = (bf16[384,768]{1,0:T(8,128)(2,1)S(1)}, bf16[384,768]{1,0:T(8,128)(2,1)S(1)}, u32[]{:S(2)}, u32[]{:S(2)}) collective-permute-start(bf16[384,768]{1,0:T(8,128)(2,1)S(1)} %pad_maximum_fusion.9.refs_5_.refs_0_), channel_id=1, source_target_pairs={{0,16},{8,24},{16,0},{24,8},{1,17},{9,25},{17,1},{25,9},{2,18},{10... | collective-permute-start | bytes 1769480 | tf_op jit(solution)/shard_map/ppermute | solution.py:631
  53.9 32.1 %collective-permute-start.5 = (bf16[256,1536]{1,0:T(8,128)(2,1)S(1)}, bf16[256,1536]{1,0:T(8,128)(2,1)}, u32[]{:S(2)}, u32[]{:S(2)}) collective-permute-start(bf16[256,1536]{1,0:T(8,128)(2,1)S(1)} %get-tuple-element.213.refs_0_), channel_id=1, source_target_pairs={{0,4},{4,0},{1,5},{5,1},{2,6},{6,2},{3,7},{7,3},{8,12},{12,8},{9,1... | collective-permute-start | bytes 2359304 | tf_op jit(solution)/shard_map/ppermute | solution.py:571
  54.0 32.1 %collective-permute-start.6 = (bf16[256,1536]{1,0:T(8,128)(2,1)S(1)}, bf16[256,1536]{1,0:T(8,128)(2,1)}, u32[]{:S(2)}, u32[]{:S(2)}) collective-permute-start(bf16[256,1536]{1,0:T(8,128)(2,1)S(1)} %get-tuple-element.213.refs_0_), channel_id=1, source_target_pairs={{1,0},{0,1},{3,2},{2,3},{5,4},{4,5},{7,6},{6,7},{9,8},{8,9},{11,10... | collective-permute-start | bytes 2359304 | tf_op jit(solution)/shard_map/ppermute | solution.py:621
  86.1 26.7 %collective-permute-start.9 = (bf16[256,1536]{1,0:T(8,128)(2,1)S(1)}, bf16[256,1536]{1,0:T(8,128)(2,1)}, u32[]{:S(2)}, u32[]{:S(2)}) collective-permute-start(bf16[256,1536]{1,0:T(8,128)(2,1)S(1)} %broadcast_select_fusion.5.refs_1_), channel_id=1, source_target_pairs={{1,0},{0,1},{3,2},{2,3},{5,4},{4,5},{7,6},{6,7},{9,8},{8,9},{11,10... | collective-permute-start | bytes 2359304 | tf_op jit(solution)/shard_map/ppermute | solution.py:621
  130.9 38.1 %collective-permute-start.18 = (bf16[192,2048]{1,0:T(8,128)(2,1)S(1)}, bf16[192,2048]{1,0:T(8,128)(2,1)S(1)}, u32[]{:S(2)}, u32[]{:S(2)}) collective-permute-start(bf16[192,2048]{1,0:T(8,128)(2,1)S(1)} %pad_maximum_fusion.5), channel_id=1, source_target_pairs={{0,2},{6,4},{4,0},{2,6},{1,3},{7,5},{5,1},{3,7},{8,10},{14,12},{12... | collective-permute-start | bytes 2359304 | tf_op jit(solution)/shard_map/ppermute | solution.py:580
  130.9 38.2 %collective-permute-start.19 = (bf16[192,2048]{1,0:T(8,128)(2,1)S(1)}, bf16[192,2048]{1,0:T(8,128)(2,1)S(1)}, u32[]{:S(2)}, u32[]{:S(2)}) collective-permute-start(bf16[192,2048]{1,0:T(8,128)(2,1)S(1)} %pad_maximum_fusion.5), channel_id=1, source_target_pairs={{2,4},{4,2},{3,5},{5,3},{10,12},{12,10},{11,13},{13,11},{18,20},{2... | collective-permute-start | bytes 2359304 | tf_op jit(solution)/shard_map/ppermute | solution.py:580
  135.8 33.3 %collective-permute-start.20 = (bf16[192,768]{1,0:T(8,128)(2,1)}, bf16[192,768]{1,0:T(8,128)(2,1)S(1)}, u32[]{:S(2)}, u32[]{:S(2)}) collective-permute-start(bf16[192,768]{1,0:T(8,128)(2,1)} %slice.251), channel_id=1, source_target_pairs={{0,8},{8,0},{16,24},{24,16},{1,9},{9,1},{17,25},{25,17},{2,10},{10... | collective-permute-start | bytes 884744 | tf_op jit(solution)/shard_map/ppermute | solution.py:631
  138.0 31.0 %collective-permute-start.21 = (bf16[192,768]{1,0:T(8,128)(2,1)}, bf16[192,768]{1,0:T(8,128)(2,1)}, u32[]{:S(2)}, u32[]{:S(2)}) collective-permute-start(bf16[192,768]{1,0:T(8,128)(2,1)} %slice.252), channel_id=1, source_target_pairs={{0,16},{8,24},{16,0},{24,8},{1,17},{9,25},{17,1},{25,9},{2,18},{10... | collective-permute-start | bytes 884744 | tf_op jit(solution)/shard_map/ppermute | solution.py:631
  191.8 36.0 %collective-permute-start.27 = (bf16[1536,768]{1,0:T(8,128)(2,1)}, bf16[1536,768]{1,0:T(8,128)(2,1)S(1)}, u32[]{:S(2)}, u32[]{:S(2)}) collective-permute-start(bf16[1536,768]{1,0:T(8,128)(2,1)} %assemble_out.1), channel_id=1, source_target_pairs={{0,4},{4,0},{1,5},{5,1},{2,6},{6,2},{3,7},{7,3},{8,12},{12,8},{9,1... | collective-permute-start | bytes 7077896 | tf_op jit(solution)/shard_map/ppermute | solution.py:571
  192.4 35.3 %collective-permute-start.30 = (bf16[384,1024]{1,0:T(8,128)(2,1)S(1)}, bf16[384,1024]{1,0:T(8,128)(2,1)S(1)}, u32[]{:S(2)}, u32[]{:S(2)}) collective-permute-start(bf16[384,1024]{1,0:T(8,128)(2,1)S(1)} %pad_maximum_fusion.6.refs_7_.refs_9_.refs_11_), channel_id=1, source_target_pairs={{0,8},{8,0},{16,24},{24,16},{1,9},{9,1},{17,25},{25,17},{2,10},{10... | collective-permute-start | bytes 2359304 | tf_op jit(solution)/shard_map/ppermute | solution.py:631
  193.8 33.9 %collective-permute-start.31 = (bf16[384,1024]{1,0:T(8,128)(2,1)S(1)}, bf16[384,1024]{1,0:T(8,128)(2,1)S(1)}, u32[]{:S(2)}, u32[]{:S(2)}) collective-permute-start(bf16[384,1024]{1,0:T(8,128)(2,1)S(1)} %pad_maximum_fusion.6.refs_7_.refs_9_.refs_11_), channel_id=1, source_target_pairs={{0,16},{8,24},{16,0},{24,8},{1,17},{9,25},{17,1},{25,9},{2,18},{10... | collective-permute-start | bytes 2359304 | tf_op jit(solution)/shard_map/ppermute | solution.py:631
  195.6 30.7 %collective-permute-start.28 = (bf16[256,1536]{1,0:T(8,128)(2,1)S(1)}, bf16[256,1536]{1,0:T(8,128)(2,1)S(1)}, u32[]{:S(2)}, u32[]{:S(2)}) collective-permute-start(bf16[256,1536]{1,0:T(8,128)(2,1)S(1)} %slice.258), channel_id=1, source_target_pairs={{2,4},{4,2},{3,5},{5,3},{10,12},{12,10},{11,13},{13,11},{18,20},{2... | collective-permute-start | bytes 2359304 | tf_op jit(solution)/shard_map/ppermute | solution.py:580
  213.9 25.7 %collective-permute-start.33 = (bf16[192,1024]{1,0:T(8,128)(2,1)S(1)}, bf16[192,1024]{1,0:T(8,128)(2,1)S(1)}, u32[]{:S(2)}, u32[]{:S(2)}) collective-permute-start(bf16[192,1024]{1,0:T(8,128)(2,1)S(1)} %slice.260), channel_id=1, source_target_pairs={{0,8},{8,0},{16,24},{24,16},{1,9},{9,1},{17,25},{25,17},{2,10},{10... | collective-permute-start | bytes 1179656 | tf_op jit(solution)/shard_map/ppermute | solution.py:631
  256.5 25.8 %collective-permute-start.39 = (bf16[256,1536]{1,0:T(8,128)(2,1)}, bf16[256,1536]{1,0:T(8,128)(2,1)}, u32[]{:S(2)}, u32[]{:S(2)}) collective-permute-start(bf16[256,1536]{1,0:T(8,128)(2,1)} %slice.265), channel_id=1, source_target_pairs={{1,0},{0,1},{3,2},{2,3},{5,4},{4,5},{7,6},{6,7},{9,8},{8,9},{11,10... | collective-permute-start | bytes 2359304 | tf_op jit(solution)/shard_map/ppermute | solution.py:621
  256.5 25.8 %collective-permute-start.40 = (bf16[384,1024]{1,0:T(8,128)(2,1)}, bf16[384,1024]{1,0:T(8,128)(2,1)}, u32[]{:S(2)}, u32[]{:S(2)}) collective-permute-start(bf16[384,1024]{1,0:T(8,128)(2,1)} %pad_maximum_fusion.8.refs_14_.refs_16_), channel_id=1, source_target_pairs={{0,8},{8,0},{16,24},{24,16},{1,9},{9,1},{17,25},{25,17},{2,10},{10... | collective-permute-start | bytes 2359304 | tf_op jit(solution)/shard_map/ppermute | solution.py:631
  309.3 27.0 %collective-permute-start.47 = (bf16[256,1536]{1,0:T(8,128)(2,1)}, bf16[256,1536]{1,0:T(8,128)(2,1)}, u32[]{:S(2)}, u32[]{:S(2)}) collective-permute-start(bf16[256,1536]{1,0:T(8,128)(2,1)} %slice.269), channel_id=1, source_target_pairs={{1,0},{0,1},{3,2},{2,3},{5,4},{4,5},{7,6},{6,7},{9,8},{8,9},{11,10... | collective-permute-start | bytes 2359304 | tf_op jit(solution)/shard_map/ppermute | solution.py:621
  311.1 25.2 %collective-permute-start.48 = (bf16[256,1536]{1,0:T(8,128)(2,1)}, bf16[256,1536]{1,0:T(8,128)(2,1)}, u32[]{:S(2)}, u32[]{:S(2)}) collective-permute-start(bf16[256,1536]{1,0:T(8,128)(2,1)} %collective-permute-done.43.refs_1_), channel_id=1, source_target_pairs={{0,4},{4,0},{1,5},{5,1},{2,6},{6,2},{3,7},{7,3},{8,12},{12,8},{9,1... | collective-permute-start | bytes 2359304 | tf_op jit(solution)/shard_map/ppermute | solution.py:571
  416.7 120.4 %reduce-scatter.6.cloned.1.call-start = ((), (), s32[]{:S(2)}) async-start(), calls=%async_computation.4 | async-start | bytes 3932160 | tf_op jit(solution)/shard_map/reduce_scatter | solution.py:921
  443.6 174.3 %reduce-scatter.8.cloned.1.call-start = ((), (), s32[]{:S(2)}) async-start(), calls=%async_computation.5 | async-start | bytes 2949120 | tf_op jit(solution)/shard_map/reduce_scatter | solution.py:946
  487.4 53.6 %collective-permute-start.64 = (bf16[512,1536]{1,0:T(8,128)(2,1)S(1)}, bf16[512,1536]{1,0:T(8,128)(2,1)S(1)}, u32[]{:S(2)}, u32[]{:S(2)}) collective-permute-start(bf16[512,1536]{1,0:T(8,128)(2,1)S(1)} %copy-done.30), channel_id=1, source_target_pairs={{2,4},{4,2},{3,5},{5,3},{10,12},{12,10},{11,13},{13,11},{18,20},{2... | collective-permute-start | bytes 4718600 | tf_op jit(solution)/shard_map/ppermute | solution.py:580
  491.9 49.1 %collective-permute-start.65 = (bf16[192,2048]{1,0:T(8,128)(2,1)}, bf16[192,2048]{1,0:T(8,128)(2,1)}, u32[]{:S(2)}, u32[]{:S(2)}) collective-permute-start(bf16[192,2048]{1,0:T(8,128)(2,1)} %get-tuple-element.440), channel_id=1, source_target_pairs={{2,0},{4,6},{0,4},{6,2},{3,1},{5,7},{1,5},{7,3},{10,8},{12,14},{8,... | collective-permute-start | bytes 2359304 | tf_op jit(solution)/shard_map/ppermute | solution.py:580
  573.4 29.4 %collective-permute-start.69 = (bf16[256,1536]{1,0:T(8,128)(2,1)S(1)}, bf16[256,1536]{1,0:T(8,128)(2,1)S(1)}, u32[]{:S(2)}, u32[]{:S(2)}) collective-permute-start(bf16[256,1536]{1,0:T(8,128)(2,1)S(1)} %slice.285), channel_id=1, source_target_pairs={{0,1},{1,0},{2,3},{3,2},{4,5},{5,4},{6,7},{7,6},{8,9},{9,8},{10,11... | collective-permute-start | bytes 2359304 | tf_op jit(solution)/shard_map/ppermute | solution.py:626
  641.6 25.3 %collective-permute-start.80 = (bf16[192,768]{1,0:T(8,128)(2,1)S(1)}, bf16[192,768]{1,0:T(8,128)(2,1)S(1)}, u32[]{:S(2)}, u32[]{:S(2)}) collective-permute-start(bf16[192,768]{1,0:T(8,128)(2,1)S(1)} %get-tuple-element.460), channel_id=1, source_target_pairs={{2,4},{4,2},{3,5},{5,3},{10,12},{12,10},{11,13},{13,11},{18,20},{2... | collective-permute-start | bytes 884744 | tf_op jit(solution)/shard_map/ppermute | solution.py:580
  648.9 36.9 %collective-permute-start.78 = (bf16[256,1536]{1,0:T(8,128)(2,1)}, bf16[256,1536]{1,0:T(8,128)(2,1)S(1)}, u32[]{:S(2)}, u32[]{:S(2)}) collective-permute-start(bf16[256,1536]{1,0:T(8,128)(2,1)} %fusion.2), channel_id=1, source_target_pairs={{2,4},{4,2},{3,5},{5,3},{10,12},{12,10},{11,13},{13,11},{18,20},{2... | collective-permute-start | bytes 2359304 | tf_op jit(solution)/shard_map/ppermute | solution.py:580
  654.0 31.0 %collective-permute-start.82 = (bf16[192,384]{1,0:T(8,128)(2,1)S(1)}, bf16[192,384]{1,0:T(8,128)(2,1)S(1)}, u32[]{:S(2)}, u32[]{:S(2)}) collective-permute-start(bf16[192,384]{1,0:T(8,128)(2,1)S(1)} %get-tuple-element.462), channel_id=1, source_target_pairs={{2,0},{4,6},{0,4},{6,2},{3,1},{5,7},{1,5},{7,3},{10,8},{12,14},{8,... | collective-permute-start | bytes 442376 | tf_op jit(solution)/shard_map/ppermute | solution.py:580
  654.1 30.9 %collective-permute-start.83 = (bf16[192,384]{1,0:T(8,128)(2,1)S(1)}, bf16[192,384]{1,0:T(8,128)(2,1)S(1)}, u32[]{:S(2)}, u32[]{:S(2)}) collective-permute-start(bf16[192,384]{1,0:T(8,128)(2,1)S(1)} %get-tuple-element.461), channel_id=1, source_target_pairs={{2,4},{4,2},{3,5},{5,3},{10,12},{12,10},{11,13},{13,11},{18,20},{2... | collective-permute-start | bytes 442376 | tf_op jit(solution)/shard_map/ppermute | solution.py:580
  (154 other events, 1981.2 us)
Sparse Core Ops, SparseCore 0:
  416.9 70.4 reduce-scatter.3
  490.3 43.9 reduce-scatter.5
  548.0 42.9 reduce-scatter.7

commit v3 on v2

--- a/solution.py
+++ b/solution.py
@@ -717,8 +717,7 @@
     gate_up_shard = jnp.concatenate([gate_weight, up_weight], axis=1)
     part_rows = rows // 2
     upper = swap(tokens[:part_rows])
-    shard = jnp.concatenate([qkv_shard, out_weight], axis=1)
-    shard_moved = send_z(shard)
+    shard_moved = send_z(qkv_shard)
     lengths = swap(seq_lengths)
     gains = lax.all_gather(jnp.stack([attn_gain, mlp_gain]), ("yx", "core"), axis=1, tiled=True).astype(f32)
     upper, lengths, second_part, gains, *shard_moved = stage(upper, lengths, tokens[part_rows:], gains, *shard_moved)
@@ -726,9 +725,7 @@
 
     upper_far = [from_near(upper, k) for k in others]
     lower = swap(second_part)
-    pair, out_pair = (
-        pair_of(*(x[:, cols] for x in (shard, *shard_moved))) for cols in (slice(0, qkv_cols), slice(qkv_cols, None))
-    )
+    pair = pair_of(qkv_shard, *shard_moved)
     taken = neighbours(pair)
     upper_sib = flip(upper, "core")
 
@@ -751,100 +748,90 @@
     start_row = jnp.tile(doc_start.reshape(-1, 1, SUB), (1, 1, q_heads // kv_heads))
     layout = (place, *bounds(TILE), cosine, sine, doc_start[:, None])
     layout_back = (place, *bounds(SUB), cosine, sine, start_row)
-    lower, upper_sib, out_pair, *moved = stage(lower, upper_sib, out_pair, *upper_far, *taken, *layout, *layout_back)
+    lower, upper_sib, down_shard, out_shard, *moved = stage(
+        lower, upper_sib, down_weight, out_weight, *upper_far, *taken, *layout, *layout_back
+    )
     upper_far, moved = moved[: near - 1], moved[near - 1 :]
     taken, moved = moved[: len(taken)], moved[len(taken) :]
     layout, layout_back = moved[: len(layout)], moved[len(layout) :]
 
     lower_far = [from_near(lower, k) for k in others]
     lower_sib = flip(lower, "core")
-    out_far = [from_near(out_pair, k) for k in others]
+    down_out = crossed(down_shard, OUT)
     blocks = blocks_of(pair, taken, diagonal(taken))
     projecting = [(*blocks, qkv_cols)]
     gain_row = gain_one[None]
     outs = [(tokens.shape[1], bf16, "all"), (qkv_cols, bf16, "all")]
     parts = [upper, lower, upper_sib, lower_sib]
     normed = piece_call(project_kernel, "project", 0, near, me, parts, [gain_row], [], projecting, [], outs)
-    gate_up_shard, *moved = stage(gate_up_shard, *lower_far, *out_far, *normed)
-    lower_far, out_far, normed = moved[: near - 1], moved[near - 1 : 2 * near - 2], moved[2 * near - 2 :]
-
-    out_own = jnp.concatenate([out_pair, *out_far], axis=1)
-    out_taken = neighbours(out_own)
+    gate_up_shard, down_out, down_shard, out_shard, *moved = stage(
+        gate_up_shard, down_out, down_shard, out_shard, *lower_far, *normed
+    )
+    lower_far, normed = moved[: near - 1], moved[near - 1 :]
+
+    down_cross = crossed(down_shard, CROSS)
+    out_moved = send_z(out_shard)
     for k in others:
         parts = [upper_far[k - 1], lower_far[k - 1], flip(upper_far[k - 1], "core"), flip(lower_far[k - 1], "core")]
         normed = piece_call(project_kernel, "project", k, near, me, parts, [gain_row], [], projecting, normed, outs)
     norm_one, qkv = normed
-    gate_up_shard, qkv, out_own, *out_taken = stage(gate_up_shard, qkv, out_own, *out_taken)
+    gate_up_shard, qkv, down_cross, *out_moved = stage(gate_up_shard, qkv, down_cross, *out_moved)
 
     gate_up_moved = send_z(gate_up_shard)
-    out_halves = diagonal(out_taken)
-    context, sums = attend(qkv, 2 * near, layout, q_heads, kv_heads)
-    down_shard, cotangent, *moved = stage(down_weight, cotangent, *context, *gate_up_moved, *out_halves)
-    context, gate_up_moved, out_halves = moved[: 2 * near], moved[2 * near : 2 * near + 2], moved[2 * near + 2 :]
-
-    quarters = {(0, 0): context[0]}
-    for k in range(near):
-        for e in range(2):
-            if (e, k) != (0, 0):
-                quarters[e, (near - k) % near] = shift(context[2 * k + e], e, k)
+    out_pair = pair_of(out_weight, *out_moved)
+    out_far = [from_near(out_pair, k) for k in others]
+    context, sums = attend(qkv, near, layout, q_heads, kv_heads)
+    cotangent, *moved = stage(cotangent, *context, *gate_up_moved, *out_far)
+    context, gate_up_moved, out_far = moved[:near], moved[near : near + 2], moved[near + 2 :]
+
+    quarters = [context[0]] + [None] * (near - 1)
+    for k in others:
+        quarters[near - k] = to_near(context[k], k)
+    cot_upper = crossed(cotangent[:part_rows], CROSS)
     pairs = [
         pair_of(*(x[:, n * hidden_cols : (n + 1) * hidden_cols] for x in (gate_up_shard, *gate_up_moved)))
         for n in range(2)
     ]
     gate_taken = neighbours(pairs[0])
-    order = [(e, k) for e in range(2) for k in range(near)]
-    up_pair, down_shard, cotangent, *moved = stage(
-        pairs[1], down_shard, cotangent, *(quarters[at] for at in order), *gate_taken, *out_halves
-    )
-    quarters, moved = moved[: 2 * near], moved[2 * near :]
-    gate_taken, out_halves = moved[: len(gate_taken)], moved[len(gate_taken) :]
+    w_out = lax.all_gather(jnp.concatenate([out_pair, *out_far], axis=1), "yx", axis=0, tiled=True)
+    up_pair, cotangent, cot_upper, *moved = stage(pairs[1], cotangent, cot_upper, *quarters, *gate_taken)
+    quarters, gate_taken = moved[:near], moved[near:]
 
     up_taken = neighbours(up_pair)
-    cot_upper = crossed(cotangent[:part_rows], CROSS)
-    down_out = crossed(down_shard, OUT)
-    w_out_near = assemble(
-        "assemble_out", me, *blocks_of(out_own, out_taken, out_halves), tokens.shape[1], near * query_cols
-    )
-    w_out_sib = flip(w_out_near, "core")
+    cot_lower = crossed(cotangent[part_rows:], CROSS)
     residual = jnp.concatenate([upper, lower], axis=0).astype(f32)
     scale_one = lax.rsqrt(jnp.mean(residual * residual, axis=-1, keepdims=True) + EPSILON)
-    w_out_sib, w_out_near, scale_one, cotangent, cot_upper, down_shard, down_out, *up_taken = stage(
-        w_out_sib, w_out_near, scale_one, cotangent, cot_upper, down_shard, down_out, *up_taken
-    )
+    context_all = jnp.concatenate(quarters, axis=1)
+    w_out, scale_one, cot_lower, context_all, *up_taken = stage(w_out, scale_one, cot_lower, context_all, *up_taken)
 
     gate_halves, up_halves = diagonal(gate_taken), diagonal(up_taken)
-    down_cross = crossed(down_shard, CROSS)
-    own_context = jnp.concatenate(quarters[:near], axis=1)
-    sib_context = jnp.concatenate(quarters[near:], axis=1)
-    mid = residual + times_transpose(own_context, w_out_near) + times_transpose(sib_context, w_out_sib)
+    branch_sib = flip(times_transpose(context_all[rows:], w_out).astype(bf16), "core")
+    mid = residual + times_transpose(context_all[:rows], w_out) + branch_sib.astype(f32)
     scale_two, norm_two = norm_rows(mid, gain_two)
-    norm_two, cotangent, cot_upper, down_cross, *moved = stage(
-        norm_two, cotangent, cot_upper, down_cross, *gate_halves, *up_halves
-    )
+    norm_two, *moved = stage(norm_two, *gate_halves, *up_halves)
     gate_halves, up_halves = moved[: len(gate_halves)], moved[len(gate_halves) :]
     norm_sib = flip(norm_two, "core")
-    down_pair = pair_of(down_shard, down_out, down_cross)
-    norm_two, norm_sib, down_pair = stage(norm_two, norm_sib, down_pair)
+    cot = jnp.where(straight(), cotangent, jnp.concatenate([cot_upper, cot_lower], axis=0))
+    cot_sib = flip(cot, "core")
+    down_pair = pair_of(down_weight, down_out, down_cross)
+    norm_two, norm_sib, cot, cot_sib, down_pair = stage(norm_two, norm_sib, cot, cot_sib, down_pair)
 
     upper_far = [from_near(norm_two[:part_rows], k) for k in others]
     down_taken = neighbours(down_pair)
-    cot_lower = crossed(cotangent[part_rows:], CROSS)
     gate_blocks = blocks_of(pairs[0], gate_taken, gate_halves)
     up_blocks = blocks_of(up_pair, up_taken, up_halves, hidden_cols)
     gate_up = ([*gate_blocks[0], *up_blocks[0]], gate_blocks[1] + up_blocks[1], 2 * hidden_cols)
     outs = [(norm_two.shape[1], bf16, "all"), (2 * hidden_cols, f32, "all"), (hidden_cols, bf16, "all")]
     earlier = piece_call(gate_kernel, "gate", 0, near, me, [norm_two, norm_sib], [], [], [gate_up], [], outs)
-    norm_two, cot_lower, *moved = stage(norm_two, cot_lower, *upper_far, *down_taken, *earlier)
+    norm_two, *moved = stage(norm_two, *upper_far, *down_taken, *earlier)
     upper_far, moved = moved[: near - 1], moved[near - 1 :]
     down_taken, earlier = moved[: len(down_taken)], moved[len(down_taken) :]
 
     lower_far = [from_near(norm_two[part_rows:], k) for k in others]
     upper_far_sib = [flip(x, "core") for x in upper_far]
     down_halves = diagonal(down_taken)
-    cot = jnp.where(straight(), cotangent, jnp.concatenate([cot_upper, cot_lower], axis=0))
-    cot_sib = flip(cot, "core")
     w_project = assemble("assemble_project", me, *blocks, tokens.shape[1], qkv_cols)
-    cot, cot_sib, w_project, *moved = stage(cot, cot_sib, w_project, *lower_far, *upper_far_sib, *down_halves)
+    w_project, *moved = stage(w_project, *lower_far, *upper_far_sib, *down_halves)
     lower_far, upper_far_sib, down_halves = moved[: near - 1], moved[near - 1 : 2 * near - 2], moved[2 * near - 2 :]
     lower_far_sib = [flip(x, "core") for x in lower_far]
 
@@ -924,16 +911,19 @@
     mid_back, _ = norm_back(mid, scale_two, gain_two, d_norm_two)
     d_mid = cot.astype(f32) + mid_back
     d_attn = d_mid.astype(bf16)
-    both = [dot32(d_attn, w).astype(bf16) for w in (w_out_near, w_out_sib)]
-    d_quarters = [both[e][:, k * query_cols : (k + 1) * query_cols] for e, k in order]
-    d_attn, *moved = stage(d_attn, *d_quarters, *out_lower)
-    d_quarters, out_lower = moved[: 2 * near], moved[2 * near :]
-
-    d_context = [None] * (2 * near)
-    for (e, k), x in zip(order, d_quarters, strict=True):
-        d_context[(near - k) % near * 2 + e] = x if (e, k) == (0, 0) else shift(x, e, k)
-    grad_out_sib = flip(rows_product(d_attn, sib_context).astype(bf16), "core")
-    grad_out = (rows_product(d_attn, own_context) + grad_out_sib.astype(f32)).astype(bf16)
+    d_attn_sib = flip(d_attn, "core")
+    both = [dot32(x, w_out).astype(bf16) for x in (d_attn, d_attn_sib)]
+    d_quarters = [
+        jnp.concatenate([x[:, k * query_cols : (k + 1) * query_cols] for x in both], axis=0) for k in range(near)
+    ]
+    d_attn, d_attn_sib, *moved = stage(d_attn, d_attn_sib, *d_quarters, *out_lower)
+    d_quarters, out_lower = moved[:near], moved[near:]
+
+    d_context = [d_quarters[0]] + [None] * (near - 1)
+    for k in others:
+        d_context[near - k] = to_near(d_quarters[k], k)
+    grad_out = rows_product(d_attn, context_all[:rows]) + rows_product(d_attn_sib, context_all[rows:])
+    grad_out = grad_out.astype(bf16)
     output_own = mid + joined(*near_back[2:])
     for one, two in zip(out_upper, out_lower, strict=True):
         output_own = output_own + jnp.concatenate([one, two], axis=0).astype(f32)

time: 703 us -> 686 us (0.976)
  blocking collectives: 25 us -> 35 us
  waiting for transfers between devices: 201 us -> 191 us
  local copies, waits for them, and re-layouts: 44.6 us -> 35.6 us
    ppermute x24 -> x20, waiting for transfers between devices: 28.7 us -> 56.9 us  [across(): return lax.ppermute(x, 'yx', [(a, a ^ j) for a in range(n)])]
    ppermute x22 -> x24, waiting for transfers between devices: 102 us -> 77.7 us  [crossed(): return lax.ppermute(x, ('core', 'zh'), perm)]
    ppermute x7 -> x9, waiting for transfers between devices: 16.2 us -> 37.6 us  [to_near(): return lax.ppermute(x, 'zl', [(j, (j + k) % n) for j in range(n)])]
    ppermute x6 -> x0, waiting for transfers between devices: 20 us -> none  [shift(): lax.ppermute(x, ('core', 'zl'), [(c * n + l, (c ^ e) * n + (l + k) % n) f...]
    psum x1, blocking collectives: 15.7 us -> 25.7 us  [body(): lax.psum(jnp.stack([jnp.sum(qkv_shard.astype(f32) * grad_project, axis=1)...]
    ppermute x7, waiting for transfers between devices: 16.2 us -> 7.27 us  [from_near(): return lax.ppermute(x, 'zl', [((j + k) % n, j) for j in range(n)])]
    ppermute x24 -> x20, starting transfers between devices: 24.5 us -> 19.1 us  [across(): return lax.ppermute(x, 'yx', [(a, a ^ j) for a in range(n)])]
    ppermute x22 -> x24, starting transfers between devices: 53.3 us -> 58.5 us  [crossed(): return lax.ppermute(x, ('core', 'zh'), perm)]
  transfers between devices with their start and end apart: 87 -> 82, of which waited for: 34 -> 36; matrix products, arithmetic and copies ran while one was open for 20% -> 19% of each run, Pallas kernels for 25% -> 26%
where the time goes in v3:
time: 686 us; the launch traced here: 676 us
  waiting for transfers between devices  191 us (28%)
  Pallas kernels  175 us (26%)
  starting transfers between devices  100 us (15%)
  other arithmetic  65.1 us (9%)
  matrix products  58.8 us (9%)
  local copies, waits for them, and re-layouts  35.6 us (5%)
  blocking collectives  35 us (5%)
  between operations  15.8 us (2%)
    pallas_call x6, Pallas kernels, piece_call(): pl.pallas_call(functools.partial(kernel, count, tuple((where for _, where...  97.2 us
    ppermute x24, waiting for transfers between devices, crossed(): return lax.ppermute(x, ('core', 'zh'), perm)  77.7 us
    ppermute x24, starting transfers between devices, crossed(): return lax.ppermute(x, ('core', 'zh'), perm)  58.5 us
    ppermute x20, waiting for transfers between devices, across(): return lax.ppermute(x, 'yx', [(a, a ^ j) for a in range(n)])  56.9 us
    pallas_call x1, Pallas kernels, attend_back(): pl.pallas_call(functools.partial(backward_kernel, pieces, ratio, bool(ear...  45.7 us
    dot_general x5, matrix products, rows_product(): lax.dot_general(left, right, (((0,), (0,)), ((), ())), preferred_element_...  40.2 us
    ppermute x9, waiting for transfers between devices, to_near(): return lax.ppermute(x, 'zl', [(j, (j + k) % n) for j in range(n)])  37.6 us
    pallas_call x1, Pallas kernels, attend(): pl.pallas_call(functools.partial(forward_kernel, pieces, ratio), out_shap...  29 us
  transfers between devices with their start and end apart: 82, of which 36 were waited for; matrix products, arithmetic and copies ran while one was open for 19% of the time, Pallas kernels for 26%

profile of v3, /device:TPU:16, one launch (start us, length us, event | category | flops | bytes accessed | tf_op | source)
XLA Modules:
  0.0 676.3 jit_solution(7776869424226967233)
XLA Ops:
  11.7 4.5 collective-permute-start
  18.8 9.3 %all-gather = bf16[8,192,2]{1,2,0:T(2,128)(2,1)S(1)} all-gather(bf16[1,192,2]{1,2,0:T(2,128)(2,1)S(1)} %fusion.23), channel_id=1, replica_groups=mesh['yx'=4,'core'=2,'zh'=2,'zl'=2] {'yx','core'}, dimensions={0}, use_global_device_ids=true | all-gather | bytes 6912 | tf_op jit(solution)/shard_map/all_gather | solution.py:722
  28.9 9.4 %collective-permute-done.1 = s32[1,4]{1,0:T(1,128)S(1)} collective-permute-done((s32[1,4]{1,0:T(1,128)S(1)}, s32[1,4]{1,0:T(1,128)S(1)}, u32[]{:S(2)}, u32[]{:S(2)}) %collective-permute-start.1) | collective-permute-done | bytes 48 | tf_op jit(solution)/shard_map/ppermute | solution.py:580
  45.0 5.8 collective-permute-start.6
  61.2 14.6 %collective-permute-done.4 = bf16[256,1536]{1,0:T(8,128)(2,1)} collective-permute-done((bf16[256,1536]{1,0:T(8,128)(2,1)S(1)}, bf16[256,1536]{1,0:T(8,128)(2,1)}, u32[]{:S(2)}, u32[]{:S(2)}) %collective-permute-start.4) | collective-permute-done | bytes 786464 | tf_op jit(solution)/shard_map/ppermute | solution.py:580
  82.5 6.8 %collective-permute-done.12.refs_8_.refs_3_ = bf16[192,768]{1,0:T(8,128)(2,1)S(1)} collective-permute-done((bf16[192,768]{1,0:T(8,128)(2,1)}, bf16[192,768]{1,0:T(8,128)(2,1)S(1)}, u32[]{:S(2)}, u32[]{:S(2)}) %collective-permute-start.12) | collective-permute-done | bytes 294944 | tf_op jit(solution)/shard_map/ppermute | solution.py:631
  91.0 8.5 %project_0.1 = (bf16[2048,1536]{1,0:T(8,128)(2,1)}, bf16[2048,768]{1,0:T(8,128)(2,1)}) custom-call(s32[1]{0:T(128)} %bitcast.7.me, bf16[256,1536]{1,0:T(8,128)(2,1)} %copy-done.12, bf16[256,1536]{1,0:T(8,128)(2,1)} %copy-done.9, bf16[256,1536]{1,0:T(8,128)(2,1)} %collective-permute-done.5.refs_2_, bf16[256,1536]{1,0:T(8,128)(2,1)} %collective-permute-done.11.refs_3_, ...), custom_call_target="tpu_custom_call" | custom-call | flops 1048576 | bytes 65536 | tf_op jit(solution)/shard_map/project_0/pallas_call | solution.py:522
  111.0 8.5 %project_1.1 = (bf16[2048,1536]{1,0:T(8,128)(2,1)}, bf16[2048,768]{1,0:T(8,128)(2,1)}) custom-call(s32[1]{0:T(128)} %bitcast.7.me, bf16[256,1536]{1,0:T(8,128)(2,1)} %collective-permute-done.6.refs_0_, bf16[256,1536]{1,0:T(8,128)(2,1)} %collective-permute-done.10.refs_1_, ...), custom_call_target="tpu_custom_call", output_to_operand_aliasing={{0}: (11, {}), {1}: (12, {})} | custom-call | flops 1048576 | bytes 65536 | tf_op jit(solution)/shard_map/project_1/pallas_call | solution.py:522
  122.5 4.8 collective-permute-start.20
  128.8 29.0 %attention_forward.1 = (bf16[1024,384]{1,0:T(8,128)(2,1)}, bf16[1024,384]{1,0:T(8,128)(2,1)}, f32[4,1,1024]{2,1,0:T(1,128)}, f32[4,1,1024]{2,1,0:T(1,128)}) custom-call(s32[16]{0:T(128)} %pad_add_fusion.refs_0_, s32[4]{0:T(128)} %get-tuple-element.221.refs_1_, s32[4]{0:T(128)} %get-tuple-element.222.refs_2_, f32[2048,128]{1,0:T(8,128)} %get-tuple-element.344.refs_3_, ...), custom_call_target="tpu_custom_call" | custom-call | flops 1048576 | bytes 65536 | tf_op jit(solution)/shard_map/attention_forward/pallas_call | solution.py:333
  166.4 18.1 %collective-permute-done.24.refs_3_.refs_5_.refs_7_ = bf16[384,1024]{1,0:T(8,128)(2,1)S(1)} collective-permute-done((bf16[384,1024]{1,0:T(8,128)(2,1)S(1)}, bf16[384,1024]{1,0:T(8,128)(2,1)S(1)}, u32[]{:S(2)}, u32[]{:S(2)}) %collective-permute-start.24) | collective-permute-done | bytes 786464 | tf_op jit(solution)/shard_map/ppermute | solution.py:631
  198.0 13.1 %collective-permute-done.26 = bf16[256,1536]{1,0:T(8,128)(2,1)S(1)} collective-permute-done((bf16[256,1536]{1,0:T(8,128)(2,1)S(1)}, bf16[256,1536]{1,0:T(8,128)(2,1)S(1)}, u32[]{:S(2)}, u32[]{:S(2)}) %collective-permute-start.26) | collective-permute-done | bytes 786464 | tf_op jit(solution)/shard_map/ppermute | solution.py:580
  211.0 5.1 collective-permute-done.27.refs_8_.refs_10_.refs_12_
  233.8 7.0 %collective-permute-done.32.refs_10_.refs_12_.refs_14_ = bf16[192,1024]{1,0:T(8,128)(2,1)S(1)} collective-permute-done((bf16[192,1024]{1,0:T(8,128)(2,1)S(1)}, bf16[192,1024]{1,0:T(8,128)(2,1)S(1)}, u32[]{:S(2)}, u32[]{:S(2)}) %collective-permute-start.32) | collective-permute-done | bytes 393248 | tf_op jit(solution)/shard_map/ppermute | solution.py:631
  247.9 14.2 %gate_0.1 = (bf16[2048,1536]{1,0:T(8,128)(2,1)}, f32[2048,2048]{1,0:T(8,128)}, bf16[2048,1024]{1,0:T(8,128)(2,1)}) custom-call(s32[1]{0:T(128)} %bitcast.7.me, bf16[512,1536]{1,0:T(8,128)(2,1)} %copy-done.8, bf16[512,1536]{1,0:T(8,128)(2,1)} %copy-done.48, bf16[384,1024]{1,0:T(8,128)(2,1)} %copy-done.2, bf16[384,1024]{1,0:T(8,128)(2,1)} %copy-done.4, ...), custom_call_target="tpu_custom_call" | custom-call | flops 1048576 | bytes 65536 | tf_op jit(solution)/shard_map/gate_0/pallas_call | solution.py:522
  289.9 25.2 %gate_back_0.1 = (bf16[2048,1536]{1,0:T(8,128)(2,1)}, bf16[2048,2048]{1,0:T(8,128)(2,1)}, bf16[512,1536]{1,0:T(8,128)(2,1)}, bf16[512,1536]{1,0:T(8,128)(2,1)}, ...) custom-call(s32[1]{0:T(128)} %bitcast.7.me, bf16[512,1536]{1,0:T(8,128)(2,1)} %copy-done.1, ...), custom_call_target="tpu_custom_call" | custom-call | flops 1048576 | bytes 65536 | tf_op jit(solution)/shard_map/gate_back_0/pallas_call | solution.py:522
  318.8 19.3 %gate_1.1 = (bf16[2048,1536]{1,0:T(8,128)(2,1)}, f32[2048,2048]{1,0:T(8,128)}, bf16[2048,1024]{1,0:T(8,128)(2,1)}, bf16[512,1536]{1,0:T(8,128)(2,1)}, bf16[512,1536]{1,0:T(8,128)(2,1)}) custom-call(s32[1]{0:T(128)} %bitcast.7.me, bf16[256,1536]{1,0:T(8,128)(2,1)} %collective-permute-done.36.refs_0_, ...), custom_call_target="tpu_custom_call", output_to_operand_aliasing={{0}: (20, {}), {1}: (21, {}), {2}: (22, {})} | custom-call | flops 1048576 | bytes 65536 | tf_op jit(solution)/shard_map/gate_1/pallas_call | solution.py:522
  346.6 21.5 %gate_back_1.1 = (bf16[2048,1536]{1,0:T(8,128)(2,1)}, bf16[2048,2048]{1,0:T(8,128)(2,1)}, bf16[512,1536]{1,0:T(8,128)(2,1)}, bf16[512,1536]{1,0:T(8,128)(2,1)}) custom-call(s32[1]{0:T(128)} %bitcast.7.me, bf16[256,1536]{1,0:T(8,128)(2,1)} %collective-permute-done.43.refs_0_, ...), custom_call_target="tpu_custom_call", output_to_operand_aliasing={{0}: (22, {}), {1}: (23, {})} | custom-call | flops 1048576 | bytes 65536 | tf_op jit(solution)/shard_map/gate_back_1/pallas_call | solution.py:522
  377.0 19.1 %convolution_convert_fusion = bf16[1536,2048]{1,0:T(8,128)(2,1)} fusion(bf16[2048,1536]{1,0:T(8,128)(2,1)} %get-tuple-element.297, bf16[2048,2048]{1,0:T(8,128)(2,1)} %get-tuple-element.318), kind=kOutput, calls=%fused_computation | convolution fusion | flops 12888047616 | bytes 20971520 | tf_op jit(solution)/shard_map/dot_general | solution.py:63
  399.1 11.2 %convolution_convert_fusion.1 = bf16[1536,1024]{1,0:T(8,128)(2,1)} fusion(bf16[2048,1536]{1,0:T(8,128)(2,1)} %get-tuple-element.323, bf16[2048,1024]{1,0:T(8,128)(2,1)} %get-tuple-element.304.refs_5_), kind=kOutput, calls=%fused_computation.2 | convolution fusion | flops 6444023808 | bytes 13631488 | tf_op jit(solution)/shard_map/dot_general | solution.py:63
  413.1 5.5 collective-permute-done.53
  421.6 6.0 fusion.24
  436.7 11.0 %collective-permute-done.55 = bf16[256,1536]{1,0:T(8,128)(2,1)S(1)} collective-permute-done((bf16[256,1536]{1,0:T(8,128)(2,1)S(1)}, bf16[256,1536]{1,0:T(8,128)(2,1)S(1)}, u32[]{:S(2)}, u32[]{:S(2)}) %collective-permute-start.55) | collective-permute-done | bytes 786464 | tf_op jit(solution)/shard_map/ppermute | solution.py:626
  457.7 9.8 %collective-permute-done.57.refs_12_ = bf16[1024,384]{1,0:T(8,128)(2,1)} collective-permute-done((bf16[1024,384]{1,0:T(8,128)(2,1)}, bf16[1024,384]{1,0:T(8,128)(2,1)}, u32[]{:S(2)}, u32[]{:S(2)}) %collective-permute-start.57) | collective-permute-done | bytes 786464 | tf_op jit(solution)/shard_map/ppermute | solution.py:626
  474.7 45.7 %attention_backward_0.1 = bf16[2048,768]{1,0:T(8,128)(2,1)} custom-call(s32[16]{0:T(128)} %pad_add_fusion.refs_0_, s32[8]{0:T(128)} %get-tuple-element.342.refs_1_, s32[8]{0:T(128)} %get-tuple-element.343.refs_2_, f32[2048,128]{1,0:T(8,128)} %get-tuple-element.344.refs_3_, f32[2048,128]{1,0:T(8,128)} %get-tuple-element.345.refs_4_, ...), custom_call_target="tpu_custom_call" | custom-call | flops 1048576 | bytes 65536 | tf_op jit(solution)/shard_map/attention_backward_0/pallas_call | solution.py:363
  527.7 5.6 collective-permute-start.60
  539.7 10.7 %collective-permute-done.60 = bf16[192,2048]{1,0:T(8,128)(2,1)S(1)} collective-permute-done((bf16[192,2048]{1,0:T(8,128)(2,1)}, bf16[192,2048]{1,0:T(8,128)(2,1)S(1)}, u32[]{:S(2)}, u32[]{:S(2)}) %collective-permute-start.60) | collective-permute-done | bytes 786464 | tf_op jit(solution)/shard_map/ppermute | solution.py:580
  554.6 5.5 convolution_convert_fusion.2
  571.5 9.8 %collective-permute-done.67 = bf16[192,1024]{1,0:T(8,128)(2,1)S(1)} collective-permute-done((bf16[192,1024]{1,0:T(8,128)(2,1)S(1)}, bf16[192,1024]{1,0:T(8,128)(2,1)S(1)}, u32[]{:S(2)}, u32[]{:S(2)}) %collective-permute-start.67) | collective-permute-done | bytes 393248 | tf_op jit(solution)/shard_map/ppermute | solution.py:580
  598.3 12.7 %collective-permute-done.68 = bf16[256,1536]{1,0:T(8,128)(2,1)} collective-permute-done((bf16[256,1536]{1,0:T(8,128)(2,1)}, bf16[256,1536]{1,0:T(8,128)(2,1)}, u32[]{:S(2)}, u32[]{:S(2)}) %collective-permute-start.68) | collective-permute-done | bytes 786464 | tf_op jit(solution)/shard_map/ppermute | solution.py:580
  611.0 6.9 %collective-permute-done.69 = bf16[256,1536]{1,0:T(8,128)(2,1)} collective-permute-done((bf16[256,1536]{1,0:T(8,128)(2,1)}, bf16[256,1536]{1,0:T(8,128)(2,1)}, u32[]{:S(2)}, u32[]{:S(2)}) %collective-permute-start.69) | collective-permute-done | bytes 786464 | tf_op jit(solution)/shard_map/ppermute | solution.py:626
  638.6 25.7 %psum.7 = f32[2,192]{1,0:T(2,128)S(1)} all-reduce(f32[2,192]{1,0:T(2,128)S(1)} %pad_maximum_fusion.18), channel_id=1, replica_groups=mesh['yx'=4,'core'=2,'zh'=2,'zl'=2] {'zh','zl'}, use_global_device_ids=true, to_apply=%region_12.13 | all-reduce | flops 384 | bytes 3072 | tf_op jit(solution)/shard_map/psum | solution.py:1001
  (445 shorter events, 250.5 us)
Async XLA Ops:
  7.2 209.7 %all-gather.3.cloned.1.call-start = ((), (), s32[]{:S(2)}) async-start(), calls=%async_computation.3 | async-start | bytes 2949120 | tf_op jit(solution)/shard_map/all_gather | solution.py:796
  8.5 31.2 %collective-permute-start.2 = (bf16[192,768]{1,0:T(8,128)(2,1)S(1)}, bf16[192,768]{1,0:T(8,128)(2,1)}, u32[]{:S(2)}, u32[]{:S(2)}) collective-permute-start(bf16[192,768]{1,0:T(8,128)(2,1)S(1)} %pad_maximum_fusion.16), channel_id=1, source_target_pairs={{0,2},{6,4},{4,0},{2,6},{1,3},{7,5},{5,1},{3,7},{8,10},{14,12},{12... | collective-permute-start | bytes 884744 | tf_op jit(solution)/shard_map/ppermute | solution.py:580
  8.6 31.2 %collective-permute-start.3 = (bf16[192,768]{1,0:T(8,128)(2,1)S(1)}, bf16[192,768]{1,0:T(8,128)(2,1)}, u32[]{:S(2)}, u32[]{:S(2)}) collective-permute-start(bf16[192,768]{1,0:T(8,128)(2,1)S(1)} %pad_maximum_fusion.16), channel_id=1, source_target_pairs={{2,4},{4,2},{3,5},{5,3},{10,12},{12,10},{11,13},{13,11},{18,20},{2... | collective-permute-start | bytes 884744 | tf_op jit(solution)/shard_map/ppermute | solution.py:580
  11.7 26.7 %collective-permute-start = (bf16[256,1536]{1,0:T(8,128)(2,1)S(1)}, bf16[256,1536]{1,0:T(8,128)(2,1)}, u32[]{:S(2)}, u32[]{:S(2)}) collective-permute-start(bf16[256,1536]{1,0:T(8,128)(2,1)S(1)} %slice.227), channel_id=1, source_target_pairs={{2,4},{4,2},{3,5},{5,3},{10,12},{12,10},{11,13},{13,11},{18,20},{2... | collective-permute-start | bytes 2359304 | tf_op jit(solution)/shard_map/ppermute | solution.py:580
  41.5 35.5 %collective-permute-start.7 = (bf16[384,768]{1,0:T(8,128)(2,1)S(1)}, bf16[384,768]{1,0:T(8,128)(2,1)S(1)}, u32[]{:S(2)}, u32[]{:S(2)}) collective-permute-start(bf16[384,768]{1,0:T(8,128)(2,1)S(1)} %pad_maximum_fusion.12.refs_5_.refs_0_), channel_id=1, source_target_pairs={{0,8},{8,0},{16,24},{24,16},{1,9},{9,1},{17,25},{25,17},{2,10},{10... | collective-permute-start | bytes 1769480 | tf_op jit(solution)/shard_map/ppermute | solution.py:631
  43.1 33.9 %collective-permute-start.8 = (bf16[384,768]{1,0:T(8,128)(2,1)S(1)}, bf16[384,768]{1,0:T(8,128)(2,1)S(1)}, u32[]{:S(2)}, u32[]{:S(2)}) collective-permute-start(bf16[384,768]{1,0:T(8,128)(2,1)S(1)} %pad_maximum_fusion.12.refs_5_.refs_0_), channel_id=1, source_target_pairs={{0,16},{8,24},{16,0},{24,8},{1,17},{9,25},{17,1},{25,9},{2,18},{10... | collective-permute-start | bytes 1769480 | tf_op jit(solution)/shard_map/ppermute | solution.py:631
  44.9 32.1 %collective-permute-start.5 = (bf16[256,1536]{1,0:T(8,128)(2,1)S(1)}, bf16[256,1536]{1,0:T(8,128)(2,1)}, u32[]{:S(2)}, u32[]{:S(2)}) collective-permute-start(bf16[256,1536]{1,0:T(8,128)(2,1)S(1)} %get-tuple-element.196.refs_0_), channel_id=1, source_target_pairs={{0,4},{4,0},{1,5},{5,1},{2,6},{6,2},{3,7},{7,3},{8,12},{12,8},{9,1... | collective-permute-start | bytes 2359304 | tf_op jit(solution)/shard_map/ppermute | solution.py:571
  45.0 32.0 %collective-permute-start.6 = (bf16[256,1536]{1,0:T(8,128)(2,1)S(1)}, bf16[256,1536]{1,0:T(8,128)(2,1)}, u32[]{:S(2)}, u32[]{:S(2)}) collective-permute-start(bf16[256,1536]{1,0:T(8,128)(2,1)S(1)} %get-tuple-element.196.refs_0_), channel_id=1, source_target_pairs={{1,0},{0,1},{3,2},{2,3},{5,4},{4,5},{7,6},{6,7},{9,8},{8,9},{11,10... | collective-permute-start | bytes 2359304 | tf_op jit(solution)/shard_map/ppermute | solution.py:621
  51.0 24.8 %collective-permute-start.4 = (bf16[256,1536]{1,0:T(8,128)(2,1)S(1)}, bf16[256,1536]{1,0:T(8,128)(2,1)}, u32[]{:S(2)}, u32[]{:S(2)}) collective-permute-start(bf16[256,1536]{1,0:T(8,128)(2,1)S(1)} %get-tuple-element.197), channel_id=1, source_target_pairs={{2,4},{4,2},{3,5},{5,3},{10,12},{12,10},{11,13},{13,11},{18,20},{2... | collective-permute-start | bytes 2359304 | tf_op jit(solution)/shard_map/ppermute | solution.py:580
  77.2 26.2 %collective-permute-start.10 = (bf16[256,1536]{1,0:T(8,128)(2,1)S(1)}, bf16[256,1536]{1,0:T(8,128)(2,1)}, u32[]{:S(2)}, u32[]{:S(2)}) collective-permute-start(bf16[256,1536]{1,0:T(8,128)(2,1)S(1)} %broadcast_select_fusion.5.refs_1_), channel_id=1, source_target_pairs={{1,0},{0,1},{3,2},{2,3},{5,4},{4,5},{7,6},{6,7},{9,8},{8,9},{11,10... | collective-permute-start | bytes 2359304 | tf_op jit(solution)/shard_map/ppermute | solution.py:621
  121.8 36.1 %collective-permute-start.19 = (bf16[192,2048]{1,0:T(8,128)(2,1)S(1)}, bf16[192,2048]{1,0:T(8,128)(2,1)S(1)}, u32[]{:S(2)}, u32[]{:S(2)}) collective-permute-start(bf16[192,2048]{1,0:T(8,128)(2,1)S(1)} %pad_maximum_fusion.6), channel_id=1, source_target_pairs={{0,2},{6,4},{4,0},{2,6},{1,3},{7,5},{5,1},{3,7},{8,10},{14,12},{12... | collective-permute-start | bytes 2359304 | tf_op jit(solution)/shard_map/ppermute | solution.py:580
  122.5 35.4 %collective-permute-start.20 = (bf16[192,2048]{1,0:T(8,128)(2,1)S(1)}, bf16[192,2048]{1,0:T(8,128)(2,1)S(1)}, u32[]{:S(2)}, u32[]{:S(2)}) collective-permute-start(bf16[192,2048]{1,0:T(8,128)(2,1)S(1)} %pad_maximum_fusion.6), channel_id=1, source_target_pairs={{2,4},{4,2},{3,5},{5,3},{10,12},{12,10},{11,13},{13,11},{18,20},{2... | collective-permute-start | bytes 2359304 | tf_op jit(solution)/shard_map/ppermute | solution.py:580
  127.4 30.5 %collective-permute-start.21 = (bf16[384,384]{1,0:T(8,128)(2,1)S(1)}, bf16[384,384]{1,0:T(8,128)(2,1)S(1)}, u32[]{:S(2)}, u32[]{:S(2)}) collective-permute-start(bf16[384,384]{1,0:T(8,128)(2,1)S(1)} %pad_maximum_fusion.17), channel_id=1, source_target_pairs={{1,0},{0,1},{3,2},{2,3},{5,4},{4,5},{7,6},{6,7},{9,8},{8,9},{11,10... | collective-permute-start | bytes 884744 | tf_op jit(solution)/shard_map/ppermute | solution.py:621
  158.8 308.7 %reduce-scatter.4.cloned.1.call-start = ((), (), s32[]{:S(2)}) async-start(), calls=%async_computation.4 | async-start | bytes 7864320 | tf_op jit(solution)/shard_map/reduce_scatter | solution.py:901
  159.1 25.4 %collective-permute-start.24 = (bf16[384,1024]{1,0:T(8,128)(2,1)S(1)}, bf16[384,1024]{1,0:T(8,128)(2,1)S(1)}, u32[]{:S(2)}, u32[]{:S(2)}) collective-permute-start(bf16[384,1024]{1,0:T(8,128)(2,1)S(1)} %pad_maximum_fusion.8.refs_2_.refs_4_.refs_6_), channel_id=1, source_target_pairs={{0,8},{8,0},{16,24},{24,16},{1,9},{9,1},{17,25},{25,17},{2,10},{10... | collective-permute-start | bytes 2359304 | tf_op jit(solution)/shard_map/ppermute | solution.py:631
  159.7 25.0 %collective-permute-start.25 = (bf16[384,1024]{1,0:T(8,128)(2,1)S(1)}, bf16[384,1024]{1,0:T(8,128)(2,1)S(1)}, u32[]{:S(2)}, u32[]{:S(2)}) collective-permute-start(bf16[384,1024]{1,0:T(8,128)(2,1)S(1)} %pad_maximum_fusion.8.refs_2_.refs_4_.refs_6_), channel_id=1, source_target_pairs={{0,16},{8,24},{16,0},{24,8},{1,17},{9,25},{17,1},{25,9},{2,18},{10... | collective-permute-start | bytes 2359304 | tf_op jit(solution)/shard_map/ppermute | solution.py:631
  160.8 24.0 %collective-permute-start.22 = (bf16[256,1536]{1,0:T(8,128)(2,1)S(1)}, bf16[256,1536]{1,0:T(8,128)(2,1)S(1)}, u32[]{:S(2)}, u32[]{:S(2)}) collective-permute-start(bf16[256,1536]{1,0:T(8,128)(2,1)S(1)} %slice.239), channel_id=1, source_target_pairs={{2,4},{4,2},{3,5},{5,3},{10,12},{12,10},{11,13},{13,11},{18,20},{2... | collective-permute-start | bytes 2359304 | tf_op jit(solution)/shard_map/ppermute | solution.py:580
  165.0 24.0 %collective-permute-start.23 = (bf16[1024,384]{1,0:T(8,128)(2,1)S(1)}, bf16[1024,384]{1,0:T(8,128)(2,1)S(1)}, u32[]{:S(2)}, u32[]{:S(2)}) collective-permute-start(bf16[1024,384]{1,0:T(8,128)(2,1)S(1)} %copy-done.55), channel_id=1, source_target_pairs={{0,1},{1,0},{2,3},{3,2},{4,5},{5,4},{6,7},{7,6},{8,9},{9,8},{10,11... | collective-permute-start | bytes 2359304 | tf_op jit(solution)/shard_map/ppermute | solution.py:626
  193.1 23.0 %collective-permute-start.27 = (bf16[384,1024]{1,0:T(8,128)(2,1)S(1)}, bf16[384,1024]{1,0:T(8,128)(2,1)S(1)}, u32[]{:S(2)}, u32[]{:S(2)}) collective-permute-start(bf16[384,1024]{1,0:T(8,128)(2,1)S(1)} %pad_maximum_fusion.7.refs_7_.refs_9_.refs_11_), channel_id=1, source_target_pairs={{0,8},{8,0},{16,24},{24,16},{1,9},{9,1},{17,25},{25,17},{2,10},{10... | collective-permute-start | bytes 2359304 | tf_op jit(solution)/shard_map/ppermute | solution.py:631
  194.2 22.8 %collective-permute-start.28 = (bf16[384,1024]{1,0:T(8,128)(2,1)S(1)}, bf16[384,1024]{1,0:T(8,128)(2,1)S(1)}, u32[]{:S(2)}, u32[]{:S(2)}) collective-permute-start(bf16[384,1024]{1,0:T(8,128)(2,1)S(1)} %pad_maximum_fusion.7.refs_7_.refs_9_.refs_11_), channel_id=1, source_target_pairs={{0,16},{8,24},{16,0},{24,8},{1,17},{9,25},{17,1},{25,9},{2,18},{10... | collective-permute-start | bytes 2359304 | tf_op jit(solution)/shard_map/ppermute | solution.py:631
  280.4 34.8 %collective-permute-start.43 = (bf16[256,1536]{1,0:T(8,128)(2,1)}, bf16[256,1536]{1,0:T(8,128)(2,1)}, u32[]{:S(2)}, u32[]{:S(2)}) collective-permute-start(bf16[256,1536]{1,0:T(8,128)(2,1)} %slice.255), channel_id=1, source_target_pairs={{1,0},{0,1},{3,2},{2,3},{5,4},{4,5},{7,6},{6,7},{9,8},{8,9},{11,10... | collective-permute-start | bytes 2359304 | tf_op jit(solution)/shard_map/ppermute | solution.py:621
  289.9 25.3 %collective-permute-start.44 = (bf16[256,1536]{1,0:T(8,128)(2,1)}, bf16[256,1536]{1,0:T(8,128)(2,1)}, u32[]{:S(2)}, u32[]{:S(2)}) collective-permute-start(bf16[256,1536]{1,0:T(8,128)(2,1)} %collective-permute-done.39.refs_1_), channel_id=1, source_target_pairs={{0,4},{4,0},{1,5},{5,1},{2,6},{6,2},{3,7},{7,3},{8,12},{12,8},{9,1... | collective-permute-start | bytes 2359304 | tf_op jit(solution)/shard_map/ppermute | solution.py:571
  396.2 124.2 %reduce-scatter.6.cloned.1.call-start = ((), (), s32[]{:S(2)}) async-start(), calls=%async_computation.5 | async-start | bytes 3932160 | tf_op jit(solution)/shard_map/reduce_scatter | solution.py:908
  420.9 175.4 %reduce-scatter.8.cloned.1.call-start = ((), (), s32[]{:S(2)}) async-start(), calls=%async_computation.6 | async-start | bytes 2949120 | tf_op jit(solution)/shard_map/reduce_scatter | solution.py:936
  427.6 25.7 %collective-permute-start.56 = (bf16[512,1536]{1,0:T(8,128)(2,1)}, bf16[512,1536]{1,0:T(8,128)(2,1)}, u32[]{:S(2)}, u32[]{:S(2)}) collective-permute-start(bf16[512,1536]{1,0:T(8,128)(2,1)} %get-tuple-element.334), channel_id=1, source_target_pairs={{0,4},{4,0},{1,5},{5,1},{2,6},{6,2},{3,7},{7,3},{8,12},{12,8},{9,1... | collective-permute-start | bytes 4718600 | tf_op jit(solution)/shard_map/ppermute | solution.py:571
  467.5 54.3 %collective-permute-start.58 = (bf16[512,1536]{1,0:T(8,128)(2,1)}, bf16[512,1536]{1,0:T(8,128)(2,1)}, u32[]{:S(2)}, u32[]{:S(2)}) collective-permute-start(bf16[512,1536]{1,0:T(8,128)(2,1)} %add_convert_fusion.1), channel_id=1, source_target_pairs={{2,4},{4,2},{3,5},{5,3},{10,12},{12,10},{11,13},{13,11},{18,20},{2... | collective-permute-start | bytes 4718600 | tf_op jit(solution)/shard_map/ppermute | solution.py:580
  472.5 49.3 %collective-permute-start.59 = (bf16[192,2048]{1,0:T(8,128)(2,1)}, bf16[192,2048]{1,0:T(8,128)(2,1)S(1)}, u32[]{:S(2)}, u32[]{:S(2)}) collective-permute-start(bf16[192,2048]{1,0:T(8,128)(2,1)} %get-tuple-element.406), channel_id=1, source_target_pairs={{2,0},{4,6},{0,4},{6,2},{3,1},{5,7},{1,5},{7,3},{10,8},{12,14},{8,... | collective-permute-start | bytes 2359304 | tf_op jit(solution)/shard_map/ppermute | solution.py:580
  551.9 29.4 %collective-permute-start.63 = (bf16[256,1536]{1,0:T(8,128)(2,1)S(1)}, bf16[256,1536]{1,0:T(8,128)(2,1)S(1)}, u32[]{:S(2)}, u32[]{:S(2)}) collective-permute-start(bf16[256,1536]{1,0:T(8,128)(2,1)S(1)} %slice.271), channel_id=1, source_target_pairs={{0,1},{1,0},{2,3},{3,2},{4,5},{5,4},{6,7},{7,6},{8,9},{9,8},{10,11... | collective-permute-start | bytes 2359304 | tf_op jit(solution)/shard_map/ppermute | solution.py:626
  593.3 24.6 %collective-permute-start.69 = (bf16[256,1536]{1,0:T(8,128)(2,1)}, bf16[256,1536]{1,0:T(8,128)(2,1)}, u32[]{:S(2)}, u32[]{:S(2)}) collective-permute-start(bf16[256,1536]{1,0:T(8,128)(2,1)} %slice.280), channel_id=1, source_target_pairs={{0,1},{1,0},{2,3},{3,2},{4,5},{5,4},{6,7},{7,6},{8,9},{9,8},{10,11... | collective-permute-start | bytes 2359304 | tf_op jit(solution)/shard_map/ppermute | solution.py:626
  630.1 37.0 %collective-permute-start.72 = (bf16[256,1536]{1,0:T(8,128)(2,1)}, bf16[256,1536]{1,0:T(8,128)(2,1)S(1)}, u32[]{:S(2)}, u32[]{:S(2)}) collective-permute-start(bf16[256,1536]{1,0:T(8,128)(2,1)} %fusion.2), channel_id=1, source_target_pairs={{2,4},{4,2},{3,5},{5,3},{10,12},{12,10},{11,13},{13,11},{18,20},{2... | collective-permute-start | bytes 2359304 | tf_op jit(solution)/shard_map/ppermute | solution.py:580
  635.4 31.0 %collective-permute-start.76 = (bf16[192,384]{1,0:T(8,128)(2,1)S(1)}, bf16[192,384]{1,0:T(8,128)(2,1)S(1)}, u32[]{:S(2)}, u32[]{:S(2)}) collective-permute-start(bf16[192,384]{1,0:T(8,128)(2,1)S(1)} %get-tuple-element.428), channel_id=1, source_target_pairs={{2,0},{4,6},{0,4},{6,2},{3,1},{5,7},{1,5},{7,3},{10,8},{12,14},{8,... | collective-permute-start | bytes 442376 | tf_op jit(solution)/shard_map/ppermute | solution.py:580
  635.5 30.9 %collective-permute-start.77 = (bf16[192,384]{1,0:T(8,128)(2,1)S(1)}, bf16[192,384]{1,0:T(8,128)(2,1)S(1)}, u32[]{:S(2)}, u32[]{:S(2)}) collective-permute-start(bf16[192,384]{1,0:T(8,128)(2,1)S(1)} %get-tuple-element.427), channel_id=1, source_target_pairs={{2,4},{4,2},{3,5},{5,3},{10,12},{12,10},{11,13},{13,11},{18,20},{2... | collective-permute-start | bytes 442376 | tf_op jit(solution)/shard_map/ppermute | solution.py:580
  (137 other events, 1692.1 us)
Sparse Core Ops, SparseCore 0:
  158.9 53.6 all-gather.2
  396.3 70.4 reduce-scatter.3
  469.8 43.9 reduce-scatter.5
  527.8 40.7 reduce-scatter.7

commit v4 on v3

--- a/solution.py
+++ b/solution.py
@@ -720,14 +720,16 @@
     shard_moved = send_z(qkv_shard)
     lengths = swap(seq_lengths)
     gains = lax.all_gather(jnp.stack([attn_gain, mlp_gain]), ("yx", "core"), axis=1, tiled=True).astype(f32)
-    upper, lengths, second_part, gains, *shard_moved = stage(upper, lengths, tokens[part_rows:], gains, *shard_moved)
+    upper, lengths, second_part, out_shard, gains, *shard_moved = stage(
+        upper, lengths, tokens[part_rows:], out_weight, gains, *shard_moved
+    )
     gain_one, gain_two = gains[0], gains[1]
 
     upper_far = [from_near(upper, k) for k in others]
     lower = swap(second_part)
     pair = pair_of(qkv_shard, *shard_moved)
     taken = neighbours(pair)
-    upper_sib = flip(upper, "core")
+    out_out = crossed(out_shard, OUT)
 
     subs = jnp.arange(group_rows // SUB, dtype=jnp.int32)
     per_device = rows // SUB
@@ -748,41 +750,39 @@
     start_row = jnp.tile(doc_start.reshape(-1, 1, SUB), (1, 1, q_heads // kv_heads))
     layout = (place, *bounds(TILE), cosine, sine, doc_start[:, None])
     layout_back = (place, *bounds(SUB), cosine, sine, start_row)
-    lower, upper_sib, down_shard, out_shard, *moved = stage(
-        lower, upper_sib, down_weight, out_weight, *upper_far, *taken, *layout, *layout_back
-    )
+    lower, out_out, out_shard, *moved = stage(lower, out_out, out_shard, *upper_far, *taken, *layout, *layout_back)
     upper_far, moved = moved[: near - 1], moved[near - 1 :]
     taken, moved = moved[: len(taken)], moved[len(taken) :]
     layout, layout_back = moved[: len(layout)], moved[len(layout) :]
 
     lower_far = [from_near(lower, k) for k in others]
-    lower_sib = flip(lower, "core")
-    down_out = crossed(down_shard, OUT)
+    own = jnp.concatenate([upper, lower], axis=0)
+    own_sib = flip(own, "core")
+    out_cross = crossed(out_shard, CROSS)
     blocks = blocks_of(pair, taken, diagonal(taken))
     projecting = [(*blocks, qkv_cols)]
     gain_row = gain_one[None]
     outs = [(tokens.shape[1], bf16, "all"), (qkv_cols, bf16, "all")]
-    parts = [upper, lower, upper_sib, lower_sib]
-    normed = piece_call(project_kernel, "project", 0, near, me, parts, [gain_row], [], projecting, [], outs)
-    gate_up_shard, down_out, down_shard, out_shard, *moved = stage(
-        gate_up_shard, down_out, down_shard, out_shard, *lower_far, *normed
-    )
+    normed = piece_call(project_kernel, "project", 0, near, me, [own, own_sib], [gain_row], [], projecting, [], outs)
+    gate_up_shard, out_cross, down_shard, *moved = stage(gate_up_shard, out_cross, down_weight, *lower_far, *normed)
     lower_far, normed = moved[: near - 1], moved[near - 1 :]
 
-    down_cross = crossed(down_shard, CROSS)
-    out_moved = send_z(out_shard)
+    out_pair = pair_of(out_weight, out_out, out_cross)
+    out_far = [from_near(out_pair, k) for k in others]
+    down_moved = send_z(down_shard)
     for k in others:
-        parts = [upper_far[k - 1], lower_far[k - 1], flip(upper_far[k - 1], "core"), flip(lower_far[k - 1], "core")]
+        far = jnp.concatenate([upper_far[k - 1], lower_far[k - 1]], axis=0)
+        parts = [far, flip(far, "core")]
         normed = piece_call(project_kernel, "project", k, near, me, parts, [gain_row], [], projecting, normed, outs)
     norm_one, qkv = normed
-    gate_up_shard, qkv, down_cross, *out_moved = stage(gate_up_shard, qkv, down_cross, *out_moved)
+    gate_up_shard, qkv, out_pair, *moved = stage(gate_up_shard, qkv, out_pair, *out_far, *down_moved)
+    out_far, down_moved = moved[: near - 1], moved[near - 1 :]
 
     gate_up_moved = send_z(gate_up_shard)
-    out_pair = pair_of(out_weight, *out_moved)
-    out_far = [from_near(out_pair, k) for k in others]
+    w_out = lax.all_gather(jnp.concatenate([out_pair, *out_far], axis=1), "yx", axis=0, tiled=True)
     context, sums = attend(qkv, near, layout, q_heads, kv_heads)
-    cotangent, *moved = stage(cotangent, *context, *gate_up_moved, *out_far)
-    context, gate_up_moved, out_far = moved[:near], moved[near : near + 2], moved[near + 2 :]
+    cotangent, *moved = stage(cotangent, *context, *gate_up_moved)
+    context, gate_up_moved = moved[:near], moved[near:]
 
     quarters = [context[0]] + [None] * (near - 1)
     for k in others:
@@ -793,47 +793,49 @@
         for n in range(2)
     ]
     gate_taken = neighbours(pairs[0])
-    w_out = lax.all_gather(jnp.concatenate([out_pair, *out_far], axis=1), "yx", axis=0, tiled=True)
-    up_pair, cotangent, cot_upper, *moved = stage(pairs[1], cotangent, cot_upper, *quarters, *gate_taken)
+    residual = own.astype(f32)
+    scale_one = lax.rsqrt(jnp.mean(residual * residual, axis=-1, keepdims=True) + EPSILON)
+    up_pair, cotangent, cot_upper, w_out, scale_one, *moved = stage(
+        pairs[1], cotangent, cot_upper, w_out, scale_one, *quarters, *gate_taken
+    )
     quarters, gate_taken = moved[:near], moved[near:]
 
     up_taken = neighbours(up_pair)
     cot_lower = crossed(cotangent[part_rows:], CROSS)
-    residual = jnp.concatenate([upper, lower], axis=0).astype(f32)
-    scale_one = lax.rsqrt(jnp.mean(residual * residual, axis=-1, keepdims=True) + EPSILON)
     context_all = jnp.concatenate(quarters, axis=1)
-    w_out, scale_one, cot_lower, context_all, *up_taken = stage(w_out, scale_one, cot_lower, context_all, *up_taken)
-
-    gate_halves, up_halves = diagonal(gate_taken), diagonal(up_taken)
     branch_sib = flip(times_transpose(context_all[rows:], w_out).astype(bf16), "core")
     mid = residual + times_transpose(context_all[:rows], w_out) + branch_sib.astype(f32)
     scale_two, norm_two = norm_rows(mid, gain_two)
-    norm_two, *moved = stage(norm_two, *gate_halves, *up_halves)
+    norm_two, cot_lower, *up_taken = stage(norm_two, cot_lower, *up_taken)
+
+    upper_far = [from_near(norm_two[:part_rows], k) for k in others]
+    gate_halves, up_halves = diagonal(gate_taken), diagonal(up_taken)
+    cot = jnp.where(straight(), cotangent, jnp.concatenate([cot_upper, cot_lower], axis=0))
+    down_pair = pair_of(down_weight, *down_moved)
+    w_project = assemble("assemble_project", me, *blocks, tokens.shape[1], qkv_cols)
+    norm_two, cot, down_pair, w_project, *moved = stage(
+        norm_two, cot, down_pair, w_project, *upper_far, *gate_halves, *up_halves
+    )
+    upper_far, moved = moved[: near - 1], moved[near - 1 :]
     gate_halves, up_halves = moved[: len(gate_halves)], moved[len(gate_halves) :]
-    norm_sib = flip(norm_two, "core")
-    cot = jnp.where(straight(), cotangent, jnp.concatenate([cot_upper, cot_lower], axis=0))
-    cot_sib = flip(cot, "core")
-    down_pair = pair_of(down_weight, down_out, down_cross)
-    norm_two, norm_sib, cot, cot_sib, down_pair = stage(norm_two, norm_sib, cot, cot_sib, down_pair)
-
-    upper_far = [from_near(norm_two[:part_rows], k) for k in others]
+
+    lower_far = [from_near(norm_two[part_rows:], k) for k in others]
+    norm_sib, cot_sib = flip(norm_two, "core"), flip(cot, "core")
     down_taken = neighbours(down_pair)
     gate_blocks = blocks_of(pairs[0], gate_taken, gate_halves)
     up_blocks = blocks_of(up_pair, up_taken, up_halves, hidden_cols)
     gate_up = ([*gate_blocks[0], *up_blocks[0]], gate_blocks[1] + up_blocks[1], 2 * hidden_cols)
     outs = [(norm_two.shape[1], bf16, "all"), (2 * hidden_cols, f32, "all"), (hidden_cols, bf16, "all")]
     earlier = piece_call(gate_kernel, "gate", 0, near, me, [norm_two, norm_sib], [], [], [gate_up], [], outs)
-    norm_two, *moved = stage(norm_two, *upper_far, *down_taken, *earlier)
-    upper_far, moved = moved[: near - 1], moved[near - 1 :]
+    cot_sib, *moved = stage(cot_sib, *lower_far, *down_taken, *earlier)
+    lower_far, moved = moved[: near - 1], moved[near - 1 :]
     down_taken, earlier = moved[: len(down_taken)], moved[len(down_taken) :]
 
-    lower_far = [from_near(norm_two[part_rows:], k) for k in others]
-    upper_far_sib = [flip(x, "core") for x in upper_far]
+    norm_far = [jnp.concatenate(x, axis=0) for x in zip(upper_far, lower_far, strict=True)]
+    norm_far_sib = [flip(x, "core") for x in norm_far]
     down_halves = diagonal(down_taken)
-    w_project = assemble("assemble_project", me, *blocks, tokens.shape[1], qkv_cols)
-    w_project, *moved = stage(w_project, *lower_far, *upper_far_sib, *down_halves)
-    lower_far, upper_far_sib, down_halves = moved[: near - 1], moved[near - 1 : 2 * near - 2], moved[2 * near - 2 :]
-    lower_far_sib = [flip(x, "core") for x in lower_far]
+    cot, *moved = stage(cot, *norm_far, *norm_far_sib, *down_halves)
+    norm_far, norm_far_sib, down_halves = moved[: near - 1], moved[near - 1 : 2 * near - 2], moved[2 * near - 2 :]
 
     cot_upper_far = [from_near(cot[:part_rows], k) for k in others]
     down = (*blocks_of(down_pair, down_taken, down_halves), hidden_cols)
@@ -851,17 +853,17 @@
     norm_two_all, gate_up_all, hidden_all = earlier
     grad_all, d_gate_up_all, *near_back = way_back(0, [cot, cot_sib], [])
     cot, *moved = stage(
-        cot, norm_two_all, gate_up_all, hidden_all, grad_all, d_gate_up_all, *near_back, *cot_upper_far, *lower_far_sib
+        cot, norm_two_all, gate_up_all, hidden_all, grad_all, d_gate_up_all, *near_back, *cot_upper_far
     )
     earlier, moved = moved[:3], moved[3:]
     grad_all, d_gate_up_all, *moved = moved
-    near_back, cot_upper_far, lower_far_sib = moved[:4], moved[4 : near + 3], moved[near + 3 :]
+    near_back, cot_upper_far = moved[:4], moved[4:]
 
     cot_lower_far = [from_near(cot[part_rows:], k) for k in others]
     cot_upper_far_sib = [flip(x, "core") for x in cot_upper_far]
     out_far = []
     for k in others:
-        parts = [upper_far[k - 1], lower_far[k - 1], upper_far_sib[k - 1], lower_far_sib[k - 1]]
+        parts = [norm_far[k - 1], norm_far_sib[k - 1]]
         *earlier, out_own, out_sib = piece_call(
             gate_kernel, "gate", k, near, me, parts, [], [], [gate_up, down], earlier, gate_outs + halves
         )
@@ -891,76 +893,96 @@
     )
 
     moved_upper = [to_near(d_norm_sent[k - 1][:part_rows], k) for k in others]
-    grad_gate_up = rows_product(norm_two_all, d_gate_up_all).astype(bf16)
-    grad_gate_up, grad_all, near_own, near_sib, *moved = stage(
-        grad_gate_up, grad_all, near_own, near_sib, *moved_upper, *d_norm_sent
+    grad_gate, grad_up = (
+        rows_product(norm_two_all, d_gate_up_all[:, n * hidden_cols : (n + 1) * hidden_cols]).astype(bf16)
+        for n in range(2)
+    )
+    output_near = joined(*near_back[2:])
+    grad_gate, grad_up, grad_all, near_own, near_sib, output_near, *moved = stage(
+        grad_gate, grad_up, grad_all, near_own, near_sib, output_near, *moved_upper, *d_norm_sent
     )
     moved_upper, d_norm_sent = moved[: near - 1], moved[near - 1 :]
 
     moved_lower = [to_near(d_norm_sent[k - 1][part_rows:], k) for k in others]
-    gate_up_part = lax.psum_scatter(grad_gate_up, "yx", scatter_dimension=0, tiled=True)
+    gate_part = lax.psum_scatter(grad_gate, "yx", scatter_dimension=0, tiled=True)
     d_norm_two = joined(near_own, near_sib)
     grad_down = rows_product(grad_all, hidden_all).astype(bf16)
-    grad_down, d_norm_two, *moved = stage(grad_down, d_norm_two, *out_sums, *moved_lower)
+
+    def output_part(at, moved):
+        part = mid[at] + output_near[at]
+        for x in moved:
+            part = part + x.astype(f32)
+        return part.astype(bf16)
+
+    output_upper = output_part(slice(0, part_rows), out_upper)
+    grad_down, d_norm_two, output_upper, *moved = stage(grad_down, d_norm_two, output_upper, *out_sums, *moved_lower)
     out_sums, moved_lower = moved[: near - 1], moved[near - 1 :]
 
-    out_lower = [to_near(out_sums[k - 1][part_rows:], k) for k in others]
-    down_part = lax.psum_scatter(grad_down, "yx", scatter_dimension=0, tiled=True)
+    quarter = part_rows // 2
+    out_lower = [[to_near(out_sums[k - 1][part_rows : part_rows + quarter], k) for k in others]]
+    up_part = lax.psum_scatter(grad_up, "yx", scatter_dimension=0, tiled=True)
     for one, two in zip(moved_upper, moved_lower, strict=True):
         d_norm_two = d_norm_two + jnp.concatenate([one, two], axis=0).astype(f32)
     mid_back, _ = norm_back(mid, scale_two, gain_two, d_norm_two)
     d_mid = cot.astype(f32) + mid_back
     d_attn = d_mid.astype(bf16)
+    d_attn, *moved = stage(d_attn, *out_lower[0], *out_sums)
+    out_lower[0], out_sums = moved[: near - 1], moved[near - 1 :]
+
+    out_lower.append([to_near(out_sums[k - 1][part_rows + quarter :], k) for k in others])
     d_attn_sib = flip(d_attn, "core")
     both = [dot32(x, w_out).astype(bf16) for x in (d_attn, d_attn_sib)]
     d_quarters = [
         jnp.concatenate([x[:, k * query_cols : (k + 1) * query_cols] for x in both], axis=0) for k in range(near)
     ]
-    d_attn, d_attn_sib, *moved = stage(d_attn, d_attn_sib, *d_quarters, *out_lower)
-    d_quarters, out_lower = moved[:near], moved[near:]
+    d_attn, d_attn_sib, *moved = stage(d_attn, d_attn_sib, *d_quarters, *out_lower[1])
+    d_quarters, out_lower[1] = moved[:near], moved[near:]
 
     d_context = [d_quarters[0]] + [None] * (near - 1)
     for k in others:
         d_context[near - k] = to_near(d_quarters[k], k)
+    upper_crossed = crossed(output_upper, CROSS)
     grad_out = rows_product(d_attn, context_all[:rows]) + rows_product(d_attn_sib, context_all[rows:])
     grad_out = grad_out.astype(bf16)
-    output_own = mid + joined(*near_back[2:])
-    for one, two in zip(out_upper, out_lower, strict=True):
-        output_own = output_own + jnp.concatenate([one, two], axis=0).astype(f32)
-    output_own = output_own.astype(bf16)
-    grad_out, output_own, gate_up_part, *d_context = stage(grad_out, output_own, gate_up_part, *d_context)
-
-    output_crossed = crossed(output_own, CROSS)
-    gate_up_keep, gate_up_give = give_z(gate_up_part)
-    gate_up_back = crossed(gate_up_give, BACK)
+    output_lower = output_part(
+        slice(part_rows, rows), [jnp.concatenate(x, axis=0) for x in zip(*out_lower, strict=True)]
+    )
+    grad_out, output_lower, gate_part, upper_crossed, *d_context = stage(
+        grad_out, output_lower, gate_part, upper_crossed, *d_context
+    )
+
+    lower_crossed = crossed(output_lower, CROSS)
+    output = jnp.concatenate([output_upper, output_lower], axis=0)
+    gate_keep, gate_give = give_z(gate_part)
+    gate_home = [crossed(gate_give, BACK), crossed(gate_keep, CROSS)]
+    down_part = lax.psum_scatter(grad_down, "yx", scatter_dimension=0, tiled=True)
     out_part = lax.psum_scatter(grad_out, "yx", scatter_dimension=0, tiled=True)
     d_qkv = attend_back(list(range(kv_heads)), qkv, d_context, context, sums, [], layout_back, q_heads, kv_heads)
-    d_qkv, output_crossed, gate_up_back, gate_up_keep, down_part = stage(
-        d_qkv, output_crossed, gate_up_back, gate_up_keep, down_part
-    )
+    d_qkv, lower_crossed, up_part, *gate_home = stage(d_qkv, lower_crossed, up_part, *gate_home)
+    output = jnp.where(straight(), output, jnp.concatenate([upper_crossed, lower_crossed], axis=0))
 
     def back_part(k):
         own, sib = (d_qkv[(2 * k + e) * rows : (2 * k + e + 1) * rows] for e in range(2))
         taken = flip(times_transpose(sib, w_project).astype(bf16), "core")
         return times_transpose(own, w_project) + taken.astype(f32)
 
-    gate_up_cross = crossed(gate_up_keep, CROSS)
+    up_keep, up_give = give_z(up_part)
+    up_home = [crossed(up_give, BACK), crossed(up_keep, CROSS)]
     d_sent = [back_part(k).astype(bf16) for k in others]
-    d_qkv, gate_up_cross, down_part, *d_sent = stage(d_qkv, gate_up_cross, down_part, *d_sent)
+    d_qkv, *moved = stage(d_qkv, *d_sent, *up_home)
+    d_sent, up_home = moved[: near - 1], moved[near - 1 :]
 
     d_upper = [to_near(d_sent[k - 1][:part_rows], k) for k in others]
-    down_keep, down_give = give_z(down_part)
-    down_home = [crossed(down_give, BACK), crossed(down_keep, CROSS)]
     grad_project = rows_product(norm_one, d_qkv).astype(bf16)
     project_sent = send_yx(grad_project, (0, qkv_cols))
     total = back_part(0)
-    total, grad_project, *moved = stage(total, grad_project, *d_upper, *d_sent, *project_sent, *down_home)
-    d_upper, d_sent, project_sent, down_home = (
-        moved[: near - 1], moved[near - 1 : 2 * near - 2], moved[2 * near - 2 : -2], moved[-2:],
-    )
+    total, grad_project, down_part, *moved = stage(total, grad_project, down_part, *d_upper, *d_sent, *project_sent)
+    d_upper, d_sent, project_sent = moved[: near - 1], moved[near - 1 : 2 * near - 2], moved[2 * near - 2 :]
 
     d_lower = [to_near(d_sent[k - 1][part_rows:], k) for k in others]
     project_rest, project_own = join_yx(grad_project, (0, qkv_cols), project_sent)
+    down_keep, down_give = give_z(down_part)
+    down_back = crossed(down_give, BACK)
 
     def input_part(at, moved):
         part = total[at]
@@ -971,10 +993,11 @@
 
     input_upper = input_part(slice(0, part_rows), d_upper)
     upper_crossed = crossed(input_upper, CROSS)
-    total, input_upper, upper_crossed, out_part, *moved = stage(
-        total, input_upper, upper_crossed, out_part, *d_lower, *project_rest
+    total, input_upper, upper_crossed, out_part, down_back, down_keep, *moved = stage(
+        total, input_upper, upper_crossed, out_part, down_back, down_keep, *d_lower, *project_rest
     )
     d_lower, project_rest = moved[: near - 1], moved[near - 1 :]
+    down_cross = crossed(down_keep, CROSS)
 
     project_keep, project_give = give_z(total_yx(project_rest, project_own))
     project_home = [crossed(project_give, BACK), crossed(project_keep, CROSS)]
@@ -988,9 +1011,8 @@
     out_home = [crossed(out_give, BACK), crossed(out_keep, CROSS)]
     grad_project = sum_z(project_keep, *project_home)
     grad_out = sum_z(out_keep, *out_home)
-    grad_down = sum_z(down_keep, *down_home)
-    grad_gate_up = sum_z(gate_up_keep, gate_up_back, gate_up_cross)
-    output = jnp.where(straight(), output_own, output_crossed)
+    grad_down = sum_z(down_keep, down_back, down_cross)
+    grad_gate, grad_up = sum_z(gate_keep, *gate_home), sum_z(up_keep, *up_home)
     input_grad = jnp.concatenate(
         [
             jnp.where(straight(), input_upper, upper_crossed),
@@ -1002,7 +1024,7 @@
         jnp.stack(
             [
                 jnp.sum(qkv_shard.astype(f32) * grad_project, axis=1),
-                jnp.sum(gate_up_shard.astype(f32) * grad_gate_up, axis=1),
+                jnp.sum(gate_weight.astype(f32) * grad_gate + up_weight.astype(f32) * grad_up, axis=1),
             ]
         ),
         ("zh", "zl"),
@@ -1016,8 +1038,8 @@
         grad_project[:, query_cols + key_cols :],
         grad_out,
         gain_grads[1],
-        grad_gate_up[:, :hidden_cols],
-        grad_gate_up[:, hidden_cols:],
+        grad_gate,
+        grad_up,
         grad_down,
     )
 

time: 686 us -> 709 us (1.034)
  waiting for transfers between devices: 191 us -> 166 us
  matrix products: 58.8 us -> 75.7 us
  starting transfers between devices: 100 us -> 116 us
  other arithmetic: 65.1 us -> 80.2 us
  blocking collectives: 35 us -> 24.9 us
  local copies, waits for them, and re-layouts: 35.6 us -> 44.8 us
    ppermute x20, waiting for transfers between devices: 56.9 us -> 40.2 us  [across(): return lax.ppermute(x, 'yx', [(a, a ^ j) for a in range(n)])]
    psum x1, blocking collectives: 25.7 us -> 15.6 us  [body(): lax.psum(jnp.stack([jnp.sum(qkv_shard.astype(f32) * grad_project, axis=1)...]
    ppermute x24 -> x27, starting transfers between devices: 58.5 us -> 67.8 us  [crossed(): return lax.ppermute(x, ('core', 'zh'), perm)]
    ppermute x18 -> x15, waiting for transfers between devices: 11.2 us -> 3.21 us  [flip(): return lax.ppermute(x, axis, FLIP)]
    dot_general x5 -> x6, matrix products: 40.2 us -> 47.8 us  [rows_product(): lax.dot_general(left, right, (((0,), (0,)), ((), ())), preferred_element_...]
    unnamed x174 -> x198, local copies, waits for them, and re-layouts: 9.59 us -> 16.5 us
    ppermute x9 -> x10, waiting for transfers between devices: 37.6 us -> 42.9 us  [to_near(): return lax.ppermute(x, 'zl', [(j, (j + k) % n) for j in range(n)])]
    ppermute x24 -> x27, waiting for transfers between devices: 77.7 us -> 74.3 us  [crossed(): return lax.ppermute(x, ('core', 'zh'), perm)]
  transfers between devices with their start and end apart: 82 -> 84, of which waited for: 36 -> 33; matrix products, arithmetic and copies ran while one was open for 19% -> 24% of each run, Pallas kernels for 26% -> 25%
where the time goes in v4:
time: 709 us; the launch traced here: 699 us
  Pallas kernels  175 us (25%)
  waiting for transfers between devices  166 us (23%)
  starting transfers between devices  116 us (16%)
  other arithmetic  80.2 us (11%)
  matrix products  75.7 us (11%)
  local copies, waits for them, and re-layouts  44.8 us (6%)
  blocking collectives  24.9 us (4%)
  between operations  15.8 us (2%)
    pallas_call x6, Pallas kernels, piece_call(): pl.pallas_call(functools.partial(kernel, count, tuple((where for _, where...  97.4 us
    ppermute x27, waiting for transfers between devices, crossed(): return lax.ppermute(x, ('core', 'zh'), perm)  74.3 us
    ppermute x27, starting transfers between devices, crossed(): return lax.ppermute(x, ('core', 'zh'), perm)  67.8 us
    dot_general x6, matrix products, rows_product(): lax.dot_general(left, right, (((0,), (0,)), ((), ())), preferred_element_...  47.8 us
    pallas_call x1, Pallas kernels, attend_back(): pl.pallas_call(functools.partial(backward_kernel, pieces, ratio, bool(ear...  45.4 us
    ppermute x10, waiting for transfers between devices, to_near(): return lax.ppermute(x, 'zl', [(j, (j + k) % n) for j in range(n)])  42.9 us
    ppermute x20, waiting for transfers between devices, across(): return lax.ppermute(x, 'yx', [(a, a ^ j) for a in range(n)])  40.2 us
    pallas_call x1, Pallas kernels, attend(): pl.pallas_call(functools.partial(forward_kernel, pieces, ratio), out_shap...  29.6 us
  transfers between devices with their start and end apart: 84, of which 33 were waited for; matrix products, arithmetic and copies ran while one was open for 24% of the time, Pallas kernels for 25%

profile of v4, /device:TPU:16, one launch (start us, length us, event | category | flops | bytes accessed | tf_op | source)
XLA Modules:
  0.0 699.2 jit_solution(12803983300453109047)
XLA Ops:
  19.3 9.3 %all-gather = bf16[8,192,2]{1,2,0:T(2,128)(2,1)S(1)} all-gather(bf16[1,192,2]{1,2,0:T(2,128)(2,1)S(1)} %fusion.37), channel_id=1, replica_groups=mesh['yx'=4,'core'=2,'zh'=2,'zl'=2] {'yx','core'}, dimensions={0}, use_global_device_ids=true | all-gather | bytes 6912 | tf_op jit(solution)/shard_map/all_gather | solution.py:722
  29.3 9.0 %collective-permute-done.1 = s32[1,4]{1,0:T(1,128)S(1)} collective-permute-done((s32[1,4]{1,0:T(1,128)S(1)}, s32[1,4]{1,0:T(1,128)S(1)}, u32[]{:S(2)}, u32[]{:S(2)}) %collective-permute-start.1) | collective-permute-done | bytes 48 | tf_op jit(solution)/shard_map/ppermute | solution.py:580
  44.4 5.8 collective-permute-start.6
  61.9 13.1 %collective-permute-done.4 = bf16[256,1536]{1,0:T(8,128)(2,1)} collective-permute-done((bf16[256,1536]{1,0:T(8,128)(2,1)}, bf16[256,1536]{1,0:T(8,128)(2,1)}, u32[]{:S(2)}, u32[]{:S(2)}) %collective-permute-start.4) | collective-permute-done | bytes 786464 | tf_op jit(solution)/shard_map/ppermute | solution.py:580
  94.1 8.5 %project_0.1 = (bf16[2048,1536]{1,0:T(8,128)(2,1)}, bf16[2048,768]{1,0:T(8,128)(2,1)}) custom-call(s32[1]{0:T(128)} %bitcast.7.me, bf16[512,1536]{1,0:T(8,128)(2,1)} %copy-done.1, bf16[512,1536]{1,0:T(8,128)(2,1)} %collective-permute-done.11.refs_1_, f32[1,1536]{1,0:T(1,128)} %get-tuple-element.440.refs_2_, bf16[384,768]{1,0:T(8,128)(2,1)} %copy-done.15, ...), custom_call_target="tpu_custom_call" | custom-call | flops 1048576 | bytes 65536 | tf_op jit(solution)/shard_map/project_0/pallas_call | solution.py:522
  110.9 8.5 %project_1.1 = (bf16[2048,1536]{1,0:T(8,128)(2,1)}, bf16[2048,768]{1,0:T(8,128)(2,1)}) custom-call(s32[1]{0:T(128)} %bitcast.7.me, bf16[512,1536]{1,0:T(8,128)(2,1)} %copy-done.32, bf16[512,1536]{1,0:T(8,128)(2,1)} %copy-done.50, f32[1,1536]{1,0:T(1,128)} %get-tuple-element.440.refs_2_, ...), custom_call_target="tpu_custom_call", output_to_operand_aliasing={{0}: (9, {}), {1}: (10, {})} | custom-call | flops 1048576 | bytes 65536 | tf_op jit(solution)/shard_map/project_1/pallas_call | solution.py:522
  124.7 7.0 collective-permute-start.19
  133.1 29.6 %attention_forward.1 = (bf16[1024,384]{1,0:T(8,128)(2,1)}, bf16[1024,384]{1,0:T(8,128)(2,1)}, f32[4,1,1024]{2,1,0:T(1,128)}, f32[4,1,1024]{2,1,0:T(1,128)}) custom-call(s32[16]{0:T(128)} %pad_add_fusion.refs_0_, s32[4]{0:T(128)} %get-tuple-element.225.refs_1_, s32[4]{0:T(128)} %get-tuple-element.226.refs_2_, f32[2048,128]{1,0:T(8,128)} %get-tuple-element.352.refs_3_, ...), custom_call_target="tpu_custom_call" | custom-call | flops 1048576 | bytes 65536 | tf_op jit(solution)/shard_map/attention_forward/pallas_call | solution.py:333
  172.7 9.5 %collective-permute-done.22.refs_3_.refs_5_.refs_7_ = bf16[384,1024]{1,0:T(8,128)(2,1)S(1)} collective-permute-done((bf16[384,1024]{1,0:T(8,128)(2,1)S(1)}, bf16[384,1024]{1,0:T(8,128)(2,1)S(1)}, u32[]{:S(2)}, u32[]{:S(2)}) %collective-permute-start.22) | collective-permute-done | bytes 786464 | tf_op jit(solution)/shard_map/ppermute | solution.py:631
  188.4 5.0 collective-permute-done.21
  210.3 12.7 %collective-permute-done.25 = bf16[256,1536]{1,0:T(8,128)(2,1)S(1)} collective-permute-done((bf16[256,1536]{1,0:T(8,128)(2,1)S(1)}, bf16[256,1536]{1,0:T(8,128)(2,1)S(1)}, u32[]{:S(2)}, u32[]{:S(2)}) %collective-permute-start.25) | collective-permute-done | bytes 786464 | tf_op jit(solution)/shard_map/ppermute | solution.py:580
  248.6 14.3 %gate_0.1 = (bf16[2048,1536]{1,0:T(8,128)(2,1)}, f32[2048,2048]{1,0:T(8,128)}, bf16[2048,1024]{1,0:T(8,128)(2,1)}) custom-call(s32[1]{0:T(128)} %bitcast.7.me, bf16[512,1536]{1,0:T(8,128)(2,1)} %copy-done.10, bf16[512,1536]{1,0:T(8,128)(2,1)} %collective-permute-done.37.refs_1_, bf16[384,1024]{1,0:T(8,128)(2,1)} %copy-done, bf16[384,1024]{1,0:T(8,128)(2,1)} %copy-done.4, ...), custom_call_target="tpu_custom_call" | custom-call | flops 1048576 | bytes 65536 | tf_op jit(solution)/shard_map/gate_0/pallas_call | solution.py:522
  272.6 8.5 %collective-permute-done.39.refs_17_.refs_15_.refs_19_ = bf16[192,1024]{1,0:T(8,128)(2,1)S(1)} collective-permute-done((bf16[192,1024]{1,0:T(8,128)(2,1)S(1)}, bf16[192,1024]{1,0:T(8,128)(2,1)S(1)}, u32[]{:S(2)}, u32[]{:S(2)}) %collective-permute-start.39) | collective-permute-done | bytes 393248 | tf_op jit(solution)/shard_map/ppermute | solution.py:631
  285.6 25.2 %gate_back_0.1 = (bf16[2048,1536]{1,0:T(8,128)(2,1)}, bf16[2048,2048]{1,0:T(8,128)(2,1)}, bf16[512,1536]{1,0:T(8,128)(2,1)}, bf16[512,1536]{1,0:T(8,128)(2,1)}, ...) custom-call(s32[1]{0:T(128)} %bitcast.7.me, bf16[512,1536]{1,0:T(8,128)(2,1)} %maximum_select_fusion.refs_0_, ...), custom_call_target="tpu_custom_call" | custom-call | flops 1048576 | bytes 65536 | tf_op jit(solution)/shard_map/gate_back_0/pallas_call | solution.py:522
  314.1 19.4 %gate_1.1 = (bf16[2048,1536]{1,0:T(8,128)(2,1)}, f32[2048,2048]{1,0:T(8,128)}, bf16[2048,1024]{1,0:T(8,128)(2,1)}, bf16[512,1536]{1,0:T(8,128)(2,1)}, bf16[512,1536]{1,0:T(8,128)(2,1)}) custom-call(s32[1]{0:T(128)} %bitcast.7.me, ...), custom_call_target="tpu_custom_call", output_to_operand_aliasing={{0}: (18, {}), {1}: (19, {}), {2}: (20, {})} | custom-call | flops 1048576 | bytes 65536 | tf_op jit(solution)/shard_map/gate_1/pallas_call | solution.py:522
  342.4 21.5 %gate_back_1.1 = (bf16[2048,1536]{1,0:T(8,128)(2,1)}, bf16[2048,2048]{1,0:T(8,128)(2,1)}, bf16[512,1536]{1,0:T(8,128)(2,1)}, bf16[512,1536]{1,0:T(8,128)(2,1)}) custom-call(s32[1]{0:T(128)} %bitcast.7.me, bf16[256,1536]{1,0:T(8,128)(2,1)} %collective-permute-done.41.refs_0_, ...), custom_call_target="tpu_custom_call", output_to_operand_aliasing={{0}: (22, {}), {1}: (23, {})} | custom-call | flops 1048576 | bytes 65536 | tf_op jit(solution)/shard_map/gate_back_1/pallas_call | solution.py:522
  372.1 10.2 %fusion.7 = bf16[1536,1024]{1,0:T(8,128)(2,1)} fusion(bf16[2048,1536]{1,0:T(8,128)(2,1)} %get-tuple-element.299, bf16[2048,2048]{1,0:T(8,128)(2,1)S(1)} %copy-done.16), kind=kOutput, calls=%fused_computation.7 | convolution fusion | flops 6444023808 | bytes 13631488 | tf_op jit(solution)/shard_map/dot_general | solution.py:63
  382.3 11.3 %fusion.4 = bf16[1536,1024]{1,0:T(8,128)(2,1)} fusion(bf16[2048,1536]{1,0:T(8,128)(2,1)} %get-tuple-element.299, bf16[2048,2048]{1,0:T(8,128)(2,1)} %get-tuple-element.320), kind=kOutput, calls=%fused_computation.6 | convolution fusion | flops 6444023808 | bytes 13631488 | tf_op jit(solution)/shard_map/dot_general | solution.py:63
  394.5 11.4 %convolution_convert_fusion = bf16[1536,1024]{1,0:T(8,128)(2,1)} fusion(bf16[2048,1536]{1,0:T(8,128)(2,1)} %get-tuple-element.327, bf16[2048,1024]{1,0:T(8,128)(2,1)} %get-tuple-element.306.refs_5_), kind=kOutput, calls=%fused_computation.5 | convolution fusion | flops 6444023808 | bytes 13631488 | tf_op jit(solution)/shard_map/dot_general | solution.py:63
  412.9 14.2 %collective-permute-done.51 = bf16[256,1536]{1,0:T(8,128)(2,1)S(1)} collective-permute-done((bf16[256,1536]{1,0:T(8,128)(2,1)S(1)}, bf16[256,1536]{1,0:T(8,128)(2,1)S(1)}, u32[]{:S(2)}, u32[]{:S(2)}) %collective-permute-start.51) | collective-permute-done | bytes 786464 | tf_op jit(solution)/shard_map/ppermute | solution.py:626
  430.8 4.9 fusion.38
  439.0 5.8 collective-permute-start.55
  456.7 11.6 %collective-permute-done.54 = bf16[128,1536]{1,0:T(8,128)(2,1)S(1)} collective-permute-done((bf16[128,1536]{1,0:T(8,128)(2,1)S(1)}, bf16[128,1536]{1,0:T(8,128)(2,1)S(1)}, u32[]{:S(2)}, u32[]{:S(2)}) %collective-permute-start.54) | collective-permute-done | bytes 393248 | tf_op jit(solution)/shard_map/ppermute | solution.py:626
  489.7 45.4 %attention_backward_0.1 = bf16[2048,768]{1,0:T(8,128)(2,1)} custom-call(s32[16]{0:T(128)} %pad_add_fusion.refs_0_, s32[8]{0:T(128)} %get-tuple-element.350.refs_1_, s32[8]{0:T(128)} %get-tuple-element.351.refs_2_, f32[2048,128]{1,0:T(8,128)} %get-tuple-element.352.refs_3_, f32[2048,128]{1,0:T(8,128)} %get-tuple-element.353.refs_4_, ...), custom_call_target="tpu_custom_call" | custom-call | flops 1048576 | bytes 65536 | tf_op jit(solution)/shard_map/attention_backward_0/pallas_call | solution.py:363
  545.9 4.7 fusion.11
  550.6 5.2 collective-permute-done.61
  567.5 7.7 %convolution_convert_fusion.1 = bf16[1536,768]{1,0:T(8,128)(2,1)S(1)} fusion(bf16[2048,1536]{1,0:T(8,128)(2,1)} %get-tuple-element.366, bf16[2048,768]{1,0:T(8,128)(2,1)S(1)} %copy-done.39), kind=kOutput, calls=%fused_computation.8 | convolution fusion | flops 4833017856 | bytes 11796480 | tf_op jit(solution)/shard_map/dot_general | solution.py:63
  608.7 12.5 %collective-permute-done.68 = bf16[192,1024]{1,0:T(8,128)(2,1)S(1)} collective-permute-done((bf16[192,1024]{1,0:T(8,128)(2,1)S(1)}, bf16[192,1024]{1,0:T(8,128)(2,1)S(1)}, u32[]{:S(2)}, u32[]{:S(2)}) %collective-permute-start.68) | collective-permute-done | bytes 393248 | tf_op jit(solution)/shard_map/ppermute | solution.py:580
  621.9 6.6 collective-permute-done.69
  628.5 6.6 collective-permute-start.78
  652.7 12.3 %collective-permute-done.73 = bf16[192,768]{1,0:T(8,128)(2,1)S(1)} collective-permute-done((bf16[192,768]{1,0:T(8,128)(2,1)S(1)}, bf16[192,768]{1,0:T(8,128)(2,1)S(1)}, u32[]{:S(2)}, u32[]{:S(2)}) %collective-permute-start.73) | collective-permute-done | bytes 294944 | tf_op jit(solution)/shard_map/ppermute | solution.py:580
  668.5 15.6 %psum.7 = f32[2,192]{1,0:T(2,128)S(1)} all-reduce(f32[2,192]{1,0:T(2,128)S(1)} %pad_maximum_fusion.17), channel_id=1, replica_groups=mesh['yx'=4,'core'=2,'zh'=2,'zl'=2] {'zh','zl'}, use_global_device_ids=true, to_apply=%region_13.14 | all-reduce | flops 384 | bytes 3072 | tf_op jit(solution)/shard_map/psum | solution.py:1023
  (480 shorter events, 290.5 us)
Async XLA Ops:
  7.2 186.1 %all-gather.3.cloned.1.call-start = ((), (), s32[]{:S(2)}) async-start(), calls=%async_computation.4 | async-start | bytes 2949120 | tf_op jit(solution)/shard_map/all_gather | solution.py:782
  8.5 31.1 %collective-permute-start.2 = (bf16[192,768]{1,0:T(8,128)(2,1)S(1)}, bf16[192,768]{1,0:T(8,128)(2,1)}, u32[]{:S(2)}, u32[]{:S(2)}) collective-permute-start(bf16[192,768]{1,0:T(8,128)(2,1)S(1)} %pad_maximum_fusion.15), channel_id=1, source_target_pairs={{0,2},{6,4},{4,0},{2,6},{1,3},{7,5},{5,1},{3,7},{8,10},{14,12},{12... | collective-permute-start | bytes 884744 | tf_op jit(solution)/shard_map/ppermute | solution.py:580
  8.6 31.1 %collective-permute-start.3 = (bf16[192,768]{1,0:T(8,128)(2,1)S(1)}, bf16[192,768]{1,0:T(8,128)(2,1)}, u32[]{:S(2)}, u32[]{:S(2)}) collective-permute-start(bf16[192,768]{1,0:T(8,128)(2,1)S(1)} %pad_maximum_fusion.15), channel_id=1, source_target_pairs={{2,4},{4,2},{3,5},{5,3},{10,12},{12,10},{11,13},{13,11},{18,20},{2... | collective-permute-start | bytes 884744 | tf_op jit(solution)/shard_map/ppermute | solution.py:580
  11.7 26.7 %collective-permute-start = (bf16[256,1536]{1,0:T(8,128)(2,1)S(1)}, bf16[256,1536]{1,0:T(8,128)(2,1)S(1)}, u32[]{:S(2)}, u32[]{:S(2)}) collective-permute-start(bf16[256,1536]{1,0:T(8,128)(2,1)S(1)} %slice.248), channel_id=1, source_target_pairs={{2,4},{4,2},{3,5},{5,3},{10,12},{12,10},{11,13},{13,11},{18,20},{2... | collective-permute-start | bytes 2359304 | tf_op jit(solution)/shard_map/ppermute | solution.py:580
  41.0 36.1 %collective-permute-start.7 = (bf16[384,768]{1,0:T(8,128)(2,1)S(1)}, bf16[384,768]{1,0:T(8,128)(2,1)S(1)}, u32[]{:S(2)}, u32[]{:S(2)}) collective-permute-start(bf16[384,768]{1,0:T(8,128)(2,1)S(1)} %pad_maximum_fusion.11.refs_3_.refs_0_), channel_id=1, source_target_pairs={{0,8},{8,0},{16,24},{24,16},{1,9},{9,1},{17,25},{25,17},{2,10},{10... | collective-permute-start | bytes 1769480 | tf_op jit(solution)/shard_map/ppermute | solution.py:631
  42.6 34.6 %collective-permute-start.8 = (bf16[384,768]{1,0:T(8,128)(2,1)S(1)}, bf16[384,768]{1,0:T(8,128)(2,1)S(1)}, u32[]{:S(2)}, u32[]{:S(2)}) collective-permute-start(bf16[384,768]{1,0:T(8,128)(2,1)S(1)} %pad_maximum_fusion.11.refs_3_.refs_0_), channel_id=1, source_target_pairs={{0,16},{8,24},{16,0},{24,8},{1,17},{9,25},{17,1},{25,9},{2,18},{10... | collective-permute-start | bytes 1769480 | tf_op jit(solution)/shard_map/ppermute | solution.py:631
  44.4 32.7 %collective-permute-start.6 = (bf16[256,1536]{1,0:T(8,128)(2,1)}, bf16[256,1536]{1,0:T(8,128)(2,1)}, u32[]{:S(2)}, u32[]{:S(2)}) collective-permute-start(bf16[256,1536]{1,0:T(8,128)(2,1)} %get-tuple-element.201), channel_id=1, source_target_pairs={{1,0},{0,1},{3,2},{2,3},{5,4},{4,5},{7,6},{6,7},{9,8},{8,9},{11,10... | collective-permute-start | bytes 2359304 | tf_op jit(solution)/shard_map/ppermute | solution.py:621
  51.7 23.4 %collective-permute-start.4 = (bf16[256,1536]{1,0:T(8,128)(2,1)}, bf16[256,1536]{1,0:T(8,128)(2,1)}, u32[]{:S(2)}, u32[]{:S(2)}) collective-permute-start(bf16[256,1536]{1,0:T(8,128)(2,1)} %get-tuple-element.202), channel_id=1, source_target_pairs={{2,4},{4,2},{3,5},{5,3},{10,12},{12,10},{11,13},{13,11},{18,20},{2... | collective-permute-start | bytes 2359304 | tf_op jit(solution)/shard_map/ppermute | solution.py:580
  78.9 23.8 %collective-permute-start.10 = (bf16[256,1536]{1,0:T(8,128)(2,1)}, bf16[256,1536]{1,0:T(8,128)(2,1)}, u32[]{:S(2)}, u32[]{:S(2)}) collective-permute-start(bf16[256,1536]{1,0:T(8,128)(2,1)} %broadcast_select_fusion.2), channel_id=1, source_target_pairs={{1,0},{0,1},{3,2},{2,3},{5,4},{4,5},{7,6},{6,7},{9,8},{8,9},{11,10... | collective-permute-start | bytes 2359304 | tf_op jit(solution)/shard_map/ppermute | solution.py:621
  124.6 356.7 %reduce-scatter.5.cloned.1.call-start = ((), (), s32[]{:S(2)}) async-start(), calls=%async_computation.5 | async-start | bytes 3932160 | tf_op jit(solution)/shard_map/reduce_scatter | solution.py:907
  124.7 38.0 %collective-permute-start.18 = (bf16[192,2048]{1,0:T(8,128)(2,1)S(1)}, bf16[192,2048]{1,0:T(8,128)(2,1)S(1)}, u32[]{:S(2)}, u32[]{:S(2)}) collective-permute-start(bf16[192,2048]{1,0:T(8,128)(2,1)S(1)} %copy-done.37), channel_id=1, source_target_pairs={{0,2},{6,4},{4,0},{2,6},{1,3},{7,5},{5,1},{3,7},{8,10},{14,12},{12... | collective-permute-start | bytes 2359304 | tf_op jit(solution)/shard_map/ppermute | solution.py:580
  124.7 37.9 %collective-permute-start.19 = (bf16[192,2048]{1,0:T(8,128)(2,1)S(1)}, bf16[192,2048]{1,0:T(8,128)(2,1)S(1)}, u32[]{:S(2)}, u32[]{:S(2)}) collective-permute-start(bf16[192,2048]{1,0:T(8,128)(2,1)S(1)} %copy-done.37), channel_id=1, source_target_pairs={{2,4},{4,2},{3,5},{5,3},{10,12},{12,10},{11,13},{13,11},{18,20},{2... | collective-permute-start | bytes 2359304 | tf_op jit(solution)/shard_map/ppermute | solution.py:580
  169.3 24.0 %collective-permute-start.21 = (bf16[1024,384]{1,0:T(8,128)(2,1)S(1)}, bf16[1024,384]{1,0:T(8,128)(2,1)S(1)}, u32[]{:S(2)}, u32[]{:S(2)}) collective-permute-start(bf16[1024,384]{1,0:T(8,128)(2,1)S(1)} %copy-done.63), channel_id=1, source_target_pairs={{0,1},{1,0},{2,3},{3,2},{4,5},{5,4},{6,7},{7,6},{8,9},{9,8},{10,11... | collective-permute-start | bytes 2359304 | tf_op jit(solution)/shard_map/ppermute | solution.py:626
  199.6 23.4 %collective-permute-start.26 = (bf16[384,1024]{1,0:T(8,128)(2,1)}, bf16[384,1024]{1,0:T(8,128)(2,1)S(1)}, u32[]{:S(2)}, u32[]{:S(2)}) collective-permute-start(bf16[384,1024]{1,0:T(8,128)(2,1)} %pad_maximum_fusion.6.refs_7_.refs_9_.refs_11_), channel_id=1, source_target_pairs={{0,8},{8,0},{16,24},{24,16},{1,9},{9,1},{17,25},{25,17},{2,10},{10... | collective-permute-start | bytes 2359304 | tf_op jit(solution)/shard_map/ppermute | solution.py:631
  284.7 26.1 %collective-permute-start.41 = (bf16[256,1536]{1,0:T(8,128)(2,1)}, bf16[256,1536]{1,0:T(8,128)(2,1)}, u32[]{:S(2)}, u32[]{:S(2)}) collective-permute-start(bf16[256,1536]{1,0:T(8,128)(2,1)} %slice.276), channel_id=1, source_target_pairs={{1,0},{0,1},{3,2},{2,3},{5,4},{4,5},{7,6},{6,7},{9,8},{8,9},{11,10... | collective-permute-start | bytes 2359304 | tf_op jit(solution)/shard_map/ppermute | solution.py:621
  393.6 141.5 %reduce-scatter.7.cloned.1.call-start = ((), (), s32[]{:S(2)}) async-start(), calls=%async_computation.6 | async-start | bytes 3932160 | tf_op jit(solution)/shard_map/reduce_scatter | solution.py:923
  394.4 189.8 %reduce-scatter.9.cloned.1.call-start = ((), (), s32[]{:S(2)}) async-start(), calls=%async_computation.7 | async-start | bytes 3932160 | tf_op jit(solution)/shard_map/reduce_scatter | solution.py:958
  438.9 183.0 %reduce-scatter.11.cloned.1.call-start = ((), (), s32[]{:S(2)}) async-start(), calls=%async_computation.8 | async-start | bytes 2949120 | tf_op jit(solution)/shard_map/reduce_scatter | solution.py:959
  439.0 40.0 %collective-permute-start.55 = (bf16[256,1536]{1,0:T(8,128)(2,1)}, bf16[256,1536]{1,0:T(8,128)(2,1)}, u32[]{:S(2)}, u32[]{:S(2)}) collective-permute-start(bf16[256,1536]{1,0:T(8,128)(2,1)} %fusion.17), channel_id=1, source_target_pairs={{2,4},{4,2},{3,5},{5,3},{10,12},{12,10},{11,13},{13,11},{18,20},{2... | collective-permute-start | bytes 2359304 | tf_op jit(solution)/shard_map/ppermute | solution.py:580
  481.3 53.9 %collective-permute-start.57 = (bf16[256,1536]{1,0:T(8,128)(2,1)}, bf16[256,1536]{1,0:T(8,128)(2,1)S(1)}, u32[]{:S(2)}, u32[]{:S(2)}) collective-permute-start(bf16[256,1536]{1,0:T(8,128)(2,1)} %fusion.15), channel_id=1, source_target_pairs={{2,4},{4,2},{3,5},{5,3},{10,12},{12,10},{11,13},{13,11},{18,20},{2... | collective-permute-start | bytes 2359304 | tf_op jit(solution)/shard_map/ppermute | solution.py:580
  486.9 48.3 %collective-permute-start.58 = (bf16[192,1024]{1,0:T(8,128)(2,1)}, bf16[192,1024]{1,0:T(8,128)(2,1)}, u32[]{:S(2)}, u32[]{:S(2)}) collective-permute-start(bf16[192,1024]{1,0:T(8,128)(2,1)} %get-tuple-element.427), channel_id=1, source_target_pairs={{2,0},{4,6},{0,4},{6,2},{3,1},{5,7},{1,5},{7,3},{10,8},{12,14},{8,... | collective-permute-start | bytes 1179656 | tf_op jit(solution)/shard_map/ppermute | solution.py:580
  486.9 48.3 %collective-permute-start.59 = (bf16[192,1024]{1,0:T(8,128)(2,1)S(1)}, bf16[192,1024]{1,0:T(8,128)(2,1)}, u32[]{:S(2)}, u32[]{:S(2)}) collective-permute-start(bf16[192,1024]{1,0:T(8,128)(2,1)S(1)} %get-tuple-element.426), channel_id=1, source_target_pairs={{2,4},{4,2},{3,5},{5,3},{10,12},{12,10},{11,13},{13,11},{18,20},{2... | collective-permute-start | bytes 1179656 | tf_op jit(solution)/shard_map/ppermute | solution.py:580
  589.8 31.4 %collective-permute-start.71 = (bf16[384,768]{1,0:T(8,128)(2,1)S(1)}, bf16[384,768]{1,0:T(8,128)(2,1)}, u32[]{:S(2)}, u32[]{:S(2)}) collective-permute-start(bf16[384,768]{1,0:T(8,128)(2,1)S(1)} %pad_maximum_fusion.14), channel_id=1, source_target_pairs={{0,16},{8,24},{16,0},{24,8},{1,17},{9,25},{17,1},{25,9},{2,18},{10... | collective-permute-start | bytes 1769480 | tf_op jit(solution)/shard_map/ppermute | solution.py:631
  590.6 31.3 %collective-permute-start.70 = (bf16[384,768]{1,0:T(8,128)(2,1)S(1)}, bf16[384,768]{1,0:T(8,128)(2,1)}, u32[]{:S(2)}, u32[]{:S(2)}) collective-permute-start(bf16[384,768]{1,0:T(8,128)(2,1)S(1)} %pad_maximum_fusion.13), channel_id=1, source_target_pairs={{0,8},{8,0},{16,24},{24,16},{1,9},{9,1},{17,25},{25,17},{2,10},{10... | collective-permute-start | bytes 1769480 | tf_op jit(solution)/shard_map/ppermute | solution.py:631
  596.7 25.2 %collective-permute-start.67 = (bf16[256,1536]{1,0:T(8,128)(2,1)}, bf16[256,1536]{1,0:T(8,128)(2,1)}, u32[]{:S(2)}, u32[]{:S(2)}) collective-permute-start(bf16[256,1536]{1,0:T(8,128)(2,1)} %fusion.13), channel_id=1, source_target_pairs={{2,4},{4,2},{3,5},{5,3},{10,12},{12,10},{11,13},{13,11},{18,20},{2... | collective-permute-start | bytes 2359304 | tf_op jit(solution)/shard_map/ppermute | solution.py:580
  599.7 28.8 %collective-permute-start.69 = (bf16[256,1536]{1,0:T(8,128)(2,1)}, bf16[256,1536]{1,0:T(8,128)(2,1)}, u32[]{:S(2)}, u32[]{:S(2)}) collective-permute-start(bf16[256,1536]{1,0:T(8,128)(2,1)} %slice.310), channel_id=1, source_target_pairs={{0,1},{1,0},{2,3},{3,2},{4,5},{5,4},{6,7},{7,6},{8,9},{9,8},{10,11... | collective-permute-start | bytes 2359304 | tf_op jit(solution)/shard_map/ppermute | solution.py:626
  628.5 57.7 %collective-permute-start.78 = (bf16[192,1024]{1,0:T(8,128)(2,1)S(1)}, bf16[192,1024]{1,0:T(8,128)(2,1)}, u32[]{:S(2)}, u32[]{:S(2)}) collective-permute-start(bf16[192,1024]{1,0:T(8,128)(2,1)S(1)} %get-tuple-element.390), channel_id=1, source_target_pairs={{2,4},{4,2},{3,5},{5,3},{10,12},{12,10},{11,13},{13,11},{18,20},{2... | collective-permute-start | bytes 1179656 | tf_op jit(solution)/shard_map/ppermute | solution.py:580
  638.1 26.9 %collective-permute-start.73 = (bf16[192,768]{1,0:T(8,128)(2,1)S(1)}, bf16[192,768]{1,0:T(8,128)(2,1)S(1)}, u32[]{:S(2)}, u32[]{:S(2)}) collective-permute-start(bf16[192,768]{1,0:T(8,128)(2,1)S(1)} %get-tuple-element.434), channel_id=1, source_target_pairs={{2,0},{4,6},{0,4},{6,2},{3,1},{5,7},{1,5},{7,3},{10,8},{12,14},{8,... | collective-permute-start | bytes 884744 | tf_op jit(solution)/shard_map/ppermute | solution.py:580
  638.3 29.9 %collective-permute-start.74 = (bf16[192,768]{1,0:T(8,128)(2,1)S(1)}, bf16[192,768]{1,0:T(8,128)(2,1)S(1)}, u32[]{:S(2)}, u32[]{:S(2)}) collective-permute-start(bf16[192,768]{1,0:T(8,128)(2,1)S(1)} %get-tuple-element.435), channel_id=1, source_target_pairs={{2,4},{4,2},{3,5},{5,3},{10,12},{12,10},{11,13},{13,11},{18,20},{2... | collective-permute-start | bytes 884744 | tf_op jit(solution)/shard_map/ppermute | solution.py:580
  645.9 44.1 %collective-permute-start.72 = (bf16[256,1536]{1,0:T(8,128)(2,1)}, bf16[256,1536]{1,0:T(8,128)(2,1)S(1)}, u32[]{:S(2)}, u32[]{:S(2)}) collective-permute-start(bf16[256,1536]{1,0:T(8,128)(2,1)} %fusion.12), channel_id=1, source_target_pairs={{2,4},{4,2},{3,5},{5,3},{10,12},{12,10},{11,13},{13,11},{18,20},{2... | collective-permute-start | bytes 2359304 | tf_op jit(solution)/shard_map/ppermute | solution.py:580
  651.4 36.9 %collective-permute-start.76 = (bf16[192,384]{1,0:T(8,128)(2,1)}, bf16[192,384]{1,0:T(8,128)(2,1)}, u32[]{:S(2)}, u32[]{:S(2)}) collective-permute-start(bf16[192,384]{1,0:T(8,128)(2,1)} %get-tuple-element.439), channel_id=1, source_target_pairs={{2,0},{4,6},{0,4},{6,2},{3,1},{5,7},{1,5},{7,3},{10,8},{12,14},{8,... | collective-permute-start | bytes 442376 | tf_op jit(solution)/shard_map/ppermute | solution.py:580
  665.0 23.3 %collective-permute-start.77 = (bf16[192,384]{1,0:T(8,128)(2,1)S(1)}, bf16[192,384]{1,0:T(8,128)(2,1)}, u32[]{:S(2)}, u32[]{:S(2)}) collective-permute-start(bf16[192,384]{1,0:T(8,128)(2,1)S(1)} %get-tuple-element.438), channel_id=1, source_target_pairs={{2,4},{4,2},{3,5},{5,3},{10,12},{12,10},{11,13},{13,11},{18,20},{2... | collective-permute-start | bytes 442376 | tf_op jit(solution)/shard_map/ppermute | solution.py:580
  (149 other events, 1589.1 us)
Sparse Core Ops, SparseCore 0:
  124.7 39.6 all-gather.2
  393.8 45.8 reduce-scatter.4
  442.6 43.9 reduce-scatter.6
  489.4 43.9 reduce-scatter.8
  539.9 36.7 reduce-scatter.10

commit v5 on v4

--- a/solution.py
+++ b/solution.py
@@ -793,54 +793,55 @@
         for n in range(2)
     ]
     gate_taken = neighbours(pairs[0])
+    w_project = assemble("assemble_project", me, *blocks, tokens.shape[1], qkv_cols)
     residual = own.astype(f32)
     scale_one = lax.rsqrt(jnp.mean(residual * residual, axis=-1, keepdims=True) + EPSILON)
-    up_pair, cotangent, cot_upper, w_out, scale_one, *moved = stage(
-        pairs[1], cotangent, cot_upper, w_out, scale_one, *quarters, *gate_taken
+    up_pair, cotangent, cot_upper, w_out, scale_one, w_project, *moved = stage(
+        pairs[1], cotangent, cot_upper, w_out, scale_one, w_project, *quarters, *gate_taken
     )
     quarters, gate_taken = moved[:near], moved[near:]
 
     up_taken = neighbours(up_pair)
-    cot_lower = crossed(cotangent[part_rows:], CROSS)
+    gate_halves = diagonal(gate_taken)
     context_all = jnp.concatenate(quarters, axis=1)
     branch_sib = flip(times_transpose(context_all[rows:], w_out).astype(bf16), "core")
     mid = residual + times_transpose(context_all[:rows], w_out) + branch_sib.astype(f32)
     scale_two, norm_two = norm_rows(mid, gain_two)
-    norm_two, cot_lower, *up_taken = stage(norm_two, cot_lower, *up_taken)
-
-    upper_far = [from_near(norm_two[:part_rows], k) for k in others]
-    gate_halves, up_halves = diagonal(gate_taken), diagonal(up_taken)
-    cot = jnp.where(straight(), cotangent, jnp.concatenate([cot_upper, cot_lower], axis=0))
+    norm_two, cotangent, *moved = stage(norm_two, cotangent, *up_taken, *gate_halves)
+    up_taken, gate_halves = moved[: len(up_taken)], moved[len(up_taken) :]
+
+    quarter = part_rows // 2
+    far_quarters = [[from_near(norm_two[:quarter], k) for k in others]]
+    norm_sib = flip(norm_two, "core")
+    up_halves = diagonal(up_taken)
     down_pair = pair_of(down_weight, *down_moved)
-    w_project = assemble("assemble_project", me, *blocks, tokens.shape[1], qkv_cols)
-    norm_two, cot, down_pair, w_project, *moved = stage(
-        norm_two, cot, down_pair, w_project, *upper_far, *gate_halves, *up_halves
-    )
-    upper_far, moved = moved[: near - 1], moved[near - 1 :]
-    gate_halves, up_halves = moved[: len(gate_halves)], moved[len(gate_halves) :]
-
-    lower_far = [from_near(norm_two[part_rows:], k) for k in others]
-    norm_sib, cot_sib = flip(norm_two, "core"), flip(cot, "core")
+    norm_two, norm_sib, down_pair, cotangent, *moved = stage(
+        norm_two, norm_sib, down_pair, cotangent, *far_quarters[0], *up_halves
+    )
+    far_quarters[0], up_halves = moved[: near - 1], moved[near - 1 :]
+
+    far_quarters.append([from_near(norm_two[quarter:part_rows], k) for k in others])
+    cot_lower = crossed(cotangent[part_rows:], CROSS)
     down_taken = neighbours(down_pair)
     gate_blocks = blocks_of(pairs[0], gate_taken, gate_halves)
     up_blocks = blocks_of(up_pair, up_taken, up_halves, hidden_cols)
     gate_up = ([*gate_blocks[0], *up_blocks[0]], gate_blocks[1] + up_blocks[1], 2 * hidden_cols)
-    outs = [(norm_two.shape[1], bf16, "all"), (2 * hidden_cols, f32, "all"), (hidden_cols, bf16, "all")]
-    earlier = piece_call(gate_kernel, "gate", 0, near, me, [norm_two, norm_sib], [], [], [gate_up], [], outs)
-    cot_sib, *moved = stage(cot_sib, *lower_far, *down_taken, *earlier)
-    lower_far, moved = moved[: near - 1], moved[near - 1 :]
+    gate_outs = [(norm_two.shape[1], bf16, "all"), (2 * hidden_cols, f32, "all"), (hidden_cols, bf16, "all")]
+    earlier = piece_call(gate_kernel, "gate", 0, near, me, [norm_two, norm_sib], [], [], [gate_up], [], gate_outs)
+    norm_two, cotangent, cot_lower, *moved = stage(
+        norm_two, cotangent, cot_lower, *far_quarters[1], *down_taken, *earlier
+    )
+    far_quarters[1], moved = moved[: near - 1], moved[near - 1 :]
     down_taken, earlier = moved[: len(down_taken)], moved[len(down_taken) :]
 
-    norm_far = [jnp.concatenate(x, axis=0) for x in zip(upper_far, lower_far, strict=True)]
-    norm_far_sib = [flip(x, "core") for x in norm_far]
+    lower_far = [from_near(norm_two[part_rows:], k) for k in others]
+    cot = jnp.where(straight(), cotangent, jnp.concatenate([cot_upper, cot_lower], axis=0))
+    cot_sib = flip(cot, "core")
+    cot_upper_far = [from_near(jnp.where(straight(), cotangent[:part_rows], cot_upper), k) for k in others]
     down_halves = diagonal(down_taken)
-    cot, *moved = stage(cot, *norm_far, *norm_far_sib, *down_halves)
-    norm_far, norm_far_sib, down_halves = moved[: near - 1], moved[near - 1 : 2 * near - 2], moved[2 * near - 2 :]
-
-    cot_upper_far = [from_near(cot[:part_rows], k) for k in others]
     down = (*blocks_of(down_pair, down_taken, down_halves), hidden_cols)
     width = norm_two.shape[1]
-    gate_outs, outs = outs, [(width, bf16, "all"), (2 * hidden_cols, bf16, "all")]
+    outs = [(width, bf16, "all"), (2 * hidden_cols, bf16, "all")]
     halves = [(width, bf16, "own"), (width, bf16, "sibling")]
 
     def way_back(k, parts, earlier):
@@ -853,36 +854,36 @@
     norm_two_all, gate_up_all, hidden_all = earlier
     grad_all, d_gate_up_all, *near_back = way_back(0, [cot, cot_sib], [])
     cot, *moved = stage(
-        cot, norm_two_all, gate_up_all, hidden_all, grad_all, d_gate_up_all, *near_back, *cot_upper_far
-    )
-    earlier, moved = moved[:3], moved[3:]
-    grad_all, d_gate_up_all, *moved = moved
-    near_back, cot_upper_far = moved[:4], moved[4:]
+        cot, norm_two_all, gate_up_all, hidden_all, grad_all, d_gate_up_all, *near_back, *cot_upper_far, *lower_far
+    )
+    earlier, (grad_all, d_gate_up_all), near_back, moved = moved[:3], moved[3:5], moved[5:9], moved[9:]
+    cot_upper_far, lower_far = moved[: near - 1], moved[near - 1 :]
 
     cot_lower_far = [from_near(cot[part_rows:], k) for k in others]
-    cot_upper_far_sib = [flip(x, "core") for x in cot_upper_far]
     out_far = []
     for k in others:
-        parts = [norm_far[k - 1], norm_far_sib[k - 1]]
+        norm_far = jnp.concatenate([*(x[k - 1] for x in far_quarters), lower_far[k - 1]], axis=0)
+        parts = [norm_far, flip(norm_far, "core")]
         *earlier, out_own, out_sib = piece_call(
             gate_kernel, "gate", k, near, me, parts, [], [], [gate_up, down], earlier, gate_outs + halves
         )
         out_far += [out_own, out_sib]
-    grad_all, d_gate_up_all, *moved = stage(
-        grad_all, d_gate_up_all, *near_back, *cot_lower_far, *cot_upper_far_sib, *earlier, *out_far
+    grad_all, d_gate_up_all, w_project, *moved = stage(
+        grad_all, d_gate_up_all, w_project, *near_back, *cot_lower_far, *earlier, *out_far
     )
     near_back, cot_lower_far, moved = moved[:4], moved[4 : near + 3], moved[near + 3 :]
-    cot_upper_far_sib, earlier, out_far = moved[: near - 1], moved[near - 1 : near + 2], moved[near + 2 :]
+    earlier, out_far = moved[:3], moved[3:]
     norm_two_all, gate_up_all, hidden_all = earlier
-    cot_lower_far_sib = [flip(x, "core") for x in cot_lower_far]
+    cot_far = [jnp.concatenate(x, axis=0) for x in zip(cot_upper_far, cot_lower_far, strict=True)]
+    cot_far_sib = [flip(x, "core") for x in cot_far]
     out_sums = [joined(*out_far[2 * n : 2 * n + 2]).astype(bf16) for n in range(near - 1)]
-    moved = stage(*cot_lower_far_sib, *out_sums)
-    cot_lower_far_sib, out_sums = moved[: near - 1], moved[near - 1 :]
+    moved = stage(*cot_far_sib, *out_sums)
+    cot_far_sib, out_sums = moved[: near - 1], moved[near - 1 :]
 
     out_upper = [to_near(out_sums[k - 1][:part_rows], k) for k in others]
     back = []
     for k in others:
-        parts = [cot_upper_far[k - 1], cot_lower_far[k - 1], cot_upper_far_sib[k - 1], cot_lower_far_sib[k - 1]]
+        parts = [cot_far[k - 1], cot_far_sib[k - 1]]
         grad_all, d_gate_up_all, *more = way_back(k, parts, [grad_all, d_gate_up_all])
         back.append(more)
     grad_all, d_gate_up_all, *moved = stage(grad_all, d_gate_up_all, *(x for more in back for x in more), *out_upper)
@@ -897,15 +898,14 @@
         rows_product(norm_two_all, d_gate_up_all[:, n * hidden_cols : (n + 1) * hidden_cols]).astype(bf16)
         for n in range(2)
     )
-    output_near = joined(*near_back[2:])
-    grad_gate, grad_up, grad_all, near_own, near_sib, output_near, *moved = stage(
-        grad_gate, grad_up, grad_all, near_own, near_sib, output_near, *moved_upper, *d_norm_sent
+    d_norm_two, output_near = joined(near_own, near_sib), joined(*near_back[2:])
+    grad_gate, grad_up, grad_all, d_norm_two, output_near, *moved = stage(
+        grad_gate, grad_up, grad_all, d_norm_two, output_near, *moved_upper, *d_norm_sent
     )
     moved_upper, d_norm_sent = moved[: near - 1], moved[near - 1 :]
 
     moved_lower = [to_near(d_norm_sent[k - 1][part_rows:], k) for k in others]
     gate_part = lax.psum_scatter(grad_gate, "yx", scatter_dimension=0, tiled=True)
-    d_norm_two = joined(near_own, near_sib)
     grad_down = rows_product(grad_all, hidden_all).astype(bf16)
 
     def output_part(at, moved):
@@ -914,11 +914,10 @@
             part = part + x.astype(f32)
         return part.astype(bf16)
 
+    grad_down, d_norm_two, output_near, *moved = stage(grad_down, d_norm_two, output_near, *out_sums, *moved_lower)
+    out_sums, moved_lower = moved[: near - 1], moved[near - 1 :]
     output_upper = output_part(slice(0, part_rows), out_upper)
-    grad_down, d_norm_two, output_upper, *moved = stage(grad_down, d_norm_two, output_upper, *out_sums, *moved_lower)
-    out_sums, moved_lower = moved[: near - 1], moved[near - 1 :]
-
-    quarter = part_rows // 2
+
     out_lower = [[to_near(out_sums[k - 1][part_rows : part_rows + quarter], k) for k in others]]
     up_part = lax.psum_scatter(grad_up, "yx", scatter_dimension=0, tiled=True)
     for one, two in zip(moved_upper, moved_lower, strict=True):
@@ -926,7 +925,7 @@
     mid_back, _ = norm_back(mid, scale_two, gain_two, d_norm_two)
     d_mid = cot.astype(f32) + mid_back
     d_attn = d_mid.astype(bf16)
-    d_attn, *moved = stage(d_attn, *out_lower[0], *out_sums)
+    d_attn, output_upper, *moved = stage(d_attn, output_upper, *out_lower[0], *out_sums)
     out_lower[0], out_sums = moved[: near - 1], moved[near - 1 :]
 
     out_lower.append([to_near(out_sums[k - 1][part_rows + quarter :], k) for k in others])
@@ -947,18 +946,21 @@
     output_lower = output_part(
         slice(part_rows, rows), [jnp.concatenate(x, axis=0) for x in zip(*out_lower, strict=True)]
     )
-    grad_out, output_lower, gate_part, upper_crossed, *d_context = stage(
-        grad_out, output_lower, gate_part, upper_crossed, *d_context
+    grad_out, output_lower, gate_part, up_part, upper_crossed, *d_context = stage(
+        grad_out, output_lower, gate_part, up_part, upper_crossed, *d_context
     )
 
     lower_crossed = crossed(output_lower, CROSS)
     output = jnp.concatenate([output_upper, output_lower], axis=0)
     gate_keep, gate_give = give_z(gate_part)
     gate_home = [crossed(gate_give, BACK), crossed(gate_keep, CROSS)]
+    up_keep, up_give = give_z(up_part)
+    up_home = [crossed(up_give, BACK), crossed(up_keep, CROSS)]
     down_part = lax.psum_scatter(grad_down, "yx", scatter_dimension=0, tiled=True)
     out_part = lax.psum_scatter(grad_out, "yx", scatter_dimension=0, tiled=True)
     d_qkv = attend_back(list(range(kv_heads)), qkv, d_context, context, sums, [], layout_back, q_heads, kv_heads)
-    d_qkv, lower_crossed, up_part, *gate_home = stage(d_qkv, lower_crossed, up_part, *gate_home)
+    d_qkv, lower_crossed, down_part, *moved = stage(d_qkv, lower_crossed, down_part, *gate_home, *up_home)
+    gate_home, up_home = moved[:2], moved[2:]
     output = jnp.where(straight(), output, jnp.concatenate([upper_crossed, lower_crossed], axis=0))
 
     def back_part(k):
@@ -966,60 +968,43 @@
         taken = flip(times_transpose(sib, w_project).astype(bf16), "core")
         return times_transpose(own, w_project) + taken.astype(f32)
 
-    up_keep, up_give = give_z(up_part)
-    up_home = [crossed(up_give, BACK), crossed(up_keep, CROSS)]
+    down_keep, down_give = give_z(down_part)
+    down_home = [crossed(down_give, BACK), crossed(down_keep, CROSS)]
     d_sent = [back_part(k).astype(bf16) for k in others]
-    d_qkv, *moved = stage(d_qkv, *d_sent, *up_home)
-    d_sent, up_home = moved[: near - 1], moved[near - 1 :]
+    d_qkv, *moved = stage(d_qkv, *d_sent, *down_home)
+    d_sent, down_home = moved[: near - 1], moved[near - 1 :]
 
     d_upper = [to_near(d_sent[k - 1][:part_rows], k) for k in others]
     grad_project = rows_product(norm_one, d_qkv).astype(bf16)
     project_sent = send_yx(grad_project, (0, qkv_cols))
     total = back_part(0)
-    total, grad_project, down_part, *moved = stage(total, grad_project, down_part, *d_upper, *d_sent, *project_sent)
+    total, grad_project, *moved = stage(total, grad_project, *d_upper, *d_sent, *project_sent)
     d_upper, d_sent, project_sent = moved[: near - 1], moved[near - 1 : 2 * near - 2], moved[2 * near - 2 :]
 
     d_lower = [to_near(d_sent[k - 1][part_rows:], k) for k in others]
     project_rest, project_own = join_yx(grad_project, (0, qkv_cols), project_sent)
-    down_keep, down_give = give_z(down_part)
-    down_back = crossed(down_give, BACK)
-
-    def input_part(at, moved):
-        part = total[at]
-        for x in moved:
-            part = part + x.astype(f32)
-        back, _ = norm_back(residual[at], scale_one[at], gain_one, part)
-        return (d_mid[at] + back).astype(bf16)
-
-    input_upper = input_part(slice(0, part_rows), d_upper)
-    upper_crossed = crossed(input_upper, CROSS)
-    total, input_upper, upper_crossed, out_part, down_back, down_keep, *moved = stage(
-        total, input_upper, upper_crossed, out_part, down_back, down_keep, *d_lower, *project_rest
-    )
+    out_part, *moved = stage(out_part, *d_lower, *project_rest)
     d_lower, project_rest = moved[: near - 1], moved[near - 1 :]
-    down_cross = crossed(down_keep, CROSS)
-
+    d_moved = [jnp.concatenate(x, axis=0) for x in zip(d_upper, d_lower, strict=True)]
     project_keep, project_give = give_z(total_yx(project_rest, project_own))
+
     project_home = [crossed(project_give, BACK), crossed(project_keep, CROSS)]
-    input_lower = input_part(slice(part_rows, rows), d_lower)
-    lower_crossed = crossed(input_lower, CROSS)
+    for part in d_moved:
+        total = total + part.astype(f32)
+    input_back, _ = norm_back(residual, scale_one, gain_one, total)
+    input_own = (d_mid + input_back).astype(bf16)
     out_moved = [to_near(out_part[:, k * query_cols : (k + 1) * query_cols], k) for k in others]
     out_quarter = out_part[:, :query_cols].astype(f32)
     for part in out_moved:
         out_quarter = out_quarter + part.astype(f32)
     out_keep, out_give = give_z(out_quarter.astype(bf16))
+    input_own, out_keep, out_give, *project_home = stage(input_own, out_keep, out_give, *project_home)
     out_home = [crossed(out_give, BACK), crossed(out_keep, CROSS)]
+    input_grad = jnp.where(straight(), input_own, crossed(input_own, CROSS)).astype(f32)
     grad_project = sum_z(project_keep, *project_home)
     grad_out = sum_z(out_keep, *out_home)
-    grad_down = sum_z(down_keep, down_back, down_cross)
+    grad_down = sum_z(down_keep, *down_home)
     grad_gate, grad_up = sum_z(gate_keep, *gate_home), sum_z(up_keep, *up_home)
-    input_grad = jnp.concatenate(
-        [
-            jnp.where(straight(), input_upper, upper_crossed),
-            jnp.where(straight(), input_lower, lower_crossed),
-        ],
-        axis=0,
-    ).astype(f32)
     gain_grads = lax.psum(
         jnp.stack(
             [

time: 709 us -> 707 us (level)
  blocking collectives: 24.9 us -> 48.6 us
  waiting for transfers between devices: 166 us -> 154 us
    ppermute x27 -> x26, waiting for transfers between devices: 74.3 us -> 35.3 us  [crossed(): return lax.ppermute(x, ('core', 'zh'), perm)]
    psum x1, blocking collectives: 15.6 us -> 39.3 us  [body(): lax.psum(jnp.stack([jnp.sum(qkv_shard.astype(f32) * grad_project, axis=1)...]
    reduce_scatter x1, waiting for transfers between devices: 0.01 us -> 15.3 us  [body(): up_part = lax.psum_scatter(grad_up, 'yx', scatter_dimension=0, tiled=True)]
    ppermute x20, waiting for transfers between devices: 40.2 us -> 51.9 us  [across(): return lax.ppermute(x, 'yx', [(a, a ^ j) for a in range(n)])]
    ppermute x27 -> x26, starting transfers between devices: 67.8 us -> 59.9 us  [crossed(): return lax.ppermute(x, ('core', 'zh'), perm)]
    ppermute x10, waiting for transfers between devices: 42.9 us -> 35.2 us  [to_near(): return lax.ppermute(x, 'zl', [(j, (j + k) % n) for j in range(n)])]
    ppermute x7 -> x8, waiting for transfers between devices: 4.54 us -> 12.2 us  [from_near(): return lax.ppermute(x, 'zl', [((j + k) % n, j) for j in range(n)])]
    unnamed x198 -> x200, local copies, waits for them, and re-layouts: 16.5 us -> 13.9 us
  transfers between devices with their start and end apart: 84 -> 83, of which waited for: 33 -> 32; matrix products, arithmetic and copies ran while one was open for 24% -> 23% of each run, Pallas kernels for 25% -> 25%
where the time goes in v5:
time: 707 us; the launch traced here: 697 us
  Pallas kernels  176 us (25%)
  waiting for transfers between devices  154 us (22%)
  starting transfers between devices  113 us (16%)
  other arithmetic  74.5 us (11%)
  matrix products  68.7 us (10%)
  blocking collectives  48.6 us (7%)
  local copies, waits for them, and re-layouts  47 us (7%)
  between operations  15.8 us (2%)
    pallas_call x6, Pallas kernels, piece_call(): pl.pallas_call(functools.partial(kernel, count, tuple((where for _, where...  97.5 us
    ppermute x26, starting transfers between devices, crossed(): return lax.ppermute(x, ('core', 'zh'), perm)  59.9 us
    ppermute x20, waiting for transfers between devices, across(): return lax.ppermute(x, 'yx', [(a, a ^ j) for a in range(n)])  51.9 us
    dot_general x6, matrix products, rows_product(): lax.dot_general(left, right, (((0,), (0,)), ((), ())), preferred_element_...  46.7 us
    pallas_call x1, Pallas kernels, attend_back(): pl.pallas_call(functools.partial(backward_kernel, pieces, ratio, bool(ear...  45.6 us
    psum x1, blocking collectives, body(): lax.psum(jnp.stack([jnp.sum(qkv_shard.astype(f32) * grad_project, axis=1)...  39.3 us
    ppermute x26, waiting for transfers between devices, crossed(): return lax.ppermute(x, ('core', 'zh'), perm)  35.3 us
    ppermute x10, waiting for transfers between devices, to_near(): return lax.ppermute(x, 'zl', [(j, (j + k) % n) for j in range(n)])  35.2 us
  transfers between devices with their start and end apart: 83, of which 32 were waited for; matrix products, arithmetic and copies ran while one was open for 23% of the time, Pallas kernels for 25%

profile of v5, /device:TPU:16, one launch (start us, length us, event | category | flops | bytes accessed | tf_op | source)
XLA Modules:
  0.0 697.0 jit_solution(9401961735594955400)
XLA Ops:
  21.0 9.3 %all-gather = bf16[8,192,2]{1,2,0:T(2,128)(2,1)S(1)} all-gather(bf16[1,192,2]{1,2,0:T(2,128)(2,1)S(1)} %fusion.41), channel_id=1, replica_groups=mesh['yx'=4,'core'=2,'zh'=2,'zl'=2] {'yx','core'}, dimensions={0}, use_global_device_ids=true | all-gather | bytes 6912 | tf_op jit(solution)/shard_map/all_gather | solution.py:722
  31.0 7.3 %collective-permute-done.1 = s32[1,4]{1,0:T(1,128)S(1)} collective-permute-done((s32[1,4]{1,0:T(1,128)}, s32[1,4]{1,0:T(1,128)S(1)}, u32[]{:S(2)}, u32[]{:S(2)}) %collective-permute-start.1) | collective-permute-done | bytes 48 | tf_op jit(solution)/shard_map/ppermute | solution.py:580
  44.5 5.8 collective-permute-start.6
  62.0 13.1 %collective-permute-done.4 = bf16[256,1536]{1,0:T(8,128)(2,1)} collective-permute-done((bf16[256,1536]{1,0:T(8,128)(2,1)}, bf16[256,1536]{1,0:T(8,128)(2,1)}, u32[]{:S(2)}, u32[]{:S(2)}) %collective-permute-start.4) | collective-permute-done | bytes 786464 | tf_op jit(solution)/shard_map/ppermute | solution.py:580
  94.8 8.7 %project_0.1 = (bf16[2048,1536]{1,0:T(8,128)(2,1)}, bf16[2048,768]{1,0:T(8,128)(2,1)}) custom-call(s32[1]{0:T(128)} %bitcast.7.me, bf16[512,1536]{1,0:T(8,128)(2,1)} %copy-done, bf16[512,1536]{1,0:T(8,128)(2,1)} %collective-permute-done.11.refs_1_, f32[1,1536]{1,0:T(1,128)} %get-tuple-element.442.refs_2_, bf16[384,768]{1,0:T(8,128)(2,1)} %copy-done.20, ...), custom_call_target="tpu_custom_call" | custom-call | flops 1048576 | bytes 65536 | tf_op jit(solution)/shard_map/project_0/pallas_call | solution.py:522
  110.0 8.6 %project_1.1 = (bf16[2048,1536]{1,0:T(8,128)(2,1)}, bf16[2048,768]{1,0:T(8,128)(2,1)}) custom-call(s32[1]{0:T(128)} %bitcast.7.me, bf16[512,1536]{1,0:T(8,128)(2,1)} %copy-done.36, bf16[512,1536]{1,0:T(8,128)(2,1)} %collective-permute-done.14.refs_1_, f32[1,1536]{1,0:T(1,128)} %get-tuple-element.442.refs_2_, ...), custom_call_target="tpu_custom_call", output_to_operand_aliasing={{0}: (9, {}), {1}: (10, {})} | custom-call | flops 1048576 | bytes 65536 | tf_op jit(solution)/shard_map/project_1/pallas_call | solution.py:522
  124.4 7.2 %collective-permute-start.19 = (bf16[192,2048]{1,0:T(8,128)(2,1)S(1)}, bf16[192,2048]{1,0:T(8,128)(2,1)S(1)}, u32[]{:S(2)}, u32[]{:S(2)}) collective-permute-start(bf16[192,2048]{1,0:T(8,128)(2,1)S(1)} %copy-done.42), channel_id=1, source_target_pairs={{2,4},{4,2},{3,5},{5,3},{10,12},{12,10},{11,13},{13,11},{18,20},{2... | collective-permute-start | bytes 2359304 | tf_op jit(solution)/shard_map/ppermute | solution.py:580
  133.0 29.4 %attention_forward.1 = (bf16[1024,384]{1,0:T(8,128)(2,1)}, bf16[1024,384]{1,0:T(8,128)(2,1)}, f32[4,1,1024]{2,1,0:T(1,128)}, f32[4,1,1024]{2,1,0:T(1,128)}) custom-call(s32[16]{0:T(128)} %pad_add_fusion.refs_0_, s32[4]{0:T(128)} %get-tuple-element.226.refs_1_, s32[4]{0:T(128)} %get-tuple-element.227.refs_2_, f32[2048,128]{1,0:T(8,128)} %get-tuple-element.353.refs_3_, ...), custom_call_target="tpu_custom_call" | custom-call | flops 1048576 | bytes 65536 | tf_op jit(solution)/shard_map/attention_forward/pallas_call | solution.py:333
  177.4 5.7 collective-permute-done.22.refs_3_.refs_5_
  189.9 5.2 collective-permute-done.21
  205.5 21.6 %collective-permute-done.27.refs_5_.refs_7_ = bf16[192,1024]{1,0:T(8,128)(2,1)S(1)} collective-permute-done((bf16[192,1024]{1,0:T(8,128)(2,1)S(1)}, bf16[192,1024]{1,0:T(8,128)(2,1)S(1)}, u32[]{:S(2)}, u32[]{:S(2)}) %collective-permute-start.27) | collective-permute-done | bytes 393248 | tf_op jit(solution)/shard_map/ppermute | solution.py:631
  232.1 6.9 collective-permute-done.30
  248.8 14.1 %gate_0.1 = (bf16[2048,1536]{1,0:T(8,128)(2,1)}, f32[2048,2048]{1,0:T(8,128)}, bf16[2048,1024]{1,0:T(8,128)(2,1)}) custom-call(s32[1]{0:T(128)} %bitcast.7.me, bf16[512,1536]{1,0:T(8,128)(2,1)} %copy-done.11, bf16[512,1536]{1,0:T(8,128)(2,1)} %copy-done.54, bf16[384,1024]{1,0:T(8,128)(2,1)} %copy-done.4, bf16[384,1024]{1,0:T(8,128)(2,1)} %copy-done.6, ...), custom_call_target="tpu_custom_call" | custom-call | flops 1048576 | bytes 65536 | tf_op jit(solution)/shard_map/gate_0/pallas_call | solution.py:522
  276.7 5.9 collective-permute-done.38.refs_17_.refs_15_
  285.5 25.2 %gate_back_0.1 = (bf16[2048,1536]{1,0:T(8,128)(2,1)}, bf16[2048,2048]{1,0:T(8,128)(2,1)}, bf16[512,1536]{1,0:T(8,128)(2,1)}, bf16[512,1536]{1,0:T(8,128)(2,1)}, ...) custom-call(s32[1]{0:T(128)} %bitcast.7.me, bf16[512,1536]{1,0:T(8,128)(2,1)} %copy-done.5, ...), custom_call_target="tpu_custom_call" | custom-call | flops 1048576 | bytes 65536 | tf_op jit(solution)/shard_map/gate_back_0/pallas_call | solution.py:522
  316.6 19.4 %gate_1.1 = (bf16[2048,1536]{1,0:T(8,128)(2,1)}, f32[2048,2048]{1,0:T(8,128)}, bf16[2048,1024]{1,0:T(8,128)(2,1)}, bf16[512,1536]{1,0:T(8,128)(2,1)}, bf16[512,1536]{1,0:T(8,128)(2,1)}) custom-call(s32[1]{0:T(128)} %bitcast.7.me, ...), custom_call_target="tpu_custom_call", output_to_operand_aliasing={{0}: (18, {}), {1}: (19, {}), {2}: (20, {})} | custom-call | flops 1048576 | bytes 65536 | tf_op jit(solution)/shard_map/gate_1/pallas_call | solution.py:522
  344.9 21.6 %gate_back_1.1 = (bf16[2048,1536]{1,0:T(8,128)(2,1)}, bf16[2048,2048]{1,0:T(8,128)(2,1)}, bf16[512,1536]{1,0:T(8,128)(2,1)}, bf16[512,1536]{1,0:T(8,128)(2,1)}) custom-call(s32[1]{0:T(128)} %bitcast.7.me, bf16[512,1536]{1,0:T(8,128)(2,1)} %copy-done.31, bf16[512,1536]{1,0:T(8,128)(2,1)} %copy-done.53, ...), custom_call_target="tpu_custom_call", output_to_operand_aliasing={{0}: (20, {}), {1}: (21, {})} | custom-call | flops 1048576 | bytes 65536 | tf_op jit(solution)/shard_map/gate_back_1/pallas_call | solution.py:522
  374.1 10.2 %fusion.7 = bf16[1536,1024]{1,0:T(8,128)(2,1)} fusion(bf16[2048,1536]{1,0:T(8,128)(2,1)} %get-tuple-element.299, bf16[2048,2048]{1,0:T(8,128)(2,1)S(1)} %copy-done.21), kind=kOutput, calls=%fused_computation.11 | convolution fusion | flops 6444023808 | bytes 13631488 | tf_op jit(solution)/shard_map/dot_general | solution.py:63
  384.3 11.2 %fusion.4 = bf16[1536,1024]{1,0:T(8,128)(2,1)} fusion(bf16[2048,1536]{1,0:T(8,128)(2,1)} %get-tuple-element.299, bf16[2048,2048]{1,0:T(8,128)(2,1)} %get-tuple-element.320), kind=kOutput, calls=%fused_computation.10 | convolution fusion | flops 6444023808 | bytes 13631488 | tf_op jit(solution)/shard_map/dot_general | solution.py:63
  404.2 11.9 %convolution_convert_fusion = bf16[1536,1024]{1,0:T(8,128)(2,1)} fusion(bf16[2048,1536]{1,0:T(8,128)(2,1)} %get-tuple-element.327, bf16[2048,1024]{1,0:T(8,128)(2,1)} %get-tuple-element.306.refs_3_), kind=kOutput, calls=%fused_computation.9 | convolution fusion | flops 6444023808 | bytes 13631488 | tf_op jit(solution)/shard_map/dot_general | solution.py:63
  416.1 6.1 collective-permute-done.51
  429.2 5.8 fusion.42
  437.7 6.0 collective-permute-start.55
  448.6 5.7 collective-permute-done.54
  464.6 10.8 %collective-permute-done.56.refs_12_ = bf16[1024,384]{1,0:T(8,128)(2,1)} collective-permute-done((bf16[1024,384]{1,0:T(8,128)(2,1)}, bf16[1024,384]{1,0:T(8,128)(2,1)}, u32[]{:S(2)}, u32[]{:S(2)}) %collective-permute-start.56) | collective-permute-done | bytes 786464 | tf_op jit(solution)/shard_map/ppermute | solution.py:626
  475.3 15.3 %reduce-scatter.7.cloned.1.call-done = bf16[384,1024]{1,0:T(8,128)(2,1)} async-done(((bf16[1536,1024]{1,0:T(8,128)(2,1)}), bf16[384,1024]{1,0:T(8,128)(2,1)}) %reduce-scatter.7.cloned.1.call-update) | async-done | bytes 786448 | tf_op jit(solution)/shard_map/reduce_scatter | solution.py:922
  501.8 45.6 %attention_backward_0.1 = bf16[2048,768]{1,0:T(8,128)(2,1)} custom-call(s32[16]{0:T(128)} %pad_add_fusion.refs_0_, s32[8]{0:T(128)} %get-tuple-element.351.refs_1_, s32[8]{0:T(128)} %get-tuple-element.352.refs_2_, f32[2048,128]{1,0:T(8,128)} %get-tuple-element.353.refs_3_, f32[2048,128]{1,0:T(8,128)} %get-tuple-element.354.refs_4_, ...), custom_call_target="tpu_custom_call" | custom-call | flops 1048576 | bytes 65536 | tf_op jit(solution)/shard_map/attention_backward_0/pallas_call | solution.py:363
  562.7 6.5 collective-permute-done.63
  578.9 8.9 %convolution_convert_fusion.1 = bf16[1536,768]{1,0:T(8,128)(2,1)S(1)} fusion(bf16[2048,1536]{1,0:T(8,128)(2,1)} %get-tuple-element.369, bf16[2048,768]{1,0:T(8,128)(2,1)} %attention_backward_0.1), kind=kOutput, calls=%fused_computation.12 | convolution fusion | flops 4833017856 | bytes 11796480 | tf_op jit(solution)/shard_map/dot_general | solution.py:63
  608.9 5.9 collective-permute-done.71
  630.8 5.7 collective-permute-done.72
  645.3 39.3 %psum.7 = f32[2,192]{1,0:T(2,128)S(1)} all-reduce(f32[2,192]{1,0:T(2,128)S(1)} %pad_maximum_fusion.18), channel_id=1, replica_groups=mesh['yx'=4,'core'=2,'zh'=2,'zl'=2] {'zh','zl'}, use_global_device_ids=true, to_apply=%region_12.13 | all-reduce | flops 384 | bytes 3072 | tf_op jit(solution)/shard_map/psum | solution.py:1008
  (476 shorter events, 271.3 us)
Async XLA Ops:
  7.2 187.9 %all-gather.3.cloned.1.call-start = ((), (), s32[]{:S(2)}) async-start(), calls=%async_computation.4 | async-start | bytes 2949120 | tf_op jit(solution)/shard_map/all_gather | solution.py:782
  8.4 32.3 %collective-permute-start.2 = (bf16[192,768]{1,0:T(8,128)(2,1)S(1)}, bf16[192,768]{1,0:T(8,128)(2,1)S(1)}, u32[]{:S(2)}, u32[]{:S(2)}) collective-permute-start(bf16[192,768]{1,0:T(8,128)(2,1)S(1)} %pad_maximum_fusion.16), channel_id=1, source_target_pairs={{0,2},{6,4},{4,0},{2,6},{1,3},{7,5},{5,1},{3,7},{8,10},{14,12},{12... | collective-permute-start | bytes 884744 | tf_op jit(solution)/shard_map/ppermute | solution.py:580
  8.5 32.3 %collective-permute-start.3 = (bf16[192,768]{1,0:T(8,128)(2,1)S(1)}, bf16[192,768]{1,0:T(8,128)(2,1)S(1)}, u32[]{:S(2)}, u32[]{:S(2)}) collective-permute-start(bf16[192,768]{1,0:T(8,128)(2,1)S(1)} %pad_maximum_fusion.16), channel_id=1, source_target_pairs={{2,4},{4,2},{3,5},{5,3},{10,12},{12,10},{11,13},{13,11},{18,20},{2... | collective-permute-start | bytes 884744 | tf_op jit(solution)/shard_map/ppermute | solution.py:580
  12.5 25.8 %collective-permute-start = (bf16[256,1536]{1,0:T(8,128)(2,1)}, bf16[256,1536]{1,0:T(8,128)(2,1)}, u32[]{:S(2)}, u32[]{:S(2)}) collective-permute-start(bf16[256,1536]{1,0:T(8,128)(2,1)} %slice.227), channel_id=1, source_target_pairs={{2,4},{4,2},{3,5},{5,3},{10,12},{12,10},{11,13},{13,11},{18,20},{2... | collective-permute-start | bytes 2359304 | tf_op jit(solution)/shard_map/ppermute | solution.py:580
  41.1 36.1 %collective-permute-start.7 = (bf16[384,768]{1,0:T(8,128)(2,1)S(1)}, bf16[384,768]{1,0:T(8,128)(2,1)S(1)}, u32[]{:S(2)}, u32[]{:S(2)}) collective-permute-start(bf16[384,768]{1,0:T(8,128)(2,1)S(1)} %pad_maximum_fusion.12.refs_3_.refs_0_), channel_id=1, source_target_pairs={{0,8},{8,0},{16,24},{24,16},{1,9},{9,1},{17,25},{25,17},{2,10},{10... | collective-permute-start | bytes 1769480 | tf_op jit(solution)/shard_map/ppermute | solution.py:631
  42.7 34.5 %collective-permute-start.8 = (bf16[384,768]{1,0:T(8,128)(2,1)S(1)}, bf16[384,768]{1,0:T(8,128)(2,1)}, u32[]{:S(2)}, u32[]{:S(2)}) collective-permute-start(bf16[384,768]{1,0:T(8,128)(2,1)S(1)} %pad_maximum_fusion.12.refs_3_.refs_0_), channel_id=1, source_target_pairs={{0,16},{8,24},{16,0},{24,8},{1,17},{9,25},{17,1},{25,9},{2,18},{10... | collective-permute-start | bytes 1769480 | tf_op jit(solution)/shard_map/ppermute | solution.py:631
  44.5 32.7 %collective-permute-start.6 = (bf16[256,1536]{1,0:T(8,128)(2,1)}, bf16[256,1536]{1,0:T(8,128)(2,1)}, u32[]{:S(2)}, u32[]{:S(2)}) collective-permute-start(bf16[256,1536]{1,0:T(8,128)(2,1)} %get-tuple-element.202), channel_id=1, source_target_pairs={{1,0},{0,1},{3,2},{2,3},{5,4},{4,5},{7,6},{6,7},{9,8},{8,9},{11,10... | collective-permute-start | bytes 2359304 | tf_op jit(solution)/shard_map/ppermute | solution.py:621
  78.8 24.7 %collective-permute-start.10 = (bf16[256,1536]{1,0:T(8,128)(2,1)}, bf16[256,1536]{1,0:T(8,128)(2,1)}, u32[]{:S(2)}, u32[]{:S(2)}) collective-permute-start(bf16[256,1536]{1,0:T(8,128)(2,1)} %broadcast_select_fusion), channel_id=1, source_target_pairs={{1,0},{0,1},{3,2},{2,3},{5,4},{4,5},{7,6},{6,7},{9,8},{8,9},{11,10... | collective-permute-start | bytes 2359304 | tf_op jit(solution)/shard_map/ppermute | solution.py:621
  124.3 351.1 %reduce-scatter.5.cloned.1.call-start = ((), (), s32[]{:S(2)}) async-start(), calls=%async_computation.5 | async-start | bytes 3932160 | tf_op jit(solution)/shard_map/reduce_scatter | solution.py:908
  124.3 38.1 %collective-permute-start.18 = (bf16[192,2048]{1,0:T(8,128)(2,1)S(1)}, bf16[192,2048]{1,0:T(8,128)(2,1)S(1)}, u32[]{:S(2)}, u32[]{:S(2)}) collective-permute-start(bf16[192,2048]{1,0:T(8,128)(2,1)S(1)} %copy-done.42), channel_id=1, source_target_pairs={{0,2},{6,4},{4,0},{2,6},{1,3},{7,5},{5,1},{3,7},{8,10},{14,12},{12... | collective-permute-start | bytes 2359304 | tf_op jit(solution)/shard_map/ppermute | solution.py:580
  124.4 38.1 %collective-permute-start.19 = (bf16[192,2048]{1,0:T(8,128)(2,1)S(1)}, bf16[192,2048]{1,0:T(8,128)(2,1)S(1)}, u32[]{:S(2)}, u32[]{:S(2)}) collective-permute-start(bf16[192,2048]{1,0:T(8,128)(2,1)S(1)} %copy-done.42), channel_id=1, source_target_pairs={{2,4},{4,2},{3,5},{5,3},{10,12},{12,10},{11,13},{13,11},{18,20},{2... | collective-permute-start | bytes 2359304 | tf_op jit(solution)/shard_map/ppermute | solution.py:580
  170.7 24.3 %collective-permute-start.21 = (bf16[1024,384]{1,0:T(8,128)(2,1)}, bf16[1024,384]{1,0:T(8,128)(2,1)}, u32[]{:S(2)}, u32[]{:S(2)}) collective-permute-start(bf16[1024,384]{1,0:T(8,128)(2,1)} %get-tuple-element.240.refs_14_), channel_id=1, source_target_pairs={{0,1},{1,0},{2,3},{3,2},{4,5},{5,4},{6,7},{7,6},{8,9},{9,8},{10,11... | collective-permute-start | bytes 2359304 | tf_op jit(solution)/shard_map/ppermute | solution.py:626
  198.5 28.9 %collective-permute-start.25 = (bf16[384,1024]{1,0:T(8,128)(2,1)}, bf16[384,1024]{1,0:T(8,128)(2,1)S(1)}, u32[]{:S(2)}, u32[]{:S(2)}) collective-permute-start(bf16[384,1024]{1,0:T(8,128)(2,1)} %pad_maximum_fusion.7.refs_7_.refs_9_), channel_id=1, source_target_pairs={{0,8},{8,0},{16,24},{24,16},{1,9},{9,1},{17,25},{25,17},{2,10},{10... | collective-permute-start | bytes 2359304 | tf_op jit(solution)/shard_map/ppermute | solution.py:631
  199.1 28.3 %collective-permute-start.26 = (bf16[384,1024]{1,0:T(8,128)(2,1)}, bf16[384,1024]{1,0:T(8,128)(2,1)S(1)}, u32[]{:S(2)}, u32[]{:S(2)}) collective-permute-start(bf16[384,1024]{1,0:T(8,128)(2,1)} %pad_maximum_fusion.7.refs_7_.refs_9_), channel_id=1, source_target_pairs={{0,16},{8,24},{16,0},{24,8},{1,17},{9,25},{17,1},{25,9},{2,18},{10... | collective-permute-start | bytes 2359304 | tf_op jit(solution)/shard_map/ppermute | solution.py:631
  200.6 26.5 %collective-permute-start.27 = (bf16[192,1024]{1,0:T(8,128)(2,1)S(1)}, bf16[192,1024]{1,0:T(8,128)(2,1)S(1)}, u32[]{:S(2)}, u32[]{:S(2)}) collective-permute-start(bf16[192,1024]{1,0:T(8,128)(2,1)S(1)} %slice.246), channel_id=1, source_target_pairs={{0,8},{8,0},{16,24},{24,16},{1,9},{9,1},{17,25},{25,17},{2,10},{10... | collective-permute-start | bytes 1179656 | tf_op jit(solution)/shard_map/ppermute | solution.py:631
  202.2 25.1 %collective-permute-start.28 = (bf16[192,1024]{1,0:T(8,128)(2,1)S(1)}, bf16[192,1024]{1,0:T(8,128)(2,1)S(1)}, u32[]{:S(2)}, u32[]{:S(2)}) collective-permute-start(bf16[192,1024]{1,0:T(8,128)(2,1)S(1)} %slice.247), channel_id=1, source_target_pairs={{0,16},{8,24},{16,0},{24,8},{1,17},{9,25},{17,1},{25,9},{2,18},{10... | collective-permute-start | bytes 1179656 | tf_op jit(solution)/shard_map/ppermute | solution.py:631
  267.3 43.4 %collective-permute-start.40 = (bf16[256,1536]{1,0:T(8,128)(2,1)}, bf16[256,1536]{1,0:T(8,128)(2,1)}, u32[]{:S(2)}, u32[]{:S(2)}) collective-permute-start(bf16[256,1536]{1,0:T(8,128)(2,1)} %slice_select_fusion), channel_id=1, source_target_pairs={{1,0},{0,1},{3,2},{2,3},{5,4},{4,5},{7,6},{6,7},{9,8},{8,9},{11,10... | collective-permute-start | bytes 2359304 | tf_op jit(solution)/shard_map/ppermute | solution.py:621
  270.3 40.4 %collective-permute-start.41 = (bf16[256,1536]{1,0:T(8,128)(2,1)}, bf16[256,1536]{1,0:T(8,128)(2,1)}, u32[]{:S(2)}, u32[]{:S(2)}) collective-permute-start(bf16[256,1536]{1,0:T(8,128)(2,1)} %slice.256), channel_id=1, source_target_pairs={{1,0},{0,1},{3,2},{2,3},{5,4},{4,5},{7,6},{6,7},{9,8},{8,9},{11,10... | collective-permute-start | bytes 2359304 | tf_op jit(solution)/shard_map/ppermute | solution.py:621
  371.7 23.9 %collective-permute-start.48 = (bf16[512,1536]{1,0:T(8,128)(2,1)}, bf16[512,1536]{1,0:T(8,128)(2,1)}, u32[]{:S(2)}, u32[]{:S(2)}) collective-permute-start(bf16[512,1536]{1,0:T(8,128)(2,1)} %get-tuple-element.323), channel_id=1, source_target_pairs={{0,4},{4,0},{1,5},{5,1},{2,6},{6,2},{3,7},{7,3},{8,12},{12,8},{9,1... | collective-permute-start | bytes 4718600 | tf_op jit(solution)/shard_map/ppermute | solution.py:571
  373.8 25.8 %collective-permute-start.50 = (bf16[256,1536]{1,0:T(8,128)(2,1)}, bf16[256,1536]{1,0:T(8,128)(2,1)}, u32[]{:S(2)}, u32[]{:S(2)}) collective-permute-start(bf16[256,1536]{1,0:T(8,128)(2,1)} %slice.261), channel_id=1, source_target_pairs={{0,1},{1,0},{2,3},{3,2},{4,5},{5,4},{6,7},{7,6},{8,9},{9,8},{10,11... | collective-permute-start | bytes 2359304 | tf_op jit(solution)/shard_map/ppermute | solution.py:626
  399.6 91.1 %reduce-scatter.7.cloned.1.call-start = ((), (), s32[]{:S(2)}) async-start(), calls=%async_computation.6 | async-start | bytes 3932160 | tf_op jit(solution)/shard_map/reduce_scatter | solution.py:922
  400.4 147.1 %reduce-scatter.9.cloned.1.call-start = ((), (), s32[]{:S(2)}) async-start(), calls=%async_computation.7 | async-start | bytes 3932160 | tf_op jit(solution)/shard_map/reduce_scatter | solution.py:959
  429.2 186.9 %reduce-scatter.11.cloned.1.call-start = ((), (), s32[]{:S(2)}) async-start(), calls=%async_computation.8 | async-start | bytes 2949120 | tf_op jit(solution)/shard_map/reduce_scatter | solution.py:960
  437.7 26.9 %collective-permute-start.55 = (bf16[256,1536]{1,0:T(8,128)(2,1)}, bf16[256,1536]{1,0:T(8,128)(2,1)}, u32[]{:S(2)}, u32[]{:S(2)}) collective-permute-start(bf16[256,1536]{1,0:T(8,128)(2,1)} %fusion.21), channel_id=1, source_target_pairs={{2,4},{4,2},{3,5},{5,3},{10,12},{12,10},{11,13},{13,11},{18,20},{2... | collective-permute-start | bytes 2359304 | tf_op jit(solution)/shard_map/ppermute | solution.py:580
  490.7 56.7 %collective-permute-start.57 = (bf16[256,1536]{1,0:T(8,128)(2,1)}, bf16[256,1536]{1,0:T(8,128)(2,1)}, u32[]{:S(2)}, u32[]{:S(2)}) collective-permute-start(bf16[256,1536]{1,0:T(8,128)(2,1)} %fusion.19), channel_id=1, source_target_pairs={{2,4},{4,2},{3,5},{5,3},{10,12},{12,10},{11,13},{13,11},{18,20},{2... | collective-permute-start | bytes 2359304 | tf_op jit(solution)/shard_map/ppermute | solution.py:580
  493.8 53.6 %collective-permute-start.58 = (bf16[192,1024]{1,0:T(8,128)(2,1)S(1)}, bf16[192,1024]{1,0:T(8,128)(2,1)}, u32[]{:S(2)}, u32[]{:S(2)}) collective-permute-start(bf16[192,1024]{1,0:T(8,128)(2,1)S(1)} %get-tuple-element.429), channel_id=1, source_target_pairs={{2,0},{4,6},{0,4},{6,2},{3,1},{5,7},{1,5},{7,3},{10,8},{12,14},{8,... | collective-permute-start | bytes 1179656 | tf_op jit(solution)/shard_map/ppermute | solution.py:580
  494.0 53.4 %collective-permute-start.59 = (bf16[192,1024]{1,0:T(8,128)(2,1)S(1)}, bf16[192,1024]{1,0:T(8,128)(2,1)}, u32[]{:S(2)}, u32[]{:S(2)}) collective-permute-start(bf16[192,1024]{1,0:T(8,128)(2,1)S(1)} %get-tuple-element.428), channel_id=1, source_target_pairs={{2,4},{4,2},{3,5},{5,3},{10,12},{12,10},{11,13},{13,11},{18,20},{2... | collective-permute-start | bytes 1179656 | tf_op jit(solution)/shard_map/ppermute | solution.py:580
  499.6 47.8 %collective-permute-start.60 = (bf16[192,1024]{1,0:T(8,128)(2,1)S(1)}, bf16[192,1024]{1,0:T(8,128)(2,1)}, u32[]{:S(2)}, u32[]{:S(2)}) collective-permute-start(bf16[192,1024]{1,0:T(8,128)(2,1)S(1)} %get-tuple-element.427), channel_id=1, source_target_pairs={{2,0},{4,6},{0,4},{6,2},{3,1},{5,7},{1,5},{7,3},{10,8},{12,14},{8,... | collective-permute-start | bytes 1179656 | tf_op jit(solution)/shard_map/ppermute | solution.py:580
  499.7 47.7 %collective-permute-start.61 = (bf16[192,1024]{1,0:T(8,128)(2,1)S(1)}, bf16[192,1024]{1,0:T(8,128)(2,1)}, u32[]{:S(2)}, u32[]{:S(2)}) collective-permute-start(bf16[192,1024]{1,0:T(8,128)(2,1)S(1)} %get-tuple-element.426), channel_id=1, source_target_pairs={{2,4},{4,2},{3,5},{5,3},{10,12},{12,10},{11,13},{13,11},{18,20},{2... | collective-permute-start | bytes 1179656 | tf_op jit(solution)/shard_map/ppermute | solution.py:580
  636.7 50.1 %collective-permute-start.75 = (bf16[512,1536]{1,0:T(8,128)(2,1)S(1)}, bf16[512,1536]{1,0:T(8,128)(2,1)}, u32[]{:S(2)}, u32[]{:S(2)}) collective-permute-start(bf16[512,1536]{1,0:T(8,128)(2,1)S(1)} %fusion.15), channel_id=1, source_target_pairs={{2,4},{4,2},{3,5},{5,3},{10,12},{12,10},{11,13},{13,11},{18,20},{2... | collective-permute-start | bytes 4718600 | tf_op jit(solution)/shard_map/ppermute | solution.py:580
  641.3 44.6 %collective-permute-start.76 = (bf16[192,384]{1,0:T(8,128)(2,1)S(1)}, bf16[192,384]{1,0:T(8,128)(2,1)S(1)}, u32[]{:S(2)}, u32[]{:S(2)}) collective-permute-start(bf16[192,384]{1,0:T(8,128)(2,1)S(1)} %get-tuple-element.389), channel_id=1, source_target_pairs={{2,0},{4,6},{0,4},{6,2},{3,1},{5,7},{1,5},{7,3},{10,8},{12,14},{8,... | collective-permute-start | bytes 442376 | tf_op jit(solution)/shard_map/ppermute | solution.py:580
  641.3 44.6 %collective-permute-start.77 = (bf16[192,384]{1,0:T(8,128)(2,1)S(1)}, bf16[192,384]{1,0:T(8,128)(2,1)S(1)}, u32[]{:S(2)}, u32[]{:S(2)}) collective-permute-start(bf16[192,384]{1,0:T(8,128)(2,1)S(1)} %get-tuple-element.390), channel_id=1, source_target_pairs={{2,4},{4,2},{3,5},{5,3},{10,12},{12,10},{11,13},{13,11},{18,20},{2... | collective-permute-start | bytes 442376 | tf_op jit(solution)/shard_map/ppermute | solution.py:580
  (148 other events, 1880.5 us)
Sparse Core Ops, SparseCore 0:
  124.4 39.2 all-gather.2
  399.7 43.9 reduce-scatter.4
  446.7 43.9 reduce-scatter.6
  493.5 43.9 reduce-scatter.8
  551.3 38.1 reduce-scatter.10

commit v6 on v5

--- a/solution.py
+++ b/solution.py
@@ -769,25 +769,25 @@
 
     out_pair = pair_of(out_weight, out_out, out_cross)
     out_far = [from_near(out_pair, k) for k in others]
-    down_moved = send_z(down_shard)
+    down_out = crossed(down_shard, OUT)
     for k in others:
         far = jnp.concatenate([upper_far[k - 1], lower_far[k - 1]], axis=0)
         parts = [far, flip(far, "core")]
         normed = piece_call(project_kernel, "project", k, near, me, parts, [gain_row], [], projecting, normed, outs)
     norm_one, qkv = normed
-    gate_up_shard, qkv, out_pair, *moved = stage(gate_up_shard, qkv, out_pair, *out_far, *down_moved)
-    out_far, down_moved = moved[: near - 1], moved[near - 1 :]
+    gate_up_shard, qkv, out_pair, down_out, *out_far = stage(gate_up_shard, qkv, out_pair, down_out, *out_far)
 
     gate_up_moved = send_z(gate_up_shard)
     w_out = lax.all_gather(jnp.concatenate([out_pair, *out_far], axis=1), "yx", axis=0, tiled=True)
     context, sums = attend(qkv, near, layout, q_heads, kv_heads)
-    cotangent, *moved = stage(cotangent, *context, *gate_up_moved)
+    cotangent, down_shard, *moved = stage(cotangent, down_shard, *context, *gate_up_moved)
     context, gate_up_moved = moved[:near], moved[near:]
 
     quarters = [context[0]] + [None] * (near - 1)
     for k in others:
         quarters[near - k] = to_near(context[k], k)
     cot_upper = crossed(cotangent[:part_rows], CROSS)
+    down_cross = crossed(down_shard, CROSS)
     pairs = [
         pair_of(*(x[:, n * hidden_cols : (n + 1) * hidden_cols] for x in (gate_up_shard, *gate_up_moved)))
         for n in range(2)
@@ -796,8 +796,8 @@
     w_project = assemble("assemble_project", me, *blocks, tokens.shape[1], qkv_cols)
     residual = own.astype(f32)
     scale_one = lax.rsqrt(jnp.mean(residual * residual, axis=-1, keepdims=True) + EPSILON)
-    up_pair, cotangent, cot_upper, w_out, scale_one, w_project, *moved = stage(
-        pairs[1], cotangent, cot_upper, w_out, scale_one, w_project, *quarters, *gate_taken
+    up_pair, cotangent, cot_upper, down_cross, w_out, scale_one, w_project, *moved = stage(
+        pairs[1], cotangent, cot_upper, down_cross, w_out, scale_one, w_project, *quarters, *gate_taken
     )
     quarters, gate_taken = moved[:near], moved[near:]
 
@@ -814,7 +814,7 @@
     far_quarters = [[from_near(norm_two[:quarter], k) for k in others]]
     norm_sib = flip(norm_two, "core")
     up_halves = diagonal(up_taken)
-    down_pair = pair_of(down_weight, *down_moved)
+    down_pair = pair_of(down_weight, down_out, down_cross)
     norm_two, norm_sib, down_pair, cotangent, *moved = stage(
         norm_two, norm_sib, down_pair, cotangent, *far_quarters[0], *up_halves
     )
@@ -894,92 +894,75 @@
     )
 
     moved_upper = [to_near(d_norm_sent[k - 1][:part_rows], k) for k in others]
-    grad_gate, grad_up = (
-        rows_product(norm_two_all, d_gate_up_all[:, n * hidden_cols : (n + 1) * hidden_cols]).astype(bf16)
-        for n in range(2)
-    )
-    d_norm_two, output_near = joined(near_own, near_sib), joined(*near_back[2:])
-    grad_gate, grad_up, grad_all, d_norm_two, output_near, *moved = stage(
-        grad_gate, grad_up, grad_all, d_norm_two, output_near, *moved_upper, *d_norm_sent
+    grad_gate_up = rows_product(norm_two_all, d_gate_up_all).astype(bf16)
+    grad_gate_up, grad_all, near_own, near_sib, *moved = stage(
+        grad_gate_up, grad_all, near_own, near_sib, *moved_upper, *d_norm_sent
     )
     moved_upper, d_norm_sent = moved[: near - 1], moved[near - 1 :]
 
     moved_lower = [to_near(d_norm_sent[k - 1][part_rows:], k) for k in others]
-    gate_part = lax.psum_scatter(grad_gate, "yx", scatter_dimension=0, tiled=True)
+    gate_up_part = lax.psum_scatter(grad_gate_up, "yx", scatter_dimension=0, tiled=True)
+    d_norm_two = joined(near_own, near_sib)
     grad_down = rows_product(grad_all, hidden_all).astype(bf16)
-
-    def output_part(at, moved):
-        part = mid[at] + output_near[at]
-        for x in moved:
-            part = part + x.astype(f32)
-        return part.astype(bf16)
-
-    grad_down, d_norm_two, output_near, *moved = stage(grad_down, d_norm_two, output_near, *out_sums, *moved_lower)
+    grad_down, d_norm_two, *moved = stage(grad_down, d_norm_two, *out_sums, *moved_lower)
     out_sums, moved_lower = moved[: near - 1], moved[near - 1 :]
-    output_upper = output_part(slice(0, part_rows), out_upper)
-
-    out_lower = [[to_near(out_sums[k - 1][part_rows : part_rows + quarter], k) for k in others]]
-    up_part = lax.psum_scatter(grad_up, "yx", scatter_dimension=0, tiled=True)
+
+    out_lower = [to_near(out_sums[k - 1][part_rows:], k) for k in others]
+    down_part = lax.psum_scatter(grad_down, "yx", scatter_dimension=0, tiled=True)
     for one, two in zip(moved_upper, moved_lower, strict=True):
         d_norm_two = d_norm_two + jnp.concatenate([one, two], axis=0).astype(f32)
     mid_back, _ = norm_back(mid, scale_two, gain_two, d_norm_two)
     d_mid = cot.astype(f32) + mid_back
     d_attn = d_mid.astype(bf16)
-    d_attn, output_upper, *moved = stage(d_attn, output_upper, *out_lower[0], *out_sums)
-    out_lower[0], out_sums = moved[: near - 1], moved[near - 1 :]
-
-    out_lower.append([to_near(out_sums[k - 1][part_rows + quarter :], k) for k in others])
     d_attn_sib = flip(d_attn, "core")
     both = [dot32(x, w_out).astype(bf16) for x in (d_attn, d_attn_sib)]
     d_quarters = [
         jnp.concatenate([x[:, k * query_cols : (k + 1) * query_cols] for x in both], axis=0) for k in range(near)
     ]
-    d_attn, d_attn_sib, *moved = stage(d_attn, d_attn_sib, *d_quarters, *out_lower[1])
-    d_quarters, out_lower[1] = moved[:near], moved[near:]
+    d_attn, d_attn_sib, *moved = stage(d_attn, d_attn_sib, *d_quarters, *out_lower)
+    d_quarters, out_lower = moved[:near], moved[near:]
 
     d_context = [d_quarters[0]] + [None] * (near - 1)
     for k in others:
         d_context[near - k] = to_near(d_quarters[k], k)
-    upper_crossed = crossed(output_upper, CROSS)
     grad_out = rows_product(d_attn, context_all[:rows]) + rows_product(d_attn_sib, context_all[rows:])
     grad_out = grad_out.astype(bf16)
-    output_lower = output_part(
-        slice(part_rows, rows), [jnp.concatenate(x, axis=0) for x in zip(*out_lower, strict=True)]
-    )
-    grad_out, output_lower, gate_part, up_part, upper_crossed, *d_context = stage(
-        grad_out, output_lower, gate_part, up_part, upper_crossed, *d_context
-    )
-
-    lower_crossed = crossed(output_lower, CROSS)
-    output = jnp.concatenate([output_upper, output_lower], axis=0)
-    gate_keep, gate_give = give_z(gate_part)
-    gate_home = [crossed(gate_give, BACK), crossed(gate_keep, CROSS)]
-    up_keep, up_give = give_z(up_part)
-    up_home = [crossed(up_give, BACK), crossed(up_keep, CROSS)]
-    down_part = lax.psum_scatter(grad_down, "yx", scatter_dimension=0, tiled=True)
+    output_own = mid + joined(*near_back[2:])
+    for one, two in zip(out_upper, out_lower, strict=True):
+        output_own = output_own + jnp.concatenate([one, two], axis=0).astype(f32)
+    output_own = output_own.astype(bf16)
+    grad_out, output_own, gate_up_part, *d_context = stage(grad_out, output_own, gate_up_part, *d_context)
+
+    output_crossed = crossed(output_own, CROSS)
+    gate_up_keep, gate_up_give = give_z(gate_up_part)
+    gate_up_back = crossed(gate_up_give, BACK)
     out_part = lax.psum_scatter(grad_out, "yx", scatter_dimension=0, tiled=True)
     d_qkv = attend_back(list(range(kv_heads)), qkv, d_context, context, sums, [], layout_back, q_heads, kv_heads)
-    d_qkv, lower_crossed, down_part, *moved = stage(d_qkv, lower_crossed, down_part, *gate_home, *up_home)
-    gate_home, up_home = moved[:2], moved[2:]
-    output = jnp.where(straight(), output, jnp.concatenate([upper_crossed, lower_crossed], axis=0))
+    d_qkv, output_crossed, gate_up_back, gate_up_keep, down_part = stage(
+        d_qkv, output_crossed, gate_up_back, gate_up_keep, down_part
+    )
 
     def back_part(k):
         own, sib = (d_qkv[(2 * k + e) * rows : (2 * k + e + 1) * rows] for e in range(2))
         taken = flip(times_transpose(sib, w_project).astype(bf16), "core")
         return times_transpose(own, w_project) + taken.astype(f32)
 
+    gate_up_cross = crossed(gate_up_keep, CROSS)
+    d_sent = [back_part(k).astype(bf16) for k in others]
+    d_qkv, gate_up_cross, down_part, *d_sent = stage(d_qkv, gate_up_cross, down_part, *d_sent)
+
+    output = jnp.where(straight(), output_own, output_crossed)
+
+    d_upper = [to_near(d_sent[k - 1][:part_rows], k) for k in others]
     down_keep, down_give = give_z(down_part)
     down_home = [crossed(down_give, BACK), crossed(down_keep, CROSS)]
-    d_sent = [back_part(k).astype(bf16) for k in others]
-    d_qkv, *moved = stage(d_qkv, *d_sent, *down_home)
-    d_sent, down_home = moved[: near - 1], moved[near - 1 :]
-
-    d_upper = [to_near(d_sent[k - 1][:part_rows], k) for k in others]
     grad_project = rows_product(norm_one, d_qkv).astype(bf16)
     project_sent = send_yx(grad_project, (0, qkv_cols))
     total = back_part(0)
-    total, grad_project, *moved = stage(total, grad_project, *d_upper, *d_sent, *project_sent)
-    d_upper, d_sent, project_sent = moved[: near - 1], moved[near - 1 : 2 * near - 2], moved[2 * near - 2 :]
+    total, grad_project, *moved = stage(total, grad_project, *d_upper, *d_sent, *project_sent, *down_home)
+    d_upper, d_sent, project_sent, down_home = (
+        moved[: near - 1], moved[near - 1 : 2 * near - 2], moved[2 * near - 2 : -2], moved[-2:],
+    )
 
     d_lower = [to_near(d_sent[k - 1][part_rows:], k) for k in others]
     project_rest, project_own = join_yx(grad_project, (0, qkv_cols), project_sent)
@@ -1004,12 +987,12 @@
     grad_project = sum_z(project_keep, *project_home)
     grad_out = sum_z(out_keep, *out_home)
     grad_down = sum_z(down_keep, *down_home)
-    grad_gate, grad_up = sum_z(gate_keep, *gate_home), sum_z(up_keep, *up_home)
+    grad_gate_up = sum_z(gate_up_keep, gate_up_back, gate_up_cross)
     gain_grads = lax.psum(
         jnp.stack(
             [
                 jnp.sum(qkv_shard.astype(f32) * grad_project, axis=1),
-                jnp.sum(gate_weight.astype(f32) * grad_gate + up_weight.astype(f32) * grad_up, axis=1),
+                jnp.sum(gate_up_shard.astype(f32) * grad_gate_up, axis=1),
             ]
         ),
         ("zh", "zl"),
@@ -1023,8 +1006,8 @@
         grad_project[:, query_cols + key_cols :],
         grad_out,
         gain_grads[1],
-        grad_gate,
-        grad_up,
+        grad_gate_up[:, :hidden_cols],
+        grad_gate_up[:, hidden_cols:],
         grad_down,
     )
 

time: 707 us -> 691 us (0.977)
  starting transfers between devices: 113 us -> 102 us
  matrix products: 68.7 us -> 59.2 us
    ppermute x26 -> x23, waiting for transfers between devices: 35.3 us -> 65 us  [crossed(): return lax.ppermute(x, ('core', 'zh'), perm)]
    reduce_scatter x2 -> x1, waiting for transfers between devices: 15.3 us -> 0.01 us  [body(): lax.psum_scatter(grad_gate_up, 'yx', scatter_dimension=0, tiled=True)]
    ppermute x26 -> x23, starting transfers between devices: 59.9 us -> 50.7 us  [crossed(): return lax.ppermute(x, ('core', 'zh'), perm)]
    dot_general x6 -> x5, matrix products: 46.7 us -> 40.2 us  [rows_product(): lax.dot_general(left, right, (((0,), (0,)), ((), ())), preferred_element_...]
    ppermute x10 -> x9, waiting for transfers between devices: 35.2 us -> 30.5 us  [to_near(): return lax.ppermute(x, 'zl', [(j, (j + k) % n) for j in range(n)])]
    unnamed x200 -> x190, local copies, waits for them, and re-layouts: 13.9 us -> 15.9 us
  transfers between devices with their start and end apart: 83 -> 78, of which waited for: 32 -> 29; matrix products, arithmetic and copies ran while one was open for 23% -> 20% of each run, Pallas kernels for 25% -> 26%
where the time goes in v6:
time: 691 us; the launch traced here: 679 us
  Pallas kernels  175 us (25%)
  waiting for transfers between devices  161 us (23%)
  starting transfers between devices  102 us (15%)
  other arithmetic  69.4 us (10%)
  matrix products  59.2 us (9%)
  blocking collectives  48.9 us (7%)
  local copies, waits for them, and re-layouts  47.8 us (7%)
  between operations  15.7 us (2%)
    pallas_call x6, Pallas kernels, piece_call(): pl.pallas_call(functools.partial(kernel, count, tuple((where for _, where...  97.3 us
    ppermute x23, waiting for transfers between devices, crossed(): return lax.ppermute(x, ('core', 'zh'), perm)  65 us
    ppermute x23, starting transfers between devices, crossed(): return lax.ppermute(x, ('core', 'zh'), perm)  50.7 us
    ppermute x20, waiting for transfers between devices, across(): return lax.ppermute(x, 'yx', [(a, a ^ j) for a in range(n)])  46.1 us
    pallas_call x1, Pallas kernels, attend_back(): pl.pallas_call(functools.partial(backward_kernel, pieces, ratio, bool(ear...  45.6 us
    dot_general x5, matrix products, rows_product(): lax.dot_general(left, right, (((0,), (0,)), ((), ())), preferred_element_...  40.2 us
    psum x1, blocking collectives, body(): lax.psum(jnp.stack([jnp.sum(qkv_shard.astype(f32) * grad_project, axis=1)...  39.6 us
    ppermute x9, waiting for transfers between devices, to_near(): return lax.ppermute(x, 'zl', [(j, (j + k) % n) for j in range(n)])  30.5 us
  transfers between devices with their start and end apart: 78, of which 29 were waited for; matrix products, arithmetic and copies ran while one was open for 20% of the time, Pallas kernels for 26%

profile of v6, /device:TPU:16, one launch (start us, length us, event | category | flops | bytes accessed | tf_op | source)
XLA Modules:
  0.0 679.2 jit_solution(12995545809419322450)
XLA Ops:
  11.7 4.7 collective-permute-start
  20.2 9.3 %all-gather = bf16[8,192,2]{1,2,0:T(2,128)(2,1)S(1)} all-gather(bf16[1,192,2]{1,2,0:T(2,128)(2,1)S(1)} %fusion.27), channel_id=1, replica_groups=mesh['yx'=4,'core'=2,'zh'=2,'zl'=2] {'yx','core'}, dimensions={0}, use_global_device_ids=true | all-gather | bytes 6912 | tf_op jit(solution)/shard_map/all_gather | solution.py:722
  30.8 7.5 %collective-permute-done.1 = s32[1,4]{1,0:T(1,128)S(1)} collective-permute-done((s32[1,4]{1,0:T(1,128)}, s32[1,4]{1,0:T(1,128)S(1)}, u32[]{:S(2)}, u32[]{:S(2)}) %collective-permute-start.1) | collective-permute-done | bytes 48 | tf_op jit(solution)/shard_map/ppermute | solution.py:580
  46.2 5.9 collective-permute-start.6
  63.6 13.2 %collective-permute-done.4 = bf16[256,1536]{1,0:T(8,128)(2,1)} collective-permute-done((bf16[256,1536]{1,0:T(8,128)(2,1)}, bf16[256,1536]{1,0:T(8,128)(2,1)}, u32[]{:S(2)}, u32[]{:S(2)}) %collective-permute-start.4) | collective-permute-done | bytes 786464 | tf_op jit(solution)/shard_map/ppermute | solution.py:580
  95.0 8.7 %project_0.1 = (bf16[2048,1536]{1,0:T(8,128)(2,1)}, bf16[2048,768]{1,0:T(8,128)(2,1)}) custom-call(s32[1]{0:T(128)} %bitcast.7.me, bf16[512,1536]{1,0:T(8,128)(2,1)} %copy-done, bf16[512,1536]{1,0:T(8,128)(2,1)} %collective-permute-done.11.refs_1_, f32[1,1536]{1,0:T(1,128)} %get-tuple-element.427.refs_2_, bf16[384,768]{1,0:T(8,128)(2,1)} %copy-done.18, ...), custom_call_target="tpu_custom_call" | custom-call | flops 1048576 | bytes 65536 | tf_op jit(solution)/shard_map/project_0/pallas_call | solution.py:522
  111.2 8.5 %project_1.1 = (bf16[2048,1536]{1,0:T(8,128)(2,1)}, bf16[2048,768]{1,0:T(8,128)(2,1)}) custom-call(s32[1]{0:T(128)} %bitcast.7.me, bf16[512,1536]{1,0:T(8,128)(2,1)} %constant_dynamic-update-slice_fusion.2.refs_0_, bf16[512,1536]{1,0:T(8,128)(2,1)} %copy-done.53, ...), custom_call_target="tpu_custom_call", output_to_operand_aliasing={{0}: (9, {}), {1}: (10, {})} | custom-call | flops 1048576 | bytes 65536 | tf_op jit(solution)/shard_map/project_1/pallas_call | solution.py:522
  126.7 29.5 %attention_forward.1 = (bf16[1024,384]{1,0:T(8,128)(2,1)}, bf16[1024,384]{1,0:T(8,128)(2,1)}, f32[4,1,1024]{2,1,0:T(1,128)}, f32[4,1,1024]{2,1,0:T(1,128)}) custom-call(s32[16]{0:T(128)} %pad_add_fusion.refs_0_, s32[4]{0:T(128)} %get-tuple-element.219.refs_1_, s32[4]{0:T(128)} %get-tuple-element.220.refs_2_, f32[2048,128]{1,0:T(8,128)} %get-tuple-element.340.refs_3_, ...), custom_call_target="tpu_custom_call" | custom-call | flops 1048576 | bytes 65536 | tf_op jit(solution)/shard_map/attention_forward/pallas_call | solution.py:333
  175.8 20.9 %collective-permute-done.20 = bf16[192,1024]{1,0:T(8,128)(2,1)} collective-permute-done((bf16[192,1024]{1,0:T(8,128)(2,1)}, bf16[192,1024]{1,0:T(8,128)(2,1)}, u32[]{:S(2)}, u32[]{:S(2)}) %collective-permute-start.20) | collective-permute-done | bytes 393248 | tf_op jit(solution)/shard_map/ppermute | solution.py:580
  207.7 21.6 %collective-permute-done.27.refs_5_.refs_7_ = bf16[192,1024]{1,0:T(8,128)(2,1)S(1)} collective-permute-done((bf16[192,1024]{1,0:T(8,128)(2,1)S(1)}, bf16[192,1024]{1,0:T(8,128)(2,1)S(1)}, u32[]{:S(2)}, u32[]{:S(2)}) %collective-permute-start.27) | collective-permute-done | bytes 393248 | tf_op jit(solution)/shard_map/ppermute | solution.py:631
  234.3 7.0 %collective-permute-done.30 = bf16[128,1536]{1,0:T(8,128)(2,1)S(1)} collective-permute-done((bf16[128,1536]{1,0:T(8,128)(2,1)S(1)}, bf16[128,1536]{1,0:T(8,128)(2,1)S(1)}, u32[]{:S(2)}, u32[]{:S(2)}) %collective-permute-start.30) | collective-permute-done | bytes 393248 | tf_op jit(solution)/shard_map/ppermute | solution.py:621
  249.4 14.0 %gate_0.1 = (bf16[2048,1536]{1,0:T(8,128)(2,1)}, f32[2048,2048]{1,0:T(8,128)}, bf16[2048,1024]{1,0:T(8,128)(2,1)}) custom-call(s32[1]{0:T(128)} %bitcast.7.me, bf16[512,1536]{1,0:T(8,128)(2,1)} %copy-done.11, bf16[512,1536]{1,0:T(8,128)(2,1)} %copy-done.51, bf16[384,1024]{1,0:T(8,128)(2,1)} %copy-done.5, bf16[384,1024]{1,0:T(8,128)(2,1)} %copy-done.7, ...), custom_call_target="tpu_custom_call" | custom-call | flops 1048576 | bytes 65536 | tf_op jit(solution)/shard_map/gate_0/pallas_call | solution.py:522
  277.8 6.7 collective-permute-done.38.refs_17_.refs_15_
  286.6 25.2 %gate_back_0.1 = (bf16[2048,1536]{1,0:T(8,128)(2,1)}, bf16[2048,2048]{1,0:T(8,128)(2,1)}, bf16[512,1536]{1,0:T(8,128)(2,1)}, bf16[512,1536]{1,0:T(8,128)(2,1)}, ...) custom-call(s32[1]{0:T(128)} %bitcast.7.me, bf16[512,1536]{1,0:T(8,128)(2,1)} %copy-done.6, ...), custom_call_target="tpu_custom_call" | custom-call | flops 1048576 | bytes 65536 | tf_op jit(solution)/shard_map/gate_back_0/pallas_call | solution.py:522
  317.7 19.3 %gate_1.1 = (bf16[2048,1536]{1,0:T(8,128)(2,1)}, f32[2048,2048]{1,0:T(8,128)}, bf16[2048,1024]{1,0:T(8,128)(2,1)}, bf16[512,1536]{1,0:T(8,128)(2,1)}, bf16[512,1536]{1,0:T(8,128)(2,1)}) custom-call(s32[1]{0:T(128)} %bitcast.7.me, ...), custom_call_target="tpu_custom_call", output_to_operand_aliasing={{0}: (18, {}), {1}: (19, {}), {2}: (20, {})} | custom-call | flops 1048576 | bytes 65536 | tf_op jit(solution)/shard_map/gate_1/pallas_call | solution.py:522
  346.4 21.5 %gate_back_1.1 = (bf16[2048,1536]{1,0:T(8,128)(2,1)}, bf16[2048,2048]{1,0:T(8,128)(2,1)}, bf16[512,1536]{1,0:T(8,128)(2,1)}, bf16[512,1536]{1,0:T(8,128)(2,1)}) custom-call(s32[1]{0:T(128)} %bitcast.7.me, bf16[512,1536]{1,0:T(8,128)(2,1)} %copy-done.33, bf16[512,1536]{1,0:T(8,128)(2,1)} %copy-done.49, ...), custom_call_target="tpu_custom_call", output_to_operand_aliasing={{0}: (20, {}), {1}: (21, {})} | custom-call | flops 1048576 | bytes 65536 | tf_op jit(solution)/shard_map/gate_back_1/pallas_call | solution.py:522
  375.9 19.2 %convolution_convert_fusion = bf16[1536,2048]{1,0:T(8,128)(2,1)} fusion(bf16[2048,1536]{1,0:T(8,128)(2,1)} %get-tuple-element.293, bf16[2048,2048]{1,0:T(8,128)(2,1)} %get-tuple-element.314), kind=kOutput, calls=%fused_computation | convolution fusion | flops 12888047616 | bytes 20971520 | tf_op jit(solution)/shard_map/dot_general | solution.py:63
  398.9 11.2 %convolution_convert_fusion.1 = bf16[1536,1024]{1,0:T(8,128)(2,1)} fusion(bf16[2048,1536]{1,0:T(8,128)(2,1)} %get-tuple-element.319, bf16[2048,1024]{1,0:T(8,128)(2,1)} %get-tuple-element.300.refs_3_), kind=kOutput, calls=%fused_computation.6 | convolution fusion | flops 6444023808 | bytes 13631488 | tf_op jit(solution)/shard_map/dot_general | solution.py:63
  412.5 5.3 collective-permute-done.50
  420.9 6.1 fusion.28
  436.0 11.1 %collective-permute-done.52 = bf16[256,1536]{1,0:T(8,128)(2,1)S(1)} collective-permute-done((bf16[256,1536]{1,0:T(8,128)(2,1)S(1)}, bf16[256,1536]{1,0:T(8,128)(2,1)S(1)}, u32[]{:S(2)}, u32[]{:S(2)}) %collective-permute-start.52) | collective-permute-done | bytes 786464 | tf_op jit(solution)/shard_map/ppermute | solution.py:626
  453.5 4.3 add_convert_fusion.1
  457.8 9.1 %collective-permute-done.54.refs_12_ = bf16[1024,384]{1,0:T(8,128)(2,1)} collective-permute-done((bf16[1024,384]{1,0:T(8,128)(2,1)}, bf16[1024,384]{1,0:T(8,128)(2,1)}, u32[]{:S(2)}, u32[]{:S(2)}) %collective-permute-start.54) | collective-permute-done | bytes 786464 | tf_op jit(solution)/shard_map/ppermute | solution.py:626
  471.8 45.6 %attention_backward_0.1 = bf16[2048,768]{1,0:T(8,128)(2,1)} custom-call(s32[16]{0:T(128)} %pad_add_fusion.refs_0_, s32[8]{0:T(128)} %get-tuple-element.338.refs_1_, s32[8]{0:T(128)} %get-tuple-element.339.refs_2_, f32[2048,128]{1,0:T(8,128)} %get-tuple-element.340.refs_3_, f32[2048,128]{1,0:T(8,128)} %get-tuple-element.341.refs_4_, ...), custom_call_target="tpu_custom_call" | custom-call | flops 1048576 | bytes 65536 | tf_op jit(solution)/shard_map/attention_backward_0/pallas_call | solution.py:363
  521.9 4.5 convolution_convert_fusion.4
  526.5 5.6 collective-permute-start.57
  538.9 10.8 %collective-permute-done.57 = bf16[192,2048]{1,0:T(8,128)(2,1)S(1)} collective-permute-done((bf16[192,2048]{1,0:T(8,128)(2,1)S(1)}, bf16[192,2048]{1,0:T(8,128)(2,1)S(1)}, u32[]{:S(2)}, u32[]{:S(2)}) %collective-permute-start.57) | collective-permute-done | bytes 786464 | tf_op jit(solution)/shard_map/ppermute | solution.py:580
  553.3 5.5 convolution_convert_fusion.2
  571.6 9.2 %collective-permute-done.64 = bf16[192,1024]{1,0:T(8,128)(2,1)S(1)} collective-permute-done((bf16[192,1024]{1,0:T(8,128)(2,1)S(1)}, bf16[192,1024]{1,0:T(8,128)(2,1)S(1)}, u32[]{:S(2)}, u32[]{:S(2)}) %collective-permute-start.64) | collective-permute-done | bytes 393248 | tf_op jit(solution)/shard_map/ppermute | solution.py:580
  590.3 7.4 %collective-permute-done.67 = bf16[384,768]{1,0:T(8,128)(2,1)} collective-permute-done((bf16[384,768]{1,0:T(8,128)(2,1)}, bf16[384,768]{1,0:T(8,128)(2,1)}, u32[]{:S(2)}, u32[]{:S(2)}) %collective-permute-start.67) | collective-permute-done | bytes 589856 | tf_op jit(solution)/shard_map/ppermute | solution.py:631
  613.0 4.8 collective-permute-done.68
  627.2 39.6 %psum.7 = f32[2,192]{1,0:T(2,128)S(1)} all-reduce(f32[2,192]{1,0:T(2,128)S(1)} %pad_maximum_fusion.18), channel_id=1, replica_groups=mesh['yx'=4,'core'=2,'zh'=2,'zl'=2] {'zh','zl'}, use_global_device_ids=true, to_apply=%region_11.12 | all-reduce | flops 384 | bytes 3072 | tf_op jit(solution)/shard_map/psum | solution.py:991
  (452 shorter events, 240.9 us)
Async XLA Ops:
  7.2 189.6 %all-gather.3.cloned.1.call-start = ((), (), s32[]{:S(2)}) async-start(), calls=%async_computation.3 | async-start | bytes 2949120 | tf_op jit(solution)/shard_map/all_gather | solution.py:781
  8.4 32.3 %collective-permute-start.2 = (bf16[192,768]{1,0:T(8,128)(2,1)S(1)}, bf16[192,768]{1,0:T(8,128)(2,1)S(1)}, u32[]{:S(2)}, u32[]{:S(2)}) collective-permute-start(bf16[192,768]{1,0:T(8,128)(2,1)S(1)} %pad_maximum_fusion.16), channel_id=1, source_target_pairs={{0,2},{6,4},{4,0},{2,6},{1,3},{7,5},{5,1},{3,7},{8,10},{14,12},{12... | collective-permute-start | bytes 884744 | tf_op jit(solution)/shard_map/ppermute | solution.py:580
  8.5 32.2 %collective-permute-start.3 = (bf16[192,768]{1,0:T(8,128)(2,1)S(1)}, bf16[192,768]{1,0:T(8,128)(2,1)}, u32[]{:S(2)}, u32[]{:S(2)}) collective-permute-start(bf16[192,768]{1,0:T(8,128)(2,1)S(1)} %pad_maximum_fusion.16), channel_id=1, source_target_pairs={{2,4},{4,2},{3,5},{5,3},{10,12},{12,10},{11,13},{13,11},{18,20},{2... | collective-permute-start | bytes 884744 | tf_op jit(solution)/shard_map/ppermute | solution.py:580
  11.7 26.6 %collective-permute-start = (bf16[256,1536]{1,0:T(8,128)(2,1)S(1)}, bf16[256,1536]{1,0:T(8,128)(2,1)}, u32[]{:S(2)}, u32[]{:S(2)}) collective-permute-start(bf16[256,1536]{1,0:T(8,128)(2,1)S(1)} %slice.206), channel_id=1, source_target_pairs={{2,4},{4,2},{3,5},{5,3},{10,12},{12,10},{11,13},{13,11},{18,20},{2... | collective-permute-start | bytes 2359304 | tf_op jit(solution)/shard_map/ppermute | solution.py:580
  42.8 36.2 %collective-permute-start.7 = (bf16[384,768]{1,0:T(8,128)(2,1)S(1)}, bf16[384,768]{1,0:T(8,128)(2,1)S(1)}, u32[]{:S(2)}, u32[]{:S(2)}) collective-permute-start(bf16[384,768]{1,0:T(8,128)(2,1)S(1)} %pad_maximum_fusion.12.refs_3_.refs_0_), channel_id=1, source_target_pairs={{0,8},{8,0},{16,24},{24,16},{1,9},{9,1},{17,25},{25,17},{2,10},{10... | collective-permute-start | bytes 1769480 | tf_op jit(solution)/shard_map/ppermute | solution.py:631
  44.4 34.6 %collective-permute-start.8 = (bf16[384,768]{1,0:T(8,128)(2,1)S(1)}, bf16[384,768]{1,0:T(8,128)(2,1)S(1)}, u32[]{:S(2)}, u32[]{:S(2)}) collective-permute-start(bf16[384,768]{1,0:T(8,128)(2,1)S(1)} %pad_maximum_fusion.12.refs_3_.refs_0_), channel_id=1, source_target_pairs={{0,16},{8,24},{16,0},{24,8},{1,17},{9,25},{17,1},{25,9},{2,18},{10... | collective-permute-start | bytes 1769480 | tf_op jit(solution)/shard_map/ppermute | solution.py:631
  46.2 32.8 %collective-permute-start.6 = (bf16[256,1536]{1,0:T(8,128)(2,1)}, bf16[256,1536]{1,0:T(8,128)(2,1)}, u32[]{:S(2)}, u32[]{:S(2)}) collective-permute-start(bf16[256,1536]{1,0:T(8,128)(2,1)} %get-tuple-element.195), channel_id=1, source_target_pairs={{1,0},{0,1},{3,2},{2,3},{5,4},{4,5},{7,6},{6,7},{9,8},{8,9},{11,10... | collective-permute-start | bytes 2359304 | tf_op jit(solution)/shard_map/ppermute | solution.py:621
  53.5 23.4 %collective-permute-start.4 = (bf16[256,1536]{1,0:T(8,128)(2,1)}, bf16[256,1536]{1,0:T(8,128)(2,1)}, u32[]{:S(2)}, u32[]{:S(2)}) collective-permute-start(bf16[256,1536]{1,0:T(8,128)(2,1)} %get-tuple-element.196), channel_id=1, source_target_pairs={{2,4},{4,2},{3,5},{5,3},{10,12},{12,10},{11,13},{13,11},{18,20},{2... | collective-permute-start | bytes 2359304 | tf_op jit(solution)/shard_map/ppermute | solution.py:580
  120.8 346.1 %reduce-scatter.4.cloned.1.call-start = ((), (), s32[]{:S(2)}) async-start(), calls=%async_computation.4 | async-start | bytes 7864320 | tf_op jit(solution)/shard_map/reduce_scatter | solution.py:904
  120.8 35.4 %collective-permute-start.17 = (bf16[192,2048]{1,0:T(8,128)(2,1)S(1)}, bf16[192,2048]{1,0:T(8,128)(2,1)S(1)}, u32[]{:S(2)}, u32[]{:S(2)}) collective-permute-start(bf16[192,2048]{1,0:T(8,128)(2,1)S(1)} %pad_maximum_fusion.6), channel_id=1, source_target_pairs={{0,2},{6,4},{4,0},{2,6},{1,3},{7,5},{5,1},{3,7},{8,10},{14,12},{12... | collective-permute-start | bytes 2359304 | tf_op jit(solution)/shard_map/ppermute | solution.py:580
  121.2 35.0 %collective-permute-start.18 = (bf16[192,2048]{1,0:T(8,128)(2,1)S(1)}, bf16[192,2048]{1,0:T(8,128)(2,1)}, u32[]{:S(2)}, u32[]{:S(2)}) collective-permute-start(bf16[192,2048]{1,0:T(8,128)(2,1)S(1)} %pad_maximum_fusion.6), channel_id=1, source_target_pairs={{2,4},{4,2},{3,5},{5,3},{10,12},{12,10},{11,13},{13,11},{18,20},{2... | collective-permute-start | bytes 2359304 | tf_op jit(solution)/shard_map/ppermute | solution.py:580
  157.7 39.1 %collective-permute-start.22 = (bf16[384,1024]{1,0:T(8,128)(2,1)S(1)}, bf16[384,1024]{1,0:T(8,128)(2,1)S(1)}, u32[]{:S(2)}, u32[]{:S(2)}) collective-permute-start(bf16[384,1024]{1,0:T(8,128)(2,1)S(1)} %pad_maximum_fusion.8.refs_2_.refs_4_), channel_id=1, source_target_pairs={{0,8},{8,0},{16,24},{24,16},{1,9},{9,1},{17,25},{25,17},{2,10},{10... | collective-permute-start | bytes 2359304 | tf_op jit(solution)/shard_map/ppermute | solution.py:631
  158.9 37.8 %collective-permute-start.23 = (bf16[384,1024]{1,0:T(8,128)(2,1)S(1)}, bf16[384,1024]{1,0:T(8,128)(2,1)S(1)}, u32[]{:S(2)}, u32[]{:S(2)}) collective-permute-start(bf16[384,1024]{1,0:T(8,128)(2,1)S(1)} %pad_maximum_fusion.8.refs_2_.refs_4_), channel_id=1, source_target_pairs={{0,16},{8,24},{16,0},{24,8},{1,17},{9,25},{17,1},{25,9},{2,18},{10... | collective-permute-start | bytes 2359304 | tf_op jit(solution)/shard_map/ppermute | solution.py:631
  161.2 35.6 %collective-permute-start.19 = (bf16[256,1536]{1,0:T(8,128)(2,1)}, bf16[256,1536]{1,0:T(8,128)(2,1)}, u32[]{:S(2)}, u32[]{:S(2)}) collective-permute-start(bf16[256,1536]{1,0:T(8,128)(2,1)} %slice.218), channel_id=1, source_target_pairs={{2,4},{4,2},{3,5},{5,3},{10,12},{12,10},{11,13},{13,11},{18,20},{2... | collective-permute-start | bytes 2359304 | tf_op jit(solution)/shard_map/ppermute | solution.py:580
  165.3 31.5 %collective-permute-start.21 = (bf16[1024,384]{1,0:T(8,128)(2,1)}, bf16[1024,384]{1,0:T(8,128)(2,1)}, u32[]{:S(2)}, u32[]{:S(2)}) collective-permute-start(bf16[1024,384]{1,0:T(8,128)(2,1)} %get-tuple-element.234.refs_14_), channel_id=1, source_target_pairs={{0,1},{1,0},{2,3},{3,2},{4,5},{5,4},{6,7},{7,6},{8,9},{9,8},{10,11... | collective-permute-start | bytes 2359304 | tf_op jit(solution)/shard_map/ppermute | solution.py:626
  167.1 29.7 %collective-permute-start.20 = (bf16[192,1024]{1,0:T(8,128)(2,1)}, bf16[192,1024]{1,0:T(8,128)(2,1)}, u32[]{:S(2)}, u32[]{:S(2)}) collective-permute-start(bf16[192,1024]{1,0:T(8,128)(2,1)} %param.31), channel_id=1, source_target_pairs={{2,4},{4,2},{3,5},{5,3},{10,12},{12,10},{11,13},{13,11},{18,20},{2... | collective-permute-start | bytes 1179656 | tf_op jit(solution)/shard_map/ppermute | solution.py:580
  200.8 28.8 %collective-permute-start.25 = (bf16[384,1024]{1,0:T(8,128)(2,1)}, bf16[384,1024]{1,0:T(8,128)(2,1)S(1)}, u32[]{:S(2)}, u32[]{:S(2)}) collective-permute-start(bf16[384,1024]{1,0:T(8,128)(2,1)} %pad_maximum_fusion.7.refs_7_.refs_9_), channel_id=1, source_target_pairs={{0,8},{8,0},{16,24},{24,16},{1,9},{9,1},{17,25},{25,17},{2,10},{10... | collective-permute-start | bytes 2359304 | tf_op jit(solution)/shard_map/ppermute | solution.py:631
  201.3 28.3 %collective-permute-start.26 = (bf16[384,1024]{1,0:T(8,128)(2,1)}, bf16[384,1024]{1,0:T(8,128)(2,1)S(1)}, u32[]{:S(2)}, u32[]{:S(2)}) collective-permute-start(bf16[384,1024]{1,0:T(8,128)(2,1)} %pad_maximum_fusion.7.refs_7_.refs_9_), channel_id=1, source_target_pairs={{0,16},{8,24},{16,0},{24,8},{1,17},{9,25},{17,1},{25,9},{2,18},{10... | collective-permute-start | bytes 2359304 | tf_op jit(solution)/shard_map/ppermute | solution.py:631
  202.4 26.9 %collective-permute-start.27 = (bf16[192,1024]{1,0:T(8,128)(2,1)S(1)}, bf16[192,1024]{1,0:T(8,128)(2,1)S(1)}, u32[]{:S(2)}, u32[]{:S(2)}) collective-permute-start(bf16[192,1024]{1,0:T(8,128)(2,1)S(1)} %slice.225), channel_id=1, source_target_pairs={{0,8},{8,0},{16,24},{24,16},{1,9},{9,1},{17,25},{25,17},{2,10},{10... | collective-permute-start | bytes 1179656 | tf_op jit(solution)/shard_map/ppermute | solution.py:631
  203.7 25.9 %collective-permute-start.28 = (bf16[192,1024]{1,0:T(8,128)(2,1)S(1)}, bf16[192,1024]{1,0:T(8,128)(2,1)S(1)}, u32[]{:S(2)}, u32[]{:S(2)}) collective-permute-start(bf16[192,1024]{1,0:T(8,128)(2,1)S(1)} %slice.226), channel_id=1, source_target_pairs={{0,16},{8,24},{16,0},{24,8},{1,17},{9,25},{17,1},{25,9},{2,18},{10... | collective-permute-start | bytes 1179656 | tf_op jit(solution)/shard_map/ppermute | solution.py:631
  270.5 41.4 %collective-permute-start.40 = (bf16[256,1536]{1,0:T(8,128)(2,1)}, bf16[256,1536]{1,0:T(8,128)(2,1)}, u32[]{:S(2)}, u32[]{:S(2)}) collective-permute-start(bf16[256,1536]{1,0:T(8,128)(2,1)} %slice_select_fusion), channel_id=1, source_target_pairs={{1,0},{0,1},{3,2},{2,3},{5,4},{4,5},{7,6},{6,7},{9,8},{8,9},{11,10... | collective-permute-start | bytes 2359304 | tf_op jit(solution)/shard_map/ppermute | solution.py:621
  273.9 37.9 %collective-permute-start.41 = (bf16[256,1536]{1,0:T(8,128)(2,1)}, bf16[256,1536]{1,0:T(8,128)(2,1)}, u32[]{:S(2)}, u32[]{:S(2)}) collective-permute-start(bf16[256,1536]{1,0:T(8,128)(2,1)} %slice.235), channel_id=1, source_target_pairs={{1,0},{0,1},{3,2},{2,3},{5,4},{4,5},{7,6},{6,7},{9,8},{8,9},{11,10... | collective-permute-start | bytes 2359304 | tf_op jit(solution)/shard_map/ppermute | solution.py:621
  395.4 121.9 %reduce-scatter.6.cloned.1.call-start = ((), (), s32[]{:S(2)}) async-start(), calls=%async_computation.5 | async-start | bytes 3932160 | tf_op jit(solution)/shard_map/reduce_scatter | solution.py:911
  420.3 170.1 %reduce-scatter.8.cloned.1.call-start = ((), (), s32[]{:S(2)}) async-start(), calls=%async_computation.6 | async-start | bytes 2949120 | tf_op jit(solution)/shard_map/reduce_scatter | solution.py:939
  427.0 26.5 %collective-permute-start.53 = (bf16[512,1536]{1,0:T(8,128)(2,1)}, bf16[512,1536]{1,0:T(8,128)(2,1)}, u32[]{:S(2)}, u32[]{:S(2)}) collective-permute-start(bf16[512,1536]{1,0:T(8,128)(2,1)} %get-tuple-element.330), channel_id=1, source_target_pairs={{0,4},{4,0},{1,5},{5,1},{2,6},{6,2},{3,7},{7,3},{8,12},{12,8},{9,1... | collective-permute-start | bytes 4718600 | tf_op jit(solution)/shard_map/ppermute | solution.py:571
  466.9 53.9 %collective-permute-start.55 = (bf16[512,1536]{1,0:T(8,128)(2,1)}, bf16[512,1536]{1,0:T(8,128)(2,1)S(1)}, u32[]{:S(2)}, u32[]{:S(2)}) collective-permute-start(bf16[512,1536]{1,0:T(8,128)(2,1)} %add_convert_fusion.1), channel_id=1, source_target_pairs={{2,4},{4,2},{3,5},{5,3},{10,12},{12,10},{11,13},{13,11},{18,20},{2... | collective-permute-start | bytes 4718600 | tf_op jit(solution)/shard_map/ppermute | solution.py:580
  471.2 49.6 %collective-permute-start.56 = (bf16[192,2048]{1,0:T(8,128)(2,1)}, bf16[192,2048]{1,0:T(8,128)(2,1)S(1)}, u32[]{:S(2)}, u32[]{:S(2)}) collective-permute-start(bf16[192,2048]{1,0:T(8,128)(2,1)} %get-tuple-element.404), channel_id=1, source_target_pairs={{2,0},{4,6},{0,4},{6,2},{3,1},{5,7},{1,5},{7,3},{10,8},{12,14},{8,... | collective-permute-start | bytes 2359304 | tf_op jit(solution)/shard_map/ppermute | solution.py:580
  526.5 23.2 %collective-permute-start.57 = (bf16[192,2048]{1,0:T(8,128)(2,1)S(1)}, bf16[192,2048]{1,0:T(8,128)(2,1)S(1)}, u32[]{:S(2)}, u32[]{:S(2)}) collective-permute-start(bf16[192,2048]{1,0:T(8,128)(2,1)S(1)} %get-tuple-element.352), channel_id=1, source_target_pairs={{2,4},{4,2},{3,5},{5,3},{10,12},{12,10},{11,13},{13,11},{18,20},{2... | collective-permute-start | bytes 2359304 | tf_op jit(solution)/shard_map/ppermute | solution.py:580
  551.3 29.5 %collective-permute-start.60 = (bf16[256,1536]{1,0:T(8,128)(2,1)S(1)}, bf16[256,1536]{1,0:T(8,128)(2,1)S(1)}, u32[]{:S(2)}, u32[]{:S(2)}) collective-permute-start(bf16[256,1536]{1,0:T(8,128)(2,1)S(1)} %slice.251), channel_id=1, source_target_pairs={{0,1},{1,0},{2,3},{3,2},{4,5},{5,4},{6,7},{7,6},{8,9},{9,8},{10,11... | collective-permute-start | bytes 2359304 | tf_op jit(solution)/shard_map/ppermute | solution.py:626
  618.6 50.3 %collective-permute-start.71 = (bf16[512,1536]{1,0:T(8,128)(2,1)S(1)}, bf16[512,1536]{1,0:T(8,128)(2,1)}, u32[]{:S(2)}, u32[]{:S(2)}) collective-permute-start(bf16[512,1536]{1,0:T(8,128)(2,1)S(1)} %fusion.5), channel_id=1, source_target_pairs={{2,4},{4,2},{3,5},{5,3},{10,12},{12,10},{11,13},{13,11},{18,20},{2... | collective-permute-start | bytes 4718600 | tf_op jit(solution)/shard_map/ppermute | solution.py:580
  622.6 45.5 %collective-permute-start.72 = (bf16[192,384]{1,0:T(8,128)(2,1)}, bf16[192,384]{1,0:T(8,128)(2,1)S(1)}, u32[]{:S(2)}, u32[]{:S(2)}) collective-permute-start(bf16[192,384]{1,0:T(8,128)(2,1)} %get-tuple-element.375), channel_id=1, source_target_pairs={{2,0},{4,6},{0,4},{6,2},{3,1},{5,7},{1,5},{7,3},{10,8},{12,14},{8,... | collective-permute-start | bytes 442376 | tf_op jit(solution)/shard_map/ppermute | solution.py:580
  622.6 45.5 %collective-permute-start.73 = (bf16[192,384]{1,0:T(8,128)(2,1)S(1)}, bf16[192,384]{1,0:T(8,128)(2,1)S(1)}, u32[]{:S(2)}, u32[]{:S(2)}) collective-permute-start(bf16[192,384]{1,0:T(8,128)(2,1)S(1)} %get-tuple-element.376), channel_id=1, source_target_pairs={{2,4},{4,2},{3,5},{5,3},{10,12},{12,10},{11,13},{13,11},{18,20},{2... | collective-permute-start | bytes 442376 | tf_op jit(solution)/shard_map/ppermute | solution.py:580
  (138 other events, 2063.8 us)
Sparse Core Ops, SparseCore 0:
  120.9 38.0 all-gather.2
  395.5 70.2 reduce-scatter.3
  468.8 43.9 reduce-scatter.5
  526.6 43.3 reduce-scatter.7

commit v7 on v6

--- a/solution.py
+++ b/solution.py
@@ -786,7 +786,6 @@
     quarters = [context[0]] + [None] * (near - 1)
     for k in others:
         quarters[near - k] = to_near(context[k], k)
-    cot_upper = crossed(cotangent[:part_rows], CROSS)
     down_cross = crossed(down_shard, CROSS)
     pairs = [
         pair_of(*(x[:, n * hidden_cols : (n + 1) * hidden_cols] for x in (gate_up_shard, *gate_up_moved)))
@@ -796,31 +795,28 @@
     w_project = assemble("assemble_project", me, *blocks, tokens.shape[1], qkv_cols)
     residual = own.astype(f32)
     scale_one = lax.rsqrt(jnp.mean(residual * residual, axis=-1, keepdims=True) + EPSILON)
-    up_pair, cotangent, cot_upper, down_cross, w_out, scale_one, w_project, *moved = stage(
-        pairs[1], cotangent, cot_upper, down_cross, w_out, scale_one, w_project, *quarters, *gate_taken
+    up_pair, cotangent, down_cross, w_out, scale_one, w_project, *moved = stage(
+        pairs[1], cotangent, down_cross, w_out, scale_one, w_project, *quarters, *gate_taken
     )
     quarters, gate_taken = moved[:near], moved[near:]
 
     up_taken = neighbours(up_pair)
-    gate_halves = diagonal(gate_taken)
+    cot_upper = crossed(cotangent[:part_rows], CROSS)
     context_all = jnp.concatenate(quarters, axis=1)
     branch_sib = flip(times_transpose(context_all[rows:], w_out).astype(bf16), "core")
     mid = residual + times_transpose(context_all[:rows], w_out) + branch_sib.astype(f32)
     scale_two, norm_two = norm_rows(mid, gain_two)
-    norm_two, cotangent, *moved = stage(norm_two, cotangent, *up_taken, *gate_halves)
-    up_taken, gate_halves = moved[: len(up_taken)], moved[len(up_taken) :]
-
-    quarter = part_rows // 2
-    far_quarters = [[from_near(norm_two[:quarter], k) for k in others]]
+    norm_two, cotangent, cot_upper, *up_taken = stage(norm_two, cotangent, cot_upper, *up_taken)
+
+    upper_far = [from_near(norm_two[:part_rows], k) for k in others]
+    gate_halves, up_halves = diagonal(gate_taken), diagonal(up_taken)
+    down_pair = pair_of(down_weight, down_out, down_cross)
+    norm_two, down_pair, cotangent, *moved = stage(norm_two, down_pair, cotangent, *upper_far, *gate_halves, *up_halves)
+    upper_far, moved = moved[: near - 1], moved[near - 1 :]
+    gate_halves, up_halves = moved[: len(gate_halves)], moved[len(gate_halves) :]
+
+    lower_far = [from_near(norm_two[part_rows:], k) for k in others]
     norm_sib = flip(norm_two, "core")
-    up_halves = diagonal(up_taken)
-    down_pair = pair_of(down_weight, down_out, down_cross)
-    norm_two, norm_sib, down_pair, cotangent, *moved = stage(
-        norm_two, norm_sib, down_pair, cotangent, *far_quarters[0], *up_halves
-    )
-    far_quarters[0], up_halves = moved[: near - 1], moved[near - 1 :]
-
-    far_quarters.append([from_near(norm_two[quarter:part_rows], k) for k in others])
     cot_lower = crossed(cotangent[part_rows:], CROSS)
     down_taken = neighbours(down_pair)
     gate_blocks = blocks_of(pairs[0], gate_taken, gate_halves)
@@ -828,13 +824,12 @@
     gate_up = ([*gate_blocks[0], *up_blocks[0]], gate_blocks[1] + up_blocks[1], 2 * hidden_cols)
     gate_outs = [(norm_two.shape[1], bf16, "all"), (2 * hidden_cols, f32, "all"), (hidden_cols, bf16, "all")]
     earlier = piece_call(gate_kernel, "gate", 0, near, me, [norm_two, norm_sib], [], [], [gate_up], [], gate_outs)
-    norm_two, cotangent, cot_lower, *moved = stage(
-        norm_two, cotangent, cot_lower, *far_quarters[1], *down_taken, *earlier
-    )
-    far_quarters[1], moved = moved[: near - 1], moved[near - 1 :]
+    cotangent, cot_lower, *moved = stage(cotangent, cot_lower, *lower_far, *down_taken, *earlier)
+    lower_far, moved = moved[: near - 1], moved[near - 1 :]
     down_taken, earlier = moved[: len(down_taken)], moved[len(down_taken) :]
 
-    lower_far = [from_near(norm_two[part_rows:], k) for k in others]
+    norm_far = [jnp.concatenate(x, axis=0) for x in zip(upper_far, lower_far, strict=True)]
+    norm_far_sib = [flip(x, "core") for x in norm_far]
     cot = jnp.where(straight(), cotangent, jnp.concatenate([cot_upper, cot_lower], axis=0))
     cot_sib = flip(cot, "core")
     cot_upper_far = [from_near(jnp.where(straight(), cotangent[:part_rows], cot_upper), k) for k in others]
@@ -854,16 +849,15 @@
     norm_two_all, gate_up_all, hidden_all = earlier
     grad_all, d_gate_up_all, *near_back = way_back(0, [cot, cot_sib], [])
     cot, *moved = stage(
-        cot, norm_two_all, gate_up_all, hidden_all, grad_all, d_gate_up_all, *near_back, *cot_upper_far, *lower_far
+        cot, norm_two_all, gate_up_all, hidden_all, grad_all, d_gate_up_all, *near_back, *cot_upper_far, *norm_far_sib
     )
     earlier, (grad_all, d_gate_up_all), near_back, moved = moved[:3], moved[3:5], moved[5:9], moved[9:]
-    cot_upper_far, lower_far = moved[: near - 1], moved[near - 1 :]
+    cot_upper_far, norm_far_sib = moved[: near - 1], moved[near - 1 :]
 
     cot_lower_far = [from_near(cot[part_rows:], k) for k in others]
     out_far = []
     for k in others:
-        norm_far = jnp.concatenate([*(x[k - 1] for x in far_quarters), lower_far[k - 1]], axis=0)
-        parts = [norm_far, flip(norm_far, "core")]
+        parts = [norm_far[k - 1], norm_far_sib[k - 1]]
         *earlier, out_own, out_sib = piece_call(
             gate_kernel, "gate", k, near, me, parts, [], [], [gate_up, down], earlier, gate_outs + halves
         )
@@ -947,27 +941,27 @@
         taken = flip(times_transpose(sib, w_project).astype(bf16), "core")
         return times_transpose(own, w_project) + taken.astype(f32)
 
+    d_sent = [back_part(k).astype(bf16) for k in others]
+    d_qkv, gate_up_keep, down_part, *d_sent = stage(d_qkv, gate_up_keep, down_part, *d_sent)
+
+    output = jnp.where(straight(), output_own, output_crossed)
+
+    d_upper = [to_near(d_sent[k - 1][:part_rows], k) for k in others]
     gate_up_cross = crossed(gate_up_keep, CROSS)
-    d_sent = [back_part(k).astype(bf16) for k in others]
-    d_qkv, gate_up_cross, down_part, *d_sent = stage(d_qkv, gate_up_cross, down_part, *d_sent)
-
-    output = jnp.where(straight(), output_own, output_crossed)
-
-    d_upper = [to_near(d_sent[k - 1][:part_rows], k) for k in others]
-    down_keep, down_give = give_z(down_part)
-    down_home = [crossed(down_give, BACK), crossed(down_keep, CROSS)]
     grad_project = rows_product(norm_one, d_qkv).astype(bf16)
     project_sent = send_yx(grad_project, (0, qkv_cols))
     total = back_part(0)
-    total, grad_project, *moved = stage(total, grad_project, *d_upper, *d_sent, *project_sent, *down_home)
-    d_upper, d_sent, project_sent, down_home = (
-        moved[: near - 1], moved[near - 1 : 2 * near - 2], moved[2 * near - 2 : -2], moved[-2:],
-    )
+    total, grad_project, gate_up_cross, down_part, *moved = stage(
+        total, grad_project, gate_up_cross, down_part, *d_upper, *d_sent, *project_sent
+    )
+    d_upper, d_sent, project_sent = moved[: near - 1], moved[near - 1 : 2 * near - 2], moved[2 * near - 2 :]
 
     d_lower = [to_near(d_sent[k - 1][part_rows:], k) for k in others]
+    down_keep, down_give = give_z(down_part)
+    down_home = [crossed(down_give, BACK), crossed(down_keep, CROSS)]
     project_rest, project_own = join_yx(grad_project, (0, qkv_cols), project_sent)
-    out_part, *moved = stage(out_part, *d_lower, *project_rest)
-    d_lower, project_rest = moved[: near - 1], moved[near - 1 :]
+    out_part, *moved = stage(out_part, *d_lower, *project_rest, *down_home)
+    d_lower, project_rest, down_home = moved[: near - 1], moved[near - 1 : -2], moved[-2:]
     d_moved = [jnp.concatenate(x, axis=0) for x in zip(d_upper, d_lower, strict=True)]
     project_keep, project_give = give_z(total_yx(project_rest, project_own))
 

time: 691 us -> 685 us (level)
    ppermute x20, waiting for transfers between devices: 46.1 us -> 26.5 us  [across(): return lax.ppermute(x, 'yx', [(a, a ^ j) for a in range(n)])]
    ppermute x9, waiting for transfers between devices: 30.5 us -> 39.3 us  [to_near(): return lax.ppermute(x, 'zl', [(j, (j + k) % n) for j in range(n)])]
    ppermute x23, waiting for transfers between devices: 65 us -> 73.7 us  [crossed(): return lax.ppermute(x, ('core', 'zh'), perm)]
    ppermute x23, starting transfers between devices: 50.7 us -> 43 us  [crossed(): return lax.ppermute(x, ('core', 'zh'), perm)]
    ppermute x8 -> x7, starting transfers between devices: 16 us -> 14.5 us  [from_near(): return lax.ppermute(x, 'zl', [((j + k) % n, j) for j in range(n)])]
    unnamed x190 -> x175, local copies, waits for them, and re-layouts: 15.9 us -> 17 us
  transfers between devices with their start and end apart: 78 -> 77, of which waited for: 29 -> 32; matrix products, arithmetic and copies ran while one was open for 20% -> 20% of each run, Pallas kernels for 26% -> 26%
where the time goes in v7:
time: 685 us; the launch traced here: 675 us
  Pallas kernels  175 us (26%)
  waiting for transfers between devices  160 us (23%)
  starting transfers between devices  100 us (15%)
  other arithmetic  67.8 us (10%)
  matrix products  59 us (9%)
  blocking collectives  48.6 us (7%)
  local copies, waits for them, and re-layouts  48.5 us (7%)
  between operations  15.7 us (2%)
    pallas_call x6, Pallas kernels, piece_call(): pl.pallas_call(functools.partial(kernel, count, tuple((where for _, where...  97.3 us
    ppermute x23, waiting for transfers between devices, crossed(): return lax.ppermute(x, ('core', 'zh'), perm)  73.7 us
    pallas_call x1, Pallas kernels, attend_back(): pl.pallas_call(functools.partial(backward_kernel, pieces, ratio, bool(ear...  45.6 us
    ppermute x23, starting transfers between devices, crossed(): return lax.ppermute(x, ('core', 'zh'), perm)  43 us
    dot_general x5, matrix products, rows_product(): lax.dot_general(left, right, (((0,), (0,)), ((), ())), preferred_element_...  40.3 us
    ppermute x9, waiting for transfers between devices, to_near(): return lax.ppermute(x, 'zl', [(j, (j + k) % n) for j in range(n)])  39.3 us
    psum x1, blocking collectives, body(): lax.psum(jnp.stack([jnp.sum(qkv_shard.astype(f32) * grad_project, axis=1)...  39.3 us
    pallas_call x1, Pallas kernels, attend(): pl.pallas_call(functools.partial(forward_kernel, pieces, ratio), out_shap...  29.5 us
  transfers between devices with their start and end apart: 77, of which 32 were waited for; matrix products, arithmetic and copies ran while one was open for 20% of the time, Pallas kernels for 26%

profile of v7, /device:TPU:16, one launch (start us, length us, event | category | flops | bytes accessed | tf_op | source)
XLA Modules:
  0.0 675.4 jit_solution(5984014030945328376)
XLA Ops:
  11.7 4.7 collective-permute-start
  20.2 9.3 %all-gather = bf16[8,192,2]{1,2,0:T(2,128)(2,1)S(1)} all-gather(bf16[1,192,2]{1,2,0:T(2,128)(2,1)S(1)} %fusion.27), channel_id=1, replica_groups=mesh['yx'=4,'core'=2,'zh'=2,'zl'=2] {'yx','core'}, dimensions={0}, use_global_device_ids=true | all-gather | bytes 6912 | tf_op jit(solution)/shard_map/all_gather | solution.py:722
  30.9 7.4 %collective-permute-done.1 = s32[1,4]{1,0:T(1,128)S(1)} collective-permute-done((s32[1,4]{1,0:T(1,128)}, s32[1,4]{1,0:T(1,128)S(1)}, u32[]{:S(2)}, u32[]{:S(2)}) %collective-permute-start.1) | collective-permute-done | bytes 48 | tf_op jit(solution)/shard_map/ppermute | solution.py:580
  46.2 5.9 collective-permute-start.6
  63.6 13.3 %collective-permute-done.4 = bf16[256,1536]{1,0:T(8,128)(2,1)} collective-permute-done((bf16[256,1536]{1,0:T(8,128)(2,1)}, bf16[256,1536]{1,0:T(8,128)(2,1)}, u32[]{:S(2)}, u32[]{:S(2)}) %collective-permute-start.4) | collective-permute-done | bytes 786464 | tf_op jit(solution)/shard_map/ppermute | solution.py:580
  95.0 8.7 %project_0.1 = (bf16[2048,1536]{1,0:T(8,128)(2,1)}, bf16[2048,768]{1,0:T(8,128)(2,1)}) custom-call(s32[1]{0:T(128)} %bitcast.7.me, bf16[512,1536]{1,0:T(8,128)(2,1)} %copy-done, bf16[512,1536]{1,0:T(8,128)(2,1)} %collective-permute-done.11.refs_1_, f32[1,1536]{1,0:T(1,128)} %get-tuple-element.427.refs_2_, bf16[384,768]{1,0:T(8,128)(2,1)} %copy-done.18, ...), custom_call_target="tpu_custom_call" | custom-call | flops 1048576 | bytes 65536 | tf_op jit(solution)/shard_map/project_0/pallas_call | solution.py:522
  111.2 8.5 %project_1.1 = (bf16[2048,1536]{1,0:T(8,128)(2,1)}, bf16[2048,768]{1,0:T(8,128)(2,1)}) custom-call(s32[1]{0:T(128)} %bitcast.7.me, bf16[512,1536]{1,0:T(8,128)(2,1)} %constant_dynamic-update-slice_fusion.2.refs_0_, bf16[512,1536]{1,0:T(8,128)(2,1)} %copy-done.54, ...), custom_call_target="tpu_custom_call", output_to_operand_aliasing={{0}: (9, {}), {1}: (10, {})} | custom-call | flops 1048576 | bytes 65536 | tf_op jit(solution)/shard_map/project_1/pallas_call | solution.py:522
  121.2 4.1 collective-permute-start.18
  126.7 29.5 %attention_forward.1 = (bf16[1024,384]{1,0:T(8,128)(2,1)}, bf16[1024,384]{1,0:T(8,128)(2,1)}, f32[4,1,1024]{2,1,0:T(1,128)}, f32[4,1,1024]{2,1,0:T(1,128)}) custom-call(s32[16]{0:T(128)} %pad_add_fusion.refs_0_, s32[4]{0:T(128)} %get-tuple-element.219.refs_1_, s32[4]{0:T(128)} %get-tuple-element.220.refs_2_, f32[2048,128]{1,0:T(8,128)} %get-tuple-element.338.refs_3_, ...), custom_call_target="tpu_custom_call" | custom-call | flops 1048576 | bytes 65536 | tf_op jit(solution)/shard_map/attention_forward/pallas_call | solution.py:333
  170.5 14.6 %collective-permute-done.19 = bf16[192,1024]{1,0:T(8,128)(2,1)} collective-permute-done((bf16[192,1024]{1,0:T(8,128)(2,1)}, bf16[192,1024]{1,0:T(8,128)(2,1)}, u32[]{:S(2)}, u32[]{:S(2)}) %collective-permute-start.19) | collective-permute-done | bytes 393248 | tf_op jit(solution)/shard_map/ppermute | solution.py:580
  196.0 14.2 %collective-permute-done.24 = bf16[256,1536]{1,0:T(8,128)(2,1)S(1)} collective-permute-done((bf16[256,1536]{1,0:T(8,128)(2,1)S(1)}, bf16[256,1536]{1,0:T(8,128)(2,1)S(1)}, u32[]{:S(2)}, u32[]{:S(2)}) %collective-permute-start.24) | collective-permute-done | bytes 786464 | tf_op jit(solution)/shard_map/ppermute | solution.py:580
  217.8 5.6 collective-permute-done.28.refs_5_.refs_7_
  241.0 14.1 %gate_0.1 = (bf16[2048,1536]{1,0:T(8,128)(2,1)}, f32[2048,2048]{1,0:T(8,128)}, bf16[2048,1024]{1,0:T(8,128)(2,1)}) custom-call(s32[1]{0:T(128)} %bitcast.7.me, bf16[512,1536]{1,0:T(8,128)(2,1)} %copy-done.13, bf16[512,1536]{1,0:T(8,128)(2,1)} %collective-permute-done.36.refs_1_, bf16[384,1024]{1,0:T(8,128)(2,1)} %copy-done.5, bf16[384,1024]{1,0:T(8,128)(2,1)} %copy-done.7, ...), custom_call_target="tpu_custom_call" | custom-call | flops 1048576 | bytes 65536 | tf_op jit(solution)/shard_map/gate_0/pallas_call | solution.py:522
  255.0 7.3 %collective-permute-done.33 = bf16[256,1536]{1,0:T(8,128)(2,1)} collective-permute-done((bf16[256,1536]{1,0:T(8,128)(2,1)}, bf16[256,1536]{1,0:T(8,128)(2,1)}, u32[]{:S(2)}, u32[]{:S(2)}) %collective-permute-start.33) | collective-permute-done | bytes 786464 | tf_op jit(solution)/shard_map/ppermute | solution.py:621
  274.0 8.0 %collective-permute-done.38.refs_17_.refs_15_ = bf16[192,1024]{1,0:T(8,128)(2,1)S(1)} collective-permute-done((bf16[192,1024]{1,0:T(8,128)(2,1)S(1)}, bf16[192,1024]{1,0:T(8,128)(2,1)S(1)}, u32[]{:S(2)}, u32[]{:S(2)}) %collective-permute-start.38) | collective-permute-done | bytes 393248 | tf_op jit(solution)/shard_map/ppermute | solution.py:631
  284.2 25.2 %gate_back_0.1 = (bf16[2048,1536]{1,0:T(8,128)(2,1)}, bf16[2048,2048]{1,0:T(8,128)(2,1)}, bf16[512,1536]{1,0:T(8,128)(2,1)}, bf16[512,1536]{1,0:T(8,128)(2,1)}, ...) custom-call(s32[1]{0:T(128)} %bitcast.7.me, bf16[512,1536]{1,0:T(8,128)(2,1)} %copy-done.6, ...), custom_call_target="tpu_custom_call" | custom-call | flops 1048576 | bytes 65536 | tf_op jit(solution)/shard_map/gate_back_0/pallas_call | solution.py:522
  311.8 19.3 %gate_1.1 = (bf16[2048,1536]{1,0:T(8,128)(2,1)}, f32[2048,2048]{1,0:T(8,128)}, bf16[2048,1024]{1,0:T(8,128)(2,1)}, bf16[512,1536]{1,0:T(8,128)(2,1)}, bf16[512,1536]{1,0:T(8,128)(2,1)}) custom-call(s32[1]{0:T(128)} %bitcast.7.me, ...), custom_call_target="tpu_custom_call", output_to_operand_aliasing={{0}: (18, {}), {1}: (19, {}), {2}: (20, {})} | custom-call | flops 1048576 | bytes 65536 | tf_op jit(solution)/shard_map/gate_1/pallas_call | solution.py:522
  340.3 21.5 %gate_back_1.1 = (bf16[2048,1536]{1,0:T(8,128)(2,1)}, bf16[2048,2048]{1,0:T(8,128)(2,1)}, bf16[512,1536]{1,0:T(8,128)(2,1)}, bf16[512,1536]{1,0:T(8,128)(2,1)}) custom-call(s32[1]{0:T(128)} %bitcast.7.me, bf16[512,1536]{1,0:T(8,128)(2,1)} %copy-done.33, bf16[512,1536]{1,0:T(8,128)(2,1)} %copy-done.50, ...), custom_call_target="tpu_custom_call", output_to_operand_aliasing={{0}: (20, {}), {1}: (21, {})} | custom-call | flops 1048576 | bytes 65536 | tf_op jit(solution)/shard_map/gate_back_1/pallas_call | solution.py:522
  369.8 19.2 %convolution_convert_fusion = bf16[1536,2048]{1,0:T(8,128)(2,1)} fusion(bf16[2048,1536]{1,0:T(8,128)(2,1)} %get-tuple-element.291, bf16[2048,2048]{1,0:T(8,128)(2,1)} %get-tuple-element.312), kind=kOutput, calls=%fused_computation | convolution fusion | flops 12888047616 | bytes 20971520 | tf_op jit(solution)/shard_map/dot_general | solution.py:63
  392.9 11.2 %convolution_convert_fusion.1 = bf16[1536,1024]{1,0:T(8,128)(2,1)} fusion(bf16[2048,1536]{1,0:T(8,128)(2,1)} %get-tuple-element.317, bf16[2048,1024]{1,0:T(8,128)(2,1)} %get-tuple-element.298.refs_3_), kind=kOutput, calls=%fused_computation.6 | convolution fusion | flops 6444023808 | bytes 13631488 | tf_op jit(solution)/shard_map/dot_general | solution.py:63
  406.8 5.0 collective-permute-done.49
  414.6 5.8 fusion.28
  429.3 11.1 %collective-permute-done.51 = bf16[256,1536]{1,0:T(8,128)(2,1)S(1)} collective-permute-done((bf16[256,1536]{1,0:T(8,128)(2,1)S(1)}, bf16[256,1536]{1,0:T(8,128)(2,1)S(1)}, u32[]{:S(2)}, u32[]{:S(2)}) %collective-permute-start.51) | collective-permute-done | bytes 786464 | tf_op jit(solution)/shard_map/ppermute | solution.py:626
  447.0 4.4 add_convert_fusion.1
  451.4 8.8 %collective-permute-done.53.refs_12_ = bf16[1024,384]{1,0:T(8,128)(2,1)} collective-permute-done((bf16[1024,384]{1,0:T(8,128)(2,1)}, bf16[1024,384]{1,0:T(8,128)(2,1)}, u32[]{:S(2)}, u32[]{:S(2)}) %collective-permute-start.53) | collective-permute-done | bytes 786464 | tf_op jit(solution)/shard_map/ppermute | solution.py:626
  466.6 45.6 %attention_backward_0.1 = bf16[2048,768]{1,0:T(8,128)(2,1)} custom-call(s32[16]{0:T(128)} %pad_add_fusion.refs_0_, s32[8]{0:T(128)} %get-tuple-element.336.refs_1_, s32[8]{0:T(128)} %get-tuple-element.337.refs_2_, f32[2048,128]{1,0:T(8,128)} %get-tuple-element.338.refs_3_, f32[2048,128]{1,0:T(8,128)} %get-tuple-element.339.refs_4_, ...), custom_call_target="tpu_custom_call" | custom-call | flops 1048576 | bytes 65536 | tf_op jit(solution)/shard_map/attention_backward_0/pallas_call | solution.py:363
  516.9 4.6 convolution_convert_fusion.4
  537.9 5.5 convolution_convert_fusion.2
  552.4 9.0 %collective-permute-done.59 = bf16[256,1536]{1,0:T(8,128)(2,1)S(1)} collective-permute-done((bf16[256,1536]{1,0:T(8,128)(2,1)S(1)}, bf16[256,1536]{1,0:T(8,128)(2,1)S(1)}, u32[]{:S(2)}, u32[]{:S(2)}) %collective-permute-start.59) | collective-permute-done | bytes 786464 | tf_op jit(solution)/shard_map/ppermute | solution.py:626
  576.4 19.9 %collective-permute-done.66 = bf16[192,1024]{1,0:T(8,128)(2,1)} collective-permute-done((bf16[192,1024]{1,0:T(8,128)(2,1)S(1)}, bf16[192,1024]{1,0:T(8,128)(2,1)}, u32[]{:S(2)}, u32[]{:S(2)}) %collective-permute-start.66) | collective-permute-done | bytes 393248 | tf_op jit(solution)/shard_map/ppermute | solution.py:580
  608.1 5.1 collective-permute-done.67
  623.7 39.3 %psum.7 = f32[2,192]{1,0:T(2,128)S(1)} all-reduce(f32[2,192]{1,0:T(2,128)S(1)} %pad_maximum_fusion.18), channel_id=1, replica_groups=mesh['yx'=4,'core'=2,'zh'=2,'zl'=2] {'zh','zl'}, use_global_device_ids=true, to_apply=%region_11.12 | all-reduce | flops 384 | bytes 3072 | tf_op jit(solution)/shard_map/psum | solution.py:985
  (434 shorter events, 244.1 us)
Async XLA Ops:
  7.2 178.0 %all-gather.3.cloned.1.call-start = ((), (), s32[]{:S(2)}) async-start(), calls=%async_computation.3 | async-start | bytes 2949120 | tf_op jit(solution)/shard_map/all_gather | solution.py:781
  8.4 32.3 %collective-permute-start.2 = (bf16[192,768]{1,0:T(8,128)(2,1)S(1)}, bf16[192,768]{1,0:T(8,128)(2,1)S(1)}, u32[]{:S(2)}, u32[]{:S(2)}) collective-permute-start(bf16[192,768]{1,0:T(8,128)(2,1)S(1)} %pad_maximum_fusion.16), channel_id=1, source_target_pairs={{0,2},{6,4},{4,0},{2,6},{1,3},{7,5},{5,1},{3,7},{8,10},{14,12},{12... | collective-permute-start | bytes 884744 | tf_op jit(solution)/shard_map/ppermute | solution.py:580
  8.5 32.2 %collective-permute-start.3 = (bf16[192,768]{1,0:T(8,128)(2,1)S(1)}, bf16[192,768]{1,0:T(8,128)(2,1)}, u32[]{:S(2)}, u32[]{:S(2)}) collective-permute-start(bf16[192,768]{1,0:T(8,128)(2,1)S(1)} %pad_maximum_fusion.16), channel_id=1, source_target_pairs={{2,4},{4,2},{3,5},{5,3},{10,12},{12,10},{11,13},{13,11},{18,20},{2... | collective-permute-start | bytes 884744 | tf_op jit(solution)/shard_map/ppermute | solution.py:580
  11.7 26.6 %collective-permute-start = (bf16[256,1536]{1,0:T(8,128)(2,1)S(1)}, bf16[256,1536]{1,0:T(8,128)(2,1)}, u32[]{:S(2)}, u32[]{:S(2)}) collective-permute-start(bf16[256,1536]{1,0:T(8,128)(2,1)S(1)} %slice.203), channel_id=1, source_target_pairs={{2,4},{4,2},{3,5},{5,3},{10,12},{12,10},{11,13},{13,11},{18,20},{2... | collective-permute-start | bytes 2359304 | tf_op jit(solution)/shard_map/ppermute | solution.py:580
  42.8 36.2 %collective-permute-start.7 = (bf16[384,768]{1,0:T(8,128)(2,1)S(1)}, bf16[384,768]{1,0:T(8,128)(2,1)S(1)}, u32[]{:S(2)}, u32[]{:S(2)}) collective-permute-start(bf16[384,768]{1,0:T(8,128)(2,1)S(1)} %pad_maximum_fusion.12.refs_3_.refs_0_), channel_id=1, source_target_pairs={{0,8},{8,0},{16,24},{24,16},{1,9},{9,1},{17,25},{25,17},{2,10},{10... | collective-permute-start | bytes 1769480 | tf_op jit(solution)/shard_map/ppermute | solution.py:631
  44.4 34.6 %collective-permute-start.8 = (bf16[384,768]{1,0:T(8,128)(2,1)S(1)}, bf16[384,768]{1,0:T(8,128)(2,1)S(1)}, u32[]{:S(2)}, u32[]{:S(2)}) collective-permute-start(bf16[384,768]{1,0:T(8,128)(2,1)S(1)} %pad_maximum_fusion.12.refs_3_.refs_0_), channel_id=1, source_target_pairs={{0,16},{8,24},{16,0},{24,8},{1,17},{9,25},{17,1},{25,9},{2,18},{10... | collective-permute-start | bytes 1769480 | tf_op jit(solution)/shard_map/ppermute | solution.py:631
  46.2 32.8 %collective-permute-start.6 = (bf16[256,1536]{1,0:T(8,128)(2,1)}, bf16[256,1536]{1,0:T(8,128)(2,1)}, u32[]{:S(2)}, u32[]{:S(2)}) collective-permute-start(bf16[256,1536]{1,0:T(8,128)(2,1)} %get-tuple-element.195), channel_id=1, source_target_pairs={{1,0},{0,1},{3,2},{2,3},{5,4},{4,5},{7,6},{6,7},{9,8},{8,9},{11,10... | collective-permute-start | bytes 2359304 | tf_op jit(solution)/shard_map/ppermute | solution.py:621
  120.7 339.7 %reduce-scatter.4.cloned.1.call-start = ((), (), s32[]{:S(2)}) async-start(), calls=%async_computation.4 | async-start | bytes 7864320 | tf_op jit(solution)/shard_map/reduce_scatter | solution.py:898
  120.8 35.4 %collective-permute-start.17 = (bf16[192,2048]{1,0:T(8,128)(2,1)S(1)}, bf16[192,2048]{1,0:T(8,128)(2,1)S(1)}, u32[]{:S(2)}, u32[]{:S(2)}) collective-permute-start(bf16[192,2048]{1,0:T(8,128)(2,1)S(1)} %pad_maximum_fusion.6), channel_id=1, source_target_pairs={{0,2},{6,4},{4,0},{2,6},{1,3},{7,5},{5,1},{3,7},{8,10},{14,12},{12... | collective-permute-start | bytes 2359304 | tf_op jit(solution)/shard_map/ppermute | solution.py:580
  121.2 35.0 %collective-permute-start.18 = (bf16[192,2048]{1,0:T(8,128)(2,1)S(1)}, bf16[192,2048]{1,0:T(8,128)(2,1)}, u32[]{:S(2)}, u32[]{:S(2)}) collective-permute-start(bf16[192,2048]{1,0:T(8,128)(2,1)S(1)} %pad_maximum_fusion.6), channel_id=1, source_target_pairs={{2,4},{4,2},{3,5},{5,3},{10,12},{12,10},{11,13},{13,11},{18,20},{2... | collective-permute-start | bytes 2359304 | tf_op jit(solution)/shard_map/ppermute | solution.py:580
  157.7 27.5 %collective-permute-start.21 = (bf16[384,1024]{1,0:T(8,128)(2,1)S(1)}, bf16[384,1024]{1,0:T(8,128)(2,1)S(1)}, u32[]{:S(2)}, u32[]{:S(2)}) collective-permute-start(bf16[384,1024]{1,0:T(8,128)(2,1)S(1)} %pad_maximum_fusion.8.refs_2_.refs_4_), channel_id=1, source_target_pairs={{0,8},{8,0},{16,24},{24,16},{1,9},{9,1},{17,25},{25,17},{2,10},{10... | collective-permute-start | bytes 2359304 | tf_op jit(solution)/shard_map/ppermute | solution.py:631
  158.9 26.2 %collective-permute-start.22 = (bf16[384,1024]{1,0:T(8,128)(2,1)S(1)}, bf16[384,1024]{1,0:T(8,128)(2,1)S(1)}, u32[]{:S(2)}, u32[]{:S(2)}) collective-permute-start(bf16[384,1024]{1,0:T(8,128)(2,1)S(1)} %pad_maximum_fusion.8.refs_2_.refs_4_), channel_id=1, source_target_pairs={{0,16},{8,24},{16,0},{24,8},{1,17},{9,25},{17,1},{25,9},{2,18},{10... | collective-permute-start | bytes 2359304 | tf_op jit(solution)/shard_map/ppermute | solution.py:631
  160.2 24.9 %collective-permute-start.20 = (bf16[1024,384]{1,0:T(8,128)(2,1)}, bf16[1024,384]{1,0:T(8,128)(2,1)}, u32[]{:S(2)}, u32[]{:S(2)}) collective-permute-start(bf16[1024,384]{1,0:T(8,128)(2,1)} %get-tuple-element.234.refs_14_), channel_id=1, source_target_pairs={{0,1},{1,0},{2,3},{3,2},{4,5},{5,4},{6,7},{7,6},{8,9},{9,8},{10,11... | collective-permute-start | bytes 2359304 | tf_op jit(solution)/shard_map/ppermute | solution.py:626
  236.0 26.4 %collective-permute-start.33 = (bf16[256,1536]{1,0:T(8,128)(2,1)}, bf16[256,1536]{1,0:T(8,128)(2,1)}, u32[]{:S(2)}, u32[]{:S(2)}) collective-permute-start(bf16[256,1536]{1,0:T(8,128)(2,1)} %slice.228), channel_id=1, source_target_pairs={{1,0},{0,1},{3,2},{2,3},{5,4},{4,5},{7,6},{6,7},{9,8},{8,9},{11,10... | collective-permute-start | bytes 2359304 | tf_op jit(solution)/shard_map/ppermute | solution.py:621
  237.7 24.7 %collective-permute-start.34 = (bf16[384,1024]{1,0:T(8,128)(2,1)}, bf16[384,1024]{1,0:T(8,128)(2,1)}, u32[]{:S(2)}, u32[]{:S(2)}) collective-permute-start(bf16[384,1024]{1,0:T(8,128)(2,1)} %pad_maximum_fusion.9.refs_14_.refs_12_), channel_id=1, source_target_pairs={{0,8},{8,0},{16,24},{24,16},{1,9},{9,1},{17,25},{25,17},{2,10},{10... | collective-permute-start | bytes 2359304 | tf_op jit(solution)/shard_map/ppermute | solution.py:631
  238.3 24.1 %collective-permute-start.35 = (bf16[384,1024]{1,0:T(8,128)(2,1)}, bf16[384,1024]{1,0:T(8,128)(2,1)}, u32[]{:S(2)}, u32[]{:S(2)}) collective-permute-start(bf16[384,1024]{1,0:T(8,128)(2,1)} %pad_maximum_fusion.9.refs_14_.refs_12_), channel_id=1, source_target_pairs={{0,16},{8,24},{16,0},{24,8},{1,17},{9,25},{17,1},{25,9},{2,18},{10... | collective-permute-start | bytes 2359304 | tf_op jit(solution)/shard_map/ppermute | solution.py:631
  267.0 42.4 %collective-permute-start.41 = (bf16[512,1536]{1,0:T(8,128)(2,1)}, bf16[512,1536]{1,0:T(8,128)(2,1)}, u32[]{:S(2)}, u32[]{:S(2)}) collective-permute-start(bf16[512,1536]{1,0:T(8,128)(2,1)} %constant_dynamic-update-slice_fusion.6.refs_0_), channel_id=1, source_target_pairs={{0,4},{4,0},{1,5},{5,1},{2,6},{6,2},{3,7},{7,3},{8,12},{12,8},{9,1... | collective-permute-start | bytes 4718600 | tf_op jit(solution)/shard_map/ppermute | solution.py:571
  268.0 41.4 %collective-permute-start.40 = (bf16[256,1536]{1,0:T(8,128)(2,1)}, bf16[256,1536]{1,0:T(8,128)(2,1)}, u32[]{:S(2)}, u32[]{:S(2)}) collective-permute-start(bf16[256,1536]{1,0:T(8,128)(2,1)} %slice_select_fusion), channel_id=1, source_target_pairs={{1,0},{0,1},{3,2},{2,3},{5,4},{4,5},{7,6},{6,7},{9,8},{8,9},{11,10... | collective-permute-start | bytes 2359304 | tf_op jit(solution)/shard_map/ppermute | solution.py:621
  389.3 122.9 %reduce-scatter.6.cloned.1.call-start = ((), (), s32[]{:S(2)}) async-start(), calls=%async_computation.5 | async-start | bytes 3932160 | tf_op jit(solution)/shard_map/reduce_scatter | solution.py:905
  413.9 161.5 %reduce-scatter.8.cloned.1.call-start = ((), (), s32[]{:S(2)}) async-start(), calls=%async_computation.6 | async-start | bytes 2949120 | tf_op jit(solution)/shard_map/reduce_scatter | solution.py:933
  420.3 26.7 %collective-permute-start.52 = (bf16[512,1536]{1,0:T(8,128)(2,1)}, bf16[512,1536]{1,0:T(8,128)(2,1)}, u32[]{:S(2)}, u32[]{:S(2)}) collective-permute-start(bf16[512,1536]{1,0:T(8,128)(2,1)} %get-tuple-element.328), channel_id=1, source_target_pairs={{0,4},{4,0},{1,5},{5,1},{2,6},{6,2},{3,7},{7,3},{8,12},{12,8},{9,1... | collective-permute-start | bytes 4718600 | tf_op jit(solution)/shard_map/ppermute | solution.py:571
  460.5 54.4 %collective-permute-start.54 = (bf16[512,1536]{1,0:T(8,128)(2,1)}, bf16[512,1536]{1,0:T(8,128)(2,1)S(1)}, u32[]{:S(2)}, u32[]{:S(2)}) collective-permute-start(bf16[512,1536]{1,0:T(8,128)(2,1)} %add_convert_fusion.1), channel_id=1, source_target_pairs={{2,4},{4,2},{3,5},{5,3},{10,12},{12,10},{11,13},{13,11},{18,20},{2... | collective-permute-start | bytes 4718600 | tf_op jit(solution)/shard_map/ppermute | solution.py:580
  465.4 49.5 %collective-permute-start.55 = (bf16[192,2048]{1,0:T(8,128)(2,1)S(1)}, bf16[192,2048]{1,0:T(8,128)(2,1)S(1)}, u32[]{:S(2)}, u32[]{:S(2)}) collective-permute-start(bf16[192,2048]{1,0:T(8,128)(2,1)S(1)} %get-tuple-element.404), channel_id=1, source_target_pairs={{2,0},{4,6},{0,4},{6,2},{3,1},{5,7},{1,5},{7,3},{10,8},{12,14},{8,... | collective-permute-start | bytes 2359304 | tf_op jit(solution)/shard_map/ppermute | solution.py:580
  532.2 29.2 %collective-permute-start.59 = (bf16[256,1536]{1,0:T(8,128)(2,1)S(1)}, bf16[256,1536]{1,0:T(8,128)(2,1)S(1)}, u32[]{:S(2)}, u32[]{:S(2)}) collective-permute-start(bf16[256,1536]{1,0:T(8,128)(2,1)S(1)} %slice.247), channel_id=1, source_target_pairs={{0,1},{1,0},{2,3},{3,2},{4,5},{5,4},{6,7},{7,6},{8,9},{9,8},{10,11... | collective-permute-start | bytes 2359304 | tf_op jit(solution)/shard_map/ppermute | solution.py:626
  535.7 26.3 %collective-permute-start.58 = (bf16[192,2048]{1,0:T(8,128)(2,1)S(1)}, bf16[192,2048]{1,0:T(8,128)(2,1)S(1)}, u32[]{:S(2)}, u32[]{:S(2)}) collective-permute-start(bf16[192,2048]{1,0:T(8,128)(2,1)S(1)} %copy-done.45), channel_id=1, source_target_pairs={{2,4},{4,2},{3,5},{5,3},{10,12},{12,10},{11,13},{13,11},{18,20},{2... | collective-permute-start | bytes 2359304 | tf_op jit(solution)/shard_map/ppermute | solution.py:580
  563.0 33.3 %collective-permute-start.64 = (bf16[384,768]{1,0:T(8,128)(2,1)}, bf16[384,768]{1,0:T(8,128)(2,1)}, u32[]{:S(2)}, u32[]{:S(2)}) collective-permute-start(bf16[384,768]{1,0:T(8,128)(2,1)} %pad_maximum_fusion.15), channel_id=1, source_target_pairs={{0,16},{8,24},{16,0},{24,8},{1,17},{9,25},{17,1},{25,9},{2,18},{10... | collective-permute-start | bytes 1769480 | tf_op jit(solution)/shard_map/ppermute | solution.py:631
  565.3 31.1 %collective-permute-start.63 = (bf16[384,768]{1,0:T(8,128)(2,1)}, bf16[384,768]{1,0:T(8,128)(2,1)}, u32[]{:S(2)}, u32[]{:S(2)}) collective-permute-start(bf16[384,768]{1,0:T(8,128)(2,1)} %pad_maximum_fusion.14), channel_id=1, source_target_pairs={{0,8},{8,0},{16,24},{24,16},{1,9},{9,1},{17,25},{25,17},{2,10},{10... | collective-permute-start | bytes 1769480 | tf_op jit(solution)/shard_map/ppermute | solution.py:631
  567.8 28.6 %collective-permute-start.62 = (bf16[256,1536]{1,0:T(8,128)(2,1)}, bf16[256,1536]{1,0:T(8,128)(2,1)S(1)}, u32[]{:S(2)}, u32[]{:S(2)}) collective-permute-start(bf16[256,1536]{1,0:T(8,128)(2,1)} %slice.250), channel_id=1, source_target_pairs={{0,1},{1,0},{2,3},{3,2},{4,5},{5,4},{6,7},{7,6},{8,9},{9,8},{10,11... | collective-permute-start | bytes 2359304 | tf_op jit(solution)/shard_map/ppermute | solution.py:626
  570.8 25.6 %collective-permute-start.66 = (bf16[192,1024]{1,0:T(8,128)(2,1)S(1)}, bf16[192,1024]{1,0:T(8,128)(2,1)}, u32[]{:S(2)}, u32[]{:S(2)}) collective-permute-start(bf16[192,1024]{1,0:T(8,128)(2,1)S(1)} %get-tuple-element.413), channel_id=1, source_target_pairs={{2,4},{4,2},{3,5},{5,3},{10,12},{12,10},{11,13},{13,11},{18,20},{2... | collective-permute-start | bytes 1179656 | tf_op jit(solution)/shard_map/ppermute | solution.py:580
  614.0 51.2 %collective-permute-start.70 = (bf16[512,1536]{1,0:T(8,128)(2,1)S(1)}, bf16[512,1536]{1,0:T(8,128)(2,1)}, u32[]{:S(2)}, u32[]{:S(2)}) collective-permute-start(bf16[512,1536]{1,0:T(8,128)(2,1)S(1)} %fusion.5), channel_id=1, source_target_pairs={{2,4},{4,2},{3,5},{5,3},{10,12},{12,10},{11,13},{13,11},{18,20},{2... | collective-permute-start | bytes 4718600 | tf_op jit(solution)/shard_map/ppermute | solution.py:580
  620.1 44.3 %collective-permute-start.71 = (bf16[192,384]{1,0:T(8,128)(2,1)}, bf16[192,384]{1,0:T(8,128)(2,1)S(1)}, u32[]{:S(2)}, u32[]{:S(2)}) collective-permute-start(bf16[192,384]{1,0:T(8,128)(2,1)} %get-tuple-element.375), channel_id=1, source_target_pairs={{2,0},{4,6},{0,4},{6,2},{3,1},{5,7},{1,5},{7,3},{10,8},{12,14},{8,... | collective-permute-start | bytes 442376 | tf_op jit(solution)/shard_map/ppermute | solution.py:580
  620.1 44.3 %collective-permute-start.72 = (bf16[192,384]{1,0:T(8,128)(2,1)S(1)}, bf16[192,384]{1,0:T(8,128)(2,1)S(1)}, u32[]{:S(2)}, u32[]{:S(2)}) collective-permute-start(bf16[192,384]{1,0:T(8,128)(2,1)S(1)} %get-tuple-element.376), channel_id=1, source_target_pairs={{2,4},{4,2},{3,5},{5,3},{10,12},{12,10},{11,13},{13,11},{18,20},{2... | collective-permute-start | bytes 442376 | tf_op jit(solution)/shard_map/ppermute | solution.py:580
  (130 other events, 2007.7 us)
Sparse Core Ops, SparseCore 0:
  120.9 38.1 all-gather.2
  389.5 70.9 reduce-scatter.3
  463.5 43.9 reduce-scatter.5
  521.7 41.6 reduce-scatter.7

commit v8 on v7

--- a/solution.py
+++ b/solution.py
@@ -787,49 +787,39 @@
     for k in others:
         quarters[near - k] = to_near(context[k], k)
     down_cross = crossed(down_shard, CROSS)
-    pairs = [
-        pair_of(*(x[:, n * hidden_cols : (n + 1) * hidden_cols] for x in (gate_up_shard, *gate_up_moved)))
-        for n in range(2)
-    ]
-    gate_taken = neighbours(pairs[0])
+    gate_up_pair = pair_of(gate_up_shard, *gate_up_moved)
+    gate_up_taken = neighbours(gate_up_pair)
     w_project = assemble("assemble_project", me, *blocks, tokens.shape[1], qkv_cols)
     residual = own.astype(f32)
     scale_one = lax.rsqrt(jnp.mean(residual * residual, axis=-1, keepdims=True) + EPSILON)
-    up_pair, cotangent, down_cross, w_out, scale_one, w_project, *moved = stage(
-        pairs[1], cotangent, down_cross, w_out, scale_one, w_project, *quarters, *gate_taken
-    )
-    quarters, gate_taken = moved[:near], moved[near:]
-
-    up_taken = neighbours(up_pair)
+    cotangent, down_cross, w_out, scale_one, w_project, *moved = stage(
+        cotangent, down_cross, w_out, scale_one, w_project, *quarters, *gate_up_taken
+    )
+    quarters, gate_up_taken = moved[:near], moved[near:]
+
+    gate_up_halves = diagonal(gate_up_taken)
     cot_upper = crossed(cotangent[:part_rows], CROSS)
     context_all = jnp.concatenate(quarters, axis=1)
     branch_sib = flip(times_transpose(context_all[rows:], w_out).astype(bf16), "core")
     mid = residual + times_transpose(context_all[:rows], w_out) + branch_sib.astype(f32)
     scale_two, norm_two = norm_rows(mid, gain_two)
-    norm_two, cotangent, cot_upper, *up_taken = stage(norm_two, cotangent, cot_upper, *up_taken)
+    down_pair = pair_of(down_weight, down_out, down_cross)
+    norm_two, cotangent, cot_upper, down_pair, *gate_up_halves = stage(
+        norm_two, cotangent, cot_upper, down_pair, *gate_up_halves
+    )
 
     upper_far = [from_near(norm_two[:part_rows], k) for k in others]
-    gate_halves, up_halves = diagonal(gate_taken), diagonal(up_taken)
-    down_pair = pair_of(down_weight, down_out, down_cross)
-    norm_two, down_pair, cotangent, *moved = stage(norm_two, down_pair, cotangent, *upper_far, *gate_halves, *up_halves)
-    upper_far, moved = moved[: near - 1], moved[near - 1 :]
-    gate_halves, up_halves = moved[: len(gate_halves)], moved[len(gate_halves) :]
-
-    lower_far = [from_near(norm_two[part_rows:], k) for k in others]
     norm_sib = flip(norm_two, "core")
     cot_lower = crossed(cotangent[part_rows:], CROSS)
     down_taken = neighbours(down_pair)
-    gate_blocks = blocks_of(pairs[0], gate_taken, gate_halves)
-    up_blocks = blocks_of(up_pair, up_taken, up_halves, hidden_cols)
-    gate_up = ([*gate_blocks[0], *up_blocks[0]], gate_blocks[1] + up_blocks[1], 2 * hidden_cols)
+    gate_up = (*blocks_of(gate_up_pair, gate_up_taken, gate_up_halves), 2 * hidden_cols)
     gate_outs = [(norm_two.shape[1], bf16, "all"), (2 * hidden_cols, f32, "all"), (hidden_cols, bf16, "all")]
     earlier = piece_call(gate_kernel, "gate", 0, near, me, [norm_two, norm_sib], [], [], [gate_up], [], gate_outs)
-    cotangent, cot_lower, *moved = stage(cotangent, cot_lower, *lower_far, *down_taken, *earlier)
-    lower_far, moved = moved[: near - 1], moved[near - 1 :]
+    norm_two, cotangent, cot_lower, *moved = stage(norm_two, cotangent, cot_lower, *upper_far, *down_taken, *earlier)
+    upper_far, moved = moved[: near - 1], moved[near - 1 :]
     down_taken, earlier = moved[: len(down_taken)], moved[len(down_taken) :]
 
-    norm_far = [jnp.concatenate(x, axis=0) for x in zip(upper_far, lower_far, strict=True)]
-    norm_far_sib = [flip(x, "core") for x in norm_far]
+    lower_far = [from_near(norm_two[part_rows:], k) for k in others]
     cot = jnp.where(straight(), cotangent, jnp.concatenate([cot_upper, cot_lower], axis=0))
     cot_sib = flip(cot, "core")
     cot_upper_far = [from_near(jnp.where(straight(), cotangent[:part_rows], cot_upper), k) for k in others]
@@ -849,15 +839,16 @@
     norm_two_all, gate_up_all, hidden_all = earlier
     grad_all, d_gate_up_all, *near_back = way_back(0, [cot, cot_sib], [])
     cot, *moved = stage(
-        cot, norm_two_all, gate_up_all, hidden_all, grad_all, d_gate_up_all, *near_back, *cot_upper_far, *norm_far_sib
+        cot, norm_two_all, gate_up_all, hidden_all, grad_all, d_gate_up_all, *near_back, *cot_upper_far, *lower_far
     )
     earlier, (grad_all, d_gate_up_all), near_back, moved = moved[:3], moved[3:5], moved[5:9], moved[9:]
-    cot_upper_far, norm_far_sib = moved[: near - 1], moved[near - 1 :]
+    cot_upper_far, lower_far = moved[: near - 1], moved[near - 1 :]
 
     cot_lower_far = [from_near(cot[part_rows:], k) for k in others]
     out_far = []
     for k in others:
-        parts = [norm_far[k - 1], norm_far_sib[k - 1]]
+        norm_far = jnp.concatenate([upper_far[k - 1], lower_far[k - 1]], axis=0)
+        parts = [norm_far, flip(norm_far, "core")]
         *earlier, out_own, out_sib = piece_call(
             gate_kernel, "gate", k, near, me, parts, [], [], [gate_up, down], earlier, gate_outs + halves
         )
@@ -880,12 +871,18 @@
         parts = [cot_far[k - 1], cot_far_sib[k - 1]]
         grad_all, d_gate_up_all, *more = way_back(k, parts, [grad_all, d_gate_up_all])
         back.append(more)
-    grad_all, d_gate_up_all, *moved = stage(grad_all, d_gate_up_all, *(x for more in back for x in more), *out_upper)
-    far_back, out_upper = moved[: 2 * near - 2], moved[2 * near - 2 :]
+    grad_all, d_gate_up_all, *moved = stage(
+        grad_all, d_gate_up_all, *(x for more in back for x in more), *out_upper, *out_sums
+    )
+    far_back, moved = moved[: 2 * near - 2], moved[2 * near - 2 :]
+    out_upper, out_sums = moved[: near - 1], moved[near - 1 :]
+    last = part_rows + part_rows // 2
+    out_third = [to_near(out_sums[k - 1][part_rows:last], k) for k in others]
     d_norm_sent = [joined(*far_back[2 * n : 2 * n + 2]).astype(bf16) for n in range(near - 1)]
-    grad_all, d_gate_up_all, near_own, near_sib, *d_norm_sent = stage(
-        grad_all, d_gate_up_all, *near_back[:2], *d_norm_sent
-    )
+    grad_all, d_gate_up_all, near_own, near_sib, *moved = stage(
+        grad_all, d_gate_up_all, *near_back[:2], *d_norm_sent, *out_third
+    )
+    d_norm_sent, out_third = moved[: near - 1], moved[near - 1 :]
 
     moved_upper = [to_near(d_norm_sent[k - 1][:part_rows], k) for k in others]
     grad_gate_up = rows_product(norm_two_all, d_gate_up_all).astype(bf16)
@@ -901,7 +898,7 @@
     grad_down, d_norm_two, *moved = stage(grad_down, d_norm_two, *out_sums, *moved_lower)
     out_sums, moved_lower = moved[: near - 1], moved[near - 1 :]
 
-    out_lower = [to_near(out_sums[k - 1][part_rows:], k) for k in others]
+    out_lower = [to_near(out_sums[k - 1][last:], k) for k in others]
     down_part = lax.psum_scatter(grad_down, "yx", scatter_dimension=0, tiled=True)
     for one, two in zip(moved_upper, moved_lower, strict=True):
         d_norm_two = d_norm_two + jnp.concatenate([one, two], axis=0).astype(f32)
@@ -922,8 +919,8 @@
     grad_out = rows_product(d_attn, context_all[:rows]) + rows_product(d_attn_sib, context_all[rows:])
     grad_out = grad_out.astype(bf16)
     output_own = mid + joined(*near_back[2:])
-    for one, two in zip(out_upper, out_lower, strict=True):
-        output_own = output_own + jnp.concatenate([one, two], axis=0).astype(f32)
+    for pieces in zip(out_upper, out_third, out_lower, strict=True):
+        output_own = output_own + jnp.concatenate(pieces, axis=0).astype(f32)
     output_own = output_own.astype(bf16)
     grad_out, output_own, gate_up_part, *d_context = stage(grad_out, output_own, gate_up_part, *d_context)
 

time: 685 us -> 680 us (level)
    ppermute x20 -> x16, starting transfers between devices: 24.1 us -> 15.9 us  [across(): return lax.ppermute(x, 'yx', [(a, a ^ j) for a in range(n)])]
    ppermute x20 -> x16, waiting for transfers between devices: 26.5 us -> 24.2 us  [across(): return lax.ppermute(x, 'yx', [(a, a ^ j) for a in range(n)])]
    ppermute x9 -> x10, starting transfers between devices: 16.6 us -> 19 us  [to_near(): return lax.ppermute(x, 'zl', [(j, (j + k) % n) for j in range(n)])]
    unnamed x175 -> x159, local copies, waits for them, and re-layouts: 17 us -> 15.7 us
    ppermute x9 -> x10, waiting for transfers between devices: 39.3 us -> 38.3 us  [to_near(): return lax.ppermute(x, 'zl', [(j, (j + k) % n) for j in range(n)])]
  transfers between devices with their start and end apart: 77 -> 74, of which waited for: 32 -> 33; matrix products, arithmetic and copies ran while one was open for 20% -> 21% of each run, Pallas kernels for 26% -> 26%
where the time goes in v8:
time: 680 us; the launch traced here: 671 us
  Pallas kernels  175 us (26%)
  waiting for transfers between devices  162 us (24%)
  starting transfers between devices  96.4 us (14%)
  other arithmetic  66.3 us (10%)
  matrix products  59.1 us (9%)
  blocking collectives  48.7 us (7%)
  local copies, waits for them, and re-layouts  47.9 us (7%)
  between operations  15.6 us (2%)
    pallas_call x6, Pallas kernels, piece_call(): pl.pallas_call(functools.partial(kernel, count, tuple((where for _, where...  97.1 us
    ppermute x23, waiting for transfers between devices, crossed(): return lax.ppermute(x, ('core', 'zh'), perm)  73.7 us
    pallas_call x1, Pallas kernels, attend_back(): pl.pallas_call(functools.partial(backward_kernel, pieces, ratio, bool(ear...  45.1 us
    ppermute x23, starting transfers between devices, crossed(): return lax.ppermute(x, ('core', 'zh'), perm)  40.7 us
    dot_general x5, matrix products, rows_product(): lax.dot_general(left, right, (((0,), (0,)), ((), ())), preferred_element_...  40.4 us
    psum x1, blocking collectives, body(): lax.psum(jnp.stack([jnp.sum(qkv_shard.astype(f32) * grad_project, axis=1)...  39.3 us
    ppermute x10, waiting for transfers between devices, to_near(): return lax.ppermute(x, 'zl', [(j, (j + k) % n) for j in range(n)])  38.3 us
    pallas_call x1, Pallas kernels, attend(): pl.pallas_call(functools.partial(forward_kernel, pieces, ratio), out_shap...  29.4 us
  transfers between devices with their start and end apart: 74, of which 33 were waited for; matrix products, arithmetic and copies ran while one was open for 21% of the time, Pallas kernels for 26%

profile of v8, /device:TPU:16, one launch (start us, length us, event | category | flops | bytes accessed | tf_op | source)
XLA Modules:
  0.0 670.7 jit_solution(1662038070335322578)
XLA Ops:
  12.3 4.7 collective-permute-start
  20.8 9.3 %all-gather = bf16[8,192,2]{1,2,0:T(2,128)(2,1)S(1)} all-gather(bf16[1,192,2]{1,2,0:T(2,128)(2,1)S(1)} %fusion.27), channel_id=1, replica_groups=mesh['yx'=4,'core'=2,'zh'=2,'zl'=2] {'yx','core'}, dimensions={0}, use_global_device_ids=true | all-gather | bytes 6912 | tf_op jit(solution)/shard_map/all_gather | solution.py:722
  30.9 8.3 %collective-permute-done.1 = s32[1,4]{1,0:T(1,128)S(1)} collective-permute-done((s32[1,4]{1,0:T(1,128)}, s32[1,4]{1,0:T(1,128)S(1)}, u32[]{:S(2)}, u32[]{:S(2)}) %collective-permute-start.1) | collective-permute-done | bytes 48 | tf_op jit(solution)/shard_map/ppermute | solution.py:580
  45.2 5.8 collective-permute-start.6
  62.7 13.1 %collective-permute-done.4 = bf16[256,1536]{1,0:T(8,128)(2,1)} collective-permute-done((bf16[256,1536]{1,0:T(8,128)(2,1)}, bf16[256,1536]{1,0:T(8,128)(2,1)}, u32[]{:S(2)}, u32[]{:S(2)}) %collective-permute-start.4) | collective-permute-done | bytes 786464 | tf_op jit(solution)/shard_map/ppermute | solution.py:580
  94.9 8.7 %project_0.1 = (bf16[2048,1536]{1,0:T(8,128)(2,1)}, bf16[2048,768]{1,0:T(8,128)(2,1)}) custom-call(s32[1]{0:T(128)} %bitcast.7.me, bf16[512,1536]{1,0:T(8,128)(2,1)} %copy-done.2, bf16[512,1536]{1,0:T(8,128)(2,1)} %collective-permute-done.11.refs_1_, f32[1,1536]{1,0:T(1,128)} %get-tuple-element.415.refs_2_, bf16[384,768]{1,0:T(8,128)(2,1)} %copy-done.16, ...), custom_call_target="tpu_custom_call" | custom-call | flops 1048576 | bytes 65536 | tf_op jit(solution)/shard_map/project_0/pallas_call | solution.py:522
  108.5 8.5 %project_1.1 = (bf16[2048,1536]{1,0:T(8,128)(2,1)}, bf16[2048,768]{1,0:T(8,128)(2,1)}) custom-call(s32[1]{0:T(128)} %bitcast.7.me, bf16[512,1536]{1,0:T(8,128)(2,1)} %copy-done.31, bf16[512,1536]{1,0:T(8,128)(2,1)} %collective-permute-done.14.refs_1_, f32[1,1536]{1,0:T(1,128)} %get-tuple-element.415.refs_2_, ...), custom_call_target="tpu_custom_call", output_to_operand_aliasing={{0}: (9, {}), {1}: (10, {})} | custom-call | flops 1048576 | bytes 65536 | tf_op jit(solution)/shard_map/project_1/pallas_call | solution.py:522
  124.8 29.4 %attention_forward.1 = (bf16[1024,384]{1,0:T(8,128)(2,1)}, bf16[1024,384]{1,0:T(8,128)(2,1)}, f32[4,1,1024]{2,1,0:T(1,128)}, f32[4,1,1024]{2,1,0:T(1,128)}) custom-call(s32[16]{0:T(128)} %pad_add_fusion.refs_0_, s32[4]{0:T(128)} %get-tuple-element.205.refs_1_, s32[4]{0:T(128)} %get-tuple-element.206.refs_2_, f32[2048,128]{1,0:T(8,128)} %get-tuple-element.328.refs_3_, ...), custom_call_target="tpu_custom_call" | custom-call | flops 1048576 | bytes 65536 | tf_op jit(solution)/shard_map/attention_forward/pallas_call | solution.py:333
  166.3 15.6 %collective-permute-done.19 = bf16[192,1024]{1,0:T(8,128)(2,1)S(1)} collective-permute-done((bf16[192,1024]{1,0:T(8,128)(2,1)S(1)}, bf16[192,1024]{1,0:T(8,128)(2,1)S(1)}, u32[]{:S(2)}, u32[]{:S(2)}) %collective-permute-start.19) | collective-permute-done | bytes 393248 | tf_op jit(solution)/shard_map/ppermute | solution.py:580
  182.0 8.9 %collective-permute-done.21.refs_3_.refs_5_ = bf16[384,2048]{1,0:T(8,128)(2,1)S(1)} collective-permute-done((bf16[384,2048]{1,0:T(8,128)(2,1)S(1)}, bf16[384,2048]{1,0:T(8,128)(2,1)S(1)}, u32[]{:S(2)}, u32[]{:S(2)}) %collective-permute-start.21) | collective-permute-done | bytes 1572896 | tf_op jit(solution)/shard_map/ppermute | solution.py:631
  205.2 11.3 %collective-permute-done.24 = bf16[256,1536]{1,0:T(8,128)(2,1)S(1)} collective-permute-done((bf16[256,1536]{1,0:T(8,128)(2,1)S(1)}, bf16[256,1536]{1,0:T(8,128)(2,1)S(1)}, u32[]{:S(2)}, u32[]{:S(2)}) %collective-permute-start.24) | collective-permute-done | bytes 786464 | tf_op jit(solution)/shard_map/ppermute | solution.py:580
  223.8 4.8 collective-permute-start.28
  229.9 13.9 %gate_0.1 = (bf16[2048,1536]{1,0:T(8,128)(2,1)}, f32[2048,2048]{1,0:T(8,128)}, bf16[2048,1024]{1,0:T(8,128)(2,1)}) custom-call(s32[1]{0:T(128)} %bitcast.7.me, bf16[512,1536]{1,0:T(8,128)(2,1)} %copy-done.8, bf16[512,1536]{1,0:T(8,128)(2,1)} %collective-permute-done.31.refs_1_, bf16[384,2048]{1,0:T(8,128)(2,1)} %copy-done, bf16[384,2048]{1,0:T(8,128)(2,1)} %copy-done.1, ...), custom_call_target="tpu_custom_call" | custom-call | flops 1048576 | bytes 65536 | tf_op jit(solution)/shard_map/gate_0/pallas_call | solution.py:522
  243.8 7.1 %collective-permute-done.28 = bf16[256,1536]{1,0:T(8,128)(2,1)} collective-permute-done((bf16[256,1536]{1,0:T(8,128)(2,1)}, bf16[256,1536]{1,0:T(8,128)(2,1)}, u32[]{:S(2)}, u32[]{:S(2)}) %collective-permute-start.28) | collective-permute-done | bytes 786464 | tf_op jit(solution)/shard_map/ppermute | solution.py:621
  264.2 4.8 collective-permute-done.33.refs_12_.refs_10_
  271.7 25.2 %gate_back_0.1 = (bf16[2048,1536]{1,0:T(8,128)(2,1)}, bf16[2048,2048]{1,0:T(8,128)(2,1)}, bf16[512,1536]{1,0:T(8,128)(2,1)}, bf16[512,1536]{1,0:T(8,128)(2,1)}, ...) custom-call(s32[1]{0:T(128)} %bitcast.7.me, bf16[512,1536]{1,0:T(8,128)(2,1)} %copy-done.7, ...), custom_call_target="tpu_custom_call" | custom-call | flops 1048576 | bytes 65536 | tf_op jit(solution)/shard_map/gate_back_0/pallas_call | solution.py:522
  302.7 19.3 %gate_1.1 = (bf16[2048,1536]{1,0:T(8,128)(2,1)}, f32[2048,2048]{1,0:T(8,128)}, bf16[2048,1024]{1,0:T(8,128)(2,1)}, bf16[512,1536]{1,0:T(8,128)(2,1)}, bf16[512,1536]{1,0:T(8,128)(2,1)}) custom-call(s32[1]{0:T(128)} %bitcast.7.me, ...), custom_call_target="tpu_custom_call", output_to_operand_aliasing={{0}: (13, {}), {1}: (14, {}), {2}: (15, {})} | custom-call | flops 1048576 | bytes 65536 | tf_op jit(solution)/shard_map/gate_1/pallas_call | solution.py:522
  331.3 21.4 %gate_back_1.1 = (bf16[2048,1536]{1,0:T(8,128)(2,1)}, bf16[2048,2048]{1,0:T(8,128)(2,1)}, bf16[512,1536]{1,0:T(8,128)(2,1)}, bf16[512,1536]{1,0:T(8,128)(2,1)}) custom-call(s32[1]{0:T(128)} %bitcast.7.me, bf16[512,1536]{1,0:T(8,128)(2,1)} %copy-done.26, bf16[512,1536]{1,0:T(8,128)(2,1)} %copy-done.44, ...), custom_call_target="tpu_custom_call", output_to_operand_aliasing={{0}: (15, {}), {1}: (16, {})} | custom-call | flops 1048576 | bytes 65536 | tf_op jit(solution)/shard_map/gate_back_1/pallas_call | solution.py:522
  358.2 7.2 %collective-permute-done.43 = bf16[128,1536]{1,0:T(8,128)(2,1)S(1)} collective-permute-done((bf16[128,1536]{1,0:T(8,128)(2,1)S(1)}, bf16[128,1536]{1,0:T(8,128)(2,1)S(1)}, u32[]{:S(2)}, u32[]{:S(2)}) %collective-permute-start.43) | collective-permute-done | bytes 393248 | tf_op jit(solution)/shard_map/ppermute | solution.py:626
  366.9 19.2 %convolution_convert_fusion = bf16[1536,2048]{1,0:T(8,128)(2,1)} fusion(bf16[2048,1536]{1,0:T(8,128)(2,1)} %get-tuple-element.279, bf16[2048,2048]{1,0:T(8,128)(2,1)} %get-tuple-element.301), kind=kOutput, calls=%fused_computation | convolution fusion | flops 12888047616 | bytes 20971520 | tf_op jit(solution)/shard_map/dot_general | solution.py:63
  389.9 11.2 %convolution_convert_fusion.1 = bf16[1536,1024]{1,0:T(8,128)(2,1)} fusion(bf16[2048,1536]{1,0:T(8,128)(2,1)} %get-tuple-element.306, bf16[2048,1024]{1,0:T(8,128)(2,1)} %get-tuple-element.286.refs_3_), kind=kOutput, calls=%fused_computation.6 | convolution fusion | flops 6444023808 | bytes 13631488 | tf_op jit(solution)/shard_map/dot_general | solution.py:63
  403.6 5.0 collective-permute-done.46
  411.5 6.1 fusion.28
  441.5 8.4 %collective-permute-done.50.refs_12_ = bf16[1024,384]{1,0:T(8,128)(2,1)} collective-permute-done((bf16[1024,384]{1,0:T(8,128)(2,1)}, bf16[1024,384]{1,0:T(8,128)(2,1)}, u32[]{:S(2)}, u32[]{:S(2)}) %collective-permute-start.50) | collective-permute-done | bytes 786464 | tf_op jit(solution)/shard_map/ppermute | solution.py:626
  449.9 7.1 %reduce-scatter.4.cloned.1.call-done = bf16[384,2048]{1,0:T(8,128)(2,1)} async-done(((bf16[1536,2048]{1,0:T(8,128)(2,1)}), bf16[384,2048]{1,0:T(8,128)(2,1)}) %reduce-scatter.4.cloned.1.call-update) | async-done | bytes 1572880 | tf_op jit(solution)/shard_map/reduce_scatter | solution.py:895
  461.4 45.1 %attention_backward_0.1 = bf16[2048,768]{1,0:T(8,128)(2,1)} custom-call(s32[16]{0:T(128)} %pad_add_fusion.refs_0_, s32[8]{0:T(128)} %get-tuple-element.326.refs_1_, s32[8]{0:T(128)} %get-tuple-element.327.refs_2_, f32[2048,128]{1,0:T(8,128)} %get-tuple-element.328.refs_3_, f32[2048,128]{1,0:T(8,128)} %get-tuple-element.329.refs_4_, ...), custom_call_target="tpu_custom_call" | custom-call | flops 1048576 | bytes 65536 | tf_op jit(solution)/shard_map/attention_backward_0/pallas_call | solution.py:363
  512.7 4.6 convolution_convert_fusion.4
  534.1 5.5 convolution_convert_fusion.2
  548.5 9.1 %collective-permute-done.56 = bf16[256,1536]{1,0:T(8,128)(2,1)S(1)} collective-permute-done((bf16[256,1536]{1,0:T(8,128)(2,1)S(1)}, bf16[256,1536]{1,0:T(8,128)(2,1)S(1)}, u32[]{:S(2)}, u32[]{:S(2)}) %collective-permute-start.56) | collective-permute-done | bytes 786464 | tf_op jit(solution)/shard_map/ppermute | solution.py:626
  571.7 19.8 %collective-permute-done.63 = bf16[192,1024]{1,0:T(8,128)(2,1)} collective-permute-done((bf16[192,1024]{1,0:T(8,128)(2,1)S(1)}, bf16[192,1024]{1,0:T(8,128)(2,1)}, u32[]{:S(2)}, u32[]{:S(2)}) %collective-permute-start.63) | collective-permute-done | bytes 393248 | tf_op jit(solution)/shard_map/ppermute | solution.py:580
  603.4 5.1 collective-permute-done.64
  619.0 39.3 %psum.7 = f32[2,192]{1,0:T(2,128)S(1)} all-reduce(f32[2,192]{1,0:T(2,128)S(1)} %pad_maximum_fusion.17), channel_id=1, replica_groups=mesh['yx'=4,'core'=2,'zh'=2,'zl'=2] {'zh','zl'}, use_global_device_ids=true, to_apply=%region_11.12 | all-reduce | flops 384 | bytes 3072 | tf_op jit(solution)/shard_map/psum | solution.py:982
  (410 shorter events, 242.2 us)
Async XLA Ops:
  7.2 183.8 %all-gather.3.cloned.1.call-start = ((), (), s32[]{:S(2)}) async-start(), calls=%async_computation.3 | async-start | bytes 2949120 | tf_op jit(solution)/shard_map/all_gather | solution.py:781
  9.2 31.3 %collective-permute-start.2 = (bf16[192,768]{1,0:T(8,128)(2,1)}, bf16[192,768]{1,0:T(8,128)(2,1)}, u32[]{:S(2)}, u32[]{:S(2)}) collective-permute-start(bf16[192,768]{1,0:T(8,128)(2,1)} %pad_maximum_fusion.15), channel_id=1, source_target_pairs={{0,2},{6,4},{4,0},{2,6},{1,3},{7,5},{5,1},{3,7},{8,10},{14,12},{12... | collective-permute-start | bytes 884744 | tf_op jit(solution)/shard_map/ppermute | solution.py:580
  9.2 31.3 %collective-permute-start.3 = (bf16[192,768]{1,0:T(8,128)(2,1)}, bf16[192,768]{1,0:T(8,128)(2,1)}, u32[]{:S(2)}, u32[]{:S(2)}) collective-permute-start(bf16[192,768]{1,0:T(8,128)(2,1)} %pad_maximum_fusion.15), channel_id=1, source_target_pairs={{2,4},{4,2},{3,5},{5,3},{10,12},{12,10},{11,13},{13,11},{18,20},{2... | collective-permute-start | bytes 884744 | tf_op jit(solution)/shard_map/ppermute | solution.py:580
  12.3 26.8 %collective-permute-start = (bf16[256,1536]{1,0:T(8,128)(2,1)S(1)}, bf16[256,1536]{1,0:T(8,128)(2,1)S(1)}, u32[]{:S(2)}, u32[]{:S(2)}) collective-permute-start(bf16[256,1536]{1,0:T(8,128)(2,1)S(1)} %slice.182), channel_id=1, source_target_pairs={{2,4},{4,2},{3,5},{5,3},{10,12},{12,10},{11,13},{13,11},{18,20},{2... | collective-permute-start | bytes 2359304 | tf_op jit(solution)/shard_map/ppermute | solution.py:580
  41.8 36.1 %collective-permute-start.7 = (bf16[384,768]{1,0:T(8,128)(2,1)S(1)}, bf16[384,768]{1,0:T(8,128)(2,1)S(1)}, u32[]{:S(2)}, u32[]{:S(2)}) collective-permute-start(bf16[384,768]{1,0:T(8,128)(2,1)S(1)} %pad_maximum_fusion.11.refs_3_.refs_0_), channel_id=1, source_target_pairs={{0,8},{8,0},{16,24},{24,16},{1,9},{9,1},{17,25},{25,17},{2,10},{10... | collective-permute-start | bytes 1769480 | tf_op jit(solution)/shard_map/ppermute | solution.py:631
  43.4 34.6 %collective-permute-start.8 = (bf16[384,768]{1,0:T(8,128)(2,1)S(1)}, bf16[384,768]{1,0:T(8,128)(2,1)S(1)}, u32[]{:S(2)}, u32[]{:S(2)}) collective-permute-start(bf16[384,768]{1,0:T(8,128)(2,1)S(1)} %pad_maximum_fusion.11.refs_3_.refs_0_), channel_id=1, source_target_pairs={{0,16},{8,24},{16,0},{24,8},{1,17},{9,25},{17,1},{25,9},{2,18},{10... | collective-permute-start | bytes 1769480 | tf_op jit(solution)/shard_map/ppermute | solution.py:631
  45.2 32.7 %collective-permute-start.6 = (bf16[256,1536]{1,0:T(8,128)(2,1)}, bf16[256,1536]{1,0:T(8,128)(2,1)}, u32[]{:S(2)}, u32[]{:S(2)}) collective-permute-start(bf16[256,1536]{1,0:T(8,128)(2,1)} %get-tuple-element.190), channel_id=1, source_target_pairs={{1,0},{0,1},{3,2},{2,3},{5,4},{4,5},{7,6},{6,7},{9,8},{8,9},{11,10... | collective-permute-start | bytes 2359304 | tf_op jit(solution)/shard_map/ppermute | solution.py:621
  52.5 23.4 %collective-permute-start.4 = (bf16[256,1536]{1,0:T(8,128)(2,1)}, bf16[256,1536]{1,0:T(8,128)(2,1)}, u32[]{:S(2)}, u32[]{:S(2)}) collective-permute-start(bf16[256,1536]{1,0:T(8,128)(2,1)} %get-tuple-element.191), channel_id=1, source_target_pairs={{2,4},{4,2},{3,5},{5,3},{10,12},{12,10},{11,13},{13,11},{18,20},{2... | collective-permute-start | bytes 2359304 | tf_op jit(solution)/shard_map/ppermute | solution.py:580
  79.7 24.0 %collective-permute-start.10 = (bf16[256,1536]{1,0:T(8,128)(2,1)}, bf16[256,1536]{1,0:T(8,128)(2,1)}, u32[]{:S(2)}, u32[]{:S(2)}) collective-permute-start(bf16[256,1536]{1,0:T(8,128)(2,1)} %broadcast_select_fusion.6), channel_id=1, source_target_pairs={{1,0},{0,1},{3,2},{2,3},{5,4},{4,5},{7,6},{6,7},{9,8},{8,9},{11,10... | collective-permute-start | bytes 2359304 | tf_op jit(solution)/shard_map/ppermute | solution.py:621
  119.2 337.7 %reduce-scatter.4.cloned.1.call-start = ((), (), s32[]{:S(2)}) async-start(), calls=%async_computation.4 | async-start | bytes 7864320 | tf_op jit(solution)/shard_map/reduce_scatter | solution.py:895
  119.3 35.0 %collective-permute-start.17 = (bf16[192,2048]{1,0:T(8,128)(2,1)S(1)}, bf16[192,2048]{1,0:T(8,128)(2,1)S(1)}, u32[]{:S(2)}, u32[]{:S(2)}) collective-permute-start(bf16[192,2048]{1,0:T(8,128)(2,1)S(1)} %copy-done.19), channel_id=1, source_target_pairs={{0,2},{6,4},{4,0},{2,6},{1,3},{7,5},{5,1},{3,7},{8,10},{14,12},{12... | collective-permute-start | bytes 2359304 | tf_op jit(solution)/shard_map/ppermute | solution.py:580
  119.6 34.7 %collective-permute-start.18 = (bf16[192,2048]{1,0:T(8,128)(2,1)S(1)}, bf16[192,2048]{1,0:T(8,128)(2,1)S(1)}, u32[]{:S(2)}, u32[]{:S(2)}) collective-permute-start(bf16[192,2048]{1,0:T(8,128)(2,1)S(1)} %copy-done.19), channel_id=1, source_target_pairs={{2,4},{4,2},{3,5},{5,3},{10,12},{12,10},{11,13},{13,11},{18,20},{2... | collective-permute-start | bytes 2359304 | tf_op jit(solution)/shard_map/ppermute | solution.py:580
  154.6 36.3 %collective-permute-start.21 = (bf16[384,2048]{1,0:T(8,128)(2,1)S(1)}, bf16[384,2048]{1,0:T(8,128)(2,1)S(1)}, u32[]{:S(2)}, u32[]{:S(2)}) collective-permute-start(bf16[384,2048]{1,0:T(8,128)(2,1)S(1)} %pad_maximum_fusion.refs_2_.refs_4_), channel_id=1, source_target_pairs={{0,8},{8,0},{16,24},{24,16},{1,9},{9,1},{17,25},{25,17},{2,10},{10... | collective-permute-start | bytes 4718600 | tf_op jit(solution)/shard_map/ppermute | solution.py:631
  156.2 34.8 %collective-permute-start.22 = (bf16[384,2048]{1,0:T(8,128)(2,1)S(1)}, bf16[384,2048]{1,0:T(8,128)(2,1)}, u32[]{:S(2)}, u32[]{:S(2)}) collective-permute-start(bf16[384,2048]{1,0:T(8,128)(2,1)S(1)} %pad_maximum_fusion.refs_2_.refs_4_), channel_id=1, source_target_pairs={{0,16},{8,24},{16,0},{24,8},{1,17},{9,25},{17,1},{25,9},{2,18},{10... | collective-permute-start | bytes 4718600 | tf_op jit(solution)/shard_map/ppermute | solution.py:631
  156.4 25.6 %collective-permute-start.20 = (bf16[1024,384]{1,0:T(8,128)(2,1)}, bf16[1024,384]{1,0:T(8,128)(2,1)}, u32[]{:S(2)}, u32[]{:S(2)}) collective-permute-start(bf16[1024,384]{1,0:T(8,128)(2,1)} %get-tuple-element.227.refs_14_), channel_id=1, source_target_pairs={{0,1},{1,0},{2,3},{3,2},{4,5},{5,4},{6,7},{7,6},{8,9},{9,8},{10,11... | collective-permute-start | bytes 2359304 | tf_op jit(solution)/shard_map/ppermute | solution.py:626
  220.4 23.4 %collective-permute-start.27 = (bf16[256,1536]{1,0:T(8,128)(2,1)}, bf16[256,1536]{1,0:T(8,128)(2,1)}, u32[]{:S(2)}, u32[]{:S(2)}) collective-permute-start(bf16[256,1536]{1,0:T(8,128)(2,1)} %slice.197), channel_id=1, source_target_pairs={{2,4},{4,2},{3,5},{5,3},{10,12},{12,10},{11,13},{13,11},{18,20},{2... | collective-permute-start | bytes 2359304 | tf_op jit(solution)/shard_map/ppermute | solution.py:580
  223.8 27.1 %collective-permute-start.28 = (bf16[256,1536]{1,0:T(8,128)(2,1)}, bf16[256,1536]{1,0:T(8,128)(2,1)}, u32[]{:S(2)}, u32[]{:S(2)}) collective-permute-start(bf16[256,1536]{1,0:T(8,128)(2,1)} %slice.198), channel_id=1, source_target_pairs={{1,0},{0,1},{3,2},{2,3},{5,4},{4,5},{7,6},{6,7},{9,8},{8,9},{11,10... | collective-permute-start | bytes 2359304 | tf_op jit(solution)/shard_map/ppermute | solution.py:621
  254.0 42.8 %collective-permute-start.35 = (bf16[256,1536]{1,0:T(8,128)(2,1)}, bf16[256,1536]{1,0:T(8,128)(2,1)}, u32[]{:S(2)}, u32[]{:S(2)}) collective-permute-start(bf16[256,1536]{1,0:T(8,128)(2,1)} %slice_select_fusion), channel_id=1, source_target_pairs={{1,0},{0,1},{3,2},{2,3},{5,4},{4,5},{7,6},{6,7},{9,8},{8,9},{11,10... | collective-permute-start | bytes 2359304 | tf_op jit(solution)/shard_map/ppermute | solution.py:621
  256.6 40.2 %collective-permute-start.36 = (bf16[256,1536]{1,0:T(8,128)(2,1)}, bf16[256,1536]{1,0:T(8,128)(2,1)}, u32[]{:S(2)}, u32[]{:S(2)}) collective-permute-start(bf16[256,1536]{1,0:T(8,128)(2,1)} %slice.202), channel_id=1, source_target_pairs={{1,0},{0,1},{3,2},{2,3},{5,4},{4,5},{7,6},{6,7},{9,8},{8,9},{11,10... | collective-permute-start | bytes 2359304 | tf_op jit(solution)/shard_map/ppermute | solution.py:621
  386.1 120.4 %reduce-scatter.6.cloned.1.call-start = ((), (), s32[]{:S(2)}) async-start(), calls=%async_computation.5 | async-start | bytes 3932160 | tf_op jit(solution)/shard_map/reduce_scatter | solution.py:902
  411.3 159.4 %reduce-scatter.8.cloned.1.call-start = ((), (), s32[]{:S(2)}) async-start(), calls=%async_computation.6 | async-start | bytes 2949120 | tf_op jit(solution)/shard_map/reduce_scatter | solution.py:930
  456.9 53.8 %collective-permute-start.51 = (bf16[512,1536]{1,0:T(8,128)(2,1)}, bf16[512,1536]{1,0:T(8,128)(2,1)S(1)}, u32[]{:S(2)}, u32[]{:S(2)}) collective-permute-start(bf16[512,1536]{1,0:T(8,128)(2,1)} %add_convert_fusion.1), channel_id=1, source_target_pairs={{2,4},{4,2},{3,5},{5,3},{10,12},{12,10},{11,13},{13,11},{18,20},{2... | collective-permute-start | bytes 4718600 | tf_op jit(solution)/shard_map/ppermute | solution.py:580
  461.2 49.5 %collective-permute-start.52 = (bf16[192,2048]{1,0:T(8,128)(2,1)S(1)}, bf16[192,2048]{1,0:T(8,128)(2,1)S(1)}, u32[]{:S(2)}, u32[]{:S(2)}) collective-permute-start(bf16[192,2048]{1,0:T(8,128)(2,1)S(1)} %get-tuple-element.392), channel_id=1, source_target_pairs={{2,0},{4,6},{0,4},{6,2},{3,1},{5,7},{1,5},{7,3},{10,8},{12,14},{8,... | collective-permute-start | bytes 2359304 | tf_op jit(solution)/shard_map/ppermute | solution.py:580
  528.1 29.5 %collective-permute-start.56 = (bf16[256,1536]{1,0:T(8,128)(2,1)S(1)}, bf16[256,1536]{1,0:T(8,128)(2,1)S(1)}, u32[]{:S(2)}, u32[]{:S(2)}) collective-permute-start(bf16[256,1536]{1,0:T(8,128)(2,1)S(1)} %slice.219), channel_id=1, source_target_pairs={{0,1},{1,0},{2,3},{3,2},{4,5},{5,4},{6,7},{7,6},{8,9},{9,8},{10,11... | collective-permute-start | bytes 2359304 | tf_op jit(solution)/shard_map/ppermute | solution.py:626
  531.9 26.1 %collective-permute-start.55 = (bf16[192,2048]{1,0:T(8,128)(2,1)S(1)}, bf16[192,2048]{1,0:T(8,128)(2,1)S(1)}, u32[]{:S(2)}, u32[]{:S(2)}) collective-permute-start(bf16[192,2048]{1,0:T(8,128)(2,1)S(1)} %copy-done.39), channel_id=1, source_target_pairs={{2,4},{4,2},{3,5},{5,3},{10,12},{12,10},{11,13},{13,11},{18,20},{2... | collective-permute-start | bytes 2359304 | tf_op jit(solution)/shard_map/ppermute | solution.py:580
  559.0 32.5 %collective-permute-start.61 = (bf16[384,768]{1,0:T(8,128)(2,1)}, bf16[384,768]{1,0:T(8,128)(2,1)}, u32[]{:S(2)}, u32[]{:S(2)}) collective-permute-start(bf16[384,768]{1,0:T(8,128)(2,1)} %pad_maximum_fusion.14), channel_id=1, source_target_pairs={{0,16},{8,24},{16,0},{24,8},{1,17},{9,25},{17,1},{25,9},{2,18},{10... | collective-permute-start | bytes 1769480 | tf_op jit(solution)/shard_map/ppermute | solution.py:631
  561.3 30.2 %collective-permute-start.60 = (bf16[384,768]{1,0:T(8,128)(2,1)}, bf16[384,768]{1,0:T(8,128)(2,1)}, u32[]{:S(2)}, u32[]{:S(2)}) collective-permute-start(bf16[384,768]{1,0:T(8,128)(2,1)} %pad_maximum_fusion.13), channel_id=1, source_target_pairs={{0,8},{8,0},{16,24},{24,16},{1,9},{9,1},{17,25},{25,17},{2,10},{10... | collective-permute-start | bytes 1769480 | tf_op jit(solution)/shard_map/ppermute | solution.py:631
  563.1 28.5 %collective-permute-start.59 = (bf16[256,1536]{1,0:T(8,128)(2,1)}, bf16[256,1536]{1,0:T(8,128)(2,1)S(1)}, u32[]{:S(2)}, u32[]{:S(2)}) collective-permute-start(bf16[256,1536]{1,0:T(8,128)(2,1)} %slice.222), channel_id=1, source_target_pairs={{0,1},{1,0},{2,3},{3,2},{4,5},{5,4},{6,7},{7,6},{8,9},{9,8},{10,11... | collective-permute-start | bytes 2359304 | tf_op jit(solution)/shard_map/ppermute | solution.py:626
  566.1 25.5 %collective-permute-start.63 = (bf16[192,1024]{1,0:T(8,128)(2,1)S(1)}, bf16[192,1024]{1,0:T(8,128)(2,1)}, u32[]{:S(2)}, u32[]{:S(2)}) collective-permute-start(bf16[192,1024]{1,0:T(8,128)(2,1)S(1)} %get-tuple-element.401), channel_id=1, source_target_pairs={{2,4},{4,2},{3,5},{5,3},{10,12},{12,10},{11,13},{13,11},{18,20},{2... | collective-permute-start | bytes 1179656 | tf_op jit(solution)/shard_map/ppermute | solution.py:580
  609.3 51.2 %collective-permute-start.67 = (bf16[512,1536]{1,0:T(8,128)(2,1)S(1)}, bf16[512,1536]{1,0:T(8,128)(2,1)}, u32[]{:S(2)}, u32[]{:S(2)}) collective-permute-start(bf16[512,1536]{1,0:T(8,128)(2,1)S(1)} %fusion.5), channel_id=1, source_target_pairs={{2,4},{4,2},{3,5},{5,3},{10,12},{12,10},{11,13},{13,11},{18,20},{2... | collective-permute-start | bytes 4718600 | tf_op jit(solution)/shard_map/ppermute | solution.py:580
  615.4 44.3 %collective-permute-start.68 = (bf16[192,384]{1,0:T(8,128)(2,1)}, bf16[192,384]{1,0:T(8,128)(2,1)S(1)}, u32[]{:S(2)}, u32[]{:S(2)}) collective-permute-start(bf16[192,384]{1,0:T(8,128)(2,1)} %get-tuple-element.365), channel_id=1, source_target_pairs={{2,0},{4,6},{0,4},{6,2},{3,1},{5,7},{1,5},{7,3},{10,8},{12,14},{8,... | collective-permute-start | bytes 442376 | tf_op jit(solution)/shard_map/ppermute | solution.py:580
  615.4 44.3 %collective-permute-start.69 = (bf16[192,384]{1,0:T(8,128)(2,1)S(1)}, bf16[192,384]{1,0:T(8,128)(2,1)S(1)}, u32[]{:S(2)}, u32[]{:S(2)}) collective-permute-start(bf16[192,384]{1,0:T(8,128)(2,1)S(1)} %get-tuple-element.366), channel_id=1, source_target_pairs={{2,4},{4,2},{3,5},{5,3},{10,12},{12,10},{11,13},{13,11},{18,20},{2... | collective-permute-start | bytes 442376 | tf_op jit(solution)/shard_map/ppermute | solution.py:580
  (119 other events, 1727.7 us)
Sparse Core Ops, SparseCore 0:
  119.3 39.4 all-gather.2
  386.2 70.6 reduce-scatter.3
  459.9 43.9 reduce-scatter.5
  517.5 40.7 reduce-scatter.7

commit v9 on v8

--- a/solution.py
+++ b/solution.py
@@ -972,7 +972,6 @@
     for part in out_moved:
         out_quarter = out_quarter + part.astype(f32)
     out_keep, out_give = give_z(out_quarter.astype(bf16))
-    input_own, out_keep, out_give, *project_home = stage(input_own, out_keep, out_give, *project_home)
     out_home = [crossed(out_give, BACK), crossed(out_keep, CROSS)]
     input_grad = jnp.where(straight(), input_own, crossed(input_own, CROSS)).astype(f32)
     grad_project = sum_z(project_keep, *project_home)

time: 680 us -> 676 us (level)
  transfers between devices with their start and end apart: 74 -> 74, of which waited for: 33 -> 32; matrix products, arithmetic and copies ran while one was open for 21% -> 21% of each run, Pallas kernels for 26% -> 26%
where the time goes in v9:
time: 676 us; the launch traced here: 666 us
  Pallas kernels  175 us (26%)
  waiting for transfers between devices  157 us (23%)
  starting transfers between devices  96.3 us (14%)
  other arithmetic  65.4 us (10%)
  matrix products  59.1 us (9%)
  local copies, waits for them, and re-layouts  49.1 us (7%)
  blocking collectives  48.9 us (7%)
  between operations  15.6 us (2%)
    pallas_call x6, Pallas kernels, piece_call(): pl.pallas_call(functools.partial(kernel, count, tuple((where for _, where...  97.1 us
    ppermute x23, waiting for transfers between devices, crossed(): return lax.ppermute(x, ('core', 'zh'), perm)  73.8 us
    pallas_call x1, Pallas kernels, attend_back(): pl.pallas_call(functools.partial(backward_kernel, pieces, ratio, bool(ear...  45 us
    ppermute x23, starting transfers between devices, crossed(): return lax.ppermute(x, ('core', 'zh'), perm)  41 us
    dot_general x5, matrix products, rows_product(): lax.dot_general(left, right, (((0,), (0,)), ((), ())), preferred_element_...  40.4 us
    psum x1, blocking collectives, body(): lax.psum(jnp.stack([jnp.sum(qkv_shard.astype(f32) * grad_project, axis=1)...  39.5 us
    ppermute x10, waiting for transfers between devices, to_near(): return lax.ppermute(x, 'zl', [(j, (j + k) % n) for j in range(n)])  33.2 us
    pallas_call x1, Pallas kernels, attend(): pl.pallas_call(functools.partial(forward_kernel, pieces, ratio), out_shap...  29.4 us
  transfers between devices with their start and end apart: 74, of which 32 were waited for; matrix products, arithmetic and copies ran while one was open for 21% of the time, Pallas kernels for 26%

profile of v9, /device:TPU:16, one launch (start us, length us, event | category | flops | bytes accessed | tf_op | source)
XLA Modules:
  0.0 666.1 jit_solution(16378756978877696514)
XLA Ops:
  12.3 4.7 collective-permute-start
  20.8 9.3 %all-gather = bf16[8,192,2]{1,2,0:T(2,128)(2,1)S(1)} all-gather(bf16[1,192,2]{1,2,0:T(2,128)(2,1)S(1)} %fusion.27), channel_id=1, replica_groups=mesh['yx'=4,'core'=2,'zh'=2,'zl'=2] {'yx','core'}, dimensions={0}, use_global_device_ids=true | all-gather | bytes 6912 | tf_op jit(solution)/shard_map/all_gather | solution.py:722
  30.9 8.3 %collective-permute-done.1 = s32[1,4]{1,0:T(1,128)S(1)} collective-permute-done((s32[1,4]{1,0:T(1,128)}, s32[1,4]{1,0:T(1,128)S(1)}, u32[]{:S(2)}, u32[]{:S(2)}) %collective-permute-start.1) | collective-permute-done | bytes 48 | tf_op jit(solution)/shard_map/ppermute | solution.py:580
  45.2 5.8 collective-permute-start.6
  62.7 13.1 %collective-permute-done.4 = bf16[256,1536]{1,0:T(8,128)(2,1)} collective-permute-done((bf16[256,1536]{1,0:T(8,128)(2,1)}, bf16[256,1536]{1,0:T(8,128)(2,1)}, u32[]{:S(2)}, u32[]{:S(2)}) %collective-permute-start.4) | collective-permute-done | bytes 786464 | tf_op jit(solution)/shard_map/ppermute | solution.py:580
  94.9 8.7 %project_0.1 = (bf16[2048,1536]{1,0:T(8,128)(2,1)}, bf16[2048,768]{1,0:T(8,128)(2,1)}) custom-call(s32[1]{0:T(128)} %bitcast.7.me, bf16[512,1536]{1,0:T(8,128)(2,1)} %copy-done.2, bf16[512,1536]{1,0:T(8,128)(2,1)} %collective-permute-done.11.refs_1_, f32[1,1536]{1,0:T(1,128)} %get-tuple-element.405.refs_2_, bf16[384,768]{1,0:T(8,128)(2,1)} %copy-done.16, ...), custom_call_target="tpu_custom_call" | custom-call | flops 1048576 | bytes 65536 | tf_op jit(solution)/shard_map/project_0/pallas_call | solution.py:522
  108.5 8.5 %project_1.1 = (bf16[2048,1536]{1,0:T(8,128)(2,1)}, bf16[2048,768]{1,0:T(8,128)(2,1)}) custom-call(s32[1]{0:T(128)} %bitcast.7.me, bf16[512,1536]{1,0:T(8,128)(2,1)} %copy-done.31, bf16[512,1536]{1,0:T(8,128)(2,1)} %collective-permute-done.14.refs_1_, f32[1,1536]{1,0:T(1,128)} %get-tuple-element.405.refs_2_, ...), custom_call_target="tpu_custom_call", output_to_operand_aliasing={{0}: (9, {}), {1}: (10, {})} | custom-call | flops 1048576 | bytes 65536 | tf_op jit(solution)/shard_map/project_1/pallas_call | solution.py:522
  124.8 29.4 %attention_forward.1 = (bf16[1024,384]{1,0:T(8,128)(2,1)}, bf16[1024,384]{1,0:T(8,128)(2,1)}, f32[4,1,1024]{2,1,0:T(1,128)}, f32[4,1,1024]{2,1,0:T(1,128)}) custom-call(s32[16]{0:T(128)} %pad_add_fusion.refs_0_, s32[4]{0:T(128)} %get-tuple-element.200.refs_1_, s32[4]{0:T(128)} %get-tuple-element.201.refs_2_, f32[2048,128]{1,0:T(8,128)} %get-tuple-element.323.refs_3_, ...), custom_call_target="tpu_custom_call" | custom-call | flops 1048576 | bytes 65536 | tf_op jit(solution)/shard_map/attention_forward/pallas_call | solution.py:333
  156.4 4.6 collective-permute-start.20
  166.3 15.6 %collective-permute-done.19 = bf16[192,1024]{1,0:T(8,128)(2,1)S(1)} collective-permute-done((bf16[192,1024]{1,0:T(8,128)(2,1)S(1)}, bf16[192,1024]{1,0:T(8,128)(2,1)S(1)}, u32[]{:S(2)}, u32[]{:S(2)}) %collective-permute-start.19) | collective-permute-done | bytes 393248 | tf_op jit(solution)/shard_map/ppermute | solution.py:580
  182.0 8.9 %collective-permute-done.21.refs_3_.refs_5_ = bf16[384,2048]{1,0:T(8,128)(2,1)S(1)} collective-permute-done((bf16[384,2048]{1,0:T(8,128)(2,1)S(1)}, bf16[384,2048]{1,0:T(8,128)(2,1)S(1)}, u32[]{:S(2)}, u32[]{:S(2)}) %collective-permute-start.21) | collective-permute-done | bytes 1572896 | tf_op jit(solution)/shard_map/ppermute | solution.py:631
  205.2 11.3 %collective-permute-done.24 = bf16[256,1536]{1,0:T(8,128)(2,1)S(1)} collective-permute-done((bf16[256,1536]{1,0:T(8,128)(2,1)S(1)}, bf16[256,1536]{1,0:T(8,128)(2,1)S(1)}, u32[]{:S(2)}, u32[]{:S(2)}) %collective-permute-start.24) | collective-permute-done | bytes 786464 | tf_op jit(solution)/shard_map/ppermute | solution.py:580
  223.8 4.8 collective-permute-start.28
  229.9 13.9 %gate_0.1 = (bf16[2048,1536]{1,0:T(8,128)(2,1)}, f32[2048,2048]{1,0:T(8,128)}, bf16[2048,1024]{1,0:T(8,128)(2,1)}) custom-call(s32[1]{0:T(128)} %bitcast.7.me, bf16[512,1536]{1,0:T(8,128)(2,1)} %copy-done.8, bf16[512,1536]{1,0:T(8,128)(2,1)} %collective-permute-done.31.refs_1_, bf16[384,2048]{1,0:T(8,128)(2,1)} %copy-done, bf16[384,2048]{1,0:T(8,128)(2,1)} %copy-done.1, ...), custom_call_target="tpu_custom_call" | custom-call | flops 1048576 | bytes 65536 | tf_op jit(solution)/shard_map/gate_0/pallas_call | solution.py:522
  243.8 7.1 %collective-permute-done.28 = bf16[256,1536]{1,0:T(8,128)(2,1)} collective-permute-done((bf16[256,1536]{1,0:T(8,128)(2,1)}, bf16[256,1536]{1,0:T(8,128)(2,1)}, u32[]{:S(2)}, u32[]{:S(2)}) %collective-permute-start.28) | collective-permute-done | bytes 786464 | tf_op jit(solution)/shard_map/ppermute | solution.py:621
  264.2 4.8 collective-permute-done.33.refs_12_.refs_10_
  271.7 25.2 %gate_back_0.1 = (bf16[2048,1536]{1,0:T(8,128)(2,1)}, bf16[2048,2048]{1,0:T(8,128)(2,1)}, bf16[512,1536]{1,0:T(8,128)(2,1)}, bf16[512,1536]{1,0:T(8,128)(2,1)}, ...) custom-call(s32[1]{0:T(128)} %bitcast.7.me, bf16[512,1536]{1,0:T(8,128)(2,1)} %copy-done.7, ...), custom_call_target="tpu_custom_call" | custom-call | flops 1048576 | bytes 65536 | tf_op jit(solution)/shard_map/gate_back_0/pallas_call | solution.py:522
  302.7 19.3 %gate_1.1 = (bf16[2048,1536]{1,0:T(8,128)(2,1)}, f32[2048,2048]{1,0:T(8,128)}, bf16[2048,1024]{1,0:T(8,128)(2,1)}, bf16[512,1536]{1,0:T(8,128)(2,1)}, bf16[512,1536]{1,0:T(8,128)(2,1)}) custom-call(s32[1]{0:T(128)} %bitcast.7.me, ...), custom_call_target="tpu_custom_call", output_to_operand_aliasing={{0}: (13, {}), {1}: (14, {}), {2}: (15, {})} | custom-call | flops 1048576 | bytes 65536 | tf_op jit(solution)/shard_map/gate_1/pallas_call | solution.py:522
  331.3 21.4 %gate_back_1.1 = (bf16[2048,1536]{1,0:T(8,128)(2,1)}, bf16[2048,2048]{1,0:T(8,128)(2,1)}, bf16[512,1536]{1,0:T(8,128)(2,1)}, bf16[512,1536]{1,0:T(8,128)(2,1)}) custom-call(s32[1]{0:T(128)} %bitcast.7.me, bf16[512,1536]{1,0:T(8,128)(2,1)} %copy-done.26, bf16[512,1536]{1,0:T(8,128)(2,1)} %copy-done.44, ...), custom_call_target="tpu_custom_call", output_to_operand_aliasing={{0}: (15, {}), {1}: (16, {})} | custom-call | flops 1048576 | bytes 65536 | tf_op jit(solution)/shard_map/gate_back_1/pallas_call | solution.py:522
  358.2 7.2 %collective-permute-done.43 = bf16[128,1536]{1,0:T(8,128)(2,1)S(1)} collective-permute-done((bf16[128,1536]{1,0:T(8,128)(2,1)S(1)}, bf16[128,1536]{1,0:T(8,128)(2,1)S(1)}, u32[]{:S(2)}, u32[]{:S(2)}) %collective-permute-start.43) | collective-permute-done | bytes 393248 | tf_op jit(solution)/shard_map/ppermute | solution.py:626
  366.9 19.2 %convolution_convert_fusion = bf16[1536,2048]{1,0:T(8,128)(2,1)} fusion(bf16[2048,1536]{1,0:T(8,128)(2,1)} %get-tuple-element.274, bf16[2048,2048]{1,0:T(8,128)(2,1)} %get-tuple-element.296), kind=kOutput, calls=%fused_computation | convolution fusion | flops 12888047616 | bytes 20971520 | tf_op jit(solution)/shard_map/dot_general | solution.py:63
  389.9 11.2 %convolution_convert_fusion.1 = bf16[1536,1024]{1,0:T(8,128)(2,1)} fusion(bf16[2048,1536]{1,0:T(8,128)(2,1)} %get-tuple-element.301, bf16[2048,1024]{1,0:T(8,128)(2,1)} %get-tuple-element.281.refs_3_), kind=kOutput, calls=%fused_computation.6 | convolution fusion | flops 6444023808 | bytes 13631488 | tf_op jit(solution)/shard_map/dot_general | solution.py:63
  403.6 5.0 collective-permute-done.46
  411.5 6.1 fusion.28
  441.5 8.4 %collective-permute-done.50.refs_12_ = bf16[1024,384]{1,0:T(8,128)(2,1)} collective-permute-done((bf16[1024,384]{1,0:T(8,128)(2,1)}, bf16[1024,384]{1,0:T(8,128)(2,1)}, u32[]{:S(2)}, u32[]{:S(2)}) %collective-permute-start.50) | collective-permute-done | bytes 786464 | tf_op jit(solution)/shard_map/ppermute | solution.py:626
  449.9 7.1 %reduce-scatter.4.cloned.1.call-done = bf16[384,2048]{1,0:T(8,128)(2,1)} async-done(((bf16[1536,2048]{1,0:T(8,128)(2,1)}), bf16[384,2048]{1,0:T(8,128)(2,1)}) %reduce-scatter.4.cloned.1.call-update) | async-done | bytes 1572880 | tf_op jit(solution)/shard_map/reduce_scatter | solution.py:895
  461.4 45.0 %attention_backward_0.1 = bf16[2048,768]{1,0:T(8,128)(2,1)} custom-call(s32[16]{0:T(128)} %pad_add_fusion.refs_0_, s32[8]{0:T(128)} %get-tuple-element.321.refs_1_, s32[8]{0:T(128)} %get-tuple-element.322.refs_2_, f32[2048,128]{1,0:T(8,128)} %get-tuple-element.323.refs_3_, f32[2048,128]{1,0:T(8,128)} %get-tuple-element.324.refs_4_, ...), custom_call_target="tpu_custom_call" | custom-call | flops 1048576 | bytes 65536 | tf_op jit(solution)/shard_map/attention_backward_0/pallas_call | solution.py:363
  512.7 4.6 convolution_convert_fusion.4
  534.1 5.5 convolution_convert_fusion.2
  548.5 9.1 %collective-permute-done.56 = bf16[256,1536]{1,0:T(8,128)(2,1)S(1)} collective-permute-done((bf16[256,1536]{1,0:T(8,128)(2,1)S(1)}, bf16[256,1536]{1,0:T(8,128)(2,1)S(1)}, u32[]{:S(2)}, u32[]{:S(2)}) %collective-permute-start.56) | collective-permute-done | bytes 786464 | tf_op jit(solution)/shard_map/ppermute | solution.py:626
  571.7 19.8 %collective-permute-done.63 = bf16[192,1024]{1,0:T(8,128)(2,1)} collective-permute-done((bf16[192,1024]{1,0:T(8,128)(2,1)S(1)}, bf16[192,1024]{1,0:T(8,128)(2,1)}, u32[]{:S(2)}, u32[]{:S(2)}) %collective-permute-start.63) | collective-permute-done | bytes 393248 | tf_op jit(solution)/shard_map/ppermute | solution.py:580
  614.2 39.5 %psum.7 = f32[2,192]{1,0:T(2,128)S(1)} all-reduce(f32[2,192]{1,0:T(2,128)S(1)} %pad_maximum_fusion.17), channel_id=1, replica_groups=mesh['yx'=4,'core'=2,'zh'=2,'zl'=2] {'zh','zl'}, use_global_device_ids=true, to_apply=%region_11.12 | all-reduce | flops 384 | bytes 3072 | tf_op jit(solution)/shard_map/psum | solution.py:981
  (410 shorter events, 238.0 us)
Async XLA Ops:
  7.2 183.8 %all-gather.3.cloned.1.call-start = ((), (), s32[]{:S(2)}) async-start(), calls=%async_computation.3 | async-start | bytes 2949120 | tf_op jit(solution)/shard_map/all_gather | solution.py:781
  9.2 31.3 %collective-permute-start.2 = (bf16[192,768]{1,0:T(8,128)(2,1)}, bf16[192,768]{1,0:T(8,128)(2,1)}, u32[]{:S(2)}, u32[]{:S(2)}) collective-permute-start(bf16[192,768]{1,0:T(8,128)(2,1)} %pad_maximum_fusion.15), channel_id=1, source_target_pairs={{0,2},{6,4},{4,0},{2,6},{1,3},{7,5},{5,1},{3,7},{8,10},{14,12},{12... | collective-permute-start | bytes 884744 | tf_op jit(solution)/shard_map/ppermute | solution.py:580
  9.2 31.3 %collective-permute-start.3 = (bf16[192,768]{1,0:T(8,128)(2,1)}, bf16[192,768]{1,0:T(8,128)(2,1)}, u32[]{:S(2)}, u32[]{:S(2)}) collective-permute-start(bf16[192,768]{1,0:T(8,128)(2,1)} %pad_maximum_fusion.15), channel_id=1, source_target_pairs={{2,4},{4,2},{3,5},{5,3},{10,12},{12,10},{11,13},{13,11},{18,20},{2... | collective-permute-start | bytes 884744 | tf_op jit(solution)/shard_map/ppermute | solution.py:580
  12.3 26.8 %collective-permute-start = (bf16[256,1536]{1,0:T(8,128)(2,1)S(1)}, bf16[256,1536]{1,0:T(8,128)(2,1)S(1)}, u32[]{:S(2)}, u32[]{:S(2)}) collective-permute-start(bf16[256,1536]{1,0:T(8,128)(2,1)S(1)} %slice.182), channel_id=1, source_target_pairs={{2,4},{4,2},{3,5},{5,3},{10,12},{12,10},{11,13},{13,11},{18,20},{2... | collective-permute-start | bytes 2359304 | tf_op jit(solution)/shard_map/ppermute | solution.py:580
  41.8 36.1 %collective-permute-start.7 = (bf16[384,768]{1,0:T(8,128)(2,1)S(1)}, bf16[384,768]{1,0:T(8,128)(2,1)S(1)}, u32[]{:S(2)}, u32[]{:S(2)}) collective-permute-start(bf16[384,768]{1,0:T(8,128)(2,1)S(1)} %pad_maximum_fusion.11.refs_3_.refs_0_), channel_id=1, source_target_pairs={{0,8},{8,0},{16,24},{24,16},{1,9},{9,1},{17,25},{25,17},{2,10},{10... | collective-permute-start | bytes 1769480 | tf_op jit(solution)/shard_map/ppermute | solution.py:631
  43.4 34.6 %collective-permute-start.8 = (bf16[384,768]{1,0:T(8,128)(2,1)S(1)}, bf16[384,768]{1,0:T(8,128)(2,1)S(1)}, u32[]{:S(2)}, u32[]{:S(2)}) collective-permute-start(bf16[384,768]{1,0:T(8,128)(2,1)S(1)} %pad_maximum_fusion.11.refs_3_.refs_0_), channel_id=1, source_target_pairs={{0,16},{8,24},{16,0},{24,8},{1,17},{9,25},{17,1},{25,9},{2,18},{10... | collective-permute-start | bytes 1769480 | tf_op jit(solution)/shard_map/ppermute | solution.py:631
  45.2 32.7 %collective-permute-start.6 = (bf16[256,1536]{1,0:T(8,128)(2,1)}, bf16[256,1536]{1,0:T(8,128)(2,1)}, u32[]{:S(2)}, u32[]{:S(2)}) collective-permute-start(bf16[256,1536]{1,0:T(8,128)(2,1)} %get-tuple-element.185), channel_id=1, source_target_pairs={{1,0},{0,1},{3,2},{2,3},{5,4},{4,5},{7,6},{6,7},{9,8},{8,9},{11,10... | collective-permute-start | bytes 2359304 | tf_op jit(solution)/shard_map/ppermute | solution.py:621
  52.5 23.4 %collective-permute-start.4 = (bf16[256,1536]{1,0:T(8,128)(2,1)}, bf16[256,1536]{1,0:T(8,128)(2,1)}, u32[]{:S(2)}, u32[]{:S(2)}) collective-permute-start(bf16[256,1536]{1,0:T(8,128)(2,1)} %get-tuple-element.186), channel_id=1, source_target_pairs={{2,4},{4,2},{3,5},{5,3},{10,12},{12,10},{11,13},{13,11},{18,20},{2... | collective-permute-start | bytes 2359304 | tf_op jit(solution)/shard_map/ppermute | solution.py:580
  79.7 24.0 %collective-permute-start.10 = (bf16[256,1536]{1,0:T(8,128)(2,1)}, bf16[256,1536]{1,0:T(8,128)(2,1)}, u32[]{:S(2)}, u32[]{:S(2)}) collective-permute-start(bf16[256,1536]{1,0:T(8,128)(2,1)} %broadcast_select_fusion.6), channel_id=1, source_target_pairs={{1,0},{0,1},{3,2},{2,3},{5,4},{4,5},{7,6},{6,7},{9,8},{8,9},{11,10... | collective-permute-start | bytes 2359304 | tf_op jit(solution)/shard_map/ppermute | solution.py:621
  119.2 337.7 %reduce-scatter.4.cloned.1.call-start = ((), (), s32[]{:S(2)}) async-start(), calls=%async_computation.4 | async-start | bytes 7864320 | tf_op jit(solution)/shard_map/reduce_scatter | solution.py:895
  119.3 35.0 %collective-permute-start.17 = (bf16[192,2048]{1,0:T(8,128)(2,1)S(1)}, bf16[192,2048]{1,0:T(8,128)(2,1)S(1)}, u32[]{:S(2)}, u32[]{:S(2)}) collective-permute-start(bf16[192,2048]{1,0:T(8,128)(2,1)S(1)} %copy-done.19), channel_id=1, source_target_pairs={{0,2},{6,4},{4,0},{2,6},{1,3},{7,5},{5,1},{3,7},{8,10},{14,12},{12... | collective-permute-start | bytes 2359304 | tf_op jit(solution)/shard_map/ppermute | solution.py:580
  119.6 34.7 %collective-permute-start.18 = (bf16[192,2048]{1,0:T(8,128)(2,1)S(1)}, bf16[192,2048]{1,0:T(8,128)(2,1)S(1)}, u32[]{:S(2)}, u32[]{:S(2)}) collective-permute-start(bf16[192,2048]{1,0:T(8,128)(2,1)S(1)} %copy-done.19), channel_id=1, source_target_pairs={{2,4},{4,2},{3,5},{5,3},{10,12},{12,10},{11,13},{13,11},{18,20},{2... | collective-permute-start | bytes 2359304 | tf_op jit(solution)/shard_map/ppermute | solution.py:580
  154.6 36.3 %collective-permute-start.21 = (bf16[384,2048]{1,0:T(8,128)(2,1)S(1)}, bf16[384,2048]{1,0:T(8,128)(2,1)S(1)}, u32[]{:S(2)}, u32[]{:S(2)}) collective-permute-start(bf16[384,2048]{1,0:T(8,128)(2,1)S(1)} %pad_maximum_fusion.refs_2_.refs_4_), channel_id=1, source_target_pairs={{0,8},{8,0},{16,24},{24,16},{1,9},{9,1},{17,25},{25,17},{2,10},{10... | collective-permute-start | bytes 4718600 | tf_op jit(solution)/shard_map/ppermute | solution.py:631
  156.2 34.8 %collective-permute-start.22 = (bf16[384,2048]{1,0:T(8,128)(2,1)S(1)}, bf16[384,2048]{1,0:T(8,128)(2,1)}, u32[]{:S(2)}, u32[]{:S(2)}) collective-permute-start(bf16[384,2048]{1,0:T(8,128)(2,1)S(1)} %pad_maximum_fusion.refs_2_.refs_4_), channel_id=1, source_target_pairs={{0,16},{8,24},{16,0},{24,8},{1,17},{9,25},{17,1},{25,9},{2,18},{10... | collective-permute-start | bytes 4718600 | tf_op jit(solution)/shard_map/ppermute | solution.py:631
  156.4 25.6 %collective-permute-start.20 = (bf16[1024,384]{1,0:T(8,128)(2,1)}, bf16[1024,384]{1,0:T(8,128)(2,1)}, u32[]{:S(2)}, u32[]{:S(2)}) collective-permute-start(bf16[1024,384]{1,0:T(8,128)(2,1)} %get-tuple-element.222.refs_14_), channel_id=1, source_target_pairs={{0,1},{1,0},{2,3},{3,2},{4,5},{5,4},{6,7},{7,6},{8,9},{9,8},{10,11... | collective-permute-start | bytes 2359304 | tf_op jit(solution)/shard_map/ppermute | solution.py:626
  220.4 23.4 %collective-permute-start.27 = (bf16[256,1536]{1,0:T(8,128)(2,1)}, bf16[256,1536]{1,0:T(8,128)(2,1)}, u32[]{:S(2)}, u32[]{:S(2)}) collective-permute-start(bf16[256,1536]{1,0:T(8,128)(2,1)} %slice.197), channel_id=1, source_target_pairs={{2,4},{4,2},{3,5},{5,3},{10,12},{12,10},{11,13},{13,11},{18,20},{2... | collective-permute-start | bytes 2359304 | tf_op jit(solution)/shard_map/ppermute | solution.py:580
  223.8 27.1 %collective-permute-start.28 = (bf16[256,1536]{1,0:T(8,128)(2,1)}, bf16[256,1536]{1,0:T(8,128)(2,1)}, u32[]{:S(2)}, u32[]{:S(2)}) collective-permute-start(bf16[256,1536]{1,0:T(8,128)(2,1)} %slice.198), channel_id=1, source_target_pairs={{1,0},{0,1},{3,2},{2,3},{5,4},{4,5},{7,6},{6,7},{9,8},{8,9},{11,10... | collective-permute-start | bytes 2359304 | tf_op jit(solution)/shard_map/ppermute | solution.py:621
  254.0 42.8 %collective-permute-start.35 = (bf16[256,1536]{1,0:T(8,128)(2,1)}, bf16[256,1536]{1,0:T(8,128)(2,1)}, u32[]{:S(2)}, u32[]{:S(2)}) collective-permute-start(bf16[256,1536]{1,0:T(8,128)(2,1)} %slice_select_fusion), channel_id=1, source_target_pairs={{1,0},{0,1},{3,2},{2,3},{5,4},{4,5},{7,6},{6,7},{9,8},{8,9},{11,10... | collective-permute-start | bytes 2359304 | tf_op jit(solution)/shard_map/ppermute | solution.py:621
  256.6 40.2 %collective-permute-start.36 = (bf16[256,1536]{1,0:T(8,128)(2,1)}, bf16[256,1536]{1,0:T(8,128)(2,1)}, u32[]{:S(2)}, u32[]{:S(2)}) collective-permute-start(bf16[256,1536]{1,0:T(8,128)(2,1)} %slice.202), channel_id=1, source_target_pairs={{1,0},{0,1},{3,2},{2,3},{5,4},{4,5},{7,6},{6,7},{9,8},{8,9},{11,10... | collective-permute-start | bytes 2359304 | tf_op jit(solution)/shard_map/ppermute | solution.py:621
  386.1 120.3 %reduce-scatter.6.cloned.1.call-start = ((), (), s32[]{:S(2)}) async-start(), calls=%async_computation.5 | async-start | bytes 3932160 | tf_op jit(solution)/shard_map/reduce_scatter | solution.py:902
  411.3 159.4 %reduce-scatter.8.cloned.1.call-start = ((), (), s32[]{:S(2)}) async-start(), calls=%async_computation.6 | async-start | bytes 2949120 | tf_op jit(solution)/shard_map/reduce_scatter | solution.py:930
  456.9 53.8 %collective-permute-start.51 = (bf16[512,1536]{1,0:T(8,128)(2,1)}, bf16[512,1536]{1,0:T(8,128)(2,1)S(1)}, u32[]{:S(2)}, u32[]{:S(2)}) collective-permute-start(bf16[512,1536]{1,0:T(8,128)(2,1)} %add_convert_fusion.1), channel_id=1, source_target_pairs={{2,4},{4,2},{3,5},{5,3},{10,12},{12,10},{11,13},{13,11},{18,20},{2... | collective-permute-start | bytes 4718600 | tf_op jit(solution)/shard_map/ppermute | solution.py:580
  461.2 49.5 %collective-permute-start.52 = (bf16[192,2048]{1,0:T(8,128)(2,1)S(1)}, bf16[192,2048]{1,0:T(8,128)(2,1)S(1)}, u32[]{:S(2)}, u32[]{:S(2)}) collective-permute-start(bf16[192,2048]{1,0:T(8,128)(2,1)S(1)} %get-tuple-element.382), channel_id=1, source_target_pairs={{2,0},{4,6},{0,4},{6,2},{3,1},{5,7},{1,5},{7,3},{10,8},{12,14},{8,... | collective-permute-start | bytes 2359304 | tf_op jit(solution)/shard_map/ppermute | solution.py:580
  528.1 29.5 %collective-permute-start.56 = (bf16[256,1536]{1,0:T(8,128)(2,1)S(1)}, bf16[256,1536]{1,0:T(8,128)(2,1)S(1)}, u32[]{:S(2)}, u32[]{:S(2)}) collective-permute-start(bf16[256,1536]{1,0:T(8,128)(2,1)S(1)} %slice.219), channel_id=1, source_target_pairs={{0,1},{1,0},{2,3},{3,2},{4,5},{5,4},{6,7},{7,6},{8,9},{9,8},{10,11... | collective-permute-start | bytes 2359304 | tf_op jit(solution)/shard_map/ppermute | solution.py:626
  531.9 26.1 %collective-permute-start.55 = (bf16[192,2048]{1,0:T(8,128)(2,1)S(1)}, bf16[192,2048]{1,0:T(8,128)(2,1)S(1)}, u32[]{:S(2)}, u32[]{:S(2)}) collective-permute-start(bf16[192,2048]{1,0:T(8,128)(2,1)S(1)} %copy-done.39), channel_id=1, source_target_pairs={{2,4},{4,2},{3,5},{5,3},{10,12},{12,10},{11,13},{13,11},{18,20},{2... | collective-permute-start | bytes 2359304 | tf_op jit(solution)/shard_map/ppermute | solution.py:580
  559.0 32.5 %collective-permute-start.61 = (bf16[384,768]{1,0:T(8,128)(2,1)}, bf16[384,768]{1,0:T(8,128)(2,1)}, u32[]{:S(2)}, u32[]{:S(2)}) collective-permute-start(bf16[384,768]{1,0:T(8,128)(2,1)} %pad_maximum_fusion.14), channel_id=1, source_target_pairs={{0,16},{8,24},{16,0},{24,8},{1,17},{9,25},{17,1},{25,9},{2,18},{10... | collective-permute-start | bytes 1769480 | tf_op jit(solution)/shard_map/ppermute | solution.py:631
  561.3 30.2 %collective-permute-start.60 = (bf16[384,768]{1,0:T(8,128)(2,1)}, bf16[384,768]{1,0:T(8,128)(2,1)}, u32[]{:S(2)}, u32[]{:S(2)}) collective-permute-start(bf16[384,768]{1,0:T(8,128)(2,1)} %pad_maximum_fusion.13), channel_id=1, source_target_pairs={{0,8},{8,0},{16,24},{24,16},{1,9},{9,1},{17,25},{25,17},{2,10},{10... | collective-permute-start | bytes 1769480 | tf_op jit(solution)/shard_map/ppermute | solution.py:631
  563.1 28.5 %collective-permute-start.59 = (bf16[256,1536]{1,0:T(8,128)(2,1)}, bf16[256,1536]{1,0:T(8,128)(2,1)S(1)}, u32[]{:S(2)}, u32[]{:S(2)}) collective-permute-start(bf16[256,1536]{1,0:T(8,128)(2,1)} %slice.222), channel_id=1, source_target_pairs={{0,1},{1,0},{2,3},{3,2},{4,5},{5,4},{6,7},{7,6},{8,9},{9,8},{10,11... | collective-permute-start | bytes 2359304 | tf_op jit(solution)/shard_map/ppermute | solution.py:626
  566.1 25.5 %collective-permute-start.63 = (bf16[192,1024]{1,0:T(8,128)(2,1)S(1)}, bf16[192,1024]{1,0:T(8,128)(2,1)}, u32[]{:S(2)}, u32[]{:S(2)}) collective-permute-start(bf16[192,1024]{1,0:T(8,128)(2,1)S(1)} %get-tuple-element.391), channel_id=1, source_target_pairs={{2,4},{4,2},{3,5},{5,3},{10,12},{12,10},{11,13},{13,11},{18,20},{2... | collective-permute-start | bytes 1179656 | tf_op jit(solution)/shard_map/ppermute | solution.py:580
  604.1 51.8 %collective-permute-start.64 = (bf16[512,1536]{1,0:T(8,128)(2,1)S(1)}, bf16[512,1536]{1,0:T(8,128)(2,1)}, u32[]{:S(2)}, u32[]{:S(2)}) collective-permute-start(bf16[512,1536]{1,0:T(8,128)(2,1)S(1)} %fusion.5), channel_id=1, source_target_pairs={{2,4},{4,2},{3,5},{5,3},{10,12},{12,10},{11,13},{13,11},{18,20},{2... | collective-permute-start | bytes 4718600 | tf_op jit(solution)/shard_map/ppermute | solution.py:580
  610.6 44.5 %collective-permute-start.68 = (bf16[192,384]{1,0:T(8,128)(2,1)S(1)}, bf16[192,384]{1,0:T(8,128)(2,1)S(1)}, u32[]{:S(2)}, u32[]{:S(2)}) collective-permute-start(bf16[192,384]{1,0:T(8,128)(2,1)S(1)} %get-tuple-element.404), channel_id=1, source_target_pairs={{2,0},{4,6},{0,4},{6,2},{3,1},{5,7},{1,5},{7,3},{10,8},{12,14},{8,... | collective-permute-start | bytes 442376 | tf_op jit(solution)/shard_map/ppermute | solution.py:580
  610.7 44.4 %collective-permute-start.69 = (bf16[192,384]{1,0:T(8,128)(2,1)S(1)}, bf16[192,384]{1,0:T(8,128)(2,1)S(1)}, u32[]{:S(2)}, u32[]{:S(2)}) collective-permute-start(bf16[192,384]{1,0:T(8,128)(2,1)S(1)} %get-tuple-element.403), channel_id=1, source_target_pairs={{2,4},{4,2},{3,5},{5,3},{10,12},{12,10},{11,13},{13,11},{18,20},{2... | collective-permute-start | bytes 442376 | tf_op jit(solution)/shard_map/ppermute | solution.py:580
  (119 other events, 1694.3 us)
Sparse Core Ops, SparseCore 0:
  119.3 39.4 all-gather.2
  386.2 70.6 reduce-scatter.3
  459.9 43.9 reduce-scatter.5
  517.5 40.7 reduce-scatter.7
